TPU v7x, 32 devices: a whole 2x2x4 slice. The times are simulated.
32 devices in a mesh: fluid: 2 (over core), zon: 8 (over z, x), mer: 2 (over y).
Axes of the slice: x: 2, y: 2, z: 4, core: 2. Of those that a mesh axis runs over, the one named last changes fastest.
Arguments:
- state: float32 [2, 2, 64, 128, 256], P('fluid', None, None, 'zon', 'mer'), may hold values from -6 to 6
- flow: bfloat16 [2, 2, 64, 128, 256], P('fluid', None, None, 'zon', 'mer'), may hold values from -0.5 to 0.5
- diffusion: float32 [2, 2, 64], P('fluid'), may hold values from 0.02 to 0.2
- column_solve: float32 [2, 64, 64], P('fluid'), may hold values from -1 to 1, as said below
- exchange_rate: float32 [2, 2], P('fluid'), may hold values from 0.2 to 0.6
- block_map: int32 [8], P('mer'), may hold values from 0 to 7, as said below
- ice_mask: int32 [8], P('mer'), may hold values from 0 to 1
Outputs:
- final_state: float32 [2, 2, 64, 128, 256], P('fluid', None, None, 'zon', 'mer')
Inputs may be any that keep to these rules, and one draw needn't show every extreme that they name: `column_solve`: entries of the vertical inverses lie within this range; their diagonal is positive. `block_map`: each meridional section of 4 blocks, blocks k * 4 to (k + 1) * 4 - 1, is mapped onto itself by a permutation.
All inputs are finite; a program needn't handle non-finite values.
Results may differ from a plain program's by a relative error of at most 0.0003.
Values may be sent and summed in bfloat16 or wider, within the bound.
No kernel may reach another device: no remote copies, remote signals or barrier semaphores. Data moves between devices by JAX's collectives and lax.ppermute only.
A program may use at most 64 MiB of HBM per device.

v0:
```python
import jax
import jax.numpy as jnp
from jax import lax
from jax.sharding import PartitionSpec as P

STEPS = 2


def with_halo(cells, sides, width, closed):
    for axis, dim in sides:
        count = lax.axis_size(axis)
        ends = count if closed else count - 1
        head = lax.slice_in_dim(cells, 0, width, axis=dim)
        tail = lax.slice_in_dim(cells, cells.shape[dim] - width, cells.shape[dim], axis=dim)
        cells = jnp.concatenate(
            [
                lax.ppermute(tail, axis, [(i, (i + 1) % count) for i in range(ends)]),
                cells,
                lax.ppermute(head, axis, [((i + 1) % count, i) for i in range(ends)]),
            ],
            axis=dim,
        )
    return cells


def swapped(block, axis, distance):
    count = lax.axis_size(axis)
    route = []
    for low in range(count):
        high = low | 1 << distance
        if high != low and high < count:
            route += [(low, high), (high, low)]
    return lax.ppermute(block, axis, route)


def advance(
    extended,
    flow_frame,
    viscous,
    vertical,
    coupling,
    local_map,
    inverse,
    open_cols,
    level_pick,
    fluid_id,
):
    padded = with_halo(extended, (("mer", 3),), 1, False)
    centre = padded[:, :, 1:-1, 1:-1]
    east_cell = padded[:, :, 2:, 1:-1]
    west_cell = padded[:, :, :-2, 1:-1]
    north_cell = padded[:, :, 1:-1, 2:]
    south_cell = padded[:, :, 1:-1, :-2]
    levels = centre.shape[1]
    columns = centre.shape[2]
    merid_cols = centre.shape[3]
    block_count = local_map.shape[0]
    block_width = merid_cols // block_count
    own_rows = jnp.where(fluid_id == 0, centre[:, levels - 1], centre[:, 0])
    other_rows = swapped(own_rows, "fluid", 0)
    atm_rows = jnp.where(fluid_id == 0, own_rows, other_rows).reshape(
        -1, columns, block_count, block_width
    )
    ocean_rows = jnp.where(fluid_id == 0, other_rows, own_rows).reshape(
        -1, columns, block_count, block_width
    )
    zonal_flow = flow_frame[0].astype(jnp.float32)
    merid_flow = flow_frame[1].astype(jnp.float32)
    updated = (
        centre
        - 0.5 * zonal_flow * (east_cell - west_cell)
        - 0.5 * merid_flow * (north_cell - south_cell)
        + viscous * (east_cell + west_cell + north_cell + south_cell - 4.0 * centre)
    )
    mapped = jnp.take(atm_rows, local_map, axis=2)
    surface_flux = (mapped - ocean_rows) * open_cols[None, None, :, None]
    returned = jnp.take(surface_flux, inverse, axis=2)
    scaled = coupling[:, None, None, None]
    increment = jnp.where(fluid_id == 0, -scaled * returned, scaled * surface_flux).reshape(
        -1, columns, merid_cols
    )
    updated = updated + level_pick[None, :, None, None] * increment[:, None]
    return jnp.einsum(
        "kl,tlxy->tkxy",
        vertical,
        updated,
        precision=lax.Precision.HIGHEST,
        preferred_element_type=jnp.float32,
    )


def on_device(state, flow, diffusion, column_solve, exchange_rate, block_map, ice_mask):
    tracer_field = state[0]
    flow_local = flow[0]
    levels = tracer_field.shape[1]
    fluid_id = lax.axis_index("fluid")
    block_count = block_map.shape[0]
    local_map = block_map - lax.axis_index("mer") * block_count
    positions = jnp.arange(block_count, dtype=jnp.int32)
    inverse = jnp.sum(
        positions[:, None] * (local_map[:, None] == positions[None, :]).astype(jnp.int32), axis=0
    )
    open_cols = (1 - ice_mask).astype(jnp.float32)
    surface_level = jnp.where(fluid_id == 0, levels - 1, 0).astype(jnp.int32)
    level_pick = (jnp.arange(levels, dtype=jnp.int32) == surface_level).astype(jnp.float32)
    viscous = diffusion[0][:, :, None, None]
    vertical = column_solve[0]
    coupling = exchange_rate[0]
    for step_index in range(STEPS):
        extended = with_halo(tracer_field, (("zon", 2),), 1, True)
        tracer_field = advance(
            extended,
            flow_local,
            viscous,
            vertical,
            coupling,
            local_map,
            inverse,
            open_cols,
            level_pick,
            fluid_id,
        )
    return tracer_field[None]


def solution(mesh):
    return jax.shard_map(
        on_device,
        mesh=mesh,
        in_specs=(
            P("fluid", None, None, "zon", "mer"),
            P("fluid", None, None, "zon", "mer"),
            P("fluid", None, None),
            P("fluid", None, None),
            P("fluid", None),
            P("mer"),
            P("mer"),
        ),
        out_specs=P("fluid", None, None, "zon", "mer"),
        check_vma=False,
    )
```

profile of v0, /device:TPU:0, one launch (start us, length us, event | category | flops | bytes accessed | tf_op | source)
XLA Modules:
  0.0 63.3 jit_solution(14105102485151757328)
XLA Ops:
  0.0 0.0 copy-start.11
  0.0 1.4 %copy.128 = f32[1,2,64,16,128]{4,3,1,2,0:T(8,128)S(1)} copy(f32[1,2,64,16,128]{4,3,2,1,0:T(8,128)} %param.9) | data formatting | bytes 2097152 | tf_op args[0]
  1.5 0.5 collective-permute-start.4
  2.0 0.1 fusion.12
  2.1 5.6 %collective-permute-start = (f32[2,64,1,128]{3,2,0,1:T(1,128)S(1)}, f32[2,64,1,128]{3,2,0,1:T(1,128)S(1)}, u32[]{:S(2)}, u32[]{:S(2)}) collective-permute-start(f32[2,64,1,128]{3,2,0,1:T(1,128)S(1)} %get-tuple-element.15), channel_id=1, source_target_pairs={{2,0},{4,2},{6,4},{8,6},{10,8},{12,10},{14,12},{0,14},{3,1},{5,3},... | collective-permute-start | bytes 196616 | tf_op jit(solution)/shard_map/ppermute | solution.py:19
  7.7 0.0 collective-permute-start.1
  7.7 0.0 copy-start.4
  7.7 0.1 select_reduce_fusion
  7.8 0.5 compare_and_fusion
  8.4 0.5 bitcast_negate_fusion
  9.0 0.0 copy-done.1
  9.0 0.9 %multiply_bitcast_fusion.1 = (f32[64,16,128]{2,1,0:T(8,128)S(1)}, f32[64,16,128]{2,1,0:T(8,128)}) fusion(bf16[1,2,64,16,128]{4,3,2,1,0:T(8,128)(2,1)S(1)} %copy-done.1), kind=kLoop, calls=%fused_computation.30 | loop fusion | flops 524288 | bytes 1572864 | tf_op jit(solution)/shard_map/mul | solution.py:71
  9.8 0.5 compare_convert_fusion
  10.4 0.1 copy.95
  10.5 0.0 collective-permute-done.4
  10.5 0.1 reshape.61
  10.6 0.1 reshape.62
  10.7 0.6 gather_fusion
  11.3 0.1 fusion.5
  11.4 0.6 gather_fusion.1
  11.9 0.0 collective-permute-done
  11.9 2.7 %collective-permute-done.1 = f32[2,64,1,128]{3,2,0,1:T(1,128)S(1)} collective-permute-done((f32[2,64,1,128]{3,2,0,1:T(1,128)S(1)}, f32[2,64,1,128]{3,2,0,1:T(1,128)S(1)}, u32[]{:S(2)}, u32[]{:S(2)}) %collective-permute-start.1) | collective-permute-done | bytes 65568 | tf_op jit(solution)/shard_map/ppermute | solution.py:17
  14.7 0.3 pad_maximum_fusion
  14.9 1.7 %fusion.10 = (f32[2,64,18,1]{3,2,0,1:T(8,128)S(1)}, f32[2,64,18,1]{3,2,0,1:T(8,128)}) fusion(f32[2,64,18,128]{3,2,0,1:T(8,128)S(1)} %pad_maximum_fusion), kind=kLoop, calls=%fused_computation.61 | loop fusion | bytes 36864 | tf_op jit(solution)/shard_map/slice | solution.py:14
  16.6 1.9 %copy.91 = f32[2,64,18,1]{1,0,3,2:T(2,128)S(1)} copy(f32[2,64,18,1]{3,2,0,1:T(8,128)} %get-tuple-element.11) | data formatting | bytes 18432 | tf_op jit(solution)/shard_map/slice | solution.py:13
  18.5 1.3 %collective-permute-start.2 = (f32[2,64,18,1]{1,0,3,2:T(2,128)S(1)}, f32[2,64,18,1]{1,0,3,2:T(2,128)S(1)}, u32[]{:S(2)}, u32[]{:S(2)}) collective-permute-start(f32[2,64,18,1]{1,0,3,2:T(2,128)S(1)} %copy.91), channel_id=1, source_target_pairs={{1,0},{3,2},{5,4},{7,6},{9,8},{11,10},{13,12},{15,14},{17,16},{19,... | collective-permute-start | bytes 27656 | tf_op jit(solution)/shard_map/ppermute | solution.py:19
  19.8 0.5 copy.93
  20.4 4.5 %collective-permute-start.3 = (f32[2,64,18,1]{1,0,3,2:T(2,128)S(1)}, f32[2,64,18,1]{1,0,3,2:T(2,128)S(1)}, u32[]{:S(2)}, u32[]{:S(2)}) collective-permute-start(f32[2,64,18,1]{1,0,3,2:T(2,128)S(1)} %copy.93), channel_id=1, source_target_pairs={{0,1},{2,3},{4,5},{6,7},{8,9},{10,11},{12,13},{14,15},{16,17},{18,... | collective-permute-start | bytes 27656 | tf_op jit(solution)/shard_map/ppermute | solution.py:17
  24.9 0.7 %fusion.4 = f32[2,16,4,32]{3,1,0,2:T(8,128)S(1)} fusion(f32[4,2,16,32]{3,2,1,0:T(8,128)S(1)} %gather_fusion.1, f32[2,16,4,32]{3,1,0,2:T(8,128)S(1)} %fusion.5, f32[2]{0:T(128)} %bitcast.53, f32[2]{0:T(128)} %bitcast_negate_fusion, pred[4]{0:T(512)(128)(4,1)} %compare_and_fusion, pred[]{:T(512)S(6)} %eq.16), kind=kLoop, calls=%fused_computation.36 | loop fusion | flops 16384 | bytes 49173 | tf_op jit(solution)/shard_map/jit(_where)/select_n | solution.py:79
  25.7 0.1 mul.175
  25.8 0.0 collective-permute-done.2
  25.8 0.7 %copy.92 = f32[2,64,18,1]{3,2,0,1:T(8,128)S(1)} copy(f32[2,64,18,1]{1,0,3,2:T(2,128)S(1)} %collective-permute-done.2) | data formatting | bytes 18432 | tf_op jit(solution)/shard_map/ppermute | solution.py:19
  26.5 0.0 collective-permute-done.3
  26.6 1.8 %copy.94 = f32[2,64,18,1]{3,2,0,1:T(8,128)} copy(f32[2,64,18,1]{1,0,3,2:T(2,128)S(1)} %collective-permute-done.3) | data formatting | bytes 18432 | tf_op jit(solution)/shard_map/ppermute | solution.py:17
  28.4 3.1 %multiply_add_fusion.1 = f32[2,64,16,128]{3,2,0,1:T(8,128)S(1)} fusion(f32[2,64,16,128]{3,2,0,1:T(8,128)S(1)} %bitcast.50, f32[2,64,18,1]{3,2,0,1:T(8,128)S(1)} %copy.92, f32[2,64,1,128]{3,2,0,1:T(1,128)S(1)} %collective-permute-done, f32[2,64,1,128]{3,2,0,1:T(1,128)S(1)} %collective-permute-done.1, f32[2,64,18,1]{3,2,0,1:T(8,128)} %copy.94, ...), kind=kLoop, calls=%fused_computation.28 | loop fusion | flops 6029312 | bytes 3312384 | tf_op jit(solution)/shard_map/add | solution.py:82
  31.5 1.7 %convolution_bitcast_fusion.1 = f32[2,64,16,128]{3,1,2,0:T(8,128)S(1)} fusion(f32[2,64,16,128]{3,2,0,1:T(8,128)S(1)} %multiply_add_fusion.1, f32[1,64,64]{2,1,0:T(8,128)S(1)} %copy-done), kind=kOutput, calls=%fused_computation.7 | convolution fusion | flops 201326592 | bytes 2113536 | tf_op jit(solution)/shard_map/kl,tlxy->tkxy/dot_general | solution.py:83
  33.2 0.6 copy.105
  33.8 0.1 collective-permute-start.9
  33.9 0.1 fusion.11
  34.0 2.1 %collective-permute-start.5 = (f32[2,64,1,128]{3,2,0,1:T(1,128)S(1)}, f32[2,64,1,128]{3,2,0,1:T(1,128)S(1)}, u32[]{:S(2)}, u32[]{:S(2)}) collective-permute-start(f32[2,64,1,128]{3,2,0,1:T(1,128)S(1)} %get-tuple-element.13), channel_id=1, source_target_pairs={{2,0},{4,2},{6,4},{8,6},{10,8},{12,10},{14,12},{0,14},{3,1},{5,3},... | collective-permute-start | bytes 196616 | tf_op jit(solution)/shard_map/ppermute | solution.py:19
  36.1 0.0 collective-permute-start.6
  36.1 0.0 collective-permute-done.9
  36.1 0.1 reshape.63
  36.2 0.7 %gather_fusion.2 = f32[4,2,16,32]{3,2,1,0:T(8,128)S(1)} fusion(f32[2,16,4,32]{3,1,2,0:T(8,128)S(1)} %copy.113, s32[1024]{0:T(1024)} %copy-done.3), kind=kCustom, calls=%fused_computation.2.clone | custom fusion | bytes 32784 | tf_op jit(solution)/shard_map/jit(_take)/gather | solution.py:75
  36.9 0.1 reshape.64
  37.0 0.1 fusion.3
  37.1 0.7 %gather_fusion.3 = f32[4,2,16,32]{3,2,1,0:T(8,128)S(1)} fusion(f32[2,16,4,32]{3,1,2,0:T(8,128)S(1)} %copy.115, s32[1024]{0:T(1024)} %copy-done.2), kind=kCustom, calls=%fused_computation.3.clone | custom fusion | bytes 32784 | tf_op jit(solution)/shard_map/jit(_take)/gather | solution.py:77
  37.8 0.8 %collective-permute-done.5 = f32[2,64,1,128]{3,2,0,1:T(1,128)S(1)} collective-permute-done((f32[2,64,1,128]{3,2,0,1:T(1,128)S(1)}, f32[2,64,1,128]{3,2,0,1:T(1,128)S(1)}, u32[]{:S(2)}, u32[]{:S(2)}) %collective-permute-start.5) | collective-permute-done | bytes 65568 | tf_op jit(solution)/shard_map/ppermute | solution.py:19
  38.6 4.5 %collective-permute-done.6 = f32[2,64,1,128]{3,2,0,1:T(1,128)S(1)} collective-permute-done((f32[2,64,1,128]{3,2,0,1:T(1,128)S(1)}, f32[2,64,1,128]{3,2,0,1:T(1,128)S(1)}, u32[]{:S(2)}, u32[]{:S(2)}) %collective-permute-start.6) | collective-permute-done | bytes 65568 | tf_op jit(solution)/shard_map/ppermute | solution.py:17
  43.1 0.3 pad_maximum_fusion.1
  43.3 1.7 %fusion.9 = (f32[2,64,18,1]{3,2,0,1:T(8,128)S(1)}, f32[2,64,18,1]{3,2,0,1:T(8,128)}) fusion(f32[2,64,18,128]{3,2,0,1:T(8,128)S(1)} %pad_maximum_fusion.1), kind=kLoop, calls=%fused_computation.60 | loop fusion | bytes 36864 | tf_op jit(solution)/shard_map/slice | solution.py:14
  45.0 1.9 %copy.107 = f32[2,64,18,1]{1,0,3,2:T(2,128)S(1)} copy(f32[2,64,18,1]{3,2,0,1:T(8,128)} %get-tuple-element.9) | data formatting | bytes 18432 | tf_op jit(solution)/shard_map/slice | solution.py:13
  46.9 1.3 %collective-permute-start.7 = (f32[2,64,18,1]{1,0,3,2:T(2,128)S(1)}, f32[2,64,18,1]{1,0,3,2:T(2,128)S(1)}, u32[]{:S(2)}, u32[]{:S(2)}) collective-permute-start(f32[2,64,18,1]{1,0,3,2:T(2,128)S(1)} %copy.107), channel_id=1, source_target_pairs={{1,0},{3,2},{5,4},{7,6},{9,8},{11,10},{13,12},{15,14},{17,16},{19,... | collective-permute-start | bytes 27656 | tf_op jit(solution)/shard_map/ppermute | solution.py:19
  48.2 0.5 copy.109
  48.7 4.7 %collective-permute-start.8 = (f32[2,64,18,1]{1,0,3,2:T(2,128)S(1)}, f32[2,64,18,1]{1,0,3,2:T(2,128)S(1)}, u32[]{:S(2)}, u32[]{:S(2)}) collective-permute-start(f32[2,64,18,1]{1,0,3,2:T(2,128)S(1)} %copy.109), channel_id=1, source_target_pairs={{0,1},{2,3},{4,5},{6,7},{8,9},{10,11},{12,13},{14,15},{16,17},{18,... | collective-permute-start | bytes 27656 | tf_op jit(solution)/shard_map/ppermute | solution.py:17
  53.5 0.7 %fusion.2 = f32[2,16,4,32]{3,1,0,2:T(8,128)S(1)} fusion(f32[4,2,16,32]{3,2,1,0:T(8,128)S(1)} %gather_fusion.3, f32[2,16,4,32]{3,1,0,2:T(8,128)S(1)} %fusion.3, f32[2]{0:T(128)} %bitcast.54, f32[2]{0:T(128)} %bitcast_negate_fusion, pred[4]{0:T(512)(128)(4,1)} %compare_and_fusion, pred[]{:T(512)S(6)} %eq.16), kind=kLoop, calls=%fused_computation.32 | loop fusion | flops 16384 | bytes 49173 | tf_op jit(solution)/shard_map/jit(_where)/select_n | solution.py:79
  54.3 0.1 mul.185
  54.4 0.0 collective-permute-done.7
  54.4 0.7 %copy.108 = f32[2,64,18,1]{3,2,0,1:T(8,128)S(1)} copy(f32[2,64,18,1]{1,0,3,2:T(2,128)S(1)} %collective-permute-done.7) | data formatting | bytes 18432 | tf_op jit(solution)/shard_map/ppermute | solution.py:19
  55.1 0.0 collective-permute-done.8
  55.1 1.8 %copy.110 = f32[2,64,18,1]{3,2,0,1:T(8,128)} copy(f32[2,64,18,1]{1,0,3,2:T(2,128)S(1)} %collective-permute-done.8) | data formatting | bytes 18432 | tf_op jit(solution)/shard_map/ppermute | solution.py:17
  56.9 3.1 %multiply_add_fusion = f32[2,64,16,128]{3,2,0,1:T(8,128)S(1)} fusion(f32[2,64,16,128]{3,2,0,1:T(8,128)S(1)} %copy.105, f32[2,64,18,1]{3,2,0,1:T(8,128)S(1)} %copy.108, f32[2,64,1,128]{3,2,0,1:T(1,128)S(1)} %collective-permute-done.5, f32[2,64,1,128]{3,2,0,1:T(1,128)S(1)} %collective-permute-done.6, f32[2,64,18,1]{3,2,0,1:T(8,128)} %copy.110, ...), kind=kLoop, calls=%fused_computation.27 | loop fusion | flops 6029312 | bytes 3312384 | tf_op jit(solution)/shard_map/add | solution.py:82
  60.0 1.7 %convolution_bitcast_fusion = f32[1,2,64,16,128]{4,2,3,1,0:T(8,128)S(1)} fusion(f32[2,64,16,128]{3,2,0,1:T(8,128)S(1)} %multiply_add_fusion, f32[1,64,64]{2,1,0:T(8,128)S(1)} %copy-done), kind=kOutput, calls=%fused_computation.6 | convolution fusion | flops 201326592 | bytes 2113536 | tf_op jit(solution)/shard_map/kl,tlxy->tkxy/dot_general | solution.py:83
  61.7 1.6 %copy.118 = f32[1,2,64,16,128]{4,3,2,1,0:T(8,128)} copy(f32[1,2,64,16,128]{4,2,3,1,0:T(8,128)S(1)} %convolution_bitcast_fusion) | data formatting | bytes 2097152 | tf_op jit(solution)/shard_map/broadcast_in_dim | solution.py:123
  (41 shorter events, 0.2 us)
Async XLA Ops:
  0.0 31.5 %copy-start = (f32[1,64,64]{2,1,0:T(8,128)S(1)}, f32[1,64,64]{2,1,0:T(8,128)}, u32[]{:S(2)}) copy-start(f32[1,64,64]{2,1,0:T(8,128)} %param.12) | copy-start | bytes 49156
  0.0 7.7 %copy-start.12 = (s32[4]{0:T(128)S(1)}, s32[4]{0:T(128)}, u32[]{:S(2)}) copy-start(s32[4]{0:T(128)} %param.14) | copy-start | bytes 52
  0.0 8.4 %copy-start.13 = (s32[4]{0:T(128)S(1)}, s32[4]{0:T(128)}, u32[]{:S(2)}) copy-start(s32[4]{0:T(128)} %param.15) | copy-start | bytes 52
  0.0 8.4 %copy-start.6 = (f32[1,2]{1,0:T(1,128)S(1)}, f32[1,2]{1,0:T(1,128)}, u32[]{:S(2)}) copy-start(f32[1,2]{1,0:T(1,128)} %param.13) | copy-start | bytes 28
  0.0 9.0 %copy-start.1 = (bf16[1,2,64,16,128]{4,3,2,1,0:T(8,128)(2,1)S(1)}, bf16[1,2,64,16,128]{4,3,2,1,0:T(8,128)(2,1)}, u32[]{:S(2)}) copy-start(bf16[1,2,64,16,128]{4,3,2,1,0:T(8,128)(2,1)} %param.10) | copy-start | bytes 1572868
  0.0 10.4 %copy-start.11 = (f32[1,2,64]{2,1,0:T(2,128)S(1)}, f32[1,2,64]{2,1,0:T(2,128)}, u32[]{:S(2)}) copy-start(f32[1,2,64]{2,1,0:T(2,128)} %param.11) | copy-start | bytes 1540
  1.5 9.0 %collective-permute-start.4 = (f32[2,16,128]{2,1,0:T(8,128)S(1)}, f32[2,16,128]{2,1,0:T(8,128)S(1)}, u32[]{:S(2)}, u32[]{:S(2)}) collective-permute-start(f32[2,16,128]{2,1,0:T(8,128)S(1)} %fusion.8), channel_id=1, source_target_pairs={{0,16},{16,0},{1,17},{17,1},{2,18},{18,2},{3,19},{19,3},{4,20},{20... | collective-permute-start | bytes 49160 | tf_op jit(solution)/shard_map/ppermute | solution.py:33
  2.1 9.8 %collective-permute-start = (f32[2,64,1,128]{3,2,0,1:T(1,128)S(1)}, f32[2,64,1,128]{3,2,0,1:T(1,128)S(1)}, u32[]{:S(2)}, u32[]{:S(2)}) collective-permute-start(f32[2,64,1,128]{3,2,0,1:T(1,128)S(1)} %get-tuple-element.15), channel_id=1, source_target_pairs={{2,0},{4,2},{6,4},{8,6},{10,8},{12,10},{14,12},{0,14},{3,1},{5,3},... | collective-permute-start | bytes 196616 | tf_op jit(solution)/shard_map/ppermute | solution.py:19
  7.7 7.0 %collective-permute-start.1 = (f32[2,64,1,128]{3,2,0,1:T(1,128)S(1)}, f32[2,64,1,128]{3,2,0,1:T(1,128)S(1)}, u32[]{:S(2)}, u32[]{:S(2)}) collective-permute-start(f32[2,64,1,128]{3,2,0,1:T(1,128)S(1)} %get-tuple-element.14), channel_id=1, source_target_pairs={{0,2},{2,4},{4,6},{6,8},{8,10},{10,12},{12,14},{14,0},{1,3},{3,5},... | collective-permute-start | bytes 196616 | tf_op jit(solution)/shard_map/ppermute | solution.py:17
  7.7 6.9 %copy-start.4 = (pred[4]{0:T(512)(128)(4,1)}, pred[4]{0:T(512)(128)(4,1)S(1)}, u32[]{:S(2)}) copy-start(pred[4]{0:T(512)(128)(4,1)S(1)} %get-tuple-element.6) | copy-start | bytes 16
  8.4 6.3 %copy-start.3 = (s32[1024]{0:T(1024)}, s32[1024]{0:T(1024)S(1)}, u32[]{:S(2)}) copy-start(s32[1024]{0:T(1024)S(1)} %pad_clamp_fusion.1) | copy-start | bytes 12292
  8.4 6.3 %copy-start.9 = (f32[4]{0:T(128)}, f32[4]{0:T(128)S(1)}, u32[]{:S(2)}) copy-start(f32[4]{0:T(128)S(1)} %subtract_convert_fusion) | copy-start | bytes 52
  8.4 6.3 %copy-start.2 = (s32[1024]{0:T(1024)}, s32[1024]{0:T(1024)S(1)}, u32[]{:S(2)}) copy-start(s32[1024]{0:T(1024)S(1)} %pad_clamp_fusion) | copy-start | bytes 12292
  18.5 7.3 %collective-permute-start.2 = (f32[2,64,18,1]{1,0,3,2:T(2,128)S(1)}, f32[2,64,18,1]{1,0,3,2:T(2,128)S(1)}, u32[]{:S(2)}, u32[]{:S(2)}) collective-permute-start(f32[2,64,18,1]{1,0,3,2:T(2,128)S(1)} %copy.91), channel_id=1, source_target_pairs={{1,0},{3,2},{5,4},{7,6},{9,8},{11,10},{13,12},{15,14},{17,16},{19,... | collective-permute-start | bytes 27656 | tf_op jit(solution)/shard_map/ppermute | solution.py:19
  20.4 6.2 %collective-permute-start.3 = (f32[2,64,18,1]{1,0,3,2:T(2,128)S(1)}, f32[2,64,18,1]{1,0,3,2:T(2,128)S(1)}, u32[]{:S(2)}, u32[]{:S(2)}) collective-permute-start(f32[2,64,18,1]{1,0,3,2:T(2,128)S(1)} %copy.93), channel_id=1, source_target_pairs={{0,1},{2,3},{4,5},{6,7},{8,9},{10,11},{12,13},{14,15},{16,17},{18,... | collective-permute-start | bytes 27656 | tf_op jit(solution)/shard_map/ppermute | solution.py:17
  25.8 2.6 %copy-start.7 = (f32[64]{0:T(128)S(1)}, f32[64]{0:T(128)}, u32[]{:S(2)}) copy-start(f32[64]{0:T(128)} %compare_convert_fusion) | copy-start | bytes 772
  33.2 3.8 %copy-start.5 = (pred[4]{0:T(512)(128)(4,1)S(1)}, pred[4]{0:T(512)(128)(4,1)}, u32[]{:S(2)}) copy-start(pred[4]{0:T(512)(128)(4,1)} %copy-done.4) | copy-start | bytes 16
  33.2 3.8 %copy-start.10 = (f32[4]{0:T(128)S(1)}, f32[4]{0:T(128)}, u32[]{:S(2)}) copy-start(f32[4]{0:T(128)} %copy-done.9) | copy-start | bytes 52
  33.8 2.3 %collective-permute-start.9 = (f32[2,16,128]{2,1,0:T(8,128)S(1)}, f32[2,16,128]{2,1,0:T(8,128)S(1)}, u32[]{:S(2)}, u32[]{:S(2)}) collective-permute-start(f32[2,16,128]{2,1,0:T(8,128)S(1)} %bitcast.51), channel_id=1, source_target_pairs={{0,16},{16,0},{1,17},{17,1},{2,18},{18,2},{3,19},{19,3},{4,20},{20... | collective-permute-start | bytes 49160 | tf_op jit(solution)/shard_map/ppermute | solution.py:33
  34.0 4.5 %collective-permute-start.5 = (f32[2,64,1,128]{3,2,0,1:T(1,128)S(1)}, f32[2,64,1,128]{3,2,0,1:T(1,128)S(1)}, u32[]{:S(2)}, u32[]{:S(2)}) collective-permute-start(f32[2,64,1,128]{3,2,0,1:T(1,128)S(1)} %get-tuple-element.13), channel_id=1, source_target_pairs={{2,0},{4,2},{6,4},{8,6},{10,8},{12,10},{14,12},{0,14},{3,1},{5,3},... | collective-permute-start | bytes 196616 | tf_op jit(solution)/shard_map/ppermute | solution.py:19
  36.1 7.0 %collective-permute-start.6 = (f32[2,64,1,128]{3,2,0,1:T(1,128)S(1)}, f32[2,64,1,128]{3,2,0,1:T(1,128)S(1)}, u32[]{:S(2)}, u32[]{:S(2)}) collective-permute-start(f32[2,64,1,128]{3,2,0,1:T(1,128)S(1)} %get-tuple-element.12), channel_id=1, source_target_pairs={{0,2},{2,4},{4,6},{6,8},{8,10},{10,12},{12,14},{14,0},{1,3},{3,5},... | collective-permute-start | bytes 196616 | tf_op jit(solution)/shard_map/ppermute | solution.py:17
  46.9 7.5 %collective-permute-start.7 = (f32[2,64,18,1]{1,0,3,2:T(2,128)S(1)}, f32[2,64,18,1]{1,0,3,2:T(2,128)S(1)}, u32[]{:S(2)}, u32[]{:S(2)}) collective-permute-start(f32[2,64,18,1]{1,0,3,2:T(2,128)S(1)} %copy.107), channel_id=1, source_target_pairs={{1,0},{3,2},{5,4},{7,6},{9,8},{11,10},{13,12},{15,14},{17,16},{19,... | collective-permute-start | bytes 27656 | tf_op jit(solution)/shard_map/ppermute | solution.py:19
  48.7 6.4 %collective-permute-start.8 = (f32[2,64,18,1]{1,0,3,2:T(2,128)S(1)}, f32[2,64,18,1]{1,0,3,2:T(2,128)S(1)}, u32[]{:S(2)}, u32[]{:S(2)}) collective-permute-start(f32[2,64,18,1]{1,0,3,2:T(2,128)S(1)} %copy.109), channel_id=1, source_target_pairs={{0,1},{2,3},{4,5},{6,7},{8,9},{10,11},{12,13},{14,15},{16,17},{18,... | collective-permute-start | bytes 27656 | tf_op jit(solution)/shard_map/ppermute | solution.py:17
  54.3 2.6 %copy-start.8 = (f32[64]{0:T(128)S(1)}, f32[64]{0:T(128)}, u32[]{:S(2)}) copy-start(f32[64]{0:T(128)} %compare_convert_fusion) | copy-start | bytes 772
where the time goes:
time: 63.6 us; the launch traced here: 63.3 us
  local copies, waits for them, and re-layouts  20.4 us (32%)
  starting transfers between devices  20.1 us (32%)
  other arithmetic  10.9 us (17%)
  waiting for transfers between devices  8 us (13%)
  matrix products  3.41 us (5%)
    ppermute x4, starting transfers between devices, with_halo(): lax.ppermute(head, axis, [((i + 1) % count, i) for i in range(ends)])  10.2 us
    ppermute x4, starting transfers between devices, with_halo(): lax.ppermute(tail, axis, [(i, (i + 1) % count) for i in range(ends)])  9.26 us
    ppermute x4, waiting for transfers between devices, with_halo(): lax.ppermute(tail, axis, [(i, (i + 1) % count) for i in range(ends)])  7.23 us
    add x2, other arithmetic, advance(): updated = updated + level_pick[None, :, None, None] * increment[:, None]  6.13 us
    slice x6, local copies, waits for them, and re-layouts, with_halo(): lax.slice_in_dim(cells, cells.shape[dim] - width, cells.shape[dim], axis=...  4.64 us
    slice x2, local copies, waits for them, and re-layouts, with_halo(): head = lax.slice_in_dim(cells, 0, width, axis=dim)  3.79 us
    ppermute x2, local copies, waits for them, and re-layouts, with_halo(): lax.ppermute(tail, axis, [(i, (i + 1) % count) for i in range(ends)])  3.64 us
    dot_general x2, matrix products, advance(): jnp.einsum('kl,tlxy->tkxy', vertical, updated, precision=lax.Precision.HI...  3.41 us
  transfers between devices with their start and end apart: 10, of which 3 were waited for; matrix products, arithmetic and copies ran while one was open for 16% of the time, Pallas kernels for 0%

commit v1 on v0

v1 whole, which is shorter than its diff:
```python
import functools

import jax
import jax.numpy as jnp
from jax import lax
from jax.experimental import pallas as pl
from jax.experimental.pallas import tpu as pltpu
from jax.sharding import PartitionSpec as P

STEPS = 2


def pair_route(count, odd):
    if odd:
        return [(i, ((i + 1) ^ 1) - 1 if i + 1 < count else 0) for i in range(count - 1)][1:] + [(0, count - 1), (count - 1, 0)]
    return [(i, i ^ 1) for i in range(count)]


def pair_swap(block, axis, odd):
    return lax.ppermute(block, axis, pair_route(lax.axis_size(axis), odd))


def even_flag(axis):
    return 1 - lax.rem(lax.axis_index(axis), 2)


def send_edges(column, zon_even, mer_even, send_odd, send_even, send_mer, levels, width, tracers):
    at_even = jnp.where(zon_even == 1, width - 1, 0)
    at_odd = jnp.where(zon_even == 1, 0, width - 1)
    lane = lax.broadcasted_iota(jnp.int32, (levels, 128), 1)
    acc = [jnp.zeros((levels, 128), jnp.float32) for _ in send_mer]
    for t in range(tracers):
        send_even[t * levels:(t + 1) * levels, :] = column(t, at_even)
        send_odd[t * levels:(t + 1) * levels, :] = column(t, at_odd)
        for x in range(width):
            j = 2 * (t * width + x)
            cells = column(t, x)
            for r in range(len(send_mer)):
                up = mer_even if r == 0 else 1 - mer_even
                acc[r] = jnp.where(lane == j + up, pltpu.roll(cells, j + 2 * up, 1), acc[r])
    for r, ref in enumerate(send_mer):
        ref[...] = acc[r]


def mer_halo(recv_mer, levels, mer_count):
    place = lax.axis_index("mer")
    even = even_flag("mer")
    lane = lax.broadcasted_iota(jnp.int32, (levels, 128), 1)
    total = jnp.zeros((levels, 128), jnp.float32)
    for r, ref in enumerate(recv_mer):
        north = even if r == 0 else 1 - even
        inside = jnp.where(north == 1, place + 1 < mer_count, place > 0)
        keep = jnp.logical_and(lax.rem(lane, 2) == 1 - north, inside)
        total = total + jnp.where(keep, ref[...], 0.0)
    return total


def increments(own, other, rate, block_map, ice_mask, tracers, width):
    fluid = lax.axis_index("fluid")
    blocks = block_map.shape[0]
    wide = own.shape[1] // blocks
    first = lax.axis_index("mer") * blocks
    is_atm = fluid == 0
    atm = jnp.where(is_atm, own, other)
    ocean = jnp.where(is_atm, other, own)
    block = lax.broadcasted_iota(jnp.int32, own.shape, 1) // wide
    flux = jnp.zeros_like(own)
    for b in range(blocks):
        a = block_map[b] - first
        moved = pltpu.roll(atm, lax.rem((b - a + blocks) * wide, 128), 1)
        flux = jnp.where(block == b, (moved - ocean) * (1 - ice_mask[b]).astype(jnp.float32), flux)
    returned = jnp.zeros_like(own)
    for b in range(blocks):
        a = block_map[b] - first
        moved = pltpu.roll(flux, lax.rem((a - b + blocks) * wide, 128), 1)
        returned = jnp.where(block == a, moved, returned)
    tracer = lax.broadcasted_iota(jnp.int32, own.shape, 0) // width
    scale = jnp.full(own.shape, rate[0])
    for t in range(1, tracers):
        scale = jnp.where(tracer == t, rate[t], scale)
    return jnp.where(is_atm, -returned, flux) * scale


def split3(matrix):
    high = matrix.astype(jnp.bfloat16)
    low = (matrix - high.astype(jnp.float32)).astype(jnp.bfloat16)
    return high, low


def step_body(column, store, east_halo, west_halo, halo, incr, zonal, merid, viscous, weights, levels, width, tracers):
    lane = lax.broadcasted_iota(jnp.int32, (levels, 128), 1)
    top = lane == 127
    bottom = lane == 0
    row = lax.broadcasted_iota(jnp.int32, (levels, 128), 0)
    fluid = lax.axis_index("fluid")
    at_surface = row == jnp.where(fluid == 0, levels - 1, 0)
    for t in range(tracers):
        nu = viscous[t]
        diag = 1.0 - 4.0 * nu
        for x0 in range(0, width, 2):
            parts = []
            for x in (x0, x0 + 1):
                j = t * width + x
                q = column(t, x)
                west = west_halo(t) if x == 0 else column(t, x - 1)
                east = east_halo(t) if x == width - 1 else column(t, x + 1)
                edge = pltpu.roll(halo, (127 - 2 * j) % 128, 1)
                north = jnp.where(top, edge, pltpu.roll(q, 127, 1))
                south = jnp.where(bottom, edge, pltpu.roll(q, 1, 1))
                c = zonal(x)
                d = merid(x)
                u = diag * q + (nu - c) * east + (nu + c) * west + (nu - d) * north + (nu + d) * south
                u = u + jnp.where(at_surface, jnp.broadcast_to(incr[j:j + 1, :], u.shape), 0.0)
                parts.append(u)
            u = jnp.concatenate(parts, axis=1)
            high, low = split3(u)
            solved = jnp.dot(weights, jnp.concatenate([high, low, high], axis=0), preferred_element_type=jnp.float32)
            store(t, x0, solved[:, :128])
            store(t, x0 + 1, solved[:, 128:])


def pack_kernel(dims, state, *outs):
    tracers, levels, width, rounds = dims
    send_odd, send_even, surface = outs[:3]
    column = lambda t, x: state[pl.ds(t * levels * width + x, levels, stride=width), :]
    send_edges(column, even_flag("zon"), even_flag("mer"), send_odd, send_even, outs[3:], levels, width, tracers)
    level = jnp.where(lax.axis_index("fluid") == 0, levels - 1, 0)
    for t in range(tracers):
        start = pl.multiple_of((t * levels + level) * width, 8)
        surface[t * width:(t + 1) * width, :] = state[pl.ds(start, width), :]


def prepare(diffusion, solve, levels, tracers):
    viscous = [jnp.transpose(jnp.broadcast_to(diffusion[t:t + 1, :], (128, levels))) for t in range(tracers)]
    high, low = split3(solve[...])
    return viscous, jnp.concatenate([high, high, low], axis=1)


def halos(recv_odd, recv_even, levels):
    even = even_flag("zon") == 1
    part = lambda ref, t: ref[t * levels:(t + 1) * levels, :]
    east = lambda t: jnp.where(even, part(recv_even, t), part(recv_odd, t))
    west = lambda t: jnp.where(even, part(recv_odd, t), part(recv_even, t))
    return east, west


def first_kernel(dims, mer_count, state, flow, diffusion, solve, rate, block_map, ice_mask, own, other, recv_odd, recv_even, *rest):
    tracers, levels, width, rounds = dims
    recv_mer, rest = rest[:rounds], rest[rounds:]
    fresh, frame, send_odd, send_even, surface = rest[:5]
    send_mer = rest[5:]
    size = levels * width
    for k in range(2):
        frame_k = flow[k * size:(k + 1) * size, :].astype(jnp.float32) * 0.5
        frame[k * size:(k + 1) * size, :] = frame_k
    viscous, weights = prepare(diffusion, solve, levels, tracers)
    east, west = halos(recv_odd, recv_even, levels)
    halo = mer_halo(recv_mer, levels, mer_count)
    incr = increments(own[...], other[...], rate, block_map, ice_mask, tracers, width)
    column = lambda t, x: state[pl.ds(t * size + x, levels, stride=width), :]
    strip = lambda k: lambda x: frame[pl.ds(k * size + x, levels, stride=width), :]

    def store(t, x, value):
        fresh[pl.ds((t * width + x) * levels, levels), :] = value

    step_body(column, store, east, west, halo, incr, strip(0), strip(1), viscous, weights, levels, width, tracers)
    fresh_column = lambda t, x: fresh[pl.ds(pl.multiple_of((t * width + x) * levels, 8), levels), :]
    send_edges(fresh_column, even_flag("zon"), even_flag("mer"), send_odd, send_even, send_mer, levels, width, tracers)
    level = jnp.where(lax.axis_index("fluid") == 0, levels - 1, 0)
    for j in range(tracers * width):
        surface[j:j + 1, :] = fresh[pl.ds(j * levels + level, 1), :]


def last_kernel(dims, mer_count, fresh, frame, diffusion, solve, rate, block_map, ice_mask, own, other, recv_odd, recv_even, *rest):
    tracers, levels, width, rounds = dims
    recv_mer, out = rest[:rounds], rest[rounds]
    size = levels * width
    viscous, weights = prepare(diffusion, solve, levels, tracers)
    east, west = halos(recv_odd, recv_even, levels)
    halo = mer_halo(recv_mer, levels, mer_count)
    incr = increments(own[...], other[...], rate, block_map, ice_mask, tracers, width)
    column = lambda t, x: fresh[pl.ds((t * width + x) * levels, levels), :]
    strip = lambda k: lambda x: frame[pl.ds(k * size + x, levels, stride=width), :]

    def store(t, x, value):
        out[pl.ds(t * size + x, levels, stride=width), :] = value

    step_body(column, store, east, west, halo, incr, strip(0), strip(1), viscous, weights, levels, width, tracers)


VM = pl.BlockSpec(memory_space=pltpu.VMEM)
SM = pl.BlockSpec(memory_space=pltpu.SMEM)


def call(body, name, in_specs, out_shape):
    many = isinstance(out_shape, list)
    return pl.pallas_call(
        body,
        out_shape=out_shape,
        in_specs=in_specs,
        out_specs=[VM] * len(out_shape) if many else VM,
        name=name,
        compiler_params=pltpu.CompilerParams(vmem_limit_bytes=32 * 1024 * 1024),
    )


def on_device(state, flow, diffusion, column_solve, exchange_rate, block_map, ice_mask):
    _, tracers, levels, width, wide = state.shape
    mer_count = lax.axis_size("mer")
    rounds = 1 if mer_count == 2 else 2
    dims = (tracers, levels, width, rounds)
    size = levels * width
    cells = state.reshape(tracers * size, wide)
    flow2 = flow.reshape(2 * size, wide)
    f32 = lambda *shape: jax.ShapeDtypeStruct(shape, jnp.float32)
    packs = [f32(tracers * levels, wide)] * 2 + [f32(tracers * width, wide)] + [f32(levels, 128)] * rounds
    fixed = (diffusion[0], column_solve[0], exchange_rate[0], block_map, ice_mask)
    fixed_specs = [VM, VM, SM, SM, SM]

    def swap(send_odd, send_even, surface, *send_mer):
        moved = [pair_swap(send_odd, "zon", True), pair_swap(send_even, "zon", False)]
        moved += [pair_swap(piece, "mer", r == 1) for r, piece in enumerate(send_mer)]
        return [surface, pair_swap(surface, "fluid", False)] + moved

    packed = call(functools.partial(pack_kernel, dims), "pack", [VM], packs)(cells)
    got = swap(*packed)
    fresh, frame, *packed = call(
        functools.partial(first_kernel, dims, mer_count), "first", [VM, VM] + fixed_specs + [VM] * len(got),
        [f32(tracers * size, wide), f32(2 * size, wide)] + packs,
    )(cells, flow2, *fixed, *got)
    got = swap(*packed)
    done = call(
        functools.partial(last_kernel, dims, mer_count), "last", [VM, VM] + fixed_specs + [VM] * len(got),
        f32(tracers * size, wide),
    )(fresh, frame, *fixed, *got)
    return done.reshape(state.shape)


def solution(mesh):
    return jax.shard_map(
        on_device,
        mesh=mesh,
        in_specs=(
            P("fluid", None, None, "zon", "mer"),
            P("fluid", None, None, "zon", "mer"),
            P("fluid", None, None),
            P("fluid", None, None),
            P("fluid", None),
            P("mer"),
            P("mer"),
        ),
        out_specs=P("fluid", None, None, "zon", "mer"),
        check_vma=False,
    )
```

time: 63.6 us -> 26.8 us (0.42)
  local copies, waits for them, and re-layouts: 20.4 us -> 1.89 us
  other arithmetic: 10.9 us -> 0 us
  starting transfers between devices: 20.1 us -> 11.8 us
  Pallas kernels: 0 us -> 6.65 us
  matrix products: 3.41 us -> 0 us
  waiting for transfers between devices: 8 us -> 6.18 us
    slice x8 -> x0, local copies, waits for them, and re-layouts: 8.42 us -> none  [the longest x6 4.64 us: with_halo(): lax.slice_in_dim(cells, cells.shape[dim] - width, cells.shape[dim], axis=...]
    ppermute x10 -> x8, starting transfers between devices: 20.1 us -> 11.8 us  [pair_swap(): return lax.ppermute(block, axis, pair_route(lax.axis_size(axis), odd))]
    pallas_call x0 -> x3, Pallas kernels: none -> 6.65 us  [the longest x1 3.35 us: on_device(): call(functools.partial(last_kernel, dims, mer_count), 'last', [VM, VM] +...]
    add x2 -> x0, other arithmetic: 6.13 us -> none  [advance(): updated = updated + level_pick[None, :, None, None] * increment[:, None]]
    ppermute x4 -> x0, local copies, waits for them, and re-layouts: 5.09 us -> none  [the longest x2 3.64 us: with_halo(): lax.ppermute(tail, axis, [(i, (i + 1) % count) for i in range(ends)])]
    dot_general x2 -> x0, matrix products: 3.41 us -> none  [advance(): jnp.einsum('kl,tlxy->tkxy', vertical, updated, precision=lax.Precision.HI...]
    gather x4 -> x0, local copies, waits for them, and re-layouts: 2.45 us -> none  [the longest x2 1.22 us: advance(): returned = jnp.take(surface_flux, inverse, axis=2)]
    ppermute x10 -> x8, waiting for transfers between devices: 8 us -> 6.18 us  [pair_swap(): return lax.ppermute(block, axis, pair_route(lax.axis_size(axis), odd))]
  transfers between devices with their start and end apart: 10 -> 8, of which waited for: 3 -> 7; matrix products, arithmetic and copies ran while one was open for 16% -> 0% of each run, Pallas kernels for 0% -> 0%
where the time goes in v1:
time: 26.8 us; the launch traced here: 26.6 us
  starting transfers between devices  11.8 us (44%)
  Pallas kernels  6.65 us (25%)
  waiting for transfers between devices  6.18 us (23%)
  local copies, waits for them, and re-layouts  1.89 us (7%)
    ppermute x8, starting transfers between devices, pair_swap(): return lax.ppermute(block, axis, pair_route(lax.axis_size(axis), odd))  11.8 us
    ppermute x8, waiting for transfers between devices, pair_swap(): return lax.ppermute(block, axis, pair_route(lax.axis_size(axis), odd))  6.18 us
    pallas_call x1, Pallas kernels, on_device(): call(functools.partial(last_kernel, dims, mer_count), 'last', [VM, VM] +...  3.35 us
    pallas_call x1, Pallas kernels, on_device(): call(functools.partial(first_kernel, dims, mer_count), 'first', [VM, VM]...  2.8 us
    unnamed x14, local copies, waits for them, and re-layouts  1.89 us
  transfers between devices with their start and end apart: 8, of which 7 were waited for; matrix products, arithmetic and copies ran while one was open for 0% of the time, Pallas kernels for 0%

profile of v1, /device:TPU:0, one launch (start us, length us, event | category | flops | bytes accessed | tf_op | source)
XLA Modules:
  0.0 26.6 jit_solution(3301582409400400233)
XLA Ops:
  0.0 0.0 copy-start
  0.0 1.2 %copy-done = f32[1,2,64,16,128]{4,3,2,1,0:T(8,128)S(1)} copy-done((f32[1,2,64,16,128]{4,3,2,1,0:T(8,128)S(1)}, f32[1,2,64,16,128]{4,3,2,1,0:T(8,128)}, u32[]{:S(2)}) %copy-start) | copy-done | bytes 1048600
  1.2 0.0 copy-start.1
  1.2 0.0 copy-start.2
  1.2 0.5 %pack.1 = (f32[128,128]{1,0:T(8,128)S(1)}, f32[128,128]{1,0:T(8,128)S(1)}, f32[32,128]{1,0:T(8,128)S(1)}, f32[64,128]{1,0:T(8,128)S(1)}) custom-call(f32[2048,128]{1,0:T(8,128)S(1)} %bitcast.6), custom_call_target="tpu_custom_call" | custom-call | tf_op jit(solution)/shard_map/pack/pallas_call | solution.py:225
  1.7 6.0 %collective-permute-start.1 = (f32[128,128]{1,0:T(8,128)S(1)}, f32[128,128]{1,0:T(8,128)S(1)}, u32[]{:S(2)}, u32[]{:S(2)}) collective-permute-start(f32[128,128]{1,0:T(8,128)S(1)} %get-tuple-element.16), channel_id=1, source_target_pairs={{2,4},{4,2},{6,8},{8,6},{10,12},{12,10},{0,14},{14,0},{3,5},{5,3},... | collective-permute-start | bytes 196616 | tf_op jit(solution)/shard_map/ppermute | solution.py:20
  7.8 0.0 copy-start.5
  7.8 0.0 copy-start.6
  7.8 0.0 collective-permute-start.2
  7.8 1.5 %collective-permute-start.3 = (f32[64,128]{1,0:T(8,128)S(1)}, f32[64,128]{1,0:T(8,128)S(1)}, u32[]{:S(2)}, u32[]{:S(2)}) collective-permute-start(f32[64,128]{1,0:T(8,128)S(1)} %get-tuple-element.18), channel_id=1, source_target_pairs={{0,1},{1,0},{2,3},{3,2},{4,5},{5,4},{6,7},{7,6},{8,9},{9,8},{10,11... | collective-permute-start | bytes 98312 | tf_op jit(solution)/shard_map/ppermute | solution.py:20
  9.3 0.0 collective-permute-start
  9.3 1.2 %collective-permute-done.other = f32[32,128]{1,0:T(8,128)S(1)} collective-permute-done((f32[32,128]{1,0:T(8,128)S(1)}, f32[32,128]{1,0:T(8,128)S(1)}, u32[]{:S(2)}, u32[]{:S(2)}) %collective-permute-start) | collective-permute-done | bytes 16416 | tf_op jit(solution)/shard_map/ppermute | solution.py:20
  10.5 1.2 %collective-permute-done.3.rest_0_ = f32[64,128]{1,0:T(8,128)S(1)} collective-permute-done((f32[64,128]{1,0:T(8,128)S(1)}, f32[64,128]{1,0:T(8,128)S(1)}, u32[]{:S(2)}, u32[]{:S(2)}) %collective-permute-start.3) | collective-permute-done | bytes 32800 | tf_op jit(solution)/shard_map/ppermute | solution.py:20
  11.7 0.0 collective-permute-done.1.recv_odd
  11.7 0.3 %collective-permute-done.2.recv_even = f32[128,128]{1,0:T(8,128)S(1)} collective-permute-done((f32[128,128]{1,0:T(8,128)S(1)}, f32[128,128]{1,0:T(8,128)S(1)}, u32[]{:S(2)}, u32[]{:S(2)}) %collective-permute-start.2) | collective-permute-done | bytes 65568 | tf_op jit(solution)/shard_map/ppermute | solution.py:20
  12.0 0.0 copy-start.3
  12.0 0.0 copy-start.4
  12.0 0.0 copy-done.1
  12.0 0.0 copy-done.2
  12.1 0.0 copy-done.5
  12.1 0.0 copy-done.6
  12.1 0.6 %copy-done.3 = f32[1,2,64]{2,1,0:T(2,128)S(1)} copy-done((f32[1,2,64]{2,1,0:T(2,128)S(1)}, f32[1,2,64]{2,1,0:T(2,128)}, u32[]{:S(2)}) %copy-start.3) | copy-done | bytes 536
  12.7 0.0 copy-done.4
  12.7 2.8 %first.1 = (f32[2048,128]{1,0:T(8,128)S(1)}, f32[2048,128]{1,0:T(8,128)S(1)}, f32[128,128]{1,0:T(8,128)S(1)}, f32[128,128]{1,0:T(8,128)S(1)}, f32[32,128]{1,0:T(8,128)S(1)}, /*index=5*/f32[64,128]{1,0:T(8,128)S(1)}) custom-call(f32[2048,128]{1,0:T(8,128)S(1)} %bitcast.7, bf16[2048,128]{1,0:T(8,128)(2,1)S(1)} %bitcast.8, f32[2,64]{1,0:T(2,128)S(1)} %bitcast.11, ...), custom_call_target="tpu_custom_call" | custom-call | tf_op jit(solution)/shard_map/first/pallas_call | solution.py:227
  15.5 2.8 %collective-permute-start.5 = (f32[128,128]{1,0:T(8,128)S(1)}, f32[128,128]{1,0:T(8,128)S(1)}, u32[]{:S(2)}, u32[]{:S(2)}) collective-permute-start(f32[128,128]{1,0:T(8,128)S(1)} %get-tuple-element.22), channel_id=1, source_target_pairs={{2,4},{4,2},{6,8},{8,6},{10,12},{12,10},{0,14},{14,0},{3,5},{5,3},... | collective-permute-start | bytes 196616 | tf_op jit(solution)/shard_map/ppermute | solution.py:20
  18.3 0.0 collective-permute-start.6
  18.3 1.5 %collective-permute-start.7 = (f32[64,128]{1,0:T(8,128)S(1)}, f32[64,128]{1,0:T(8,128)S(1)}, u32[]{:S(2)}, u32[]{:S(2)}) collective-permute-start(f32[64,128]{1,0:T(8,128)S(1)} %get-tuple-element.24), channel_id=1, source_target_pairs={{0,1},{1,0},{2,3},{3,2},{4,5},{5,4},{6,7},{7,6},{8,9},{9,8},{10,11... | collective-permute-start | bytes 98312 | tf_op jit(solution)/shard_map/ppermute | solution.py:20
  19.8 0.0 collective-permute-start.4
  19.8 1.2 %collective-permute-done.4.other = f32[32,128]{1,0:T(8,128)S(1)} collective-permute-done((f32[32,128]{1,0:T(8,128)S(1)}, f32[32,128]{1,0:T(8,128)S(1)}, u32[]{:S(2)}, u32[]{:S(2)}) %collective-permute-start.4) | collective-permute-done | bytes 16416 | tf_op jit(solution)/shard_map/ppermute | solution.py:20
  21.0 1.2 %collective-permute-done.7.rest_0_ = f32[64,128]{1,0:T(8,128)S(1)} collective-permute-done((f32[64,128]{1,0:T(8,128)S(1)}, f32[64,128]{1,0:T(8,128)S(1)}, u32[]{:S(2)}, u32[]{:S(2)}) %collective-permute-start.7) | collective-permute-done | bytes 32800 | tf_op jit(solution)/shard_map/ppermute | solution.py:20
  22.2 0.5 %collective-permute-done.5.recv_odd = f32[128,128]{1,0:T(8,128)S(1)} collective-permute-done((f32[128,128]{1,0:T(8,128)S(1)}, f32[128,128]{1,0:T(8,128)S(1)}, u32[]{:S(2)}, u32[]{:S(2)}) %collective-permute-start.5) | collective-permute-done | bytes 65568 | tf_op jit(solution)/shard_map/ppermute | solution.py:20
  22.7 0.6 %collective-permute-done.6.recv_even = f32[128,128]{1,0:T(8,128)S(1)} collective-permute-done((f32[128,128]{1,0:T(8,128)S(1)}, f32[128,128]{1,0:T(8,128)S(1)}, u32[]{:S(2)}, u32[]{:S(2)}) %collective-permute-start.6) | collective-permute-done | bytes 65568 | tf_op jit(solution)/shard_map/ppermute | solution.py:20
  23.3 3.4 %last.1 = f32[2048,128]{1,0:T(8,128)} custom-call(f32[2048,128]{1,0:T(8,128)S(1)} %get-tuple-element.19.fresh, f32[2048,128]{1,0:T(8,128)S(1)} %get-tuple-element.20.frame, f32[2,64]{1,0:T(2,128)S(1)} %bitcast.12, f32[64,64]{1,0:T(8,128)S(1)} %bitcast.10, f32[2]{0:T(128)S(1)} %bitcast.14, s32[4]{0:T(128)S(1)} %copy-done.5, s32[4]{0:T(128)S(1)} %copy-done.6, ...), custom_call_target="tpu_custom_call" | custom-call | tf_op jit(solution)/shard_map/last/pallas_call | solution.py:232
Async XLA Ops:
  0.0 1.2 %copy-start = (f32[1,2,64,16,128]{4,3,2,1,0:T(8,128)S(1)}, f32[1,2,64,16,128]{4,3,2,1,0:T(8,128)}, u32[]{:S(2)}) copy-start(f32[1,2,64,16,128]{4,3,2,1,0:T(8,128)} %param.7) | copy-start | bytes 3145732
  1.2 10.8 %copy-start.1 = (bf16[1,2,64,16,128]{4,3,2,1,0:T(8,128)(2,1)S(1)}, bf16[1,2,64,16,128]{4,3,2,1,0:T(8,128)(2,1)}, u32[]{:S(2)}) copy-start(bf16[1,2,64,16,128]{4,3,2,1,0:T(8,128)(2,1)} %param.8) | copy-start | bytes 1572868
  1.2 10.8 %copy-start.2 = (f32[1,64,64]{2,1,0:T(8,128)S(1)}, f32[1,64,64]{2,1,0:T(8,128)}, u32[]{:S(2)}) copy-start(f32[1,64,64]{2,1,0:T(8,128)} %param.10) | copy-start | bytes 49156
  1.7 10.0 %collective-permute-start.1 = (f32[128,128]{1,0:T(8,128)S(1)}, f32[128,128]{1,0:T(8,128)S(1)}, u32[]{:S(2)}, u32[]{:S(2)}) collective-permute-start(f32[128,128]{1,0:T(8,128)S(1)} %get-tuple-element.16), channel_id=1, source_target_pairs={{2,4},{4,2},{6,8},{8,6},{10,12},{12,10},{0,14},{14,0},{3,5},{5,3},... | collective-permute-start | bytes 196616 | tf_op jit(solution)/shard_map/ppermute | solution.py:20
  7.8 4.3 %copy-start.5 = (s32[4]{0:T(128)S(1)}, s32[4]{0:T(128)}, u32[]{:S(2)}) copy-start(s32[4]{0:T(128)} %block_map.3) | copy-start | bytes 52
  7.8 4.3 %copy-start.6 = (s32[4]{0:T(128)S(1)}, s32[4]{0:T(128)}, u32[]{:S(2)}) copy-start(s32[4]{0:T(128)} %ice_mask.3) | copy-start | bytes 52
  7.8 4.3 %collective-permute-start.2 = (f32[128,128]{1,0:T(8,128)S(1)}, f32[128,128]{1,0:T(8,128)S(1)}, u32[]{:S(2)}, u32[]{:S(2)}) collective-permute-start(f32[128,128]{1,0:T(8,128)S(1)} %get-tuple-element.17), channel_id=1, source_target_pairs={{0,2},{2,0},{4,6},{6,4},{8,10},{10,8},{12,14},{14,12},{1,3},{3,1},... | collective-permute-start | bytes 196616 | tf_op jit(solution)/shard_map/ppermute | solution.py:20
  7.8 3.9 %collective-permute-start.3 = (f32[64,128]{1,0:T(8,128)S(1)}, f32[64,128]{1,0:T(8,128)S(1)}, u32[]{:S(2)}, u32[]{:S(2)}) collective-permute-start(f32[64,128]{1,0:T(8,128)S(1)} %get-tuple-element.18), channel_id=1, source_target_pairs={{0,1},{1,0},{2,3},{3,2},{4,5},{5,4},{6,7},{7,6},{8,9},{9,8},{10,11... | collective-permute-start | bytes 98312 | tf_op jit(solution)/shard_map/ppermute | solution.py:20
  9.3 1.2 %collective-permute-start = (f32[32,128]{1,0:T(8,128)S(1)}, f32[32,128]{1,0:T(8,128)S(1)}, u32[]{:S(2)}, u32[]{:S(2)}) collective-permute-start(f32[32,128]{1,0:T(8,128)S(1)} %get-tuple-element.15.own), channel_id=1, source_target_pairs={{0,16},{16,0},{1,17},{17,1},{2,18},{18,2},{3,19},{19,3},{4,20},{20... | collective-permute-start | bytes 49160 | tf_op jit(solution)/shard_map/ppermute | solution.py:20
  12.0 0.7 %copy-start.3 = (f32[1,2,64]{2,1,0:T(2,128)S(1)}, f32[1,2,64]{2,1,0:T(2,128)}, u32[]{:S(2)}) copy-start(f32[1,2,64]{2,1,0:T(2,128)} %param.9) | copy-start | bytes 1540
  12.0 0.7 %copy-start.4 = (f32[1,2]{1,0:T(1,128)S(1)}, f32[1,2]{1,0:T(1,128)}, u32[]{:S(2)}) copy-start(f32[1,2]{1,0:T(1,128)} %param.11) | copy-start | bytes 28
  15.5 7.1 %collective-permute-start.5 = (f32[128,128]{1,0:T(8,128)S(1)}, f32[128,128]{1,0:T(8,128)S(1)}, u32[]{:S(2)}, u32[]{:S(2)}) collective-permute-start(f32[128,128]{1,0:T(8,128)S(1)} %get-tuple-element.22), channel_id=1, source_target_pairs={{2,4},{4,2},{6,8},{8,6},{10,12},{12,10},{0,14},{14,0},{3,5},{5,3},... | collective-permute-start | bytes 196616 | tf_op jit(solution)/shard_map/ppermute | solution.py:20
  18.3 5.0 %collective-permute-start.6 = (f32[128,128]{1,0:T(8,128)S(1)}, f32[128,128]{1,0:T(8,128)S(1)}, u32[]{:S(2)}, u32[]{:S(2)}) collective-permute-start(f32[128,128]{1,0:T(8,128)S(1)} %get-tuple-element.23), channel_id=1, source_target_pairs={{0,2},{2,0},{4,6},{6,4},{8,10},{10,8},{12,14},{14,12},{1,3},{3,1},... | collective-permute-start | bytes 196616 | tf_op jit(solution)/shard_map/ppermute | solution.py:20
  18.3 3.9 %collective-permute-start.7 = (f32[64,128]{1,0:T(8,128)S(1)}, f32[64,128]{1,0:T(8,128)S(1)}, u32[]{:S(2)}, u32[]{:S(2)}) collective-permute-start(f32[64,128]{1,0:T(8,128)S(1)} %get-tuple-element.24), channel_id=1, source_target_pairs={{0,1},{1,0},{2,3},{3,2},{4,5},{5,4},{6,7},{7,6},{8,9},{9,8},{10,11... | collective-permute-start | bytes 98312 | tf_op jit(solution)/shard_map/ppermute | solution.py:20
  19.8 1.2 %collective-permute-start.4 = (f32[32,128]{1,0:T(8,128)S(1)}, f32[32,128]{1,0:T(8,128)S(1)}, u32[]{:S(2)}, u32[]{:S(2)}) collective-permute-start(f32[32,128]{1,0:T(8,128)S(1)} %get-tuple-element.21.own), channel_id=1, source_target_pairs={{0,16},{16,0},{1,17},{17,1},{2,18},{18,2},{3,19},{19,3},{4,20},{20... | collective-permute-start | bytes 49160 | tf_op jit(solution)/shard_map/ppermute | solution.py:20

commit v2 on v1

v2 whole, which is shorter than its diff:
```python
import functools

import jax
import jax.numpy as jnp
from jax import lax
from jax.experimental import pallas as pl
from jax.experimental.pallas import tpu as pltpu
from jax.sharding import PartitionSpec as P

f32, bf16 = jnp.float32, jnp.bfloat16


def ring(count, ahead):
    return [(i, (i + ahead) % count) for i in range(count)]


def pairs(count, odd):
    if odd:
        return [(i, ((i + 1) ^ 1) - 1) for i in range(1, count - 1)] + [(0, count - 1), (count - 1, 0)]
    return [(i, i ^ 1) for i in range(count)]


def mer_even():
    return 1 - lax.rem(lax.axis_index("mer"), 2)


def surface_level(levels):
    return jnp.where(lax.axis_index("fluid") == 0, levels - 1, 0)


def lanes_of(levels):
    return lax.broadcasted_iota(jnp.int32, (levels, 128), 1)


def split(value):
    high = value.astype(bf16)
    return high, (value - high.astype(f32)).astype(bf16)


def product(weights, value):
    high, low = split(value)
    return jnp.dot(weights, jnp.concatenate([high, low, high], axis=0), preferred_element_type=f32)


def part(ref, index, levels):
    return ref[index * levels:(index + 1) * levels, :]


def mer_halo(recv_mer, levels, mer_count):
    place, even = lax.axis_index("mer"), mer_even()
    lane = lanes_of(levels)
    total = jnp.zeros((levels, 128), f32)
    for r, ref in enumerate(recv_mer):
        north = even if r == 0 else 1 - even
        inside = jnp.where(north == 1, place + 1 < mer_count, place > 0)
        keep = jnp.logical_and(lax.rem(lane, 2) == 1 - north, inside)
        total = total + jnp.where(keep, ref[...], 0.0)
    return total


def pack_lanes(acc, cells, j, lane, even):
    for r in range(len(acc)):
        up = even if r == 0 else 1 - even
        acc[r] = jnp.where(lane == 2 * j + up, pltpu.roll(cells, 2 * j + 2 * up, 1), acc[r])


def both_edges(cells, j):
    return pltpu.roll(cells, (2 * j + 1) % 128, 1)


def at_edges(packed, j):
    return pltpu.roll(packed, (127 - 2 * j) % 128, 1)


def increments(own, other, rate, block_map, ice_mask, tracers, per_tracer):
    blocks = block_map.shape[0]
    wide = own.shape[1] // blocks
    first = lax.axis_index("mer") * blocks
    is_atm = lax.axis_index("fluid") == 0
    atm = jnp.where(is_atm, own, other)
    ocean = jnp.where(is_atm, other, own)
    block = lax.broadcasted_iota(jnp.int32, own.shape, 1) // wide
    flux = jnp.zeros_like(own)
    for b in range(blocks):
        a = block_map[b] - first
        moved = pltpu.roll(atm, lax.rem((b - a + blocks) * wide, 128), 1)
        flux = jnp.where(block == b, (moved - ocean) * (1 - ice_mask[b]).astype(f32), flux)
    returned = jnp.zeros_like(own)
    for b in range(blocks):
        a = block_map[b] - first
        moved = pltpu.roll(flux, lax.rem((a - b + blocks) * wide, 128), 1)
        returned = jnp.where(block == a, moved, returned)
    tracer = lax.broadcasted_iota(jnp.int32, own.shape, 0) // per_tracer
    scale = jnp.full(own.shape, rate[0])
    for t in range(1, tracers):
        scale = jnp.where(tracer == t, rate[t], scale)
    return jnp.where(is_atm, -returned, flux) * scale


def horizontal(q, east, west, c, d, nu, lane):
    north = jnp.where(lane == 127, 0.0, pltpu.roll(q, 127, 1))
    south = jnp.where(lane == 0, 0.0, pltpu.roll(q, 1, 1))
    return q - c * (east - west) - d * (north - south) + nu * ((east + west) + (north + south) - 4.0 * q)


def interior(column, strip, nu, weights, store, dims):
    tracers, levels, width = dims
    lane = lanes_of(levels)
    zero = jnp.zeros((levels, 128), f32)
    for x in range(width):
        c, d = strip(0, x), strip(1, x)
        terms = []
        for t in range(tracers):
            west = zero if x == 0 else column(t, x - 1)
            east = zero if x == width - 1 else column(t, x + 1)
            terms.append(horizontal(column(t, x), east, west, c, d, part(nu, t, levels), lane))
        solved = product(weights[...], jnp.concatenate(terms, axis=1))
        for t in range(tracers):
            store(t, x, solved[:, t * 128:(t + 1) * 128])


def pack_kernel(dims, cells, flow, diffusion, solve, rate, block_map, ice_mask, east_bound, west_bound, surface, frame, nu, weights, spread):
    tracers, levels, width = dims
    size = levels * width
    for k in range(2):
        frame[k * size:(k + 1) * size, :] = flow[k * size:(k + 1) * size, :].astype(f32) * 0.5
    for ref, edge, inner in ((east_bound, width - 1, width - 2), (west_bound, 0, 1)):
        for t in range(tracers):
            high, low = split(cells[pl.ds(t * size + edge, levels, stride=width), :])
            ref[t * levels:(t + 1) * levels, :] = high
            ref[(tracers + t) * levels:(tracers + t + 1) * levels, :] = low
            second = cells[pl.ds(t * size + inner, levels, stride=width), :].astype(bf16)
            ref[(2 * tracers + t) * levels:(2 * tracers + t + 1) * levels, :] = second
        for k in range(2):
            strip = frame[pl.ds(k * size + edge, levels, stride=width), :].astype(bf16)
            ref[(3 * tracers + k) * levels:(3 * tracers + k + 1) * levels, :] = strip
    level = surface_level(levels)
    for t in range(tracers):
        start = pl.multiple_of((t * levels + level) * width, 8)
        surface[t * width:(t + 1) * width, :] = cells[pl.ds(start, width), :]
        nu[t * levels:(t + 1) * levels, :] = jnp.transpose(jnp.broadcast_to(diffusion[t:t + 1, :], (128, levels)))
    high, low = split(solve[...])
    weights[...] = jnp.concatenate([high, high, low], axis=1)
    at_level = lax.broadcasted_iota(jnp.int32, (levels, levels), 1) == level
    spread[...] = jnp.broadcast_to(jnp.sum(jnp.where(at_level, solve[...], 0.0), axis=1, keepdims=True), (levels, 128))


def lanes_kernel(dims, cells, columns, *send_mer):
    tracers, levels, width = dims
    lane, even = lanes_of(levels), mer_even()
    acc = [jnp.zeros((levels, 128), f32) for _ in send_mer]
    for t in range(tracers):
        for x in range(width):
            j = t * width + x
            value = cells[pl.ds(t * levels * width + x, levels, stride=width), :]
            columns[j * levels:(j + 1) * levels, :] = value
            pack_lanes(acc, value, j, lane, even)
    for ref, value in zip(send_mer, acc):
        ref[...] = value


def inner_kernel(dims, columns, frame, nu, weights, partial, strips, mer_gain):
    tracers, levels, width = dims
    size = levels * width
    lane = lanes_of(levels)
    packed = jnp.zeros((levels, 128), f32)
    for k in range(2):
        for x in range(width):
            value = frame[pl.ds(k * size + x, levels, stride=width), :]
            strips[(k * width + x) * levels:(k * width + x + 1) * levels, :] = value
            if k == 1:
                packed = jnp.where(lane // 2 == x, both_edges(value, x), packed)
    gain = jnp.zeros((levels, 128), f32)
    for t in range(tracers):
        merid = packed if t == 0 else pltpu.roll(packed, 2 * t * width, 1)
        mine = part(nu, t, levels) + jnp.where(lane % 2 == 0, -merid, merid)
        gain = jnp.where(lane // (2 * width) == t, mine, gain)
    mer_gain[...] = gain

    def store(t, x, value):
        partial[pl.ds((t * width + x) * levels, levels), :] = value

    column = lambda t, x: part(columns, t * width + x, levels)
    strip = lambda k, x: part(strips, k * width + x, levels)
    interior(column, strip, nu, weights, store, dims)


def second_kernel(dims, columns, strips, nu, weights, partial):
    tracers, levels, width = dims

    def store(t, x, value):
        partial[pl.ds((t * width + x) * levels, levels), :] = value

    column = lambda t, x: part(columns, t * width + x, levels)
    strip = lambda k, x: part(strips, k * width + x, levels)
    interior(column, strip, nu, weights, store, dims)


def join_kernel(dims, mer_count, partial, strips, nu, weights, spread, mer_gain, rate, block_map, ice_mask, own, other, from_west, from_east, *rest):
    tracers, levels, width = dims
    rounds = 1 if mer_count == 2 else 2
    recv_mer = rest[:rounds]
    fresh, sides, surface = rest[rounds:rounds + 3]
    send_mer = rest[rounds + 3:]
    lane, even = lanes_of(levels), mer_even()
    incr = increments(own[...], other[...], rate, block_map, ice_mask, tracers, width)
    edges = []
    for s, ref in enumerate((from_west, from_east)):
        c = part(strips, 0 if s == 0 else width - 1, levels)
        for t in range(tracers):
            value = part(ref, t, levels).astype(f32) + part(ref, tracers + t, levels).astype(f32)
            sides[(2 * t + s) * levels:(2 * t + s + 1) * levels, :] = value
            edges.append((part(nu, t, levels) + (c if s == 0 else -c)) * value)
    solved = product(weights[...], jnp.concatenate(edges, axis=1))
    lanes = product(weights[...], mer_gain[...] * mer_halo(recv_mer, levels, mer_count))
    rim = jnp.logical_or(lane == 127, lane == 0)
    acc = [jnp.zeros((levels, 128), f32) for _ in send_mer]
    for t in range(tracers):
        for x in range(width):
            j = t * width + x
            value = part(partial, j, levels) + part(spread, 0, levels) * incr[j:j + 1, :]
            value = value + jnp.where(rim, at_edges(lanes, j), 0.0)
            if x in (0, width - 1):
                at = (0 if x == 0 else tracers) + t
                value = value + solved[:, at * 128:(at + 1) * 128]
            fresh[j * levels:(j + 1) * levels, :] = value
            pack_lanes(acc, value, j, lane, even)
        for s in range(2):
            pack_lanes(acc, part(sides, 2 * t + s, levels), tracers * width + 2 * t + s, lane, even)
    for ref, value in zip(send_mer, acc):
        ref[...] = value
    level = surface_level(levels)
    total = tracers * width
    surface[total:, :] = jnp.zeros((surface.shape[0] - total, 128), f32)
    for j in range(total):
        surface[j:j + 1, :] = fresh[pl.ds(j * levels + level, 1), :]
    for j in range(2 * tracers):
        surface[total + j:total + j + 1, :] = sides[pl.ds(j * levels + level, 1), :]


def sides_kernel(dims, columns, strips, nu, weights, sides, rate, block_map, ice_mask, own, other, from_west, from_east, edges, incr, inner_gain, outer_gain):
    tracers, levels, width = dims
    total = tracers * width
    lane = lanes_of(levels)
    incr[...] = increments(own[:total, :], other[:total, :], rate, block_map, ice_mask, tracers, width)
    extra = increments(own[total:, :], other[total:, :], rate, block_map, ice_mask, tracers, 2)
    at_level = lax.broadcasted_iota(jnp.int32, (levels, 128), 0) == surface_level(levels)
    terms, gains = [], []
    first = jnp.zeros((levels, 128), f32)
    later = jnp.zeros((levels, 128), f32)
    for s, ref in enumerate((from_west, from_east)):
        x = 0 if s == 0 else width - 1
        c, d = (part(ref, 3 * tracers + k, levels).astype(f32) for k in range(2))
        own_c = part(strips, x, levels)
        for t in range(tracers):
            mine, beyond = part(columns, t * width + x, levels), part(ref, 2 * tracers + t, levels).astype(f32)
            east, west = (mine, beyond) if s == 0 else (beyond, mine)
            value = horizontal(part(sides, 2 * t + s, levels), east, west, c, d, part(nu, t, levels), lane)
            value = value + jnp.where(at_level, jnp.broadcast_to(extra[2 * t + s:2 * t + s + 1, :], value.shape), 0.0)
            terms.append(value)
            gain = part(nu, t, levels) + (own_c if s == 0 else -own_c)
            gains.append(gain)
            j = t * width + x
            here = lane // 2 == j
            packed = both_edges(d, j)
            first = jnp.where(here, part(nu, t, levels) + jnp.where(lane % 2 == 0, -packed, packed), first)
            later = jnp.where(here, both_edges(gain, j), later)
    solved = product(weights[...], jnp.concatenate(terms, axis=1))
    solved = product(weights[...], solved * jnp.concatenate(gains, axis=1))
    for i in range(2 * tracers):
        edges[i * levels:(i + 1) * levels, :] = solved[:, i * 128:(i + 1) * 128]
    inner_gain[...] = first
    outer_gain[...] = later


def last_kernel(dims, mer_count, partial, edges, incr, weights, spread, mer_gain, inner_gain, outer_gain, *rest):
    tracers, levels, width = dims
    rounds = 1 if mer_count == 2 else 2
    recv_mer, (out, done, sems) = rest[:rounds], rest[rounds:]
    lane = lanes_of(levels)
    halo = mer_halo(recv_mer, levels, mer_count)
    corner = jnp.zeros((levels, 128), f32)
    for t in range(tracers):
        for s in range(2):
            j = t * width + (0 if s == 0 else width - 1)
            moved = pltpu.roll(halo, (2 * (j - tracers * width - 2 * t - s)) % 128, 1)
            corner = jnp.where(lane // 2 == j, moved, corner)
    corner = outer_gain[...] * product(weights[...], inner_gain[...] * corner)
    lanes = product(weights[...], mer_gain[...] * halo + corner)
    rim = jnp.logical_or(lane == 127, lane == 0)
    copies = []
    for t in range(tracers):
        for x in range(width):
            j = t * width + x
            value = part(partial, j, levels) + part(spread, 0, levels) * incr[j:j + 1, :]
            value = value + jnp.where(rim, at_edges(lanes, j), 0.0)
            if x in (0, width - 1):
                value = value + part(edges, (0 if x == 0 else tracers) + t, levels)
            done[j] = value
            copy = pltpu.make_async_copy(done.at[j], out.at[t, :, x, :], sems.at[j])
            copy.start()
            copies.append(copy)
    for copy in copies:
        copy.wait()


VM = pl.BlockSpec(memory_space=pltpu.VMEM)
SM = pl.BlockSpec(memory_space=pltpu.SMEM)


def call(body, name, in_specs, out_shape, flops, out_specs=None, scratch=()):
    many = isinstance(out_shape, list)
    return pl.pallas_call(
        body,
        out_shape=out_shape,
        in_specs=in_specs,
        out_specs=out_specs or ([VM] * len(out_shape) if many else VM),
        scratch_shapes=scratch,
        name=name,
        cost_estimate=pl.CostEstimate(flops=flops, bytes_accessed=2 << 20, transcendentals=0),
        compiler_params=pltpu.CompilerParams(vmem_limit_bytes=32 * 1024 * 1024),
    )


def on_device(state, flow, diffusion, column_solve, exchange_rate, block_map, ice_mask):
    _, tracers, levels, width, wide = state.shape
    mer_count, zon_count = lax.axis_size("mer"), lax.axis_size("zon")
    rounds = 1 if mer_count == 2 else 2
    dims = (tracers, levels, width)
    size, total = levels * width, tracers * width
    cells = state.reshape(tracers * size, wide)
    shape = lambda rows, dtype=f32: jax.ShapeDtypeStruct((rows, wide), dtype)
    small = (exchange_rate[0], block_map, ice_mask)
    small_specs = [SM] * 3
    message = shape((3 * tracers + 2) * levels, bf16)
    packed = shape(levels)

    def swap_mer(pieces):
        return [lax.ppermute(piece, "mer", pairs(mer_count, r == 1)) for r, piece in enumerate(pieces)]

    east_bound, west_bound, surface, frame, nu, weights, spread = call(
        functools.partial(pack_kernel, dims), "pack", [VM] * 4 + small_specs,
        [message, message, shape(total), shape(2 * size), shape(tracers * levels),
         jax.ShapeDtypeStruct((levels, 3 * levels), bf16), packed], 1 << 20,
    )(cells, flow.reshape(2 * size, wide), diffusion[0], column_solve[0], *small)
    from_west = lax.ppermute(east_bound, "zon", ring(zon_count, 1))
    columns, *send_mer = call(
        functools.partial(lanes_kernel, dims), "lanes", [VM], [shape(tracers * size)] + [packed] * rounds, 1 << 20,
    )(cells)
    recv_mer = swap_mer(send_mer)
    other = lax.ppermute(surface, "fluid", [(0, 1), (1, 0)])
    from_east = lax.ppermute(west_bound, "zon", ring(zon_count, -1))
    partial, strips, mer_gain = call(
        functools.partial(inner_kernel, dims), "inner", [VM] * 4,
        [shape(tracers * size), shape(2 * size), packed], 1 << 30,
    )(columns, frame, nu, weights)
    fresh, sides, fresh_surface, *send_mer = call(
        functools.partial(join_kernel, dims, mer_count), "join", [VM] * 6 + small_specs + [VM] * (4 + rounds),
        [shape(tracers * size), shape(2 * tracers * levels), shape(total + 8)] + [packed] * rounds, 1 << 26,
    )(partial, strips, nu, weights, spread, mer_gain, *small, surface, other, from_west, from_east, *recv_mer)
    recv_mer = swap_mer(send_mer)
    fresh_other = lax.ppermute(fresh_surface, "fluid", [(0, 1), (1, 0)])
    partial = call(
        functools.partial(second_kernel, dims), "second", [VM] * 4, shape(tracers * size), 1 << 30,
    )(fresh, strips, nu, weights)
    edges, incr, inner_gain, outer_gain = call(
        functools.partial(sides_kernel, dims), "sides", [VM] * 5 + small_specs + [VM] * 4,
        [shape(2 * tracers * levels), shape(total), packed, packed], 1 << 28,
    )(columns, strips, nu, weights, sides, *small, fresh_surface, fresh_other, from_west, from_east)
    done = call(
        functools.partial(last_kernel, dims, mer_count), "last", [VM] * (8 + rounds),
        jax.ShapeDtypeStruct(state.shape[1:], f32), 1 << 26,
        out_specs=pl.BlockSpec(memory_space=pl.ANY),
        scratch=[pltpu.VMEM((total, levels, wide), f32), pltpu.SemaphoreType.DMA((total,))],
    )(partial, edges, incr, weights, spread, mer_gain, inner_gain, outer_gain, *recv_mer)
    return done[None]


def solution(mesh):
    return jax.shard_map(
        on_device,
        mesh=mesh,
        in_specs=(
            P("fluid", None, None, "zon", "mer"),
            P("fluid", None, None, "zon", "mer"),
            P("fluid", None, None),
            P("fluid", None, None),
            P("fluid", None),
            P("mer"),
            P("mer"),
        ),
        out_specs=P("fluid", None, None, "zon", "mer"),
        check_vma=False,
    )
```

time: 26.8 us -> 24.1 us (0.90)
  waiting for transfers between devices: 6.18 us -> 1.48 us
  Pallas kernels: 6.65 us -> 9.08 us
  starting transfers between devices: 11.8 us -> 9.47 us
  local copies, waits for them, and re-layouts: 1.89 us -> 3.72 us
    ppermute x8 -> x6, waiting for transfers between devices: 6.18 us -> 1.48 us  [the longest x2 1.25 us: swap_mer(): lax.ppermute(piece, 'mer', pairs(mer_count, r == 1))]
    pallas_call x3 -> x7, Pallas kernels: 6.65 us -> 9.08 us  [the longest x1 2.48 us: on_device(): call(functools.partial(join_kernel, dims, mer_count), 'join', [VM] * 6 +...]
    ppermute x8 -> x6, starting transfers between devices: 11.8 us -> 9.47 us  [the longest x2 3.3 us: swap_mer(): lax.ppermute(piece, 'mer', pairs(mer_count, r == 1))]
    unnamed x14, local copies, waits for them, and re-layouts: 1.89 us -> 3.72 us
  transfers between devices with their start and end apart: 8 -> 6, of which waited for: 7 -> 3; matrix products, arithmetic and copies ran while one was open for 0% -> 0% of each run, Pallas kernels for 0% -> 16%
where the time goes in v2:
time: 24.1 us; the launch traced here: 23.8 us
  starting transfers between devices  9.47 us (39%)
  Pallas kernels  9.08 us (38%)
  local copies, waits for them, and re-layouts  3.72 us (15%)
  waiting for transfers between devices  1.48 us (6%)
    unnamed x14, local copies, waits for them, and re-layouts  3.72 us
    ppermute x2, starting transfers between devices, swap_mer(): lax.ppermute(piece, 'mer', pairs(mer_count, r == 1))  3.3 us
    ppermute x1, starting transfers between devices, on_device(): from_east = lax.ppermute(west_bound, 'zon', ring(zon_count, -1))  3.1 us
    ppermute x1, starting transfers between devices, on_device(): from_west = lax.ppermute(east_bound, 'zon', ring(zon_count, 1))  2.99 us
    pallas_call x1, Pallas kernels, on_device(): call(functools.partial(join_kernel, dims, mer_count), 'join', [VM] * 6 +...  2.48 us
    pallas_call x1, Pallas kernels, on_device(): call(functools.partial(last_kernel, dims, mer_count), 'last', [VM] * (8 +...  1.92 us
    pallas_call x1, Pallas kernels, on_device(): call(functools.partial(inner_kernel, dims), 'inner', [VM] * 4, [shape(tra...  1.32 us
    ppermute x2, waiting for transfers between devices, swap_mer(): lax.ppermute(piece, 'mer', pairs(mer_count, r == 1))  1.25 us
  transfers between devices with their start and end apart: 6, of which 3 were waited for; matrix products, arithmetic and copies ran while one was open for 0% of the time, Pallas kernels for 16%

profile of v2, /device:TPU:0, one launch (start us, length us, event | category | flops | bytes accessed | tf_op | source)
XLA Modules:
  0.0 23.8 jit_solution(15503711745015515366)
XLA Ops:
  0.0 0.0 copy-start.6
  0.0 0.0 copy-start.3
  0.0 0.0 copy-start.4
  0.0 0.0 copy-start.5
  0.0 0.7 %copy-done.6 = f32[1,2,64]{2,1,0:T(2,128)S(1)} copy-done((f32[1,2,64]{2,1,0:T(2,128)S(1)}, f32[1,2,64]{2,1,0:T(2,128)}, u32[]{:S(2)}) %copy-start.6) | copy-done | bytes 536
  0.7 0.0 copy-done.3
  0.7 0.0 copy-done.4
  0.7 0.0 copy-done.5
  0.7 0.0 copy-start
  0.7 1.2 %copy-done = f32[1,2,64,16,128]{4,3,2,1,0:T(8,128)S(1)} copy-done((f32[1,2,64,16,128]{4,3,2,1,0:T(8,128)S(1)}, f32[1,2,64,16,128]{4,3,2,1,0:T(8,128)}, u32[]{:S(2)}) %copy-start) | copy-done | bytes 1048600
  1.9 0.0 copy-start.1
  1.9 1.0 %copy-done.1 = bf16[1,2,64,16,128]{4,3,2,1,0:T(8,128)(2,1)S(1)} copy-done((bf16[1,2,64,16,128]{4,3,2,1,0:T(8,128)(2,1)S(1)}, bf16[1,2,64,16,128]{4,3,2,1,0:T(8,128)(2,1)}, u32[]{:S(2)}) %copy-start.1) | copy-done | bytes 524312
  3.0 0.0 copy-start.2
  3.0 0.8 %copy-done.2 = f32[1,64,64]{2,1,0:T(8,128)S(1)} copy-done((f32[1,64,64]{2,1,0:T(8,128)S(1)}, f32[1,64,64]{2,1,0:T(8,128)}, u32[]{:S(2)}) %copy-start.2) | copy-done | bytes 16408
  3.7 0.8 %pack.1 = (bf16[512,128]{1,0:T(8,128)(2,1)S(1)}, bf16[512,128]{1,0:T(8,128)(2,1)S(1)}, f32[32,128]{1,0:T(8,128)S(1)}, f32[2048,128]{1,0:T(8,128)S(1)}, f32[128,1...) custom-call(f32[2048,128]{1,0:T(8,128)S(1)} %bitcast.6, bf16[2048,128]{1,0:T(8,128)(2,1)S(1)} %bitcast.8, ...), custom_call_target="tpu_custom_call" | custom-call | flops 1048576 | bytes 2097152 | tf_op jit(solution)/shard_map/pack/pallas_call | solution.py:341
  4.6 3.0 %collective-permute-start.1 = (bf16[512,128]{1,0:T(8,128)(2,1)S(1)}, bf16[512,128]{1,0:T(8,128)(2,1)S(1)}, u32[]{:S(2)}, u32[]{:S(2)}) collective-permute-start(bf16[512,128]{1,0:T(8,128)(2,1)S(1)} %get-tuple-element.34), channel_id=1, source_target_pairs={{0,2},{2,4},{4,6},{6,8},{8,10},{10,12},{12,14},{14,0},{1,3},{3,5},... | collective-permute-start | bytes 393224 | tf_op jit(solution)/shard_map/ppermute | solution.py:346
  7.6 3.1 %collective-permute-start.2 = (bf16[512,128]{1,0:T(8,128)(2,1)S(1)}, bf16[512,128]{1,0:T(8,128)(2,1)S(1)}, u32[]{:S(2)}, u32[]{:S(2)}) collective-permute-start(bf16[512,128]{1,0:T(8,128)(2,1)S(1)} %get-tuple-element.35), channel_id=1, source_target_pairs={{0,14},{2,0},{4,2},{6,4},{8,6},{10,8},{12,10},{14,12},{1,15},{3,1}... | collective-permute-start | bytes 393224 | tf_op jit(solution)/shard_map/ppermute | solution.py:352
  10.7 0.5 %lanes.1 = (f32[2048,128]{1,0:T(8,128)S(1)}, f32[64,128]{1,0:T(8,128)S(1)}) custom-call(f32[2048,128]{1,0:T(8,128)S(1)} %bitcast.7), custom_call_target="tpu_custom_call" | custom-call | flops 1048576 | bytes 2097152 | tf_op jit(solution)/shard_map/lanes/pallas_call | solution.py:347
  11.1 1.7 %collective-permute-start.3 = (f32[64,128]{1,0:T(8,128)S(1)}, f32[64,128]{1,0:T(8,128)S(1)}, u32[]{:S(2)}, u32[]{:S(2)}) collective-permute-start(f32[64,128]{1,0:T(8,128)S(1)} %get-tuple-element.36), channel_id=1, source_target_pairs={{0,1},{1,0},{2,3},{3,2},{4,5},{5,4},{6,7},{7,6},{8,9},{9,8},{10,11... | collective-permute-start | bytes 98312 | tf_op jit(solution)/shard_map/ppermute | solution.py:339
  12.8 0.0 collective-permute-start
  12.8 1.3 %inner.1 = (f32[2048,128]{1,0:T(8,128)S(1)}, f32[2048,128]{1,0:T(8,128)S(1)}, f32[64,128]{1,0:T(8,128)S(1)}) custom-call(f32[2048,128]{1,0:T(8,128)S(1)} %get-tuple-element.25.columns, f32[2048,128]{1,0:T(8,128)S(1)} %get-tuple-element.26.frame, f32[128,128]{1,0:T(8,128)S(1)} %get-tuple-element.27.nu, bf16[64,192]{1,0:T(8,128)(2,1)S(1)} %get-tuple-element.28.weights), custom_call_target="tpu_custom_call" | custom-call | flops 1073741824 | bytes 2097152 | tf_op jit(solution)/shard_map/inner/pallas_call | solution.py:353
  14.2 0.0 collective-permute-done.other
  14.2 0.9 %collective-permute-done.3.rest_0_ = f32[64,128]{1,0:T(8,128)S(1)} collective-permute-done((f32[64,128]{1,0:T(8,128)S(1)}, f32[64,128]{1,0:T(8,128)S(1)}, u32[]{:S(2)}, u32[]{:S(2)}) %collective-permute-start.3) | collective-permute-done | bytes 32800 | tf_op jit(solution)/shard_map/ppermute | solution.py:339
  15.1 0.0 collective-permute-done.1.from_west
  15.1 0.2 collective-permute-done.2.from_east
  15.3 2.5 %join.1 = (f32[2048,128]{1,0:T(8,128)S(1)}, f32[256,128]{1,0:T(8,128)S(1)}, f32[40,128]{1,0:T(8,128)S(1)}, f32[64,128]{1,0:T(8,128)S(1)}) custom-call(f32[2048,128]{1,0:T(8,128)S(1)} %get-tuple-element.29.partial, f32[2048,128]{1,0:T(8,128)S(1)} %get-tuple-element.30.strips, f32[128,128]{1,0:T(8,128)S(1)} %get-tuple-element.27.nu, ...), custom_call_target="tpu_custom_call" | custom-call | flops 67108864 | bytes 2097152 | tf_op jit(solution)/shard_map/join/pallas_call | solution.py:357
  17.8 0.1 collective-permute-start.4
  17.9 1.6 %collective-permute-start.5 = (f32[64,128]{1,0:T(8,128)S(1)}, f32[64,128]{1,0:T(8,128)S(1)}, u32[]{:S(2)}, u32[]{:S(2)}) collective-permute-start(f32[64,128]{1,0:T(8,128)S(1)} %get-tuple-element.44), channel_id=1, source_target_pairs={{0,1},{1,0},{2,3},{3,2},{4,5},{5,4},{6,7},{7,6},{8,9},{9,8},{10,11... | collective-permute-start | bytes 98312 | tf_op jit(solution)/shard_map/ppermute | solution.py:339
  19.5 1.0 %second.1.partial = f32[2048,128]{1,0:T(8,128)S(1)} custom-call(f32[2048,128]{1,0:T(8,128)S(1)} %get-tuple-element.37.columns, f32[2048,128]{1,0:T(8,128)S(1)} %get-tuple-element.30.strips, f32[128,128]{1,0:T(8,128)S(1)} %get-tuple-element.27.nu, bf16[64,192]{1,0:T(8,128)(2,1)S(1)} %get-tuple-element.28.weights), custom_call_target="tpu_custom_call" | custom-call | flops 1073741824 | bytes 2097152 | tf_op jit(solution)/shard_map/second/pallas_call | solution.py:363
  20.5 0.0 collective-permute-done.4.other
  20.5 1.1 %sides.1 = (f32[256,128]{1,0:T(8,128)S(1)}, f32[32,128]{1,0:T(8,128)S(1)}, f32[64,128]{1,0:T(8,128)S(1)}, f32[64,128]{1,0:T(8,128)S(1)}) custom-call(f32[2048,128]{1,0:T(8,128)S(1)} %get-tuple-element.25.columns, f32[2048,128]{1,0:T(8,128)S(1)} %get-tuple-element.30.strips, f32[128,128]{1,0:T(8,128)S(1)} %get-tuple-element.27.nu, ...), custom_call_target="tpu_custom_call" | custom-call | flops 268435456 | bytes 2097152 | tf_op jit(solution)/shard_map/sides/pallas_call | solution.py:366
  21.6 0.3 %collective-permute-done.5.rest_0_ = f32[64,128]{1,0:T(8,128)S(1)} collective-permute-done((f32[64,128]{1,0:T(8,128)S(1)}, f32[64,128]{1,0:T(8,128)S(1)}, u32[]{:S(2)}, u32[]{:S(2)}) %collective-permute-start.5) | collective-permute-done | bytes 32800 | tf_op jit(solution)/shard_map/ppermute | solution.py:339
  21.9 1.9 %last.1 = f32[2,64,16,128]{3,2,1,0:T(8,128)} custom-call(f32[2048,128]{1,0:T(8,128)S(1)} %second.1.partial, f32[256,128]{1,0:T(8,128)S(1)} %get-tuple-element.40.edges, f32[32,128]{1,0:T(8,128)S(1)} %get-tuple-element.41.incr, bf16[64,192]{1,0:T(8,128)(2,1)S(1)} %get-tuple-element.28.weights, f32[64,128]{1,0:T(8,128)S(1)} %get-tuple-element.31.spread, ...), custom_call_target="tpu_custom_call" | custom-call | flops 67108864 | bytes 2097152 | tf_op jit(solution)/shard_map/last/pallas_call | solution.py:370
Async XLA Ops:
  0.0 0.7 %copy-start.6 = (f32[1,2,64]{2,1,0:T(2,128)S(1)}, f32[1,2,64]{2,1,0:T(2,128)}, u32[]{:S(2)}) copy-start(f32[1,2,64]{2,1,0:T(2,128)} %param.9) | copy-start | bytes 1540
  0.0 0.7 %copy-start.3 = (f32[1,2]{1,0:T(1,128)S(1)}, f32[1,2]{1,0:T(1,128)}, u32[]{:S(2)}) copy-start(f32[1,2]{1,0:T(1,128)} %param.11) | copy-start | bytes 28
  0.0 0.7 %copy-start.4 = (s32[4]{0:T(128)S(1)}, s32[4]{0:T(128)}, u32[]{:S(2)}) copy-start(s32[4]{0:T(128)} %block_map.5) | copy-start | bytes 52
  0.0 0.7 %copy-start.5 = (s32[4]{0:T(128)S(1)}, s32[4]{0:T(128)}, u32[]{:S(2)}) copy-start(s32[4]{0:T(128)} %ice_mask.5) | copy-start | bytes 52
  0.7 1.2 %copy-start = (f32[1,2,64,16,128]{4,3,2,1,0:T(8,128)S(1)}, f32[1,2,64,16,128]{4,3,2,1,0:T(8,128)}, u32[]{:S(2)}) copy-start(f32[1,2,64,16,128]{4,3,2,1,0:T(8,128)} %param.7) | copy-start | bytes 3145732
  1.9 1.0 %copy-start.1 = (bf16[1,2,64,16,128]{4,3,2,1,0:T(8,128)(2,1)S(1)}, bf16[1,2,64,16,128]{4,3,2,1,0:T(8,128)(2,1)}, u32[]{:S(2)}) copy-start(bf16[1,2,64,16,128]{4,3,2,1,0:T(8,128)(2,1)} %param.8) | copy-start | bytes 1572868
  3.0 0.8 %copy-start.2 = (f32[1,64,64]{2,1,0:T(8,128)S(1)}, f32[1,64,64]{2,1,0:T(8,128)}, u32[]{:S(2)}) copy-start(f32[1,64,64]{2,1,0:T(8,128)} %param.10) | copy-start | bytes 49156
  4.6 10.5 %collective-permute-start.1 = (bf16[512,128]{1,0:T(8,128)(2,1)S(1)}, bf16[512,128]{1,0:T(8,128)(2,1)S(1)}, u32[]{:S(2)}, u32[]{:S(2)}) collective-permute-start(bf16[512,128]{1,0:T(8,128)(2,1)S(1)} %get-tuple-element.34), channel_id=1, source_target_pairs={{0,2},{2,4},{4,6},{6,8},{8,10},{10,12},{12,14},{14,0},{1,3},{3,5},... | collective-permute-start | bytes 393224 | tf_op jit(solution)/shard_map/ppermute | solution.py:346
  7.6 7.8 %collective-permute-start.2 = (bf16[512,128]{1,0:T(8,128)(2,1)S(1)}, bf16[512,128]{1,0:T(8,128)(2,1)S(1)}, u32[]{:S(2)}, u32[]{:S(2)}) collective-permute-start(bf16[512,128]{1,0:T(8,128)(2,1)S(1)} %get-tuple-element.35), channel_id=1, source_target_pairs={{0,14},{2,0},{4,2},{6,4},{8,6},{10,8},{12,10},{14,12},{1,15},{3,1}... | collective-permute-start | bytes 393224 | tf_op jit(solution)/shard_map/ppermute | solution.py:352
  11.1 4.0 %collective-permute-start.3 = (f32[64,128]{1,0:T(8,128)S(1)}, f32[64,128]{1,0:T(8,128)S(1)}, u32[]{:S(2)}, u32[]{:S(2)}) collective-permute-start(f32[64,128]{1,0:T(8,128)S(1)} %get-tuple-element.36), channel_id=1, source_target_pairs={{0,1},{1,0},{2,3},{3,2},{4,5},{5,4},{6,7},{7,6},{8,9},{9,8},{10,11... | collective-permute-start | bytes 98312 | tf_op jit(solution)/shard_map/ppermute | solution.py:339
  12.8 1.3 %collective-permute-start = (f32[32,128]{1,0:T(8,128)S(1)}, f32[32,128]{1,0:T(8,128)S(1)}, u32[]{:S(2)}, u32[]{:S(2)}) collective-permute-start(f32[32,128]{1,0:T(8,128)S(1)} %get-tuple-element.33.own), channel_id=1, source_target_pairs={{0,16},{16,0},{1,17},{17,1},{2,18},{18,2},{3,19},{19,3},{4,20},{20... | collective-permute-start | bytes 49160 | tf_op jit(solution)/shard_map/ppermute | solution.py:351
  17.8 2.7 %collective-permute-start.4 = (f32[40,128]{1,0:T(8,128)S(1)}, f32[40,128]{1,0:T(8,128)S(1)}, u32[]{:S(2)}, u32[]{:S(2)}) collective-permute-start(f32[40,128]{1,0:T(8,128)S(1)} %get-tuple-element.39.own), channel_id=1, source_target_pairs={{0,16},{16,0},{1,17},{17,1},{2,18},{18,2},{3,19},{19,3},{4,20},{20... | collective-permute-start | bytes 61448 | tf_op jit(solution)/shard_map/ppermute | solution.py:362
  17.9 4.0 %collective-permute-start.5 = (f32[64,128]{1,0:T(8,128)S(1)}, f32[64,128]{1,0:T(8,128)S(1)}, u32[]{:S(2)}, u32[]{:S(2)}) collective-permute-start(f32[64,128]{1,0:T(8,128)S(1)} %get-tuple-element.44), channel_id=1, source_target_pairs={{0,1},{1,0},{2,3},{3,2},{4,5},{5,4},{6,7},{7,6},{8,9},{9,8},{10,11... | collective-permute-start | bytes 98312 | tf_op jit(solution)/shard_map/ppermute | solution.py:339

commit v3 on v2

v3 whole, which is shorter than its diff:
```python
import functools

import jax
import jax.numpy as jnp
from jax import lax
from jax.experimental import pallas as pl
from jax.experimental.pallas import tpu as pltpu
from jax.sharding import PartitionSpec as P

f32, bf16 = jnp.float32, jnp.bfloat16


def ring(count, ahead):
    return [(i, (i + ahead) % count) for i in range(count)]


def pairs(count, odd):
    if odd:
        return [(i, ((i + 1) ^ 1) - 1) for i in range(1, count - 1)] + [(0, count - 1), (count - 1, 0)]
    return [(i, i ^ 1) for i in range(count)]


def surface_level(levels):
    return jnp.where(lax.axis_index("fluid") == 0, levels - 1, 0)


def lanes_of(levels):
    return lax.broadcasted_iota(jnp.int32, (levels, 128), 1)


def split(value):
    high = value.astype(bf16)
    return high, (value - high.astype(f32)).astype(bf16)


def product(weights, value):
    high, low = split(value)
    return jnp.dot(weights, jnp.concatenate([high, low, high], axis=0), preferred_element_type=f32)


def part(ref, index, levels):
    return ref[index * levels:(index + 1) * levels, :]


def mer_halo(recv_mer, levels, mer_count):
    place = lax.axis_index("mer")
    even = 1 - lax.rem(place, 2)
    lane = lanes_of(levels)
    total = jnp.zeros((levels, 128), f32)
    for r, ref in enumerate(recv_mer):
        north = even if r == 0 else 1 - even
        inside = jnp.where(north == 1, place + 1 < mer_count, place > 0)
        keep = jnp.logical_and(lane % 2 == 1 - north, inside)
        moved = pltpu.roll(ref[...], jnp.where(north == 1, 127, 1), 1)
        total = total + jnp.where(keep, moved, 0.0)
    return total


def both_edges(cells, j):
    return pltpu.roll(cells, (2 * j + 1) % 128, 1)


def at_edges(packed, j):
    return pltpu.roll(packed, (127 - 2 * j) % 128, 1)


def increments(own, other, rate, block_map, ice_mask, tracers, per_tracer):
    blocks = block_map.shape[0]
    wide = own.shape[1] // blocks
    first = lax.axis_index("mer") * blocks
    is_atm = lax.axis_index("fluid") == 0
    atm = jnp.where(is_atm, own, other)
    ocean = jnp.where(is_atm, other, own)
    block = lax.broadcasted_iota(jnp.int32, own.shape, 1) // wide
    flux = jnp.zeros_like(own)
    for b in range(blocks):
        a = block_map[b] - first
        moved = pltpu.roll(atm, lax.rem((b - a + blocks) * wide, 128), 1)
        flux = jnp.where(block == b, (moved - ocean) * (1 - ice_mask[b]).astype(f32), flux)
    returned = jnp.zeros_like(own)
    for b in range(blocks):
        a = block_map[b] - first
        moved = pltpu.roll(flux, lax.rem((a - b + blocks) * wide, 128), 1)
        returned = jnp.where(block == a, moved, returned)
    tracer = lax.broadcasted_iota(jnp.int32, own.shape, 0) // per_tracer % tracers
    scale = jnp.full(own.shape, rate[0])
    for t in range(1, tracers):
        scale = jnp.where(tracer == t, rate[t], scale)
    return jnp.where(is_atm, -returned, flux) * scale


def horizontal(q, east, west, c, d, nu, lane):
    north = jnp.where(lane == 127, 0.0, pltpu.roll(q, 127, 1))
    south = jnp.where(lane == 0, 0.0, pltpu.roll(q, 1, 1))
    return q - c * (east - west) - d * (north - south) + nu * ((east + west) + (north + south) - 4.0 * q)


def interior(column, strip, nu, weights, store, dims):
    tracers, levels, width = dims
    lane = lanes_of(levels)
    zero = jnp.zeros((levels, 128), f32)
    for x in range(width):
        c, d = strip(0, x), strip(1, x)
        terms = []
        for t in range(tracers):
            west = zero if x == 0 else column(t, x - 1)
            east = zero if x == width - 1 else column(t, x + 1)
            terms.append(horizontal(column(t, x), east, west, c, d, part(nu, t, levels), lane))
        solved = product(weights[...], jnp.concatenate(terms, axis=1))
        for t in range(tracers):
            store(t, x, solved[:, t * 128:(t + 1) * 128])


def pack_kernel(dims, state, flow, east_bound, west_bound, surface, frame, columns, raw, sems):
    tracers, levels, width = dims
    size = levels * width
    level = surface_level(levels)
    places = ((east_bound, width - 1), (east_bound, width - 2), (west_bound, 0), (west_bound, 1))
    wait_columns, wait_flow, wait_rows = [], [], []
    for i, (_, x) in enumerate(places):
        for t in range(tracers):
            at = i * tracers + t
            wait_columns.append(pltpu.make_async_copy(state.at[t, :, x, :], columns.at[at], sems.at[at]))
    used = len(wait_columns)
    for k in range(2):
        wait_flow.append(pltpu.make_async_copy(flow.at[k], raw.at[k], sems.at[used + k]))
    for t in range(tracers):
        target = surface.at[pl.ds(t * width, width), :]
        wait_rows.append(pltpu.make_async_copy(state.at[t, level], target, sems.at[used + 2 + t]))
    for copy in wait_columns + wait_flow + wait_rows:
        copy.start()
    for copy in wait_columns:
        copy.wait()
    for i, (ref, _) in enumerate(places):
        for t in range(tracers):
            high, low = split(columns[i * tracers + t])
            if i % 2 == 0:
                ref[t * levels:(t + 1) * levels, :] = high
                ref[(tracers + t) * levels:(tracers + t + 1) * levels, :] = low
            else:
                ref[(2 * tracers + t) * levels:(2 * tracers + t + 1) * levels, :] = high
    for k, copy in enumerate(wait_flow):
        copy.wait()
        frame[k * size:(k + 1) * size, :] = raw[k].reshape(size, 128).astype(f32) * 0.5
        for ref, x in ((east_bound, width - 1), (west_bound, 0)):
            strip = frame[pl.ds(k * size + x, levels, stride=width), :].astype(bf16)
            ref[(3 * tracers + k) * levels:(3 * tracers + k + 1) * levels, :] = strip
    for copy in wait_rows:
        copy.wait()


def lanes_kernel(dims, cells, diffusion, solve, rate, block_map, ice_mask, columns, send_mer, nu, weights, spread):
    tracers, levels, width = dims
    lane = lanes_of(levels)
    packed = jnp.zeros((levels, 128), f32)
    for t in range(tracers):
        for x in range(width):
            j = t * width + x
            value = cells[pl.ds(t * levels * width + x, levels, stride=width), :]
            columns[j * levels:(j + 1) * levels, :] = value
            packed = jnp.where(lane // 2 == j, both_edges(value, j), packed)
        nu[t * levels:(t + 1) * levels, :] = jnp.transpose(jnp.broadcast_to(diffusion[t:t + 1, :], (128, levels)))
    send_mer[...] = packed
    high, low = split(solve[...])
    weights[...] = jnp.concatenate([high, high, low], axis=1)
    at_level = lax.broadcasted_iota(jnp.int32, (levels, levels), 1) == surface_level(levels)
    spread[...] = jnp.broadcast_to(jnp.sum(jnp.where(at_level, solve[...], 0.0), axis=1, keepdims=True), (levels, 128))


def inner_kernel(dims, columns, frame, nu, weights, partial, strips, mer_gain, edge_lanes, rows):
    tracers, levels, width = dims
    size = levels * width
    lane = lanes_of(levels)
    packed = jnp.zeros((levels, 128), f32)
    for k in range(2):
        for x in range(width):
            value = frame[pl.ds(k * size + x, levels, stride=width), :]
            strips[(k * width + x) * levels:(k * width + x + 1) * levels, :] = value
            if k == 1:
                packed = jnp.where(lane // 2 == x, both_edges(value, x), packed)
    gain = jnp.zeros((levels, 128), f32)
    for t in range(tracers):
        merid = packed if t == 0 else pltpu.roll(packed, 2 * t * width, 1)
        mine = part(nu, t, levels) + jnp.where(lane % 2 == 0, -merid, merid)
        gain = jnp.where(lane // (2 * width) == t, mine, gain)
    mer_gain[...] = gain
    found = [jnp.zeros((levels, 128), f32)]

    def store(t, x, value):
        j = t * width + x
        partial[j * levels:(j + 1) * levels, :] = value
        found[0] = jnp.where(lane // 2 == j, both_edges(value, j), found[0])

    column = lambda t, x: part(columns, t * width + x, levels)
    strip = lambda k, x: part(strips, k * width + x, levels)
    interior(column, strip, nu, weights, store, dims)
    edge_lanes[...] = found[0]
    level = surface_level(levels)
    for j in range(tracers * width):
        rows[j:j + 1, :] = partial[pl.ds(j * levels + level, 1), :]


def side_terms(ref, s, strips, nu, sides, dims):
    tracers, levels, width = dims
    c = part(strips, 0 if s == 0 else width - 1, levels)
    terms = []
    for t in range(tracers):
        value = part(ref, t, levels).astype(f32) + part(ref, tracers + t, levels).astype(f32)
        sides[t * levels:(t + 1) * levels, :] = value
        terms.append((part(nu, t, levels) + (c if s == 0 else -c)) * value)
    return terms


def side_lanes(packed, s, sides, solved, lane, dims):
    tracers, levels, width = dims
    for t in range(tracers):
        j = t * width + (0 if s == 0 else width - 1)
        packed = packed + jnp.where(lane // 2 == j, both_edges(part(solved, t, levels), j), 0.0)
        j = tracers * width + s * tracers + t
        packed = jnp.where(lane // 2 == j, both_edges(part(sides, t, levels), j), packed)
    return packed


def side_rows(fresh, surface, s, sides, solved, row, level, dims):
    tracers, levels, width = dims
    total = tracers * width
    for t in range(tracers):
        line = solved[pl.ds(t * levels + level, 1), :]
        fresh = fresh + jnp.where(row == t * width + (0 if s == 0 else width - 1), line, 0.0)
        at = total + s * tracers + t
        surface[at:at + 1, :] = sides[pl.ds(t * levels + level, 1), :]
    return fresh


def west_kernel(dims, mer_count, strips, nu, weights, spread, mer_gain, edge_lanes, rows, rate, block_map, ice_mask, own, other, from_west, *rest):
    tracers, levels, width = dims
    total = tracers * width
    rounds = len(rest) - 6
    recv_mer, (sides, solved, lanes, incr, half_lanes, surface) = rest[:rounds], rest[rounds:]
    lane = lanes_of(levels)
    terms = side_terms(from_west, 0, strips, nu, sides, dims)
    terms.append(mer_gain[...] * mer_halo(recv_mer, levels, mer_count))
    result = product(weights[...], jnp.concatenate(terms, axis=1))
    flux = increments(own[...], other[...], rate, block_map, ice_mask, tracers, width)
    incr[...] = flux
    for t in range(tracers):
        solved[t * levels:(t + 1) * levels, :] = result[:, t * 128:(t + 1) * 128]
    lanes[...] = result[:, tracers * 128:]
    row = lax.broadcasted_iota(jnp.int32, (total, 128), 0)
    rows_lane = lax.broadcasted_iota(jnp.int32, (total, 128), 1)
    turned = pltpu.roll(flux, 1, 1, stride=2, stride_axis=0)
    turned = jnp.sum(jnp.where(rows_lane // 2 == row, turned, 0.0), axis=0, keepdims=True)
    packed = edge_lanes[...] + lanes[...] + spread[...] * turned
    half_lanes[...] = side_lanes(packed, 0, sides, solved, lane, dims)
    level = surface_level(levels)
    fresh = rows[...] + spread[pl.ds(level, 1), :] * flux
    line = jnp.broadcast_to(lanes[pl.ds(level, 1), :], (total, 128))
    line = jnp.take_along_axis(line, 2 * row + (rows_lane == 0).astype(jnp.int32), axis=1)
    fresh = fresh + jnp.where(jnp.logical_or(rows_lane == 127, rows_lane == 0), line, 0.0)
    surface[total:, :] = jnp.zeros((surface.shape[0] - total, 128), f32)
    surface[:total, :] = side_rows(fresh, surface, 0, sides, solved, row, level, dims)


def east_kernel(dims, strips, nu, weights, half_lanes, half_surface, from_east, sides, solved, surface, send_mer):
    tracers, levels, width = dims
    total = tracers * width
    lane = lanes_of(levels)
    terms = side_terms(from_east, 1, strips, nu, sides, dims)
    result = product(weights[...], jnp.concatenate(terms, axis=1))
    for t in range(tracers):
        solved[t * levels:(t + 1) * levels, :] = result[:, t * 128:(t + 1) * 128]
    send_mer[...] = side_lanes(half_lanes[...], 1, sides, solved, lane, dims)
    surface[...] = half_surface[...]
    row = lax.broadcasted_iota(jnp.int32, (total, 128), 0)
    surface[:total, :] = side_rows(half_surface[:total, :], surface, 1, sides, solved, row, surface_level(levels), dims)


def middle_kernel(dims, partial, strips, nu, weights, spread, west_sides, east_sides, west_solved, east_solved, lanes, incr, columns, rate, block_map, ice_mask, own, other, from_west, from_east, again, edges, flux, inner_gain, outer_gain, fresh):
    tracers, levels, width = dims
    total = tracers * width
    lane = lanes_of(levels)
    flux[...] = increments(own[:total, :], other[:total, :], rate, block_map, ice_mask, tracers, width)
    extra = increments(own[total:, :], other[total:, :], rate, block_map, ice_mask, tracers, 1)
    at_level = lax.broadcasted_iota(jnp.int32, (levels, 128), 0) == surface_level(levels)
    terms, gains = [], []
    first = jnp.zeros((levels, 128), f32)
    later = jnp.zeros((levels, 128), f32)
    for s, (ref, sides) in enumerate(((from_west, west_sides), (from_east, east_sides))):
        x = 0 if s == 0 else width - 1
        c, d = (part(ref, 3 * tracers + k, levels).astype(f32) for k in range(2))
        own_c = part(strips, x, levels)
        for t in range(tracers):
            mine, beyond = part(columns, t * width + x, levels), part(ref, 2 * tracers + t, levels).astype(f32)
            east, west = (mine, beyond) if s == 0 else (beyond, mine)
            value = horizontal(part(sides, t, levels), east, west, c, d, part(nu, t, levels), lane)
            value = value + jnp.where(at_level, jnp.broadcast_to(extra[s * tracers + t:s * tracers + t + 1, :], value.shape), 0.0)
            terms.append(value)
            gain = part(nu, t, levels) + (own_c if s == 0 else -own_c)
            gains.append(gain)
            j = t * width + x
            here = lane // 2 == j
            packed = both_edges(d, j)
            first = jnp.where(here, part(nu, t, levels) + jnp.where(lane % 2 == 0, -packed, packed), first)
            later = jnp.where(here, both_edges(gain, j), later)
    inner_gain[...] = first
    outer_gain[...] = later
    result = product(weights[...], jnp.concatenate(terms, axis=1))
    result = product(weights[...], result * jnp.concatenate(gains, axis=1))
    for i in range(2 * tracers):
        edges[i * levels:(i + 1) * levels, :] = result[:, i * 128:(i + 1) * 128]
    rim = jnp.logical_or(lane == 127, lane == 0)
    for t in range(tracers):
        for x in range(width):
            j = t * width + x
            value = part(partial, j, levels) + spread[...] * incr[j:j + 1, :]
            value = value + jnp.where(rim, at_edges(lanes[...], j), 0.0)
            if x in (0, width - 1):
                value = value + part(west_solved if x == 0 else east_solved, t, levels)
            fresh[j * levels:(j + 1) * levels, :] = value

    def store(t, x, value):
        again[pl.ds((t * width + x) * levels, levels), :] = value

    column = lambda t, x: part(fresh, t * width + x, levels)
    strip = lambda k, x: part(strips, k * width + x, levels)
    interior(column, strip, nu, weights, store, dims)


def last_kernel(dims, mer_count, partial, edges, incr, weights, spread, mer_gain, inner_gain, outer_gain, *rest):
    tracers, levels, width = dims
    rounds = len(rest) - 3
    recv_mer, (out, done, sems) = rest[:rounds], rest[rounds:]
    lane = lanes_of(levels)
    halo = mer_halo(recv_mer, levels, mer_count)
    lanes = product(weights[...], mer_gain[...] * halo)
    corner = jnp.zeros((levels, 128), f32)
    for t in range(tracers):
        for s in range(2):
            j = t * width + (0 if s == 0 else width - 1)
            moved = pltpu.roll(halo, (2 * (j - tracers * width - s * tracers - t)) % 128, 1)
            corner = jnp.where(lane // 2 == j, moved, corner)
    corner = outer_gain[...] * product(weights[...], inner_gain[...] * corner)
    corner = product(weights[...], corner) + lanes
    rim = jnp.logical_or(lane == 127, lane == 0)
    copies = []
    for x in list(range(1, width - 1)) + [0, width - 1]:
        for t in range(tracers):
            j = t * width + x
            value = part(partial, j, levels) + spread[...] * incr[j:j + 1, :]
            value = value + jnp.where(rim, at_edges(corner if x in (0, width - 1) else lanes, j), 0.0)
            if x in (0, width - 1):
                value = value + part(edges, (0 if x == 0 else tracers) + t, levels)
            done[j] = value
            copy = pltpu.make_async_copy(done.at[j], out.at[t, :, x, :], sems.at[j])
            copy.start()
            copies.append(copy)
    for copy in copies:
        copy.wait()


VM = pl.BlockSpec(memory_space=pltpu.VMEM)
SM = pl.BlockSpec(memory_space=pltpu.SMEM)
HB = pl.BlockSpec(memory_space=pltpu.HBM)


def call(body, name, in_specs, out_shape, flops, out_specs=None, scratch=()):
    many = isinstance(out_shape, list)
    return pl.pallas_call(
        body,
        out_shape=out_shape,
        in_specs=in_specs,
        out_specs=out_specs or ([VM] * len(out_shape) if many else VM),
        scratch_shapes=scratch,
        name=name,
        cost_estimate=pl.CostEstimate(flops=flops, bytes_accessed=2 << 20, transcendentals=0),
        compiler_params=pltpu.CompilerParams(vmem_limit_bytes=32 * 1024 * 1024),
    )


def on_device(state, flow, diffusion, column_solve, exchange_rate, block_map, ice_mask):
    _, tracers, levels, width, wide = state.shape
    mer_count, zon_count = lax.axis_size("mer"), lax.axis_size("zon")
    rounds = 1 if mer_count == 2 else 2
    dims = (tracers, levels, width)
    size, total = levels * width, tracers * width
    shape = lambda rows, dtype=f32: jax.ShapeDtypeStruct((rows, wide), dtype)
    small = (exchange_rate[0], block_map, ice_mask)
    small_specs = [SM] * 3
    message = shape((3 * tracers + 2) * levels, bf16)
    packed = shape(levels)
    kept = shape(tracers * size)
    halved = shape(tracers * levels)
    sided = shape(2 * tracers * levels)

    def swap_mer(piece):
        return [lax.ppermute(piece, "mer", pairs(mer_count, r == 1)) for r in range(rounds)]

    def swap_fluid(piece):
        return lax.ppermute(piece, "fluid", [(0, 1), (1, 0)])

    east_bound, west_bound, surface, frame = call(
        functools.partial(pack_kernel, dims), "pack", [HB] * 2, [message, message, shape(total), shape(2 * size)], 1 << 20,
        scratch=[pltpu.VMEM((4 * tracers, levels, wide), f32), pltpu.VMEM((2, levels, width, wide), bf16),
                 pltpu.SemaphoreType.DMA((5 * tracers + 2,))],
    )(pltpu.with_memory_space_constraint(state[0], pltpu.HBM), pltpu.with_memory_space_constraint(flow[0], pltpu.HBM))
    from_west = lax.ppermute(east_bound, "zon", ring(zon_count, 1))
    columns, send_mer, nu, weights, spread = call(
        functools.partial(lanes_kernel, dims), "lanes", [VM] * 3 + small_specs,
        [kept, packed, shape(tracers * levels), jax.ShapeDtypeStruct((levels, 3 * levels), bf16), packed], 1 << 20,
    )(state.reshape(tracers * size, wide), diffusion[0], column_solve[0], *small)
    west_bound, send_mer, surface = lax.optimization_barrier((west_bound, send_mer, surface))
    recv_mer = swap_mer(send_mer)
    other = swap_fluid(surface)
    from_east = lax.ppermute(west_bound, "zon", ring(zon_count, -1))
    partial, strips, mer_gain, edge_lanes, rows = call(
        functools.partial(inner_kernel, dims), "inner", [VM] * 4, [kept, shape(2 * size), packed, packed, shape(total)], 1 << 30,
    )(columns, frame, nu, weights)
    west_sides, west_solved, lanes, incr, half_lanes, half_surface = call(
        functools.partial(west_kernel, dims, mer_count), "west", [VM] * 7 + small_specs + [VM] * (3 + rounds),
        [halved, halved, packed, shape(total), packed, shape(total + 8)], 1 << 33,
    )(strips, nu, weights, spread, mer_gain, edge_lanes, rows, *small, surface, other, from_west, *recv_mer)
    east_sides, east_solved, fresh_surface, send_mer = call(
        functools.partial(east_kernel, dims), "east", [VM] * 6, [halved, halved, shape(total + 8), packed], 1 << 26,
    )(strips, nu, weights, half_lanes, half_surface, from_east)
    recv_mer = swap_mer(send_mer)
    fresh_other = swap_fluid(fresh_surface)
    again, edges, flux, inner_gain, outer_gain = call(
        functools.partial(middle_kernel, dims), "middle", [VM] * 12 + small_specs + [VM] * 4,
        [kept, sided, shape(total), packed, packed], 1 << 30, scratch=[pltpu.VMEM((tracers * size, wide), f32)],
    )(partial, strips, nu, weights, spread, west_sides, east_sides, west_solved, east_solved, lanes, incr, columns, *small, fresh_surface, fresh_other, from_west, from_east)
    done = call(
        functools.partial(last_kernel, dims, mer_count), "last", [VM] * (8 + rounds),
        jax.ShapeDtypeStruct(state.shape[1:], f32), 1 << 26,
        out_specs=pl.BlockSpec(memory_space=pl.ANY),
        scratch=[pltpu.VMEM((total, levels, wide), f32), pltpu.SemaphoreType.DMA((total,))],
    )(again, edges, flux, weights, spread, mer_gain, inner_gain, outer_gain, *recv_mer)
    return done[None]


def solution(mesh):
    return jax.shard_map(
        on_device,
        mesh=mesh,
        in_specs=(
            P("fluid", None, None, "zon", "mer"),
            P("fluid", None, None, "zon", "mer"),
            P("fluid", None, None),
            P("fluid", None, None),
            P("fluid", None),
            P("mer"),
            P("mer"),
        ),
        out_specs=P("fluid", None, None, "zon", "mer"),
        check_vma=False,
    )
```

time: 24.1 us -> 21.5 us (0.89)
  local copies, waits for them, and re-layouts: 3.72 us -> 0.67 us
  Pallas kernels: 9.08 us -> 10.7 us
  starting transfers between devices: 9.47 us -> 8.35 us
    unnamed x14 -> x12, local copies, waits for them, and re-layouts: 3.72 us -> 0.67 us
    pallas_call x6, Pallas kernels: 7.16 us -> 8.99 us  [the longest x1 3.29 us: on_device(): call(functools.partial(inner_kernel, dims), 'inner', [VM] * 4, [kept, sha...]
    ppermute x2, starting transfers between devices: 3.3 us -> 1.98 us  [swap_mer(): lax.ppermute(piece, 'mer', pairs(mer_count, r == 1))]
    ppermute x2, waiting for transfers between devices: 0.01 us -> 0.78 us  [swap_fluid(): return lax.ppermute(piece, 'fluid', [(0, 1), (1, 0)])]
    ppermute x2, waiting for transfers between devices: 1.25 us -> 0.73 us  [swap_mer(): lax.ppermute(piece, 'mer', pairs(mer_count, r == 1))]
  transfers between devices with their start and end apart: 6 -> 6, of which waited for: 3 -> 2; matrix products, arithmetic and copies ran while one was open for 0% -> 0% of each run, Pallas kernels for 16% -> 34%
where the time goes in v3:
time: 21.5 us; the launch traced here: 21.3 us
  Pallas kernels  10.7 us (50%)
  starting transfers between devices  8.35 us (39%)
  waiting for transfers between devices  1.52 us (7%)
  local copies, waits for them, and re-layouts  0.67 us (3%)
    pallas_call x1, Pallas kernels, on_device(): call(functools.partial(inner_kernel, dims), 'inner', [VM] * 4, [kept, sha...  3.29 us
    ppermute x1, starting transfers between devices, on_device(): from_east = lax.ppermute(west_bound, 'zon', ring(zon_count, -1))  3.23 us
    ppermute x1, starting transfers between devices, on_device(): from_west = lax.ppermute(east_bound, 'zon', ring(zon_count, 1))  3 us
    pallas_call x1, Pallas kernels, on_device(): call(functools.partial(middle_kernel, dims), 'middle', [VM] * 12 + small_...  2.07 us
    ppermute x2, starting transfers between devices, swap_mer(): lax.ppermute(piece, 'mer', pairs(mer_count, r == 1))  1.98 us
    pallas_call x1, Pallas kernels, on_device(): call(functools.partial(last_kernel, dims, mer_count), 'last', [VM] * (8 +...  1.7 us
    pallas_call x1, Pallas kernels, on_device(): call(functools.partial(pack_kernel, dims), 'pack', [HB] * 2, [message, me...  1.48 us
    pallas_call x1, Pallas kernels, on_device(): call(functools.partial(lanes_kernel, dims), 'lanes', [VM] * 3 + small_spe...  1.03 us
  transfers between devices with their start and end apart: 6, of which 2 were waited for; matrix products, arithmetic and copies ran while one was open for 0% of the time, Pallas kernels for 34%

profile of v3, /device:TPU:0, one launch (start us, length us, event | category | flops | bytes accessed | tf_op | source)
XLA Modules:
  0.0 21.3 jit_solution(8517801902213864561)
XLA Ops:
  0.0 0.0 copy-start
  0.0 0.0 copy-start.1
  0.0 0.0 copy-start.4
  0.0 0.0 copy-start.5
  0.0 1.5 %pack.1 = (bf16[512,128]{1,0:T(8,128)(2,1)S(1)}, bf16[512,128]{1,0:T(8,128)(2,1)S(1)}, f32[32,128]{1,0:T(8,128)S(1)}, f32[2048,128]{1,0:T(8,128)S(1)}) custom-call(f32[2,64,16,128]{3,2,1,0:T(8,128)} %bitcast.7, bf16[2,64,16,128]{3,2,1,0:T(8,128)(2,1)} %bitcast.14), custom_call_target="tpu_custom_call" | custom-call | flops 1048576 | bytes 2097152 | tf_op jit(solution)/shard_map/pack/pallas_call | solution.py:401
  1.5 3.0 %collective-permute-start.1 = (bf16[512,128]{1,0:T(8,128)(2,1)S(1)}, bf16[512,128]{1,0:T(8,128)(2,1)S(1)}, u32[]{:S(2)}, u32[]{:S(2)}) collective-permute-start(bf16[512,128]{1,0:T(8,128)(2,1)S(1)} %get-tuple-element.51), channel_id=1, source_target_pairs={{0,2},{2,4},{4,6},{6,8},{8,10},{10,12},{12,14},{14,0},{1,3},{3,5},... | collective-permute-start | bytes 393224 | tf_op jit(solution)/shard_map/ppermute | solution.py:406
  4.5 0.0 copy-start.2
  4.5 0.0 copy-start.3
  4.5 0.0 copy-done
  4.5 0.0 copy-done.1
  4.5 0.0 copy-done.4
  4.5 0.0 copy-done.5
  4.5 0.6 %copy-done.2 = f32[1,2,64]{2,1,0:T(2,128)S(1)} copy-done((f32[1,2,64]{2,1,0:T(2,128)S(1)}, f32[1,2,64]{2,1,0:T(2,128)}, u32[]{:S(2)}) %copy-start.2) | copy-done | bytes 536
  5.2 0.0 copy-done.3
  5.2 1.0 %lanes.1 = (f32[2048,128]{1,0:T(8,128)S(1)}, f32[64,128]{1,0:T(8,128)S(1)}, f32[128,128]{1,0:T(8,128)S(1)}, bf16[64,192]{1,0:T(8,128)(2,1)S(1)}, f32[64,128]{1,0:T(8,128)S(1)}) custom-call(f32[2048,128]{1,0:T(8,128)S(1)} %bitcast.8, f32[2,64]{1,0:T(2,128)S(1)} %bitcast.10, f32[64,64]{1,0:T(8,128)S(1)} %bitcast.9, f32[2]{0:T(128)S(1)} %bitcast.11, ...), custom_call_target="tpu_custom_call" | custom-call | flops 1048576 | bytes 2097152 | tf_op jit(solution)/shard_map/lanes/pallas_call | solution.py:407
  6.2 0.1 collective-permute-start
  6.3 1.6 %collective-permute-start.2 = (f32[64,128]{1,0:T(8,128)S(1)}, f32[64,128]{1,0:T(8,128)S(1)}, u32[]{:S(2)}, u32[]{:S(2)}) collective-permute-start(f32[64,128]{1,0:T(8,128)S(1)} %get-tuple-element.52), channel_id=1, source_target_pairs={{0,1},{1,0},{2,3},{3,2},{4,5},{5,4},{6,7},{7,6},{8,9},{9,8},{10,11... | collective-permute-start | bytes 98312 | tf_op jit(solution)/shard_map/ppermute | solution.py:396
  7.9 3.2 %collective-permute-start.3 = (bf16[512,128]{1,0:T(8,128)(2,1)S(1)}, bf16[512,128]{1,0:T(8,128)(2,1)S(1)}, u32[]{:S(2)}, u32[]{:S(2)}) collective-permute-start(bf16[512,128]{1,0:T(8,128)(2,1)S(1)} %get-tuple-element.56), channel_id=1, source_target_pairs={{0,14},{2,0},{4,2},{6,4},{8,6},{10,8},{12,10},{14,12},{1,15},{3,1}... | collective-permute-start | bytes 393224 | tf_op jit(solution)/shard_map/ppermute | solution.py:414
  11.1 3.3 %inner.1 = (f32[2048,128]{1,0:T(8,128)S(1)}, f32[2048,128]{1,0:T(8,128)S(1)}, f32[64,128]{1,0:T(8,128)S(1)}, f32[64,128]{1,0:T(8,128)S(1)}, f32[32,128]{1,0:T(8,128)S(1)}) custom-call(f32[2048,128]{1,0:T(8,128)S(1)} %get-tuple-element.37.columns, f32[2048,128]{1,0:T(8,128)S(1)} %get-tuple-element.38.frame, f32[128,128]{1,0:T(8,128)S(1)} %get-tuple-element.39.nu, ...), custom_call_target="tpu_custom_call" | custom-call | flops 1073741824 | bytes 2097152 | tf_op jit(solution)/shard_map/inner/pallas_call | solution.py:415
  14.4 0.0 collective-permute-done.other
  14.4 0.0 collective-permute-done.2.rest_0_
  14.4 0.0 collective-permute-done.1.from_west
  14.4 0.9 %west.1 = (f32[128,128]{1,0:T(8,128)S(1)}, f32[128,128]{1,0:T(8,128)S(1)}, f32[64,128]{1,0:T(8,128)S(1)}, f32[32,128]{1,0:T(8,128)S(1)}, f32[64,128]{1,0:T(8,128)S(1)}, /*index=5*/f32[40,128]{1,0:T(8,128)S(1)}) custom-call(f32[2048,128]{1,0:T(8,128)S(1)} %get-tuple-element.42.strips, f32[128,128]{1,0:T(8,128)S(1)} %get-tuple-element.39.nu, ...), custom_call_target="tpu_custom_call" | custom-call | flops 8589934592 | bytes 2097152 | tf_op jit(solution)/shard_map/west/pallas_call | solution.py:418
  15.3 0.0 collective-permute-done.3.from_east
  15.3 0.2 %east.1 = (f32[128,128]{1,0:T(8,128)S(1)}, f32[128,128]{1,0:T(8,128)S(1)}, f32[40,128]{1,0:T(8,128)S(1)}, f32[64,128]{1,0:T(8,128)S(1)}) custom-call(f32[2048,128]{1,0:T(8,128)S(1)} %get-tuple-element.42.strips, f32[128,128]{1,0:T(8,128)S(1)} %get-tuple-element.39.nu, bf16[64,192]{1,0:T(8,128)(2,1)S(1)} %get-tuple-element.40.weights, ...), custom_call_target="tpu_custom_call" | custom-call | flops 67108864 | bytes 2097152 | tf_op jit(solution)/shard_map/east/pallas_call | solution.py:422
  15.6 0.1 collective-permute-start.4
  15.7 0.4 %collective-permute-start.5 = (f32[64,128]{1,0:T(8,128)S(1)}, f32[64,128]{1,0:T(8,128)S(1)}, u32[]{:S(2)}, u32[]{:S(2)}) collective-permute-start(f32[64,128]{1,0:T(8,128)S(1)} %get-tuple-element.68), channel_id=1, source_target_pairs={{0,1},{1,0},{2,3},{3,2},{4,5},{5,4},{6,7},{7,6},{8,9},{9,8},{10,11... | collective-permute-start | bytes 98312 | tf_op jit(solution)/shard_map/ppermute | solution.py:396
  16.0 0.8 %collective-permute-done.4.other = f32[40,128]{1,0:T(8,128)S(1)} collective-permute-done((f32[40,128]{1,0:T(8,128)S(1)}, f32[40,128]{1,0:T(8,128)S(1)}, u32[]{:S(2)}, u32[]{:S(2)}) %collective-permute-start.4) | collective-permute-done | bytes 20512 | tf_op jit(solution)/shard_map/ppermute | solution.py:399
  16.8 2.1 %middle.1 = (f32[2048,128]{1,0:T(8,128)S(1)}, f32[256,128]{1,0:T(8,128)S(1)}, f32[32,128]{1,0:T(8,128)S(1)}, f32[64,128]{1,0:T(8,128)S(1)}, f32[64,128]{1,0:T(8,128)S(1)}) custom-call(f32[2048,128]{1,0:T(8,128)S(1)} %get-tuple-element.41.partial, f32[2048,128]{1,0:T(8,128)S(1)} %get-tuple-element.42.strips, f32[128,128]{1,0:T(8,128)S(1)} %get-tuple-element.39.nu, ...), custom_call_target="tpu_custom_call" | custom-call | flops 1073741824 | bytes 2097152 | tf_op jit(solution)/shard_map/middle/pallas_call | solution.py:427
  18.9 0.7 %collective-permute-done.5.rest_0_ = f32[64,128]{1,0:T(8,128)S(1)} collective-permute-done((f32[64,128]{1,0:T(8,128)S(1)}, f32[64,128]{1,0:T(8,128)S(1)}, u32[]{:S(2)}, u32[]{:S(2)}) %collective-permute-start.5) | collective-permute-done | bytes 32800 | tf_op jit(solution)/shard_map/ppermute | solution.py:396
  19.6 1.7 %last.1 = f32[2,64,16,128]{3,2,1,0:T(8,128)} custom-call(f32[2048,128]{1,0:T(8,128)S(1)} %get-tuple-element.63.partial, f32[256,128]{1,0:T(8,128)S(1)} %get-tuple-element.64.edges, f32[32,128]{1,0:T(8,128)S(1)} %get-tuple-element.65.incr, bf16[64,192]{1,0:T(8,128)(2,1)S(1)} %get-tuple-element.40.weights, f32[64,128]{1,0:T(8,128)S(1)} %get-tuple-element.43.spread, ...), custom_call_target="tpu_custom_call" | custom-call | flops 67108864 | bytes 2097152 | tf_op jit(solution)/shard_map/last/pallas_call | solution.py:431
Async XLA Ops:
  0.0 4.5 %copy-start = (f32[1,2,64,16,128]{4,3,2,1,0:T(8,128)S(1)}, f32[1,2,64,16,128]{4,3,2,1,0:T(8,128)}, u32[]{:S(2)}) copy-start(f32[1,2,64,16,128]{4,3,2,1,0:T(8,128)} %param.7) | copy-start | bytes 3145732
  0.0 4.5 %copy-start.1 = (f32[1,64,64]{2,1,0:T(8,128)S(1)}, f32[1,64,64]{2,1,0:T(8,128)}, u32[]{:S(2)}) copy-start(f32[1,64,64]{2,1,0:T(8,128)} %param.10) | copy-start | bytes 49156
  0.0 4.5 %copy-start.4 = (s32[4]{0:T(128)S(1)}, s32[4]{0:T(128)}, u32[]{:S(2)}) copy-start(s32[4]{0:T(128)} %block_map.5) | copy-start | bytes 52
  0.0 4.5 %copy-start.5 = (s32[4]{0:T(128)S(1)}, s32[4]{0:T(128)}, u32[]{:S(2)}) copy-start(s32[4]{0:T(128)} %ice_mask.5) | copy-start | bytes 52
  1.5 12.9 %collective-permute-start.1 = (bf16[512,128]{1,0:T(8,128)(2,1)S(1)}, bf16[512,128]{1,0:T(8,128)(2,1)S(1)}, u32[]{:S(2)}, u32[]{:S(2)}) collective-permute-start(bf16[512,128]{1,0:T(8,128)(2,1)S(1)} %get-tuple-element.51), channel_id=1, source_target_pairs={{0,2},{2,4},{4,6},{6,8},{8,10},{10,12},{12,14},{14,0},{1,3},{3,5},... | collective-permute-start | bytes 393224 | tf_op jit(solution)/shard_map/ppermute | solution.py:406
  4.5 0.7 %copy-start.2 = (f32[1,2,64]{2,1,0:T(2,128)S(1)}, f32[1,2,64]{2,1,0:T(2,128)}, u32[]{:S(2)}) copy-start(f32[1,2,64]{2,1,0:T(2,128)} %param.9) | copy-start | bytes 1540
  4.5 0.7 %copy-start.3 = (f32[1,2]{1,0:T(1,128)S(1)}, f32[1,2]{1,0:T(1,128)}, u32[]{:S(2)}) copy-start(f32[1,2]{1,0:T(1,128)} %param.11) | copy-start | bytes 28
  6.2 8.2 %collective-permute-start = (f32[32,128]{1,0:T(8,128)S(1)}, f32[32,128]{1,0:T(8,128)S(1)}, u32[]{:S(2)}, u32[]{:S(2)}) collective-permute-start(f32[32,128]{1,0:T(8,128)S(1)} %get-tuple-element.50.own), channel_id=1, source_target_pairs={{0,16},{16,0},{1,17},{17,1},{2,18},{18,2},{3,19},{19,3},{4,20},{20... | collective-permute-start | bytes 49160 | tf_op jit(solution)/shard_map/ppermute | solution.py:399
  6.3 8.1 %collective-permute-start.2 = (f32[64,128]{1,0:T(8,128)S(1)}, f32[64,128]{1,0:T(8,128)S(1)}, u32[]{:S(2)}, u32[]{:S(2)}) collective-permute-start(f32[64,128]{1,0:T(8,128)S(1)} %get-tuple-element.52), channel_id=1, source_target_pairs={{0,1},{1,0},{2,3},{3,2},{4,5},{5,4},{6,7},{7,6},{8,9},{9,8},{10,11... | collective-permute-start | bytes 98312 | tf_op jit(solution)/shard_map/ppermute | solution.py:396
  7.9 7.4 %collective-permute-start.3 = (bf16[512,128]{1,0:T(8,128)(2,1)S(1)}, bf16[512,128]{1,0:T(8,128)(2,1)S(1)}, u32[]{:S(2)}, u32[]{:S(2)}) collective-permute-start(bf16[512,128]{1,0:T(8,128)(2,1)S(1)} %get-tuple-element.56), channel_id=1, source_target_pairs={{0,14},{2,0},{4,2},{6,4},{8,6},{10,8},{12,10},{14,12},{1,15},{3,1}... | collective-permute-start | bytes 393224 | tf_op jit(solution)/shard_map/ppermute | solution.py:414
  15.6 1.3 %collective-permute-start.4 = (f32[40,128]{1,0:T(8,128)S(1)}, f32[40,128]{1,0:T(8,128)S(1)}, u32[]{:S(2)}, u32[]{:S(2)}) collective-permute-start(f32[40,128]{1,0:T(8,128)S(1)} %get-tuple-element.62.own), channel_id=1, source_target_pairs={{0,16},{16,0},{1,17},{17,1},{2,18},{18,2},{3,19},{19,3},{4,20},{20... | collective-permute-start | bytes 61448 | tf_op jit(solution)/shard_map/ppermute | solution.py:399
  15.7 4.0 %collective-permute-start.5 = (f32[64,128]{1,0:T(8,128)S(1)}, f32[64,128]{1,0:T(8,128)S(1)}, u32[]{:S(2)}, u32[]{:S(2)}) collective-permute-start(f32[64,128]{1,0:T(8,128)S(1)} %get-tuple-element.68), channel_id=1, source_target_pairs={{0,1},{1,0},{2,3},{3,2},{4,5},{5,4},{6,7},{7,6},{8,9},{9,8},{10,11... | collective-permute-start | bytes 98312 | tf_op jit(solution)/shard_map/ppermute | solution.py:396

commit v4 on v3

--- a/solution.py
+++ b/solution.py
@@ -64,29 +64,40 @@
     return pltpu.roll(packed, (127 - 2 * j) % 128, 1)
 
 
-def increments(own, other, rate, block_map, ice_mask, tracers, per_tracer):
-    blocks = block_map.shape[0]
-    wide = own.shape[1] // blocks
-    first = lax.axis_index("mer") * blocks
+def increments(own, other, guide, tracers, per_tracer):
     is_atm = lax.axis_index("fluid") == 0
+    pick = lambda row: jnp.broadcast_to(guide[row:row + 1, :].astype(jnp.int32), own.shape)
     atm = jnp.where(is_atm, own, other)
     ocean = jnp.where(is_atm, other, own)
-    block = lax.broadcasted_iota(jnp.int32, own.shape, 1) // wide
-    flux = jnp.zeros_like(own)
+    flux = (jnp.take_along_axis(atm, pick(0), axis=1) - ocean) * guide[2:3, :]
+    returned = jnp.take_along_axis(flux, pick(1), axis=1)
+    tracer = lax.broadcasted_iota(jnp.int32, own.shape, 0) // per_tracer % tracers
+    scale = jnp.broadcast_to(guide[3:4, :], own.shape)
+    for t in range(1, tracers):
+        scale = jnp.where(tracer == t, guide[3 + t:4 + t, :], scale)
+    return jnp.where(is_atm, -returned, flux) * scale
+
+
+def fill_guide(guide, rate, block_map, ice_mask, tracers):
+    blocks = block_map.shape[1]
+    lane = lax.broadcasted_iota(jnp.int32, (1, 128), 1)
+    wide = 128 // blocks
+    block, within = lane // wide, lane % wide
+    first = lax.axis_index("mer") * blocks
+    mapped = jnp.zeros((1, 128), jnp.int32)
+    returned = jnp.zeros((1, 128), jnp.int32)
+    is_open = jnp.zeros((1, 128), jnp.int32)
     for b in range(blocks):
-        a = block_map[b] - first
-        moved = pltpu.roll(atm, lax.rem((b - a + blocks) * wide, 128), 1)
-        flux = jnp.where(block == b, (moved - ocean) * (1 - ice_mask[b]).astype(f32), flux)
-    returned = jnp.zeros_like(own)
-    for b in range(blocks):
-        a = block_map[b] - first
-        moved = pltpu.roll(flux, lax.rem((a - b + blocks) * wide, 128), 1)
-        returned = jnp.where(block == a, moved, returned)
-    tracer = lax.broadcasted_iota(jnp.int32, own.shape, 0) // per_tracer % tracers
-    scale = jnp.full(own.shape, rate[0])
-    for t in range(1, tracers):
-        scale = jnp.where(tracer == t, rate[t], scale)
-    return jnp.where(is_atm, -returned, flux) * scale
+        above = block_map[:, b:b + 1] - first
+        mapped = jnp.where(block == b, above, mapped)
+        returned = jnp.where(block == above, b, returned)
+        is_open = jnp.where(block == b, 1 - ice_mask[:, b:b + 1], is_open)
+    guide[...] = jnp.zeros(guide.shape, f32)
+    guide[0:1, :] = (mapped * wide + within).astype(f32)
+    guide[1:2, :] = (returned * wide + within).astype(f32)
+    guide[2:3, :] = is_open.astype(f32)
+    for t in range(tracers):
+        guide[3 + t:4 + t, :] = jnp.broadcast_to(rate[:, t:t + 1], (1, 128))
 
 
 def horizontal(q, east, west, c, d, nu, lane):
@@ -111,9 +122,12 @@
             store(t, x, solved[:, t * 128:(t + 1) * 128])
 
 
-def pack_kernel(dims, state, flow, east_bound, west_bound, surface, frame, columns, raw, sems):
+def pack_kernel(dims, state, flow, *rest):
     tracers, levels, width = dims
     size = levels * width
+    fixed = len(rest) - 7 >> 1
+    east_bound, west_bound, surface, frame = rest[fixed:fixed + 4]
+    columns, raw, sems = rest[2 * fixed + 4:]
     level = surface_level(levels)
     places = ((east_bound, width - 1), (east_bound, width - 2), (west_bound, 0), (west_bound, 1))
     wait_columns, wait_flow, wait_rows = [], [], []
@@ -127,6 +141,8 @@
     for t in range(tracers):
         target = surface.at[pl.ds(t * width, width), :]
         wait_rows.append(pltpu.make_async_copy(state.at[t, level], target, sems.at[used + 2 + t]))
+    for i in range(fixed):
+        wait_rows.append(pltpu.make_async_copy(rest[i], rest[fixed + 4 + i], sems.at[used + 2 + tracers + i]))
     for copy in wait_columns + wait_flow + wait_rows:
         copy.start()
     for copy in wait_columns:
@@ -149,7 +165,7 @@
         copy.wait()
 
 
-def lanes_kernel(dims, cells, diffusion, solve, rate, block_map, ice_mask, columns, send_mer, nu, weights, spread):
+def lanes_kernel(dims, cells, diffusion, solve, rate, block_map, ice_mask, columns, send_mer, nu, weights, spread, guide):
     tracers, levels, width = dims
     lane = lanes_of(levels)
     packed = jnp.zeros((levels, 128), f32)
@@ -164,6 +180,7 @@
     high, low = split(solve[...])
     weights[...] = jnp.concatenate([high, high, low], axis=1)
     at_level = lax.broadcasted_iota(jnp.int32, (levels, levels), 1) == surface_level(levels)
+    fill_guide(guide, rate, block_map, ice_mask, tracers)
     spread[...] = jnp.broadcast_to(jnp.sum(jnp.where(at_level, solve[...], 0.0), axis=1, keepdims=True), (levels, 128))
 
 
@@ -184,18 +201,19 @@
         mine = part(nu, t, levels) + jnp.where(lane % 2 == 0, -merid, merid)
         gain = jnp.where(lane // (2 * width) == t, mine, gain)
     mer_gain[...] = gain
-    found = [jnp.zeros((levels, 128), f32)]
 
     def store(t, x, value):
         j = t * width + x
         partial[j * levels:(j + 1) * levels, :] = value
-        found[0] = jnp.where(lane // 2 == j, both_edges(value, j), found[0])
 
     column = lambda t, x: part(columns, t * width + x, levels)
     strip = lambda k, x: part(strips, k * width + x, levels)
     interior(column, strip, nu, weights, store, dims)
-    edge_lanes[...] = found[0]
     level = surface_level(levels)
+    packed = jnp.zeros((levels, 128), f32)
+    for j in range(tracers * width):
+        packed = jnp.where(lane // 2 == j, both_edges(part(partial, j, levels), j), packed)
+    edge_lanes[...] = packed
     for j in range(tracers * width):
         rows[j:j + 1, :] = partial[pl.ds(j * levels + level, 1), :]
 
@@ -232,7 +250,7 @@
     return fresh
 
 
-def west_kernel(dims, mer_count, strips, nu, weights, spread, mer_gain, edge_lanes, rows, rate, block_map, ice_mask, own, other, from_west, *rest):
+def west_kernel(dims, mer_count, strips, nu, weights, spread, mer_gain, edge_lanes, rows, guide, own, other, from_west, *rest):
     tracers, levels, width = dims
     total = tracers * width
     rounds = len(rest) - 6
@@ -241,7 +259,7 @@
     terms = side_terms(from_west, 0, strips, nu, sides, dims)
     terms.append(mer_gain[...] * mer_halo(recv_mer, levels, mer_count))
     result = product(weights[...], jnp.concatenate(terms, axis=1))
-    flux = increments(own[...], other[...], rate, block_map, ice_mask, tracers, width)
+    flux = increments(own[...], other[...], guide, tracers, width)
     incr[...] = flux
     for t in range(tracers):
         solved[t * levels:(t + 1) * levels, :] = result[:, t * 128:(t + 1) * 128]
@@ -275,12 +293,12 @@
     surface[:total, :] = side_rows(half_surface[:total, :], surface, 1, sides, solved, row, surface_level(levels), dims)
 
 
-def middle_kernel(dims, partial, strips, nu, weights, spread, west_sides, east_sides, west_solved, east_solved, lanes, incr, columns, rate, block_map, ice_mask, own, other, from_west, from_east, again, edges, flux, inner_gain, outer_gain, fresh):
+def middle_kernel(dims, partial, strips, nu, weights, spread, west_sides, east_sides, west_solved, east_solved, lanes, incr, columns, guide, own, other, from_west, from_east, again, edges, flux, inner_gain, outer_gain, fresh):
     tracers, levels, width = dims
     total = tracers * width
     lane = lanes_of(levels)
-    flux[...] = increments(own[:total, :], other[:total, :], rate, block_map, ice_mask, tracers, width)
-    extra = increments(own[total:, :], other[total:, :], rate, block_map, ice_mask, tracers, 1)
+    flux[...] = increments(own[:total, :], other[:total, :], guide, tracers, width)
+    extra = increments(own[total:, :], other[total:, :], guide, tracers, 1)
     at_level = lax.broadcasted_iota(jnp.int32, (levels, 128), 0) == surface_level(levels)
     terms, gains = [], []
     first = jnp.zeros((levels, 128), f32)
@@ -359,7 +377,6 @@
 
 
 VM = pl.BlockSpec(memory_space=pltpu.VMEM)
-SM = pl.BlockSpec(memory_space=pltpu.SMEM)
 HB = pl.BlockSpec(memory_space=pltpu.HBM)
 
 
@@ -384,8 +401,6 @@
     dims = (tracers, levels, width)
     size, total = levels * width, tracers * width
     shape = lambda rows, dtype=f32: jax.ShapeDtypeStruct((rows, wide), dtype)
-    small = (exchange_rate[0], block_map, ice_mask)
-    small_specs = [SM] * 3
     message = shape((3 * tracers + 2) * levels, bf16)
     packed = shape(levels)
     kept = shape(tracers * size)
@@ -398,16 +413,19 @@
     def swap_fluid(piece):
         return lax.ppermute(piece, "fluid", [(0, 1), (1, 0)])
 
-    east_bound, west_bound, surface, frame = call(
-        functools.partial(pack_kernel, dims), "pack", [HB] * 2, [message, message, shape(total), shape(2 * size)], 1 << 20,
+    params = (diffusion[0], column_solve[0], exchange_rate, block_map[None], ice_mask[None])
+    in_hbm = [pltpu.with_memory_space_constraint(value, pltpu.HBM) for value in (state[0], flow[0]) + params]
+    east_bound, west_bound, surface, frame, *params = call(
+        functools.partial(pack_kernel, dims), "pack", [HB] * len(in_hbm),
+        [message, message, shape(total), shape(2 * size)] + [jax.ShapeDtypeStruct(p.shape, p.dtype) for p in params], 1 << 20,
         scratch=[pltpu.VMEM((4 * tracers, levels, wide), f32), pltpu.VMEM((2, levels, width, wide), bf16),
-                 pltpu.SemaphoreType.DMA((5 * tracers + 2,))],
-    )(pltpu.with_memory_space_constraint(state[0], pltpu.HBM), pltpu.with_memory_space_constraint(flow[0], pltpu.HBM))
+                 pltpu.SemaphoreType.DMA((5 * tracers + 2 + len(params),))],
+    )(*in_hbm)
     from_west = lax.ppermute(east_bound, "zon", ring(zon_count, 1))
-    columns, send_mer, nu, weights, spread = call(
-        functools.partial(lanes_kernel, dims), "lanes", [VM] * 3 + small_specs,
-        [kept, packed, shape(tracers * levels), jax.ShapeDtypeStruct((levels, 3 * levels), bf16), packed], 1 << 20,
-    )(state.reshape(tracers * size, wide), diffusion[0], column_solve[0], *small)
+    columns, send_mer, nu, weights, spread, guide = call(
+        functools.partial(lanes_kernel, dims), "lanes", [VM] * 6,
+        [kept, packed, shape(tracers * levels), jax.ShapeDtypeStruct((levels, 3 * levels), bf16), packed, shape(8)], 1 << 20,
+    )(state.reshape(tracers * size, wide), *params)
     west_bound, send_mer, surface = lax.optimization_barrier((west_bound, send_mer, surface))
     recv_mer = swap_mer(send_mer)
     other = swap_fluid(surface)
@@ -416,18 +434,18 @@
         functools.partial(inner_kernel, dims), "inner", [VM] * 4, [kept, shape(2 * size), packed, packed, shape(total)], 1 << 30,
     )(columns, frame, nu, weights)
     west_sides, west_solved, lanes, incr, half_lanes, half_surface = call(
-        functools.partial(west_kernel, dims, mer_count), "west", [VM] * 7 + small_specs + [VM] * (3 + rounds),
+        functools.partial(west_kernel, dims, mer_count), "west", [VM] * (11 + rounds),
         [halved, halved, packed, shape(total), packed, shape(total + 8)], 1 << 33,
-    )(strips, nu, weights, spread, mer_gain, edge_lanes, rows, *small, surface, other, from_west, *recv_mer)
+    )(strips, nu, weights, spread, mer_gain, edge_lanes, rows, guide, surface, other, from_west, *recv_mer)
     east_sides, east_solved, fresh_surface, send_mer = call(
         functools.partial(east_kernel, dims), "east", [VM] * 6, [halved, halved, shape(total + 8), packed], 1 << 26,
     )(strips, nu, weights, half_lanes, half_surface, from_east)
     recv_mer = swap_mer(send_mer)
     fresh_other = swap_fluid(fresh_surface)
     again, edges, flux, inner_gain, outer_gain = call(
-        functools.partial(middle_kernel, dims), "middle", [VM] * 12 + small_specs + [VM] * 4,
+        functools.partial(middle_kernel, dims), "middle", [VM] * 17,
         [kept, sided, shape(total), packed, packed], 1 << 30, scratch=[pltpu.VMEM((tracers * size, wide), f32)],
-    )(partial, strips, nu, weights, spread, west_sides, east_sides, west_solved, east_solved, lanes, incr, columns, *small, fresh_surface, fresh_other, from_west, from_east)
+    )(partial, strips, nu, weights, spread, west_sides, east_sides, west_solved, east_solved, lanes, incr, columns, guide, fresh_surface, fresh_other, from_west, from_east)
     done = call(
         functools.partial(last_kernel, dims, mer_count), "last", [VM] * (8 + rounds),
         jax.ShapeDtypeStruct(state.shape[1:], f32), 1 << 26,

time: 21.5 us -> 20 us (0.930)
  Pallas kernels: 10.7 us -> 7.57 us
  starting transfers between devices: 8.35 us -> 9.54 us
  waiting for transfers between devices: 1.52 us -> 2.69 us
  local copies, waits for them, and re-layouts: 0.67 us -> 0.01 us
    ppermute x1, waiting for transfers between devices: 0.01 us -> 1.79 us  [on_device(): from_east = lax.ppermute(west_bound, 'zon', ring(zon_count, -1))]
    pallas_call x4, Pallas kernels: 5.46 us -> 3.86 us  [the longest x1 1.53 us: on_device(): call(functools.partial(pack_kernel, dims), 'pack', [HB] * len(in_hbm), [m...]
    pallas_call x1, Pallas kernels: 3.29 us -> 1.78 us  [on_device(): call(functools.partial(inner_kernel, dims), 'inner', [VM] * 4, [kept, sha...]
    ppermute x2, starting transfers between devices: 1.98 us -> 3.14 us  [swap_mer(): lax.ppermute(piece, 'mer', pairs(mer_count, r == 1))]
    ppermute x2, waiting for transfers between devices: 0.78 us -> 0.01 us  [swap_fluid(): return lax.ppermute(piece, 'fluid', [(0, 1), (1, 0)])]
    unnamed x12 -> x2, local copies, waits for them, and re-layouts: 0.67 us -> 0.01 us
  transfers between devices with their start and end apart: 6 -> 6, of which waited for: 2 -> 2; matrix products, arithmetic and copies ran while one was open for 0% -> 0% of each run, Pallas kernels for 34% -> 21%
where the time goes in v4:
time: 20 us; the launch traced here: 19.9 us
  starting transfers between devices  9.54 us (48%)
  Pallas kernels  7.57 us (38%)
  waiting for transfers between devices  2.69 us (13%)
    ppermute x1, starting transfers between devices, on_device(): from_east = lax.ppermute(west_bound, 'zon', ring(zon_count, -1))  3.23 us
    ppermute x2, starting transfers between devices, swap_mer(): lax.ppermute(piece, 'mer', pairs(mer_count, r == 1))  3.14 us
    ppermute x1, starting transfers between devices, on_device(): from_west = lax.ppermute(east_bound, 'zon', ring(zon_count, 1))  2.99 us
    ppermute x1, waiting for transfers between devices, on_device(): from_east = lax.ppermute(west_bound, 'zon', ring(zon_count, -1))  1.79 us
    pallas_call x1, Pallas kernels, on_device(): call(functools.partial(inner_kernel, dims), 'inner', [VM] * 4, [kept, sha...  1.78 us
    pallas_call x1, Pallas kernels, on_device(): call(functools.partial(last_kernel, dims, mer_count), 'last', [VM] * (8 +...  1.7 us
    pallas_call x1, Pallas kernels, on_device(): call(functools.partial(pack_kernel, dims), 'pack', [HB] * len(in_hbm), [m...  1.53 us
    pallas_call x1, Pallas kernels, on_device(): call(functools.partial(middle_kernel, dims), 'middle', [VM] * 17, [kept,...  1.5 us
  transfers between devices with their start and end apart: 6, of which 2 were waited for; matrix products, arithmetic and copies ran while one was open for 0% of the time, Pallas kernels for 21%

profile of v4, /device:TPU:0, one launch (start us, length us, event | category | flops | bytes accessed | tf_op | source)
XLA Modules:
  0.0 19.9 jit_solution(1819212863705805103)
XLA Ops:
  0.0 0.0 copy-start
  0.0 1.5 %pack.1 = (bf16[512,128]{1,0:T(8,128)(2,1)S(1)}, bf16[512,128]{1,0:T(8,128)(2,1)S(1)}, f32[32,128]{1,0:T(8,128)S(1)}, f32[2048,128]{1,0:T(8,128)S(1)}, f32[2,64]...) custom-call(f32[2,64,16,128]{3,2,1,0:T(8,128)} %bitcast.8, ...), custom_call_target="tpu_custom_call" | custom-call | flops 1048576 | bytes 2097152 | tf_op jit(solution)/shard_map/pack/pallas_call | solution.py:418
  1.5 3.0 %collective-permute-start.1 = (bf16[512,128]{1,0:T(8,128)(2,1)S(1)}, bf16[512,128]{1,0:T(8,128)(2,1)S(1)}, u32[]{:S(2)}, u32[]{:S(2)}) collective-permute-start(bf16[512,128]{1,0:T(8,128)(2,1)S(1)} %get-tuple-element.63), channel_id=1, source_target_pairs={{0,2},{2,4},{4,6},{6,8},{8,10},{10,12},{12,14},{14,0},{1,3},{3,5},... | collective-permute-start | bytes 393224 | tf_op jit(solution)/shard_map/ppermute | solution.py:424
  4.5 0.0 copy-done
  4.5 0.5 %lanes.1 = (f32[2048,128]{1,0:T(8,128)S(1)}, f32[64,128]{1,0:T(8,128)S(1)}, f32[128,128]{1,0:T(8,128)S(1)}, bf16[64,192]{1,0:T(8,128)(2,1)S(1)}, f32[64,128]{1,0:T(8,128)S(1)}, /*index=5*/f32[8,128]{1,0:T(8,128)S(1)}) custom-call(f32[2048,128]{1,0:T(8,128)S(1)} %bitcast.9, f32[2,64]{1,0:T(2,128)S(1)} %get-tuple-element.43.diffusion, ...), custom_call_target="tpu_custom_call" | custom-call | flops 1048576 | bytes 2097152 | tf_op jit(solution)/shard_map/lanes/pallas_call | solution.py:425
  5.0 0.1 collective-permute-start
  5.1 1.6 %collective-permute-start.2 = (f32[64,128]{1,0:T(8,128)S(1)}, f32[64,128]{1,0:T(8,128)S(1)}, u32[]{:S(2)}, u32[]{:S(2)}) collective-permute-start(f32[64,128]{1,0:T(8,128)S(1)} %get-tuple-element.64), channel_id=1, source_target_pairs={{0,1},{1,0},{2,3},{3,2},{4,5},{5,4},{6,7},{7,6},{8,9},{9,8},{10,11... | collective-permute-start | bytes 98312 | tf_op jit(solution)/shard_map/ppermute | solution.py:411
  6.7 3.2 %collective-permute-start.3 = (bf16[512,128]{1,0:T(8,128)(2,1)S(1)}, bf16[512,128]{1,0:T(8,128)(2,1)S(1)}, u32[]{:S(2)}, u32[]{:S(2)}) collective-permute-start(bf16[512,128]{1,0:T(8,128)(2,1)S(1)} %get-tuple-element.68), channel_id=1, source_target_pairs={{0,14},{2,0},{4,2},{6,4},{8,6},{10,8},{12,10},{14,12},{1,15},{3,1}... | collective-permute-start | bytes 393224 | tf_op jit(solution)/shard_map/ppermute | solution.py:432
  9.9 1.8 %inner.1 = (f32[2048,128]{1,0:T(8,128)S(1)}, f32[2048,128]{1,0:T(8,128)S(1)}, f32[64,128]{1,0:T(8,128)S(1)}, f32[64,128]{1,0:T(8,128)S(1)}, f32[32,128]{1,0:T(8,128)S(1)}) custom-call(f32[2048,128]{1,0:T(8,128)S(1)} %get-tuple-element.48.columns, f32[2048,128]{1,0:T(8,128)S(1)} %get-tuple-element.49.frame, f32[128,128]{1,0:T(8,128)S(1)} %get-tuple-element.50.nu, ...), custom_call_target="tpu_custom_call" | custom-call | flops 1073741824 | bytes 2097152 | tf_op jit(solution)/shard_map/inner/pallas_call | solution.py:433
  11.7 0.0 collective-permute-done.other
  11.7 0.0 collective-permute-done.2.rest_0_
  11.7 0.0 collective-permute-done.1.from_west
  11.8 0.3 %west.1 = (f32[128,128]{1,0:T(8,128)S(1)}, f32[128,128]{1,0:T(8,128)S(1)}, f32[64,128]{1,0:T(8,128)S(1)}, f32[32,128]{1,0:T(8,128)S(1)}, f32[64,128]{1,0:T(8,128)S(1)}, /*index=5*/f32[40,128]{1,0:T(8,128)S(1)}) custom-call(f32[2048,128]{1,0:T(8,128)S(1)} %get-tuple-element.53.strips, f32[128,128]{1,0:T(8,128)S(1)} %get-tuple-element.50.nu, ...), custom_call_target="tpu_custom_call" | custom-call | flops 8589934592 | bytes 2097152 | tf_op jit(solution)/shard_map/west/pallas_call | solution.py:436
  12.1 1.8 %collective-permute-done.3.from_east = bf16[512,128]{1,0:T(8,128)(2,1)S(1)} collective-permute-done((bf16[512,128]{1,0:T(8,128)(2,1)S(1)}, bf16[512,128]{1,0:T(8,128)(2,1)S(1)}, u32[]{:S(2)}, u32[]{:S(2)}) %collective-permute-start.3) | collective-permute-done | bytes 131104 | tf_op jit(solution)/shard_map/ppermute | solution.py:432
  13.9 0.2 %east.1 = (f32[128,128]{1,0:T(8,128)S(1)}, f32[128,128]{1,0:T(8,128)S(1)}, f32[40,128]{1,0:T(8,128)S(1)}, f32[64,128]{1,0:T(8,128)S(1)}) custom-call(f32[2048,128]{1,0:T(8,128)S(1)} %get-tuple-element.53.strips, f32[128,128]{1,0:T(8,128)S(1)} %get-tuple-element.50.nu, bf16[64,192]{1,0:T(8,128)(2,1)S(1)} %get-tuple-element.51.weights, ...), custom_call_target="tpu_custom_call" | custom-call | flops 67108864 | bytes 2097152 | tf_op jit(solution)/shard_map/east/pallas_call | solution.py:440
  14.1 0.1 collective-permute-start.4
  14.2 1.6 %collective-permute-start.5 = (f32[64,128]{1,0:T(8,128)S(1)}, f32[64,128]{1,0:T(8,128)S(1)}, u32[]{:S(2)}, u32[]{:S(2)}) collective-permute-start(f32[64,128]{1,0:T(8,128)S(1)} %get-tuple-element.80), channel_id=1, source_target_pairs={{0,1},{1,0},{2,3},{3,2},{4,5},{5,4},{6,7},{7,6},{8,9},{9,8},{10,11... | collective-permute-start | bytes 98312 | tf_op jit(solution)/shard_map/ppermute | solution.py:411
  15.8 0.0 collective-permute-done.4.other
  15.8 1.5 %middle.1 = (f32[2048,128]{1,0:T(8,128)S(1)}, f32[256,128]{1,0:T(8,128)S(1)}, f32[32,128]{1,0:T(8,128)S(1)}, f32[64,128]{1,0:T(8,128)S(1)}, f32[64,128]{1,0:T(8,128)S(1)}) custom-call(f32[2048,128]{1,0:T(8,128)S(1)} %get-tuple-element.52.partial, f32[2048,128]{1,0:T(8,128)S(1)} %get-tuple-element.53.strips, f32[128,128]{1,0:T(8,128)S(1)} %get-tuple-element.50.nu, ...), custom_call_target="tpu_custom_call" | custom-call | flops 1073741824 | bytes 2097152 | tf_op jit(solution)/shard_map/middle/pallas_call | solution.py:445
  17.3 0.9 %collective-permute-done.5.rest_0_ = f32[64,128]{1,0:T(8,128)S(1)} collective-permute-done((f32[64,128]{1,0:T(8,128)S(1)}, f32[64,128]{1,0:T(8,128)S(1)}, u32[]{:S(2)}, u32[]{:S(2)}) %collective-permute-start.5) | collective-permute-done | bytes 32800 | tf_op jit(solution)/shard_map/ppermute | solution.py:411
  18.2 1.7 %last.1 = f32[2,64,16,128]{3,2,1,0:T(8,128)} custom-call(f32[2048,128]{1,0:T(8,128)S(1)} %get-tuple-element.75.partial, f32[256,128]{1,0:T(8,128)S(1)} %get-tuple-element.76.edges, f32[32,128]{1,0:T(8,128)S(1)} %get-tuple-element.77.incr, bf16[64,192]{1,0:T(8,128)(2,1)S(1)} %get-tuple-element.51.weights, f32[64,128]{1,0:T(8,128)S(1)} %get-tuple-element.54.spread, ...), custom_call_target="tpu_custom_call" | custom-call | flops 67108864 | bytes 2097152 | tf_op jit(solution)/shard_map/last/pallas_call | solution.py:449
Async XLA Ops:
  0.0 4.5 %copy-start = (f32[1,2,64,16,128]{4,3,2,1,0:T(8,128)S(1)}, f32[1,2,64,16,128]{4,3,2,1,0:T(8,128)}, u32[]{:S(2)}) copy-start(f32[1,2,64,16,128]{4,3,2,1,0:T(8,128)} %param.7) | copy-start | bytes 3145732
  1.5 10.2 %collective-permute-start.1 = (bf16[512,128]{1,0:T(8,128)(2,1)S(1)}, bf16[512,128]{1,0:T(8,128)(2,1)S(1)}, u32[]{:S(2)}, u32[]{:S(2)}) collective-permute-start(bf16[512,128]{1,0:T(8,128)(2,1)S(1)} %get-tuple-element.63), channel_id=1, source_target_pairs={{0,2},{2,4},{4,6},{6,8},{8,10},{10,12},{12,14},{14,0},{1,3},{3,5},... | collective-permute-start | bytes 393224 | tf_op jit(solution)/shard_map/ppermute | solution.py:424
  5.0 6.7 %collective-permute-start = (f32[32,128]{1,0:T(8,128)S(1)}, f32[32,128]{1,0:T(8,128)S(1)}, u32[]{:S(2)}, u32[]{:S(2)}) collective-permute-start(f32[32,128]{1,0:T(8,128)S(1)} %get-tuple-element.62.own), channel_id=1, source_target_pairs={{0,16},{16,0},{1,17},{17,1},{2,18},{18,2},{3,19},{19,3},{4,20},{20... | collective-permute-start | bytes 49160 | tf_op jit(solution)/shard_map/ppermute | solution.py:414
  5.1 6.6 %collective-permute-start.2 = (f32[64,128]{1,0:T(8,128)S(1)}, f32[64,128]{1,0:T(8,128)S(1)}, u32[]{:S(2)}, u32[]{:S(2)}) collective-permute-start(f32[64,128]{1,0:T(8,128)S(1)} %get-tuple-element.64), channel_id=1, source_target_pairs={{0,1},{1,0},{2,3},{3,2},{4,5},{5,4},{6,7},{7,6},{8,9},{9,8},{10,11... | collective-permute-start | bytes 98312 | tf_op jit(solution)/shard_map/ppermute | solution.py:411
  6.7 7.2 %collective-permute-start.3 = (bf16[512,128]{1,0:T(8,128)(2,1)S(1)}, bf16[512,128]{1,0:T(8,128)(2,1)S(1)}, u32[]{:S(2)}, u32[]{:S(2)}) collective-permute-start(bf16[512,128]{1,0:T(8,128)(2,1)S(1)} %get-tuple-element.68), channel_id=1, source_target_pairs={{0,14},{2,0},{4,2},{6,4},{8,6},{10,8},{12,10},{14,12},{1,15},{3,1}... | collective-permute-start | bytes 393224 | tf_op jit(solution)/shard_map/ppermute | solution.py:432
  14.1 1.7 %collective-permute-start.4 = (f32[40,128]{1,0:T(8,128)S(1)}, f32[40,128]{1,0:T(8,128)S(1)}, u32[]{:S(2)}, u32[]{:S(2)}) collective-permute-start(f32[40,128]{1,0:T(8,128)S(1)} %get-tuple-element.74.own), channel_id=1, source_target_pairs={{0,16},{16,0},{1,17},{17,1},{2,18},{18,2},{3,19},{19,3},{4,20},{20... | collective-permute-start | bytes 61448 | tf_op jit(solution)/shard_map/ppermute | solution.py:414
  14.2 4.0 %collective-permute-start.5 = (f32[64,128]{1,0:T(8,128)S(1)}, f32[64,128]{1,0:T(8,128)S(1)}, u32[]{:S(2)}, u32[]{:S(2)}) collective-permute-start(f32[64,128]{1,0:T(8,128)S(1)} %get-tuple-element.80), channel_id=1, source_target_pairs={{0,1},{1,0},{2,3},{3,2},{4,5},{5,4},{6,7},{7,6},{8,9},{9,8},{10,11... | collective-permute-start | bytes 98312 | tf_op jit(solution)/shard_map/ppermute | solution.py:411

commit v5 on v4

--- a/solution.py
+++ b/solution.py
@@ -250,47 +250,48 @@
     return fresh
 
 
-def west_kernel(dims, mer_count, strips, nu, weights, spread, mer_gain, edge_lanes, rows, guide, own, other, from_west, *rest):
+def west_kernel(dims, strips, nu, weights, spread, edge_lanes, rows, guide, own, other, from_west, sides, solved, incr, half_lanes, surface):
     tracers, levels, width = dims
     total = tracers * width
-    rounds = len(rest) - 6
-    recv_mer, (sides, solved, lanes, incr, half_lanes, surface) = rest[:rounds], rest[rounds:]
     lane = lanes_of(levels)
     terms = side_terms(from_west, 0, strips, nu, sides, dims)
-    terms.append(mer_gain[...] * mer_halo(recv_mer, levels, mer_count))
     result = product(weights[...], jnp.concatenate(terms, axis=1))
     flux = increments(own[...], other[...], guide, tracers, width)
     incr[...] = flux
     for t in range(tracers):
         solved[t * levels:(t + 1) * levels, :] = result[:, t * 128:(t + 1) * 128]
-    lanes[...] = result[:, tracers * 128:]
     row = lax.broadcasted_iota(jnp.int32, (total, 128), 0)
     rows_lane = lax.broadcasted_iota(jnp.int32, (total, 128), 1)
     turned = pltpu.roll(flux, 1, 1, stride=2, stride_axis=0)
     turned = jnp.sum(jnp.where(rows_lane // 2 == row, turned, 0.0), axis=0, keepdims=True)
-    packed = edge_lanes[...] + lanes[...] + spread[...] * turned
-    half_lanes[...] = side_lanes(packed, 0, sides, solved, lane, dims)
+    half_lanes[...] = side_lanes(edge_lanes[...] + spread[...] * turned, 0, sides, solved, lane, dims)
     level = surface_level(levels)
+    surface[total:, :] = jnp.zeros((surface.shape[0] - total, 128), f32)
     fresh = rows[...] + spread[pl.ds(level, 1), :] * flux
+    surface[:total, :] = side_rows(fresh, surface, 0, sides, solved, row, level, dims)
+
+
+def east_kernel(dims, mer_count, strips, nu, weights, mer_gain, half_lanes, half_surface, from_east, *rest):
+    tracers, levels, width = dims
+    total = tracers * width
+    rounds = len(rest) - 5
+    recv_mer, (sides, solved, lanes, surface, send_mer) = rest[:rounds], rest[rounds:]
+    lane = lanes_of(levels)
+    terms = side_terms(from_east, 1, strips, nu, sides, dims)
+    terms.append(mer_gain[...] * mer_halo(recv_mer, levels, mer_count))
+    result = product(weights[...], jnp.concatenate(terms, axis=1))
+    for t in range(tracers):
+        solved[t * levels:(t + 1) * levels, :] = result[:, t * 128:(t + 1) * 128]
+    lanes[...] = result[:, tracers * 128:]
+    send_mer[...] = side_lanes(half_lanes[...] + lanes[...], 1, sides, solved, lane, dims)
+    row = lax.broadcasted_iota(jnp.int32, (total, 128), 0)
+    rows_lane = lax.broadcasted_iota(jnp.int32, (total, 128), 1)
+    level = surface_level(levels)
     line = jnp.broadcast_to(lanes[pl.ds(level, 1), :], (total, 128))
     line = jnp.take_along_axis(line, 2 * row + (rows_lane == 0).astype(jnp.int32), axis=1)
-    fresh = fresh + jnp.where(jnp.logical_or(rows_lane == 127, rows_lane == 0), line, 0.0)
-    surface[total:, :] = jnp.zeros((surface.shape[0] - total, 128), f32)
-    surface[:total, :] = side_rows(fresh, surface, 0, sides, solved, row, level, dims)
-
-
-def east_kernel(dims, strips, nu, weights, half_lanes, half_surface, from_east, sides, solved, surface, send_mer):
-    tracers, levels, width = dims
-    total = tracers * width
-    lane = lanes_of(levels)
-    terms = side_terms(from_east, 1, strips, nu, sides, dims)
-    result = product(weights[...], jnp.concatenate(terms, axis=1))
-    for t in range(tracers):
-        solved[t * levels:(t + 1) * levels, :] = result[:, t * 128:(t + 1) * 128]
-    send_mer[...] = side_lanes(half_lanes[...], 1, sides, solved, lane, dims)
-    surface[...] = half_surface[...]
-    row = lax.broadcasted_iota(jnp.int32, (total, 128), 0)
-    surface[:total, :] = side_rows(half_surface[:total, :], surface, 1, sides, solved, row, surface_level(levels), dims)
+    fresh = half_surface[:total, :] + jnp.where(jnp.logical_or(rows_lane == 127, rows_lane == 0), line, 0.0)
+    surface[total:, :] = half_surface[total:, :]
+    surface[:total, :] = side_rows(fresh, surface, 1, sides, solved, row, level, dims)
 
 
 def middle_kernel(dims, partial, strips, nu, weights, spread, west_sides, east_sides, west_solved, east_solved, lanes, incr, columns, guide, own, other, from_west, from_east, again, edges, flux, inner_gain, outer_gain, fresh):
@@ -426,20 +427,20 @@
         functools.partial(lanes_kernel, dims), "lanes", [VM] * 6,
         [kept, packed, shape(tracers * levels), jax.ShapeDtypeStruct((levels, 3 * levels), bf16), packed, shape(8)], 1 << 20,
     )(state.reshape(tracers * size, wide), *params)
-    west_bound, send_mer, surface = lax.optimization_barrier((west_bound, send_mer, surface))
     recv_mer = swap_mer(send_mer)
     other = swap_fluid(surface)
     from_east = lax.ppermute(west_bound, "zon", ring(zon_count, -1))
     partial, strips, mer_gain, edge_lanes, rows = call(
         functools.partial(inner_kernel, dims), "inner", [VM] * 4, [kept, shape(2 * size), packed, packed, shape(total)], 1 << 30,
     )(columns, frame, nu, weights)
-    west_sides, west_solved, lanes, incr, half_lanes, half_surface = call(
-        functools.partial(west_kernel, dims, mer_count), "west", [VM] * (11 + rounds),
-        [halved, halved, packed, shape(total), packed, shape(total + 8)], 1 << 33,
-    )(strips, nu, weights, spread, mer_gain, edge_lanes, rows, guide, surface, other, from_west, *recv_mer)
-    east_sides, east_solved, fresh_surface, send_mer = call(
-        functools.partial(east_kernel, dims), "east", [VM] * 6, [halved, halved, shape(total + 8), packed], 1 << 26,
-    )(strips, nu, weights, half_lanes, half_surface, from_east)
+    west_sides, west_solved, incr, half_lanes, half_surface = call(
+        functools.partial(west_kernel, dims), "west", [VM] * 10,
+        [halved, halved, shape(total), packed, shape(total + 8)], 1 << 33,
+    )(strips, nu, weights, spread, edge_lanes, rows, guide, surface, other, from_west)
+    east_sides, east_solved, lanes, fresh_surface, send_mer = call(
+        functools.partial(east_kernel, dims, mer_count), "east", [VM] * (7 + rounds),
+        [halved, halved, packed, shape(total + 8), packed], 1 << 26,
+    )(strips, nu, weights, mer_gain, half_lanes, half_surface, from_east, *recv_mer)
     recv_mer = swap_mer(send_mer)
     fresh_other = swap_fluid(fresh_surface)
     again, edges, flux, inner_gain, outer_gain = call(

time: 20 us -> 19.4 us (0.970)
  waiting for transfers between devices: 2.69 us -> 2.24 us
    ppermute x1, waiting for transfers between devices: 1.79 us -> 1.05 us  [on_device(): from_east = lax.ppermute(west_bound, 'zon', ring(zon_count, -1))]
    ppermute x2, waiting for transfers between devices: 0.89 us -> 1.18 us  [swap_mer(): lax.ppermute(piece, 'mer', pairs(mer_count, r == 1))]
  transfers between devices with their start and end apart: 6 -> 6, of which waited for: 2 -> 3; matrix products, arithmetic and copies ran while one was open for 0% -> 0% of each run, Pallas kernels for 21% -> 21%
where the time goes in v5:
time: 19.4 us; the launch traced here: 19.3 us
  starting transfers between devices  9.41 us (49%)
  Pallas kernels  7.56 us (39%)
  waiting for transfers between devices  2.24 us (12%)
    ppermute x2, starting transfers between devices, swap_mer(): lax.ppermute(piece, 'mer', pairs(mer_count, r == 1))  3.22 us
    ppermute x1, starting transfers between devices, on_device(): from_east = lax.ppermute(west_bound, 'zon', ring(zon_count, -1))  3.18 us
    ppermute x1, starting transfers between devices, on_device(): from_west = lax.ppermute(east_bound, 'zon', ring(zon_count, 1))  2.99 us
    pallas_call x1, Pallas kernels, on_device(): call(functools.partial(inner_kernel, dims), 'inner', [VM] * 4, [kept, sha...  1.78 us
    pallas_call x1, Pallas kernels, on_device(): call(functools.partial(last_kernel, dims, mer_count), 'last', [VM] * (8 +...  1.7 us
    pallas_call x1, Pallas kernels, on_device(): call(functools.partial(pack_kernel, dims), 'pack', [HB] * len(in_hbm), [m...  1.53 us
    pallas_call x1, Pallas kernels, on_device(): call(functools.partial(middle_kernel, dims), 'middle', [VM] * 17, [kept,...  1.48 us
    ppermute x2, waiting for transfers between devices, swap_mer(): lax.ppermute(piece, 'mer', pairs(mer_count, r == 1))  1.18 us
  transfers between devices with their start and end apart: 6, of which 3 were waited for; matrix products, arithmetic and copies ran while one was open for 0% of the time, Pallas kernels for 21%

profile of v5, /device:TPU:0, one launch (start us, length us, event | category | flops | bytes accessed | tf_op | source)
XLA Modules:
  0.0 19.3 jit_solution(18167894200738052873)
XLA Ops:
  0.0 0.0 copy-start
  0.0 1.5 %pack.1 = (bf16[512,128]{1,0:T(8,128)(2,1)S(1)}, bf16[512,128]{1,0:T(8,128)(2,1)S(1)}, f32[32,128]{1,0:T(8,128)S(1)}, f32[2048,128]{1,0:T(8,128)S(1)}, f32[2,64]...) custom-call(f32[2,64,16,128]{3,2,1,0:T(8,128)} %bitcast.8, ...), custom_call_target="tpu_custom_call" | custom-call | flops 1048576 | bytes 2097152 | tf_op jit(solution)/shard_map/pack/pallas_call | solution.py:419
  1.5 3.0 %collective-permute-start.1 = (bf16[512,128]{1,0:T(8,128)(2,1)S(1)}, bf16[512,128]{1,0:T(8,128)(2,1)S(1)}, u32[]{:S(2)}, u32[]{:S(2)}) collective-permute-start(bf16[512,128]{1,0:T(8,128)(2,1)S(1)} %get-tuple-element.56), channel_id=1, source_target_pairs={{0,2},{2,4},{4,6},{6,8},{8,10},{10,12},{12,14},{14,0},{1,3},{3,5},... | collective-permute-start | bytes 393224 | tf_op jit(solution)/shard_map/ppermute | solution.py:425
  4.5 0.0 collective-permute-start
  4.5 3.2 %collective-permute-start.2 = (bf16[512,128]{1,0:T(8,128)(2,1)S(1)}, bf16[512,128]{1,0:T(8,128)(2,1)S(1)}, u32[]{:S(2)}, u32[]{:S(2)}) collective-permute-start(bf16[512,128]{1,0:T(8,128)(2,1)S(1)} %get-tuple-element.61), channel_id=1, source_target_pairs={{0,14},{2,0},{4,2},{6,4},{8,6},{10,8},{12,10},{14,12},{1,15},{3,1}... | collective-permute-start | bytes 393224 | tf_op jit(solution)/shard_map/ppermute | solution.py:432
  7.7 0.0 copy-done
  7.7 0.5 %lanes.1 = (f32[2048,128]{1,0:T(8,128)S(1)}, f32[64,128]{1,0:T(8,128)S(1)}, f32[128,128]{1,0:T(8,128)S(1)}, bf16[64,192]{1,0:T(8,128)(2,1)S(1)}, f32[64,128]{1,0:T(8,128)S(1)}, /*index=5*/f32[8,128]{1,0:T(8,128)S(1)}) custom-call(f32[2048,128]{1,0:T(8,128)S(1)} %bitcast.9, f32[2,64]{1,0:T(2,128)S(1)} %get-tuple-element.40.diffusion, ...), custom_call_target="tpu_custom_call" | custom-call | flops 1048576 | bytes 2097152 | tf_op jit(solution)/shard_map/lanes/pallas_call | solution.py:426
  8.2 1.6 %collective-permute-start.3 = (f32[64,128]{1,0:T(8,128)S(1)}, f32[64,128]{1,0:T(8,128)S(1)}, u32[]{:S(2)}, u32[]{:S(2)}) collective-permute-start(f32[64,128]{1,0:T(8,128)S(1)} %get-tuple-element.62), channel_id=1, source_target_pairs={{0,1},{1,0},{2,3},{3,2},{4,5},{5,4},{6,7},{7,6},{8,9},{9,8},{10,11... | collective-permute-start | bytes 98312 | tf_op jit(solution)/shard_map/ppermute | solution.py:412
  9.9 1.8 %inner.1 = (f32[2048,128]{1,0:T(8,128)S(1)}, f32[2048,128]{1,0:T(8,128)S(1)}, f32[64,128]{1,0:T(8,128)S(1)}, f32[64,128]{1,0:T(8,128)S(1)}, f32[32,128]{1,0:T(8,128)S(1)}) custom-call(f32[2048,128]{1,0:T(8,128)S(1)} %get-tuple-element.45.columns, f32[2048,128]{1,0:T(8,128)S(1)} %get-tuple-element.46.frame, f32[128,128]{1,0:T(8,128)S(1)} %get-tuple-element.47.nu, ...), custom_call_target="tpu_custom_call" | custom-call | flops 1073741824 | bytes 2097152 | tf_op jit(solution)/shard_map/inner/pallas_call | solution.py:433
  11.6 0.0 collective-permute-done.other
  11.7 0.0 collective-permute-done.1.from_west
  11.7 0.3 %west.1 = (f32[128,128]{1,0:T(8,128)S(1)}, f32[128,128]{1,0:T(8,128)S(1)}, f32[32,128]{1,0:T(8,128)S(1)}, f32[64,128]{1,0:T(8,128)S(1)}, f32[40,128]{1,0:T(8,128)S(1)}) custom-call(f32[2048,128]{1,0:T(8,128)S(1)} %get-tuple-element.50.strips, f32[128,128]{1,0:T(8,128)S(1)} %get-tuple-element.47.nu, bf16[64,192]{1,0:T(8,128)(2,1)S(1)} %get-tuple-element.48.weights, ...), custom_call_target="tpu_custom_call" | custom-call | flops 8589934592 | bytes 2097152 | tf_op jit(solution)/shard_map/west/pallas_call | solution.py:436
  11.9 0.3 %collective-permute-done.3.rest_0_ = f32[64,128]{1,0:T(8,128)S(1)} collective-permute-done((f32[64,128]{1,0:T(8,128)S(1)}, f32[64,128]{1,0:T(8,128)S(1)}, u32[]{:S(2)}, u32[]{:S(2)}) %collective-permute-start.3) | collective-permute-done | bytes 32800 | tf_op jit(solution)/shard_map/ppermute | solution.py:412
  12.2 1.0 %collective-permute-done.2.from_east = bf16[512,128]{1,0:T(8,128)(2,1)S(1)} collective-permute-done((bf16[512,128]{1,0:T(8,128)(2,1)S(1)}, bf16[512,128]{1,0:T(8,128)(2,1)S(1)}, u32[]{:S(2)}, u32[]{:S(2)}) %collective-permute-start.2) | collective-permute-done | bytes 131104 | tf_op jit(solution)/shard_map/ppermute | solution.py:432
  13.3 0.3 %east.1 = (f32[128,128]{1,0:T(8,128)S(1)}, f32[128,128]{1,0:T(8,128)S(1)}, f32[64,128]{1,0:T(8,128)S(1)}, f32[40,128]{1,0:T(8,128)S(1)}, f32[64,128]{1,0:T(8,128)S(1)}) custom-call(f32[2048,128]{1,0:T(8,128)S(1)} %get-tuple-element.50.strips, f32[128,128]{1,0:T(8,128)S(1)} %get-tuple-element.47.nu, bf16[64,192]{1,0:T(8,128)(2,1)S(1)} %get-tuple-element.48.weights, ...), custom_call_target="tpu_custom_call" | custom-call | flops 67108864 | bytes 2097152 | tf_op jit(solution)/shard_map/east/pallas_call | solution.py:440
  13.6 0.0 collective-permute-start.4
  13.6 1.6 %collective-permute-start.5 = (f32[64,128]{1,0:T(8,128)S(1)}, f32[64,128]{1,0:T(8,128)S(1)}, u32[]{:S(2)}, u32[]{:S(2)}) collective-permute-start(f32[64,128]{1,0:T(8,128)S(1)} %get-tuple-element.74), channel_id=1, source_target_pairs={{0,1},{1,0},{2,3},{3,2},{4,5},{5,4},{6,7},{7,6},{8,9},{9,8},{10,11... | collective-permute-start | bytes 98312 | tf_op jit(solution)/shard_map/ppermute | solution.py:412
  15.2 0.0 collective-permute-done.4.other
  15.2 1.5 %middle.1 = (f32[2048,128]{1,0:T(8,128)S(1)}, f32[256,128]{1,0:T(8,128)S(1)}, f32[32,128]{1,0:T(8,128)S(1)}, f32[64,128]{1,0:T(8,128)S(1)}, f32[64,128]{1,0:T(8,128)S(1)}) custom-call(f32[2048,128]{1,0:T(8,128)S(1)} %get-tuple-element.49.partial, f32[2048,128]{1,0:T(8,128)S(1)} %get-tuple-element.50.strips, f32[128,128]{1,0:T(8,128)S(1)} %get-tuple-element.47.nu, ...), custom_call_target="tpu_custom_call" | custom-call | flops 1073741824 | bytes 2097152 | tf_op jit(solution)/shard_map/middle/pallas_call | solution.py:446
  16.7 0.9 %collective-permute-done.5.rest_0_ = f32[64,128]{1,0:T(8,128)S(1)} collective-permute-done((f32[64,128]{1,0:T(8,128)S(1)}, f32[64,128]{1,0:T(8,128)S(1)}, u32[]{:S(2)}, u32[]{:S(2)}) %collective-permute-start.5) | collective-permute-done | bytes 32800 | tf_op jit(solution)/shard_map/ppermute | solution.py:412
  17.6 1.7 %last.1 = f32[2,64,16,128]{3,2,1,0:T(8,128)} custom-call(f32[2048,128]{1,0:T(8,128)S(1)} %get-tuple-element.69.partial, f32[256,128]{1,0:T(8,128)S(1)} %get-tuple-element.70.edges, f32[32,128]{1,0:T(8,128)S(1)} %get-tuple-element.71.incr, bf16[64,192]{1,0:T(8,128)(2,1)S(1)} %get-tuple-element.48.weights, f32[64,128]{1,0:T(8,128)S(1)} %get-tuple-element.51.spread, ...), custom_call_target="tpu_custom_call" | custom-call | flops 67108864 | bytes 2097152 | tf_op jit(solution)/shard_map/last/pallas_call | solution.py:450
Async XLA Ops:
  0.0 7.7 %copy-start = (f32[1,2,64,16,128]{4,3,2,1,0:T(8,128)S(1)}, f32[1,2,64,16,128]{4,3,2,1,0:T(8,128)}, u32[]{:S(2)}) copy-start(f32[1,2,64,16,128]{4,3,2,1,0:T(8,128)} %param.7) | copy-start | bytes 3145732
  1.5 10.1 %collective-permute-start.1 = (bf16[512,128]{1,0:T(8,128)(2,1)S(1)}, bf16[512,128]{1,0:T(8,128)(2,1)S(1)}, u32[]{:S(2)}, u32[]{:S(2)}) collective-permute-start(bf16[512,128]{1,0:T(8,128)(2,1)S(1)} %get-tuple-element.56), channel_id=1, source_target_pairs={{0,2},{2,4},{4,6},{6,8},{8,10},{10,12},{12,14},{14,0},{1,3},{3,5},... | collective-permute-start | bytes 393224 | tf_op jit(solution)/shard_map/ppermute | solution.py:425
  4.5 7.1 %collective-permute-start = (f32[32,128]{1,0:T(8,128)S(1)}, f32[32,128]{1,0:T(8,128)S(1)}, u32[]{:S(2)}, u32[]{:S(2)}) collective-permute-start(f32[32,128]{1,0:T(8,128)S(1)} %get-tuple-element.55.own), channel_id=1, source_target_pairs={{0,16},{16,0},{1,17},{17,1},{2,18},{18,2},{3,19},{19,3},{4,20},{20... | collective-permute-start | bytes 49160 | tf_op jit(solution)/shard_map/ppermute | solution.py:415
  4.5 8.7 %collective-permute-start.2 = (bf16[512,128]{1,0:T(8,128)(2,1)S(1)}, bf16[512,128]{1,0:T(8,128)(2,1)S(1)}, u32[]{:S(2)}, u32[]{:S(2)}) collective-permute-start(bf16[512,128]{1,0:T(8,128)(2,1)S(1)} %get-tuple-element.61), channel_id=1, source_target_pairs={{0,14},{2,0},{4,2},{6,4},{8,6},{10,8},{12,10},{14,12},{1,15},{3,1}... | collective-permute-start | bytes 393224 | tf_op jit(solution)/shard_map/ppermute | solution.py:432
  8.2 4.0 %collective-permute-start.3 = (f32[64,128]{1,0:T(8,128)S(1)}, f32[64,128]{1,0:T(8,128)S(1)}, u32[]{:S(2)}, u32[]{:S(2)}) collective-permute-start(f32[64,128]{1,0:T(8,128)S(1)} %get-tuple-element.62), channel_id=1, source_target_pairs={{0,1},{1,0},{2,3},{3,2},{4,5},{5,4},{6,7},{7,6},{8,9},{9,8},{10,11... | collective-permute-start | bytes 98312 | tf_op jit(solution)/shard_map/ppermute | solution.py:412
  13.6 1.6 %collective-permute-start.4 = (f32[40,128]{1,0:T(8,128)S(1)}, f32[40,128]{1,0:T(8,128)S(1)}, u32[]{:S(2)}, u32[]{:S(2)}) collective-permute-start(f32[40,128]{1,0:T(8,128)S(1)} %get-tuple-element.68.own), channel_id=1, source_target_pairs={{0,16},{16,0},{1,17},{17,1},{2,18},{18,2},{3,19},{19,3},{4,20},{20... | collective-permute-start | bytes 61448 | tf_op jit(solution)/shard_map/ppermute | solution.py:415
  13.6 4.0 %collective-permute-start.5 = (f32[64,128]{1,0:T(8,128)S(1)}, f32[64,128]{1,0:T(8,128)S(1)}, u32[]{:S(2)}, u32[]{:S(2)}) collective-permute-start(f32[64,128]{1,0:T(8,128)S(1)} %get-tuple-element.74), channel_id=1, source_target_pairs={{0,1},{1,0},{2,3},{3,2},{4,5},{5,4},{6,7},{7,6},{8,9},{9,8},{10,11... | collective-permute-start | bytes 98312 | tf_op jit(solution)/shard_map/ppermute | solution.py:412

commit v6 on v5

--- a/solution.py
+++ b/solution.py
@@ -10,16 +10,17 @@
 f32, bf16 = jnp.float32, jnp.bfloat16
 
 
-def ring(count, ahead):
-    return [(i, (i + ahead) % count) for i in range(count)]
-
-
 def pairs(count, odd):
     if odd:
         return [(i, ((i + 1) ^ 1) - 1) for i in range(1, count - 1)] + [(0, count - 1), (count - 1, 0)]
     return [(i, i ^ 1) for i in range(count)]
 
 
+def side_of(odd, width):
+    east = lax.rem(lax.axis_index("zon") + (0 if odd else 1), 2)
+    return east * (width - 1), east
+
+
 def surface_level(levels):
     return jnp.where(lax.axis_index("fluid") == 0, levels - 1, 0)
 
@@ -42,22 +43,35 @@
     return ref[index * levels:(index + 1) * levels, :]
 
 
-def mer_halo(recv_mer, levels, mer_count):
+def fold(value):
+    half = value.shape[0] // 2
+    lane = lanes_of(half)
+    return jnp.where(lane < 64, value[:half], pltpu.roll(value[half:], 64, 1))
+
+
+def unfold(value):
+    return jnp.concatenate([value, pltpu.roll(value, 64, 1)], axis=0)
+
+
+def mer_sides(recv_mer, mer_count):
     place = lax.axis_index("mer")
     even = 1 - lax.rem(place, 2)
-    lane = lanes_of(levels)
-    total = jnp.zeros((levels, 128), f32)
     for r, ref in enumerate(recv_mer):
         north = even if r == 0 else 1 - even
-        inside = jnp.where(north == 1, place + 1 < mer_count, place > 0)
-        keep = jnp.logical_and(lane % 2 == 1 - north, inside)
-        moved = pltpu.roll(ref[...], jnp.where(north == 1, 127, 1), 1)
-        total = total + jnp.where(keep, moved, 0.0)
+        yield unfold(ref[...]), north, jnp.where(north == 1, place + 1 < mer_count, place > 0)
+
+
+def mer_halo(recv_mer, levels, mer_count):
+    lane = lanes_of(levels)
+    total = jnp.zeros((levels, 128), f32)
+    for value, north, inside in mer_sides(recv_mer, mer_count):
+        keep = jnp.logical_and(jnp.logical_and(lane % 2 == 1 - north, lane < 64), inside)
+        total = total + jnp.where(keep, pltpu.roll(value, jnp.where(north == 1, 127, 1), 1), 0.0)
     return total
 
 
 def both_edges(cells, j):
-    return pltpu.roll(cells, (2 * j + 1) % 128, 1)
+    return pltpu.roll(cells, 2 * j + 1, 1)
 
 
 def at_edges(packed, j):
@@ -126,12 +140,12 @@
     tracers, levels, width = dims
     size = levels * width
     fixed = len(rest) - 7 >> 1
-    east_bound, west_bound, surface, frame = rest[fixed:fixed + 4]
+    even_bound, odd_bound, surface, frame = rest[fixed:fixed + 4]
     columns, raw, sems = rest[2 * fixed + 4:]
     level = surface_level(levels)
-    places = ((east_bound, width - 1), (east_bound, width - 2), (west_bound, 0), (west_bound, 1))
+    places = (width - 1, width - 2, 0, 1)
     wait_columns, wait_flow, wait_rows = [], [], []
-    for i, (_, x) in enumerate(places):
+    for i, x in enumerate(places):
         for t in range(tracers):
             at = i * tracers + t
             wait_columns.append(pltpu.make_async_copy(state.at[t, :, x, :], columns.at[at], sems.at[at]))
@@ -147,19 +161,18 @@
         copy.start()
     for copy in wait_columns:
         copy.wait()
-    for i, (ref, _) in enumerate(places):
-        for t in range(tracers):
-            high, low = split(columns[i * tracers + t])
-            if i % 2 == 0:
-                ref[t * levels:(t + 1) * levels, :] = high
-                ref[(tracers + t) * levels:(tracers + t + 1) * levels, :] = low
-            else:
-                ref[(2 * tracers + t) * levels:(2 * tracers + t + 1) * levels, :] = high
+    for ref, odd in ((even_bound, False), (odd_bound, True)):
+        first = 2 * tracers * (1 - side_of(odd, width)[1])
+        for t in range(tracers):
+            high, low = split(columns[first + t])
+            ref[t * levels:(t + 1) * levels, :] = high
+            ref[(tracers + t) * levels:(tracers + t + 1) * levels, :] = low
+            ref[(2 * tracers + t) * levels:(2 * tracers + t + 1) * levels, :] = columns[first + tracers + t].astype(bf16)
     for k, copy in enumerate(wait_flow):
         copy.wait()
         frame[k * size:(k + 1) * size, :] = raw[k].reshape(size, 128).astype(f32) * 0.5
-        for ref, x in ((east_bound, width - 1), (west_bound, 0)):
-            strip = frame[pl.ds(k * size + x, levels, stride=width), :].astype(bf16)
+        for ref, odd in ((even_bound, False), (odd_bound, True)):
+            strip = frame[pl.ds(k * size + side_of(odd, width)[0], levels, stride=width), :].astype(bf16)
             ref[(3 * tracers + k) * levels:(3 * tracers + k + 1) * levels, :] = strip
     for copy in wait_rows:
         copy.wait()
@@ -176,7 +189,7 @@
             columns[j * levels:(j + 1) * levels, :] = value
             packed = jnp.where(lane // 2 == j, both_edges(value, j), packed)
         nu[t * levels:(t + 1) * levels, :] = jnp.transpose(jnp.broadcast_to(diffusion[t:t + 1, :], (128, levels)))
-    send_mer[...] = packed
+    send_mer[...] = fold(packed)
     high, low = split(solve[...])
     weights[...] = jnp.concatenate([high, high, low], axis=1)
     at_level = lax.broadcasted_iota(jnp.int32, (levels, levels), 1) == surface_level(levels)
@@ -218,43 +231,46 @@
         rows[j:j + 1, :] = partial[pl.ds(j * levels + level, 1), :]
 
 
-def side_terms(ref, s, strips, nu, sides, dims):
-    tracers, levels, width = dims
-    c = part(strips, 0 if s == 0 else width - 1, levels)
+def column_at(ref, index, levels):
+    return ref[pl.ds(pl.multiple_of(index * levels, 8), levels), :]
+
+
+def side_terms(ref, odd, strips, nu, sides, dims):
+    tracers, levels, width = dims
+    x, east = side_of(odd, width)
+    c = column_at(strips, x, levels) * (1 - 2 * east).astype(f32)
     terms = []
     for t in range(tracers):
         value = part(ref, t, levels).astype(f32) + part(ref, tracers + t, levels).astype(f32)
         sides[t * levels:(t + 1) * levels, :] = value
-        terms.append((part(nu, t, levels) + (c if s == 0 else -c)) * value)
+        terms.append((part(nu, t, levels) + c) * value)
     return terms
 
 
-def side_lanes(packed, s, sides, solved, lane, dims):
-    tracers, levels, width = dims
-    for t in range(tracers):
-        j = t * width + (0 if s == 0 else width - 1)
+def side_lanes(packed, odd, solved, lane, dims):
+    tracers, levels, width = dims
+    for t in range(tracers):
+        j = t * width + side_of(odd, width)[0]
         packed = packed + jnp.where(lane // 2 == j, both_edges(part(solved, t, levels), j), 0.0)
-        j = tracers * width + s * tracers + t
-        packed = jnp.where(lane // 2 == j, both_edges(part(sides, t, levels), j), packed)
     return packed
 
 
-def side_rows(fresh, surface, s, sides, solved, row, level, dims):
+def side_rows(fresh, surface, odd, sides, solved, row, level, dims):
     tracers, levels, width = dims
     total = tracers * width
     for t in range(tracers):
         line = solved[pl.ds(t * levels + level, 1), :]
-        fresh = fresh + jnp.where(row == t * width + (0 if s == 0 else width - 1), line, 0.0)
-        at = total + s * tracers + t
+        fresh = fresh + jnp.where(row == t * width + side_of(odd, width)[0], line, 0.0)
+        at = total + int(odd) * tracers + t
         surface[at:at + 1, :] = sides[pl.ds(t * levels + level, 1), :]
     return fresh
 
 
-def west_kernel(dims, strips, nu, weights, spread, edge_lanes, rows, guide, own, other, from_west, sides, solved, incr, half_lanes, surface):
+def even_kernel(dims, strips, nu, weights, spread, edge_lanes, rows, guide, own, other, from_even, sides, solved, incr, half_lanes, surface):
     tracers, levels, width = dims
     total = tracers * width
     lane = lanes_of(levels)
-    terms = side_terms(from_west, 0, strips, nu, sides, dims)
+    terms = side_terms(from_even, False, strips, nu, sides, dims)
     result = product(weights[...], jnp.concatenate(terms, axis=1))
     flux = increments(own[...], other[...], guide, tracers, width)
     incr[...] = flux
@@ -264,26 +280,36 @@
     rows_lane = lax.broadcasted_iota(jnp.int32, (total, 128), 1)
     turned = pltpu.roll(flux, 1, 1, stride=2, stride_axis=0)
     turned = jnp.sum(jnp.where(rows_lane // 2 == row, turned, 0.0), axis=0, keepdims=True)
-    half_lanes[...] = side_lanes(edge_lanes[...] + spread[...] * turned, 0, sides, solved, lane, dims)
+    half_lanes[...] = side_lanes(edge_lanes[...] + spread[...] * turned, False, solved, lane, dims)
     level = surface_level(levels)
     surface[total:, :] = jnp.zeros((surface.shape[0] - total, 128), f32)
     fresh = rows[...] + spread[pl.ds(level, 1), :] * flux
-    surface[:total, :] = side_rows(fresh, surface, 0, sides, solved, row, level, dims)
-
-
-def east_kernel(dims, mer_count, strips, nu, weights, mer_gain, half_lanes, half_surface, from_east, *rest):
+    surface[:total, :] = side_rows(fresh, surface, False, sides, solved, row, level, dims)
+
+
+def odd_kernel(dims, mer_count, strips, nu, weights, mer_gain, half_lanes, half_surface, even_sides, from_odd, *rest):
     tracers, levels, width = dims
     total = tracers * width
-    rounds = len(rest) - 5
-    recv_mer, (sides, solved, lanes, surface, send_mer) = rest[:rounds], rest[rounds:]
-    lane = lanes_of(levels)
-    terms = side_terms(from_east, 1, strips, nu, sides, dims)
+    rounds = (len(rest) - 4) // 2
+    recv_mer, (sides, solved, lanes, surface), send_mer = rest[:rounds], rest[rounds:rounds + 4], rest[rounds + 4:]
+    lane = lanes_of(levels)
+    terms = side_terms(from_odd, True, strips, nu, sides, dims)
     terms.append(mer_gain[...] * mer_halo(recv_mer, levels, mer_count))
     result = product(weights[...], jnp.concatenate(terms, axis=1))
     for t in range(tracers):
         solved[t * levels:(t + 1) * levels, :] = result[:, t * 128:(t + 1) * 128]
     lanes[...] = result[:, tracers * 128:]
-    send_mer[...] = side_lanes(half_lanes[...] + lanes[...], 1, sides, solved, lane, dims)
+    packed = side_lanes(half_lanes[...] + lanes[...], True, solved, lane, dims)
+    place = lax.axis_index("mer")
+    for r, ref in enumerate(send_mer):
+        up = lax.rem(place + 1 + r, 2)
+        message = packed
+        for s, cells in enumerate((even_sides, sides)):
+            for t in range(tracers):
+                at = s * tracers + t
+                moved = pltpu.roll(part(cells, t, levels), 2 * at + 2 * up, 1)
+                message = jnp.where(lane == 2 * at + up, moved, message)
+        ref[...] = fold(message)
     row = lax.broadcasted_iota(jnp.int32, (total, 128), 0)
     rows_lane = lax.broadcasted_iota(jnp.int32, (total, 128), 1)
     level = surface_level(levels)
@@ -291,10 +317,10 @@
     line = jnp.take_along_axis(line, 2 * row + (rows_lane == 0).astype(jnp.int32), axis=1)
     fresh = half_surface[:total, :] + jnp.where(jnp.logical_or(rows_lane == 127, rows_lane == 0), line, 0.0)
     surface[total:, :] = half_surface[total:, :]
-    surface[:total, :] = side_rows(fresh, surface, 1, sides, solved, row, level, dims)
-
-
-def middle_kernel(dims, partial, strips, nu, weights, spread, west_sides, east_sides, west_solved, east_solved, lanes, incr, columns, guide, own, other, from_west, from_east, again, edges, flux, inner_gain, outer_gain, fresh):
+    surface[:total, :] = side_rows(fresh, surface, True, sides, solved, row, level, dims)
+
+
+def middle_kernel(dims, partial, strips, nu, weights, spread, even_sides, odd_sides, even_solved, odd_solved, lanes, incr, columns, guide, own, other, from_even, from_odd, again, edges, flux, inner_gain, outer_gain, fresh):
     tracers, levels, width = dims
     total = tracers * width
     lane = lanes_of(levels)
@@ -304,17 +330,17 @@
     terms, gains = [], []
     first = jnp.zeros((levels, 128), f32)
     later = jnp.zeros((levels, 128), f32)
-    for s, (ref, sides) in enumerate(((from_west, west_sides), (from_east, east_sides))):
-        x = 0 if s == 0 else width - 1
+    for s, (ref, sides) in enumerate(((from_even, even_sides), (from_odd, odd_sides))):
+        x, east = side_of(s == 1, width)
+        ahead = (2 * east - 1).astype(f32)
         c, d = (part(ref, 3 * tracers + k, levels).astype(f32) for k in range(2))
-        own_c = part(strips, x, levels)
-        for t in range(tracers):
-            mine, beyond = part(columns, t * width + x, levels), part(ref, 2 * tracers + t, levels).astype(f32)
-            east, west = (mine, beyond) if s == 0 else (beyond, mine)
-            value = horizontal(part(sides, t, levels), east, west, c, d, part(nu, t, levels), lane)
+        own_c = column_at(strips, x, levels) * ahead
+        for t in range(tracers):
+            mine, beyond = column_at(columns, t * width + x, levels), part(ref, 2 * tracers + t, levels).astype(f32)
+            value = horizontal(part(sides, t, levels), beyond, mine, c * ahead, d, part(nu, t, levels), lane)
             value = value + jnp.where(at_level, jnp.broadcast_to(extra[s * tracers + t:s * tracers + t + 1, :], value.shape), 0.0)
             terms.append(value)
-            gain = part(nu, t, levels) + (own_c if s == 0 else -own_c)
+            gain = part(nu, t, levels) - own_c
             gains.append(gain)
             j = t * width + x
             here = lane // 2 == j
@@ -325,8 +351,10 @@
     outer_gain[...] = later
     result = product(weights[...], jnp.concatenate(terms, axis=1))
     result = product(weights[...], result * jnp.concatenate(gains, axis=1))
-    for i in range(2 * tracers):
-        edges[i * levels:(i + 1) * levels, :] = result[:, i * 128:(i + 1) * 128]
+    for s in range(2):
+        for t in range(tracers):
+            at, i = side_of(s == 1, width)[1] * tracers + t, s * tracers + t
+            edges[pl.ds(pl.multiple_of(at * levels, 8), levels), :] = result[:, i * 128:(i + 1) * 128]
     rim = jnp.logical_or(lane == 127, lane == 0)
     for t in range(tracers):
         for x in range(width):
@@ -334,7 +362,8 @@
             value = part(partial, j, levels) + spread[...] * incr[j:j + 1, :]
             value = value + jnp.where(rim, at_edges(lanes[...], j), 0.0)
             if x in (0, width - 1):
-                value = value + part(west_solved if x == 0 else east_solved, t, levels)
+                by_even = side_of(False, width)[0] == x
+                value = value + jnp.where(by_even, part(even_solved, t, levels), part(odd_solved, t, levels))
             fresh[j * levels:(j + 1) * levels, :] = value
 
     def store(t, x, value):
@@ -353,11 +382,12 @@
     halo = mer_halo(recv_mer, levels, mer_count)
     lanes = product(weights[...], mer_gain[...] * halo)
     corner = jnp.zeros((levels, 128), f32)
-    for t in range(tracers):
+    for value, north, inside in mer_sides(recv_mer, mer_count):
         for s in range(2):
-            j = t * width + (0 if s == 0 else width - 1)
-            moved = pltpu.roll(halo, (2 * (j - tracers * width - s * tracers - t)) % 128, 1)
-            corner = jnp.where(lane // 2 == j, moved, corner)
+            for t in range(tracers):
+                j = t * width + side_of(s == 1, width)[0]
+                moved = pltpu.roll(value, lax.rem(2 * (j - s * tracers - t) + 128, 128), 1)
+                corner = jnp.where(jnp.logical_and(lane == 2 * j + 1 - north, inside), moved, corner)
     corner = outer_gain[...] * product(weights[...], inner_gain[...] * corner)
     corner = product(weights[...], corner) + lanes
     rim = jnp.logical_or(lane == 127, lane == 0)
@@ -404,49 +434,50 @@
     shape = lambda rows, dtype=f32: jax.ShapeDtypeStruct((rows, wide), dtype)
     message = shape((3 * tracers + 2) * levels, bf16)
     packed = shape(levels)
+    folded = shape(levels // 2)
     kept = shape(tracers * size)
     halved = shape(tracers * levels)
     sided = shape(2 * tracers * levels)
 
-    def swap_mer(piece):
-        return [lax.ppermute(piece, "mer", pairs(mer_count, r == 1)) for r in range(rounds)]
+    def swap_mer(pieces):
+        return [lax.ppermute(piece, "mer", pairs(mer_count, r == 1)) for r, piece in enumerate(pieces)]
 
     def swap_fluid(piece):
         return lax.ppermute(piece, "fluid", [(0, 1), (1, 0)])
 
     params = (diffusion[0], column_solve[0], exchange_rate, block_map[None], ice_mask[None])
     in_hbm = [pltpu.with_memory_space_constraint(value, pltpu.HBM) for value in (state[0], flow[0]) + params]
-    east_bound, west_bound, surface, frame, *params = call(
+    even_bound, odd_bound, surface, frame, *params = call(
         functools.partial(pack_kernel, dims), "pack", [HB] * len(in_hbm),
         [message, message, shape(total), shape(2 * size)] + [jax.ShapeDtypeStruct(p.shape, p.dtype) for p in params], 1 << 20,
         scratch=[pltpu.VMEM((4 * tracers, levels, wide), f32), pltpu.VMEM((2, levels, width, wide), bf16),
                  pltpu.SemaphoreType.DMA((5 * tracers + 2 + len(params),))],
     )(*in_hbm)
-    from_west = lax.ppermute(east_bound, "zon", ring(zon_count, 1))
+    from_even = lax.ppermute(even_bound, "zon", pairs(zon_count, False))
     columns, send_mer, nu, weights, spread, guide = call(
         functools.partial(lanes_kernel, dims), "lanes", [VM] * 6,
-        [kept, packed, shape(tracers * levels), jax.ShapeDtypeStruct((levels, 3 * levels), bf16), packed, shape(8)], 1 << 20,
+        [kept, folded, shape(tracers * levels), jax.ShapeDtypeStruct((levels, 3 * levels), bf16), packed, shape(8)], 1 << 20,
     )(state.reshape(tracers * size, wide), *params)
-    recv_mer = swap_mer(send_mer)
+    recv_mer = swap_mer([send_mer] * rounds)
     other = swap_fluid(surface)
-    from_east = lax.ppermute(west_bound, "zon", ring(zon_count, -1))
+    from_odd = lax.ppermute(odd_bound, "zon", pairs(zon_count, True))
     partial, strips, mer_gain, edge_lanes, rows = call(
         functools.partial(inner_kernel, dims), "inner", [VM] * 4, [kept, shape(2 * size), packed, packed, shape(total)], 1 << 30,
     )(columns, frame, nu, weights)
-    west_sides, west_solved, incr, half_lanes, half_surface = call(
-        functools.partial(west_kernel, dims), "west", [VM] * 10,
+    even_sides, even_solved, incr, half_lanes, half_surface = call(
+        functools.partial(even_kernel, dims), "even", [VM] * 10,
         [halved, halved, shape(total), packed, shape(total + 8)], 1 << 33,
-    )(strips, nu, weights, spread, edge_lanes, rows, guide, surface, other, from_west)
-    east_sides, east_solved, lanes, fresh_surface, send_mer = call(
-        functools.partial(east_kernel, dims, mer_count), "east", [VM] * (7 + rounds),
-        [halved, halved, packed, shape(total + 8), packed], 1 << 26,
-    )(strips, nu, weights, mer_gain, half_lanes, half_surface, from_east, *recv_mer)
+    )(strips, nu, weights, spread, edge_lanes, rows, guide, surface, other, from_even)
+    odd_sides, odd_solved, lanes, fresh_surface, *send_mer = call(
+        functools.partial(odd_kernel, dims, mer_count), "odd", [VM] * (8 + rounds),
+        [halved, halved, packed, shape(total + 8)] + [folded] * rounds, 1 << 26,
+    )(strips, nu, weights, mer_gain, half_lanes, half_surface, even_sides, from_odd, *recv_mer)
     recv_mer = swap_mer(send_mer)
     fresh_other = swap_fluid(fresh_surface)
     again, edges, flux, inner_gain, outer_gain = call(
         functools.partial(middle_kernel, dims), "middle", [VM] * 17,
         [kept, sided, shape(total), packed, packed], 1 << 30, scratch=[pltpu.VMEM((tracers * size, wide), f32)],
-    )(partial, strips, nu, weights, spread, west_sides, east_sides, west_solved, east_solved, lanes, incr, columns, guide, fresh_surface, fresh_other, from_west, from_east)
+    )(partial, strips, nu, weights, spread, even_sides, odd_sides, even_solved, odd_solved, lanes, incr, columns, guide, fresh_surface, fresh_other, from_even, from_odd)
     done = call(
         functools.partial(last_kernel, dims, mer_count), "last", [VM] * (8 + rounds),
         jax.ShapeDtypeStruct(state.shape[1:], f32), 1 << 26,

time: 19.4 us -> 19.4 us (level)
  waiting for transfers between devices: 2.24 us -> 1.49 us
  starting transfers between devices: 9.41 us -> 9.81 us
  Pallas kernels: 7.56 us -> 7.87 us
    ppermute x2, waiting for transfers between devices: 1.05 us -> 0.64 us  [the longest x1 0.64 us: on_device(): from_odd = lax.ppermute(odd_bound, 'zon', pairs(zon_count, True))]
    ppermute x2, starting transfers between devices: 6.17 us -> 6.58 us  [the longest x1 3.57 us: on_device(): from_odd = lax.ppermute(odd_bound, 'zon', pairs(zon_count, True))]
    ppermute x2, waiting for transfers between devices: 1.18 us -> 0.84 us  [swap_mer(): lax.ppermute(piece, 'mer', pairs(mer_count, r == 1))]
  transfers between devices with their start and end apart: 6 -> 6, of which waited for: 3 -> 3; matrix products, arithmetic and copies ran while one was open for 0% -> 0% of each run, Pallas kernels for 21% -> 22%
where the time goes in v6:
time: 19.4 us; the launch traced here: 19.2 us
  starting transfers between devices  9.81 us (51%)
  Pallas kernels  7.87 us (41%)
  waiting for transfers between devices  1.49 us (8%)
    ppermute x1, starting transfers between devices, on_device(): from_odd = lax.ppermute(odd_bound, 'zon', pairs(zon_count, True))  3.57 us
    ppermute x2, starting transfers between devices, swap_mer(): lax.ppermute(piece, 'mer', pairs(mer_count, r == 1))  3.17 us
    ppermute x1, starting transfers between devices, on_device(): from_even = lax.ppermute(even_bound, 'zon', pairs(zon_count, False))  3 us
    pallas_call x1, Pallas kernels, on_device(): call(functools.partial(last_kernel, dims, mer_count), 'last', [VM] * (8 +...  1.81 us
    pallas_call x1, Pallas kernels, on_device(): call(functools.partial(inner_kernel, dims), 'inner', [VM] * 4, [kept, sha...  1.78 us
    pallas_call x1, Pallas kernels, on_device(): call(functools.partial(pack_kernel, dims), 'pack', [HB] * len(in_hbm), [m...  1.56 us
    pallas_call x1, Pallas kernels, on_device(): call(functools.partial(middle_kernel, dims), 'middle', [VM] * 17, [kept,...  1.53 us
    ppermute x2, waiting for transfers between devices, swap_mer(): lax.ppermute(piece, 'mer', pairs(mer_count, r == 1))  0.84 us
  transfers between devices with their start and end apart: 6, of which 3 were waited for; matrix products, arithmetic and copies ran while one was open for 0% of the time, Pallas kernels for 22%

profile of v6, /device:TPU:0, one launch (start us, length us, event | category | flops | bytes accessed | tf_op | source)
XLA Modules:
  0.0 19.2 jit_solution(13685567312596461164)
XLA Ops:
  0.0 0.0 copy-start
  0.0 1.6 %pack.1 = (bf16[512,128]{1,0:T(8,128)(2,1)S(1)}, bf16[512,128]{1,0:T(8,128)(2,1)S(1)}, f32[32,128]{1,0:T(8,128)S(1)}, f32[2048,128]{1,0:T(8,128)S(1)}, f32[2,64]...) custom-call(f32[2,64,16,128]{3,2,1,0:T(8,128)} %bitcast.8, ...), custom_call_target="tpu_custom_call" | custom-call | flops 1048576 | bytes 2097152 | tf_op jit(solution)/shard_map/pack/pallas_call | solution.py:450
  1.6 3.0 %collective-permute-start.1 = (bf16[512,128]{1,0:T(8,128)(2,1)S(1)}, bf16[512,128]{1,0:T(8,128)(2,1)S(1)}, u32[]{:S(2)}, u32[]{:S(2)}) collective-permute-start(bf16[512,128]{1,0:T(8,128)(2,1)S(1)} %get-tuple-element.56), channel_id=1, source_target_pairs={{0,2},{2,0},{4,6},{6,4},{8,10},{10,8},{12,14},{14,12},{1,3},{3,1},... | collective-permute-start | bytes 393224 | tf_op jit(solution)/shard_map/ppermute | solution.py:456
  4.6 0.0 collective-permute-start
  4.6 3.6 %collective-permute-start.2 = (bf16[512,128]{1,0:T(8,128)(2,1)S(1)}, bf16[512,128]{1,0:T(8,128)(2,1)S(1)}, u32[]{:S(2)}, u32[]{:S(2)}) collective-permute-start(bf16[512,128]{1,0:T(8,128)(2,1)S(1)} %get-tuple-element.61), channel_id=1, source_target_pairs={{2,4},{4,2},{6,8},{8,6},{10,12},{12,10},{0,14},{14,0},{3,5},{5,3},... | collective-permute-start | bytes 393224 | tf_op jit(solution)/shard_map/ppermute | solution.py:463
  8.2 0.0 copy-done
  8.2 0.6 %lanes.1 = (f32[2048,128]{1,0:T(8,128)S(1)}, f32[32,128]{1,0:T(8,128)S(1)}, f32[128,128]{1,0:T(8,128)S(1)}, bf16[64,192]{1,0:T(8,128)(2,1)S(1)}, f32[64,128]{1,0:T(8,128)S(1)}, /*index=5*/f32[8,128]{1,0:T(8,128)S(1)}) custom-call(f32[2048,128]{1,0:T(8,128)S(1)} %bitcast.9, f32[2,64]{1,0:T(2,128)S(1)} %get-tuple-element.40.diffusion, ...), custom_call_target="tpu_custom_call" | custom-call | flops 1048576 | bytes 2097152 | tf_op jit(solution)/shard_map/lanes/pallas_call | solution.py:457
  8.7 1.6 %collective-permute-start.3 = (f32[32,128]{1,0:T(8,128)S(1)}, f32[32,128]{1,0:T(8,128)S(1)}, u32[]{:S(2)}, u32[]{:S(2)}) collective-permute-start(f32[32,128]{1,0:T(8,128)S(1)} %get-tuple-element.62), channel_id=1, source_target_pairs={{0,1},{1,0},{2,3},{3,2},{4,5},{5,4},{6,7},{7,6},{8,9},{9,8},{10,11... | collective-permute-start | bytes 49160 | tf_op jit(solution)/shard_map/ppermute | solution.py:443
  10.3 1.8 %inner.1 = (f32[2048,128]{1,0:T(8,128)S(1)}, f32[2048,128]{1,0:T(8,128)S(1)}, f32[64,128]{1,0:T(8,128)S(1)}, f32[64,128]{1,0:T(8,128)S(1)}, f32[32,128]{1,0:T(8,128)S(1)}) custom-call(f32[2048,128]{1,0:T(8,128)S(1)} %get-tuple-element.45.columns, f32[2048,128]{1,0:T(8,128)S(1)} %get-tuple-element.46.frame, f32[128,128]{1,0:T(8,128)S(1)} %get-tuple-element.47.nu, ...), custom_call_target="tpu_custom_call" | custom-call | flops 1073741824 | bytes 2097152 | tf_op jit(solution)/shard_map/inner/pallas_call | solution.py:464
  12.1 0.0 collective-permute-done.other
  12.1 0.0 collective-permute-done.1.from_even
  12.1 0.2 %even.1 = (f32[128,128]{1,0:T(8,128)S(1)}, f32[128,128]{1,0:T(8,128)S(1)}, f32[32,128]{1,0:T(8,128)S(1)}, f32[64,128]{1,0:T(8,128)S(1)}, f32[40,128]{1,0:T(8,128)S(1)}) custom-call(f32[2048,128]{1,0:T(8,128)S(1)} %get-tuple-element.50.strips, f32[128,128]{1,0:T(8,128)S(1)} %get-tuple-element.47.nu, bf16[64,192]{1,0:T(8,128)(2,1)S(1)} %get-tuple-element.48.weights, ...), custom_call_target="tpu_custom_call" | custom-call | flops 8589934592 | bytes 2097152 | tf_op jit(solution)/shard_map/even/pallas_call | solution.py:467
  12.4 0.2 collective-permute-done.3.rest_0_
  12.5 0.6 %collective-permute-done.2.from_odd = bf16[512,128]{1,0:T(8,128)(2,1)S(1)} collective-permute-done((bf16[512,128]{1,0:T(8,128)(2,1)S(1)}, bf16[512,128]{1,0:T(8,128)(2,1)S(1)}, u32[]{:S(2)}, u32[]{:S(2)}) %collective-permute-start.2) | collective-permute-done | bytes 131104 | tf_op jit(solution)/shard_map/ppermute | solution.py:463
  13.2 0.4 %odd.1 = (f32[128,128]{1,0:T(8,128)S(1)}, f32[128,128]{1,0:T(8,128)S(1)}, f32[64,128]{1,0:T(8,128)S(1)}, f32[40,128]{1,0:T(8,128)S(1)}, f32[32,128]{1,0:T(8,128)S(1)}) custom-call(f32[2048,128]{1,0:T(8,128)S(1)} %get-tuple-element.50.strips, f32[128,128]{1,0:T(8,128)S(1)} %get-tuple-element.47.nu, bf16[64,192]{1,0:T(8,128)(2,1)S(1)} %get-tuple-element.48.weights, ...), custom_call_target="tpu_custom_call" | custom-call | flops 67108864 | bytes 2097152 | tf_op jit(solution)/shard_map/odd/pallas_call | solution.py:471
  13.5 0.1 collective-permute-start.4
  13.6 1.6 %collective-permute-start.5 = (f32[32,128]{1,0:T(8,128)S(1)}, f32[32,128]{1,0:T(8,128)S(1)}, u32[]{:S(2)}, u32[]{:S(2)}) collective-permute-start(f32[32,128]{1,0:T(8,128)S(1)} %get-tuple-element.74), channel_id=1, source_target_pairs={{0,1},{1,0},{2,3},{3,2},{4,5},{5,4},{6,7},{7,6},{8,9},{9,8},{10,11... | collective-permute-start | bytes 49160 | tf_op jit(solution)/shard_map/ppermute | solution.py:443
  15.2 0.0 collective-permute-done.4.other
  15.2 1.5 %middle.1 = (f32[2048,128]{1,0:T(8,128)S(1)}, f32[256,128]{1,0:T(8,128)S(1)}, f32[32,128]{1,0:T(8,128)S(1)}, f32[64,128]{1,0:T(8,128)S(1)}, f32[64,128]{1,0:T(8,128)S(1)}) custom-call(f32[2048,128]{1,0:T(8,128)S(1)} %get-tuple-element.49.partial, f32[2048,128]{1,0:T(8,128)S(1)} %get-tuple-element.50.strips, f32[128,128]{1,0:T(8,128)S(1)} %get-tuple-element.47.nu, ...), custom_call_target="tpu_custom_call" | custom-call | flops 1073741824 | bytes 2097152 | tf_op jit(solution)/shard_map/middle/pallas_call | solution.py:477
  16.7 0.7 %collective-permute-done.5.rest_0_ = f32[32,128]{1,0:T(8,128)S(1)} collective-permute-done((f32[32,128]{1,0:T(8,128)S(1)}, f32[32,128]{1,0:T(8,128)S(1)}, u32[]{:S(2)}, u32[]{:S(2)}) %collective-permute-start.5) | collective-permute-done | bytes 16416 | tf_op jit(solution)/shard_map/ppermute | solution.py:443
  17.4 1.8 %last.1 = f32[2,64,16,128]{3,2,1,0:T(8,128)} custom-call(f32[2048,128]{1,0:T(8,128)S(1)} %get-tuple-element.69.partial, f32[256,128]{1,0:T(8,128)S(1)} %get-tuple-element.70.edges, f32[32,128]{1,0:T(8,128)S(1)} %get-tuple-element.71.incr, bf16[64,192]{1,0:T(8,128)(2,1)S(1)} %get-tuple-element.48.weights, f32[64,128]{1,0:T(8,128)S(1)} %get-tuple-element.51.spread, ...), custom_call_target="tpu_custom_call" | custom-call | flops 67108864 | bytes 2097152 | tf_op jit(solution)/shard_map/last/pallas_call | solution.py:481
Async XLA Ops:
  0.0 8.2 %copy-start = (f32[1,2,64,16,128]{4,3,2,1,0:T(8,128)S(1)}, f32[1,2,64,16,128]{4,3,2,1,0:T(8,128)}, u32[]{:S(2)}) copy-start(f32[1,2,64,16,128]{4,3,2,1,0:T(8,128)} %param.7) | copy-start | bytes 3145732
  1.6 10.6 %collective-permute-start.1 = (bf16[512,128]{1,0:T(8,128)(2,1)S(1)}, bf16[512,128]{1,0:T(8,128)(2,1)S(1)}, u32[]{:S(2)}, u32[]{:S(2)}) collective-permute-start(bf16[512,128]{1,0:T(8,128)(2,1)S(1)} %get-tuple-element.56), channel_id=1, source_target_pairs={{0,2},{2,0},{4,6},{6,4},{8,10},{10,8},{12,14},{14,12},{1,3},{3,1},... | collective-permute-start | bytes 393224 | tf_op jit(solution)/shard_map/ppermute | solution.py:456
  4.6 7.5 %collective-permute-start = (f32[32,128]{1,0:T(8,128)S(1)}, f32[32,128]{1,0:T(8,128)S(1)}, u32[]{:S(2)}, u32[]{:S(2)}) collective-permute-start(f32[32,128]{1,0:T(8,128)S(1)} %get-tuple-element.55.own), channel_id=1, source_target_pairs={{0,16},{16,0},{1,17},{17,1},{2,18},{18,2},{3,19},{19,3},{4,20},{20... | collective-permute-start | bytes 49160 | tf_op jit(solution)/shard_map/ppermute | solution.py:446
  4.6 8.6 %collective-permute-start.2 = (bf16[512,128]{1,0:T(8,128)(2,1)S(1)}, bf16[512,128]{1,0:T(8,128)(2,1)S(1)}, u32[]{:S(2)}, u32[]{:S(2)}) collective-permute-start(bf16[512,128]{1,0:T(8,128)(2,1)S(1)} %get-tuple-element.61), channel_id=1, source_target_pairs={{2,4},{4,2},{6,8},{8,6},{10,12},{12,10},{0,14},{14,0},{3,5},{5,3},... | collective-permute-start | bytes 393224 | tf_op jit(solution)/shard_map/ppermute | solution.py:463
  8.7 3.8 %collective-permute-start.3 = (f32[32,128]{1,0:T(8,128)S(1)}, f32[32,128]{1,0:T(8,128)S(1)}, u32[]{:S(2)}, u32[]{:S(2)}) collective-permute-start(f32[32,128]{1,0:T(8,128)S(1)} %get-tuple-element.62), channel_id=1, source_target_pairs={{0,1},{1,0},{2,3},{3,2},{4,5},{5,4},{6,7},{7,6},{8,9},{9,8},{10,11... | collective-permute-start | bytes 49160 | tf_op jit(solution)/shard_map/ppermute | solution.py:443
  13.5 1.7 %collective-permute-start.4 = (f32[40,128]{1,0:T(8,128)S(1)}, f32[40,128]{1,0:T(8,128)S(1)}, u32[]{:S(2)}, u32[]{:S(2)}) collective-permute-start(f32[40,128]{1,0:T(8,128)S(1)} %get-tuple-element.68.own), channel_id=1, source_target_pairs={{0,16},{16,0},{1,17},{17,1},{2,18},{18,2},{3,19},{19,3},{4,20},{20... | collective-permute-start | bytes 61448 | tf_op jit(solution)/shard_map/ppermute | solution.py:446
  13.6 3.8 %collective-permute-start.5 = (f32[32,128]{1,0:T(8,128)S(1)}, f32[32,128]{1,0:T(8,128)S(1)}, u32[]{:S(2)}, u32[]{:S(2)}) collective-permute-start(f32[32,128]{1,0:T(8,128)S(1)} %get-tuple-element.74), channel_id=1, source_target_pairs={{0,1},{1,0},{2,3},{3,2},{4,5},{5,4},{6,7},{7,6},{8,9},{9,8},{10,11... | collective-permute-start | bytes 49160 | tf_op jit(solution)/shard_map/ppermute | solution.py:443

commit v7 on v6

--- a/solution.py
+++ b/solution.py
@@ -10,15 +10,21 @@
 f32, bf16 = jnp.float32, jnp.bfloat16
 
 
+SCALE = 8192.0
+
+
+def ring(count, ahead):
+    return [(i, (i + ahead) % count) for i in range(count)]
+
+
 def pairs(count, odd):
     if odd:
         return [(i, ((i + 1) ^ 1) - 1) for i in range(1, count - 1)] + [(0, count - 1), (count - 1, 0)]
     return [(i, i ^ 1) for i in range(count)]
 
 
-def side_of(odd, width):
-    east = lax.rem(lax.axis_index("zon") + (0 if odd else 1), 2)
-    return east * (width - 1), east
+def side_of(east, width):
+    return width - 1 if east else 0
 
 
 def surface_level(levels):
@@ -139,42 +145,32 @@
 def pack_kernel(dims, state, flow, *rest):
     tracers, levels, width = dims
     size = levels * width
-    fixed = len(rest) - 7 >> 1
-    even_bound, odd_bound, surface, frame = rest[fixed:fixed + 4]
-    columns, raw, sems = rest[2 * fixed + 4:]
+    fixed = len(rest) - 6 >> 1
+    east_bound, west_bound, surface, frame = rest[fixed:fixed + 4]
+    raw, sems = rest[2 * fixed + 4:]
     level = surface_level(levels)
-    places = (width - 1, width - 2, 0, 1)
-    wait_columns, wait_flow, wait_rows = [], [], []
-    for i, x in enumerate(places):
-        for t in range(tracers):
-            at = i * tracers + t
-            wait_columns.append(pltpu.make_async_copy(state.at[t, :, x, :], columns.at[at], sems.at[at]))
-    used = len(wait_columns)
+    wait_flow, copies = [], []
     for k in range(2):
-        wait_flow.append(pltpu.make_async_copy(flow.at[k], raw.at[k], sems.at[used + k]))
+        wait_flow.append(pltpu.make_async_copy(flow.at[k], raw.at[k], sems.at[k]))
+    for ref, places in ((east_bound, (width - 1, width - 2)), (west_bound, (0, 1))):
+        for i, x in enumerate(places):
+            for t in range(tracers):
+                target = ref.at[pl.ds((i * tracers + t) * levels, levels), :]
+                copies.append(pltpu.make_async_copy(state.at[t, :, x, :], target, sems.at[2 + len(copies)]))
     for t in range(tracers):
         target = surface.at[pl.ds(t * width, width), :]
-        wait_rows.append(pltpu.make_async_copy(state.at[t, level], target, sems.at[used + 2 + t]))
+        copies.append(pltpu.make_async_copy(state.at[t, level], target, sems.at[2 + len(copies)]))
     for i in range(fixed):
-        wait_rows.append(pltpu.make_async_copy(rest[i], rest[fixed + 4 + i], sems.at[used + 2 + tracers + i]))
-    for copy in wait_columns + wait_flow + wait_rows:
+        copies.append(pltpu.make_async_copy(rest[i], rest[fixed + 4 + i], sems.at[2 + len(copies)]))
+    for copy in wait_flow + copies:
         copy.start()
-    for copy in wait_columns:
-        copy.wait()
-    for ref, odd in ((even_bound, False), (odd_bound, True)):
-        first = 2 * tracers * (1 - side_of(odd, width)[1])
-        for t in range(tracers):
-            high, low = split(columns[first + t])
-            ref[t * levels:(t + 1) * levels, :] = high
-            ref[(tracers + t) * levels:(tracers + t + 1) * levels, :] = low
-            ref[(2 * tracers + t) * levels:(2 * tracers + t + 1) * levels, :] = columns[first + tracers + t].astype(bf16)
     for k, copy in enumerate(wait_flow):
         copy.wait()
         frame[k * size:(k + 1) * size, :] = raw[k].reshape(size, 128).astype(f32) * 0.5
-        for ref, odd in ((even_bound, False), (odd_bound, True)):
-            strip = frame[pl.ds(k * size + side_of(odd, width)[0], levels, stride=width), :].astype(bf16)
-            ref[(3 * tracers + k) * levels:(3 * tracers + k + 1) * levels, :] = strip
-    for copy in wait_rows:
+        for ref, x in ((east_bound, width - 1), (west_bound, 0)):
+            strip = frame[pl.ds(k * size + x, levels, stride=width), :]
+            ref[(2 * tracers + k) * levels:(2 * tracers + k + 1) * levels, :] = strip
+    for copy in copies:
         copy.wait()
 
 
@@ -231,46 +227,36 @@
         rows[j:j + 1, :] = partial[pl.ds(j * levels + level, 1), :]
 
 
-def column_at(ref, index, levels):
-    return ref[pl.ds(pl.multiple_of(index * levels, 8), levels), :]
-
-
-def side_terms(ref, odd, strips, nu, sides, dims):
-    tracers, levels, width = dims
-    x, east = side_of(odd, width)
-    c = column_at(strips, x, levels) * (1 - 2 * east).astype(f32)
-    terms = []
-    for t in range(tracers):
-        value = part(ref, t, levels).astype(f32) + part(ref, tracers + t, levels).astype(f32)
-        sides[t * levels:(t + 1) * levels, :] = value
-        terms.append((part(nu, t, levels) + c) * value)
-    return terms
-
-
-def side_lanes(packed, odd, solved, lane, dims):
-    tracers, levels, width = dims
-    for t in range(tracers):
-        j = t * width + side_of(odd, width)[0]
+def side_terms(ref, east, strips, nu, dims):
+    tracers, levels, width = dims
+    c = part(strips, side_of(east, width), levels)
+    return [(part(nu, t, levels) + (-c if east else c)) * part(ref, t, levels) for t in range(tracers)]
+
+
+def side_lanes(packed, east, solved, lane, dims):
+    tracers, levels, width = dims
+    for t in range(tracers):
+        j = t * width + side_of(east, width)
         packed = packed + jnp.where(lane // 2 == j, both_edges(part(solved, t, levels), j), 0.0)
     return packed
 
 
-def side_rows(fresh, surface, odd, sides, solved, row, level, dims):
+def side_rows(fresh, surface, east, sides, solved, row, level, dims):
     tracers, levels, width = dims
     total = tracers * width
     for t in range(tracers):
         line = solved[pl.ds(t * levels + level, 1), :]
-        fresh = fresh + jnp.where(row == t * width + side_of(odd, width)[0], line, 0.0)
-        at = total + int(odd) * tracers + t
+        fresh = fresh + jnp.where(row == t * width + side_of(east, width), line, 0.0)
+        at = total + int(east) * tracers + t
         surface[at:at + 1, :] = sides[pl.ds(t * levels + level, 1), :]
     return fresh
 
 
-def even_kernel(dims, strips, nu, weights, spread, edge_lanes, rows, guide, own, other, from_even, sides, solved, incr, half_lanes, surface):
+def west_kernel(dims, strips, nu, weights, spread, edge_lanes, rows, guide, own, other, from_west, solved, incr, half_lanes, surface):
     tracers, levels, width = dims
     total = tracers * width
     lane = lanes_of(levels)
-    terms = side_terms(from_even, False, strips, nu, sides, dims)
+    terms = side_terms(from_west, False, strips, nu, dims)
     result = product(weights[...], jnp.concatenate(terms, axis=1))
     flux = increments(own[...], other[...], guide, tracers, width)
     incr[...] = flux
@@ -284,16 +270,16 @@
     level = surface_level(levels)
     surface[total:, :] = jnp.zeros((surface.shape[0] - total, 128), f32)
     fresh = rows[...] + spread[pl.ds(level, 1), :] * flux
-    surface[:total, :] = side_rows(fresh, surface, False, sides, solved, row, level, dims)
-
-
-def odd_kernel(dims, mer_count, strips, nu, weights, mer_gain, half_lanes, half_surface, even_sides, from_odd, *rest):
+    surface[:total, :] = side_rows(fresh, surface, False, from_west, solved, row, level, dims)
+
+
+def east_kernel(dims, mer_count, strips, nu, weights, mer_gain, half_lanes, half_surface, from_west, from_east, *rest):
     tracers, levels, width = dims
     total = tracers * width
-    rounds = (len(rest) - 4) // 2
-    recv_mer, (sides, solved, lanes, surface), send_mer = rest[:rounds], rest[rounds:rounds + 4], rest[rounds + 4:]
-    lane = lanes_of(levels)
-    terms = side_terms(from_odd, True, strips, nu, sides, dims)
+    rounds = (len(rest) - 3) // 2
+    recv_mer, (solved, lanes, surface), send_mer = rest[:rounds], rest[rounds:rounds + 3], rest[rounds + 3:]
+    lane = lanes_of(levels)
+    terms = side_terms(from_east, True, strips, nu, dims)
     terms.append(mer_gain[...] * mer_halo(recv_mer, levels, mer_count))
     result = product(weights[...], jnp.concatenate(terms, axis=1))
     for t in range(tracers):
@@ -304,7 +290,7 @@
     for r, ref in enumerate(send_mer):
         up = lax.rem(place + 1 + r, 2)
         message = packed
-        for s, cells in enumerate((even_sides, sides)):
+        for s, cells in enumerate((from_west, from_east)):
             for t in range(tracers):
                 at = s * tracers + t
                 moved = pltpu.roll(part(cells, t, levels), 2 * at + 2 * up, 1)
@@ -317,10 +303,10 @@
     line = jnp.take_along_axis(line, 2 * row + (rows_lane == 0).astype(jnp.int32), axis=1)
     fresh = half_surface[:total, :] + jnp.where(jnp.logical_or(rows_lane == 127, rows_lane == 0), line, 0.0)
     surface[total:, :] = half_surface[total:, :]
-    surface[:total, :] = side_rows(fresh, surface, True, sides, solved, row, level, dims)
-
-
-def middle_kernel(dims, partial, strips, nu, weights, spread, even_sides, odd_sides, even_solved, odd_solved, lanes, incr, columns, guide, own, other, from_even, from_odd, again, edges, flux, inner_gain, outer_gain, fresh):
+    surface[:total, :] = side_rows(fresh, surface, True, from_east, solved, row, level, dims)
+
+
+def middle_kernel(dims, partial, strips, nu, weights, spread, west_solved, east_solved, lanes, incr, columns, guide, own, other, from_west, from_east, again, edges, flux, inner_gain, outer_gain, fresh):
     tracers, levels, width = dims
     total = tracers * width
     lane = lanes_of(levels)
@@ -330,17 +316,17 @@
     terms, gains = [], []
     first = jnp.zeros((levels, 128), f32)
     later = jnp.zeros((levels, 128), f32)
-    for s, (ref, sides) in enumerate(((from_even, even_sides), (from_odd, odd_sides))):
-        x, east = side_of(s == 1, width)
-        ahead = (2 * east - 1).astype(f32)
-        c, d = (part(ref, 3 * tracers + k, levels).astype(f32) for k in range(2))
-        own_c = column_at(strips, x, levels) * ahead
+    for s, ref in enumerate((from_west, from_east)):
+        x = side_of(s == 1, width)
+        c, d = (part(ref, 2 * tracers + k, levels) for k in range(2))
+        own_c = part(strips, x, levels)
         for t in range(tracers):
-            mine, beyond = column_at(columns, t * width + x, levels), part(ref, 2 * tracers + t, levels).astype(f32)
-            value = horizontal(part(sides, t, levels), beyond, mine, c * ahead, d, part(nu, t, levels), lane)
+            mine, beyond = part(columns, t * width + x, levels), part(ref, tracers + t, levels)
+            west, east = (mine, beyond) if s == 1 else (beyond, mine)
+            value = horizontal(part(ref, t, levels), east, west, c, d, part(nu, t, levels), lane)
             value = value + jnp.where(at_level, jnp.broadcast_to(extra[s * tracers + t:s * tracers + t + 1, :], value.shape), 0.0)
             terms.append(value)
-            gain = part(nu, t, levels) - own_c
+            gain = part(nu, t, levels) + (-own_c if s == 1 else own_c)
             gains.append(gain)
             j = t * width + x
             here = lane // 2 == j
@@ -351,10 +337,8 @@
     outer_gain[...] = later
     result = product(weights[...], jnp.concatenate(terms, axis=1))
     result = product(weights[...], result * jnp.concatenate(gains, axis=1))
-    for s in range(2):
-        for t in range(tracers):
-            at, i = side_of(s == 1, width)[1] * tracers + t, s * tracers + t
-            edges[pl.ds(pl.multiple_of(at * levels, 8), levels), :] = result[:, i * 128:(i + 1) * 128]
+    for i in range(2 * tracers):
+        edges[i * levels:(i + 1) * levels, :] = result[:, i * 128:(i + 1) * 128]
     rim = jnp.logical_or(lane == 127, lane == 0)
     for t in range(tracers):
         for x in range(width):
@@ -362,8 +346,7 @@
             value = part(partial, j, levels) + spread[...] * incr[j:j + 1, :]
             value = value + jnp.where(rim, at_edges(lanes[...], j), 0.0)
             if x in (0, width - 1):
-                by_even = side_of(False, width)[0] == x
-                value = value + jnp.where(by_even, part(even_solved, t, levels), part(odd_solved, t, levels))
+                value = value + part(west_solved if x == 0 else east_solved, t, levels)
             fresh[j * levels:(j + 1) * levels, :] = value
 
     def store(t, x, value):
@@ -385,8 +368,8 @@
     for value, north, inside in mer_sides(recv_mer, mer_count):
         for s in range(2):
             for t in range(tracers):
-                j = t * width + side_of(s == 1, width)[0]
-                moved = pltpu.roll(value, lax.rem(2 * (j - s * tracers - t) + 128, 128), 1)
+                j = t * width + side_of(s == 1, width)
+                moved = pltpu.roll(value, 2 * (j - s * tracers - t) % 128, 1)
                 corner = jnp.where(jnp.logical_and(lane == 2 * j + 1 - north, inside), moved, corner)
     corner = outer_gain[...] * product(weights[...], inner_gain[...] * corner)
     corner = product(weights[...], corner) + lanes
@@ -432,7 +415,7 @@
     dims = (tracers, levels, width)
     size, total = levels * width, tracers * width
     shape = lambda rows, dtype=f32: jax.ShapeDtypeStruct((rows, wide), dtype)
-    message = shape((3 * tracers + 2) * levels, bf16)
+    message = shape((2 * tracers + 2) * levels)
     packed = shape(levels)
     folded = shape(levels // 2)
     kept = shape(tracers * size)
@@ -442,42 +425,47 @@
     def swap_mer(pieces):
         return [lax.ppermute(piece, "mer", pairs(mer_count, r == 1)) for r, piece in enumerate(pieces)]
 
+    def shift_zonal(piece, ahead):
+        moved = lax.ppermute(piece, "zon", ring(zon_count, ahead))
+        return moved.astype(f32) * (1.0 / SCALE)
+
     def swap_fluid(piece):
         return lax.ppermute(piece, "fluid", [(0, 1), (1, 0)])
 
     params = (diffusion[0], column_solve[0], exchange_rate, block_map[None], ice_mask[None])
     in_hbm = [pltpu.with_memory_space_constraint(value, pltpu.HBM) for value in (state[0], flow[0]) + params]
-    even_bound, odd_bound, surface, frame, *params = call(
+    east_bound, west_bound, surface, frame, *params = call(
         functools.partial(pack_kernel, dims), "pack", [HB] * len(in_hbm),
         [message, message, shape(total), shape(2 * size)] + [jax.ShapeDtypeStruct(p.shape, p.dtype) for p in params], 1 << 20,
-        scratch=[pltpu.VMEM((4 * tracers, levels, wide), f32), pltpu.VMEM((2, levels, width, wide), bf16),
+        scratch=[pltpu.VMEM((2, levels, width, wide), bf16),
                  pltpu.SemaphoreType.DMA((5 * tracers + 2 + len(params),))],
     )(*in_hbm)
-    from_even = lax.ppermute(even_bound, "zon", pairs(zon_count, False))
+    east_bound, west_bound = lax.optimization_barrier(((east_bound * SCALE).astype(jnp.float16), (west_bound * SCALE).astype(jnp.float16)))
+    from_west = shift_zonal(east_bound, 1)
     columns, send_mer, nu, weights, spread, guide = call(
         functools.partial(lanes_kernel, dims), "lanes", [VM] * 6,
         [kept, folded, shape(tracers * levels), jax.ShapeDtypeStruct((levels, 3 * levels), bf16), packed, shape(8)], 1 << 20,
     )(state.reshape(tracers * size, wide), *params)
     recv_mer = swap_mer([send_mer] * rounds)
     other = swap_fluid(surface)
-    from_odd = lax.ppermute(odd_bound, "zon", pairs(zon_count, True))
+    from_east = shift_zonal(west_bound, -1)
     partial, strips, mer_gain, edge_lanes, rows = call(
         functools.partial(inner_kernel, dims), "inner", [VM] * 4, [kept, shape(2 * size), packed, packed, shape(total)], 1 << 30,
     )(columns, frame, nu, weights)
-    even_sides, even_solved, incr, half_lanes, half_surface = call(
-        functools.partial(even_kernel, dims), "even", [VM] * 10,
-        [halved, halved, shape(total), packed, shape(total + 8)], 1 << 33,
-    )(strips, nu, weights, spread, edge_lanes, rows, guide, surface, other, from_even)
-    odd_sides, odd_solved, lanes, fresh_surface, *send_mer = call(
-        functools.partial(odd_kernel, dims, mer_count), "odd", [VM] * (8 + rounds),
-        [halved, halved, packed, shape(total + 8)] + [folded] * rounds, 1 << 26,
-    )(strips, nu, weights, mer_gain, half_lanes, half_surface, even_sides, from_odd, *recv_mer)
+    west_solved, incr, half_lanes, half_surface = call(
+        functools.partial(west_kernel, dims), "west", [VM] * 10,
+        [halved, shape(total), packed, shape(total + 8)], 1 << 33,
+    )(strips, nu, weights, spread, edge_lanes, rows, guide, surface, other, from_west)
+    east_solved, lanes, fresh_surface, *send_mer = call(
+        functools.partial(east_kernel, dims, mer_count), "east", [VM] * (8 + rounds),
+        [halved, packed, shape(total + 8)] + [folded] * rounds, 1 << 26,
+    )(strips, nu, weights, mer_gain, half_lanes, half_surface, from_west, from_east, *recv_mer)
     recv_mer = swap_mer(send_mer)
     fresh_other = swap_fluid(fresh_surface)
     again, edges, flux, inner_gain, outer_gain = call(
-        functools.partial(middle_kernel, dims), "middle", [VM] * 17,
+        functools.partial(middle_kernel, dims), "middle", [VM] * 15,
         [kept, sided, shape(total), packed, packed], 1 << 30, scratch=[pltpu.VMEM((tracers * size, wide), f32)],
-    )(partial, strips, nu, weights, spread, even_sides, odd_sides, even_solved, odd_solved, lanes, incr, columns, guide, fresh_surface, fresh_other, from_even, from_odd)
+    )(partial, strips, nu, weights, spread, west_solved, east_solved, lanes, incr, columns, guide, fresh_surface, fresh_other, from_west, from_east)
     done = call(
         functools.partial(last_kernel, dims, mer_count), "last", [VM] * (8 + rounds),
         jax.ShapeDtypeStruct(state.shape[1:], f32), 1 << 26,

time: 19.4 us -> 18.3 us (0.943)
  waiting for transfers between devices: 1.49 us -> 0.68 us
  starting transfers between devices: 9.81 us -> 9.6 us
    ppermute x2, starting transfers between devices: 6.58 us -> 5.66 us  [shift_zonal(): moved = lax.ppermute(piece, 'zon', ring(zon_count, ahead))]
    ppermute x2, waiting for transfers between devices: 0.64 us -> 0.01 us  [shift_zonal(): moved = lax.ppermute(piece, 'zon', ring(zon_count, ahead))]
    ppermute x2, starting transfers between devices: 0.06 us -> 0.57 us  [swap_fluid(): return lax.ppermute(piece, 'fluid', [(0, 1), (1, 0)])]
    ppermute x2, starting transfers between devices: 3.17 us -> 3.36 us  [swap_mer(): lax.ppermute(piece, 'mer', pairs(mer_count, r == 1))]
  transfers between devices with their start and end apart: 6 -> 6, of which waited for: 3 -> 1; matrix products, arithmetic and copies ran while one was open for 0% -> 0% of each run, Pallas kernels for 22% -> 23%
where the time goes in v7:
time: 18.3 us; the launch traced here: 18.1 us
  starting transfers between devices  9.6 us (52%)
  Pallas kernels  7.68 us (42%)
  waiting for transfers between devices  0.68 us (4%)
    ppermute x2, starting transfers between devices, shift_zonal(): moved = lax.ppermute(piece, 'zon', ring(zon_count, ahead))  5.66 us
    ppermute x2, starting transfers between devices, swap_mer(): lax.ppermute(piece, 'mer', pairs(mer_count, r == 1))  3.36 us
    pallas_call x1, Pallas kernels, on_device(): call(functools.partial(last_kernel, dims, mer_count), 'last', [VM] * (8 +...  1.81 us
    pallas_call x1, Pallas kernels, on_device(): call(functools.partial(inner_kernel, dims), 'inner', [VM] * 4, [kept, sha...  1.8 us
    pallas_call x1, Pallas kernels, on_device(): call(functools.partial(middle_kernel, dims), 'middle', [VM] * 15, [kept,...  1.49 us
    pallas_call x1, Pallas kernels, on_device(): call(functools.partial(pack_kernel, dims), 'pack', [HB] * len(in_hbm), [m...  1.38 us
    ppermute x2, waiting for transfers between devices, swap_mer(): lax.ppermute(piece, 'mer', pairs(mer_count, r == 1))  0.67 us
    pallas_call x1, Pallas kernels, on_device(): call(functools.partial(lanes_kernel, dims), 'lanes', [VM] * 6, [kept, fol...  0.58 us
  transfers between devices with their start and end apart: 6, of which 1 were waited for; matrix products, arithmetic and copies ran while one was open for 0% of the time, Pallas kernels for 23%

profile of v7, /device:TPU:0, one launch (start us, length us, event | category | flops | bytes accessed | tf_op | source)
XLA Modules:
  0.0 18.1 jit_solution(8083948684368642022)
XLA Ops:
  0.0 0.0 copy-start
  0.0 1.4 %pack.1 = (f32[384,128]{1,0:T(8,128)S(1)}, f32[384,128]{1,0:T(8,128)S(1)}, f32[32,128]{1,0:T(8,128)S(1)}, f32[2048,128]{1,0:T(8,128)S(1)}, f32[2,64]{1,0:T(2,128...) custom-call(f32[2,64,16,128]{3,2,1,0:T(8,128)} %bitcast.8, ...), custom_call_target="tpu_custom_call" | custom-call | flops 1048576 | bytes 2097152 | tf_op jit(solution)/shard_map/pack/pallas_call | solution.py:437
  1.4 0.5 %collective-permute-start = (f32[32,128]{1,0:T(8,128)S(1)}, f32[32,128]{1,0:T(8,128)S(1)}, u32[]{:S(2)}, u32[]{:S(2)}) collective-permute-start(f32[32,128]{1,0:T(8,128)S(1)} %get-tuple-element.55.own), channel_id=1, source_target_pairs={{0,16},{16,0},{1,17},{17,1},{2,18},{18,2},{3,19},{19,3},{4,20},{20... | collective-permute-start | bytes 49160 | tf_op jit(solution)/shard_map/ppermute | solution.py:433
  2.0 2.6 %collective-permute-start.1 = (f16[384,128]{1,0:T(8,128)(2,1)S(1)}, f16[384,128]{1,0:T(8,128)(2,1)S(1)}, u32[]{:S(2)}, u32[]{:S(2)}) collective-permute-start(f16[384,128]{1,0:T(8,128)(2,1)S(1)} %get-tuple-element.58), channel_id=1, source_target_pairs={{0,2},{2,4},{4,6},{6,8},{8,10},{10,12},{12,14},{14,0},{1,3},{3,5},... | collective-permute-start | bytes 294920 | tf_op jit(solution)/shard_map/ppermute | solution.py:429
  4.5 3.1 %collective-permute-start.2 = (f16[384,128]{1,0:T(8,128)(2,1)S(1)}, f16[384,128]{1,0:T(8,128)(2,1)S(1)}, u32[]{:S(2)}, u32[]{:S(2)}) collective-permute-start(f16[384,128]{1,0:T(8,128)(2,1)S(1)} %get-tuple-element.63), channel_id=1, source_target_pairs={{0,14},{2,0},{4,2},{6,4},{8,6},{10,8},{12,10},{14,12},{1,15},{3,1}... | collective-permute-start | bytes 294920 | tf_op jit(solution)/shard_map/ppermute | solution.py:429
  7.6 0.0 copy-done
  7.6 0.6 %lanes.1 = (f32[2048,128]{1,0:T(8,128)S(1)}, f32[32,128]{1,0:T(8,128)S(1)}, f32[128,128]{1,0:T(8,128)S(1)}, bf16[64,192]{1,0:T(8,128)(2,1)S(1)}, f32[64,128]{1,0:T(8,128)S(1)}, /*index=5*/f32[8,128]{1,0:T(8,128)S(1)}) custom-call(f32[2048,128]{1,0:T(8,128)S(1)} %bitcast.9, f32[2,64]{1,0:T(2,128)S(1)} %get-tuple-element.40.diffusion, ...), custom_call_target="tpu_custom_call" | custom-call | flops 1048576 | bytes 2097152 | tf_op jit(solution)/shard_map/lanes/pallas_call | solution.py:445
  8.2 1.7 %collective-permute-start.3 = (f32[32,128]{1,0:T(8,128)S(1)}, f32[32,128]{1,0:T(8,128)S(1)}, u32[]{:S(2)}, u32[]{:S(2)}) collective-permute-start(f32[32,128]{1,0:T(8,128)S(1)} %get-tuple-element.64), channel_id=1, source_target_pairs={{0,1},{1,0},{2,3},{3,2},{4,5},{5,4},{6,7},{7,6},{8,9},{9,8},{10,11... | collective-permute-start | bytes 49160 | tf_op jit(solution)/shard_map/ppermute | solution.py:426
  9.9 1.8 %inner.1 = (f32[2048,128]{1,0:T(8,128)S(1)}, f32[2048,128]{1,0:T(8,128)S(1)}, f32[64,128]{1,0:T(8,128)S(1)}, f32[64,128]{1,0:T(8,128)S(1)}, f32[32,128]{1,0:T(8,128)S(1)}) custom-call(f32[2048,128]{1,0:T(8,128)S(1)} %get-tuple-element.45.columns, f32[2048,128]{1,0:T(8,128)S(1)} %get-tuple-element.46.frame, f32[128,128]{1,0:T(8,128)S(1)} %get-tuple-element.47.nu, ...), custom_call_target="tpu_custom_call" | custom-call | flops 1073741824 | bytes 2097152 | tf_op jit(solution)/shard_map/inner/pallas_call | solution.py:452
  11.7 0.0 collective-permute-done.1
  11.8 0.0 collective-permute-done.other
  11.8 0.2 %west.1 = (f32[128,128]{1,0:T(8,128)S(1)}, f32[32,128]{1,0:T(8,128)S(1)}, f32[64,128]{1,0:T(8,128)S(1)}, f32[40,128]{1,0:T(8,128)S(1)}) custom-call(f32[2048,128]{1,0:T(8,128)S(1)} %get-tuple-element.50.strips, f32[128,128]{1,0:T(8,128)S(1)} %get-tuple-element.47.nu, bf16[64,192]{1,0:T(8,128)(2,1)S(1)} %get-tuple-element.48.weights, ...), custom_call_target="tpu_custom_call" | custom-call | flops 8589934592 | bytes 2097152 | tf_op jit(solution)/shard_map/west/pallas_call | solution.py:455
  12.0 0.0 collective-permute-done.2
  12.1 0.0 collective-permute-done.3.rest_0_
  12.1 0.4 %east.1 = (f32[128,128]{1,0:T(8,128)S(1)}, f32[64,128]{1,0:T(8,128)S(1)}, f32[40,128]{1,0:T(8,128)S(1)}, f32[32,128]{1,0:T(8,128)S(1)}) custom-call(f32[2048,128]{1,0:T(8,128)S(1)} %get-tuple-element.50.strips, f32[128,128]{1,0:T(8,128)S(1)} %get-tuple-element.47.nu, bf16[64,192]{1,0:T(8,128)(2,1)S(1)} %get-tuple-element.48.weights, ...), custom_call_target="tpu_custom_call" | custom-call | flops 67108864 | bytes 2097152 | tf_op jit(solution)/shard_map/east/pallas_call | solution.py:459
  12.5 0.1 collective-permute-start.4
  12.5 1.6 %collective-permute-start.5 = (f32[32,128]{1,0:T(8,128)S(1)}, f32[32,128]{1,0:T(8,128)S(1)}, u32[]{:S(2)}, u32[]{:S(2)}) collective-permute-start(f32[32,128]{1,0:T(8,128)S(1)} %get-tuple-element.74), channel_id=1, source_target_pairs={{0,1},{1,0},{2,3},{3,2},{4,5},{5,4},{6,7},{7,6},{8,9},{9,8},{10,11... | collective-permute-start | bytes 49160 | tf_op jit(solution)/shard_map/ppermute | solution.py:426
  14.2 0.0 collective-permute-done.4.other
  14.2 1.5 %middle.1 = (f32[2048,128]{1,0:T(8,128)S(1)}, f32[256,128]{1,0:T(8,128)S(1)}, f32[32,128]{1,0:T(8,128)S(1)}, f32[64,128]{1,0:T(8,128)S(1)}, f32[64,128]{1,0:T(8,128)S(1)}) custom-call(f32[2048,128]{1,0:T(8,128)S(1)} %get-tuple-element.49.partial, f32[2048,128]{1,0:T(8,128)S(1)} %get-tuple-element.50.strips, f32[128,128]{1,0:T(8,128)S(1)} %get-tuple-element.47.nu, ...), custom_call_target="tpu_custom_call" | custom-call | flops 1073741824 | bytes 2097152 | tf_op jit(solution)/shard_map/middle/pallas_call | solution.py:465
  15.7 0.7 %collective-permute-done.5.rest_0_ = f32[32,128]{1,0:T(8,128)S(1)} collective-permute-done((f32[32,128]{1,0:T(8,128)S(1)}, f32[32,128]{1,0:T(8,128)S(1)}, u32[]{:S(2)}, u32[]{:S(2)}) %collective-permute-start.5) | collective-permute-done | bytes 16416 | tf_op jit(solution)/shard_map/ppermute | solution.py:426
  16.3 1.8 %last.1 = f32[2,64,16,128]{3,2,1,0:T(8,128)} custom-call(f32[2048,128]{1,0:T(8,128)S(1)} %get-tuple-element.69.partial, f32[256,128]{1,0:T(8,128)S(1)} %get-tuple-element.70.edges, f32[32,128]{1,0:T(8,128)S(1)} %get-tuple-element.71.incr, bf16[64,192]{1,0:T(8,128)(2,1)S(1)} %get-tuple-element.48.weights, f32[64,128]{1,0:T(8,128)S(1)} %get-tuple-element.51.spread, ...), custom_call_target="tpu_custom_call" | custom-call | flops 67108864 | bytes 2097152 | tf_op jit(solution)/shard_map/last/pallas_call | solution.py:469
  (3 shorter events, 0.1 us)
Async XLA Ops:
  0.0 7.6 %copy-start = (f32[1,2,64,16,128]{4,3,2,1,0:T(8,128)S(1)}, f32[1,2,64,16,128]{4,3,2,1,0:T(8,128)}, u32[]{:S(2)}) copy-start(f32[1,2,64,16,128]{4,3,2,1,0:T(8,128)} %param.7) | copy-start | bytes 3145732
  1.4 10.4 %collective-permute-start = (f32[32,128]{1,0:T(8,128)S(1)}, f32[32,128]{1,0:T(8,128)S(1)}, u32[]{:S(2)}, u32[]{:S(2)}) collective-permute-start(f32[32,128]{1,0:T(8,128)S(1)} %get-tuple-element.55.own), channel_id=1, source_target_pairs={{0,16},{16,0},{1,17},{17,1},{2,18},{18,2},{3,19},{19,3},{4,20},{20... | collective-permute-start | bytes 49160 | tf_op jit(solution)/shard_map/ppermute | solution.py:433
  2.0 9.8 %collective-permute-start.1 = (f16[384,128]{1,0:T(8,128)(2,1)S(1)}, f16[384,128]{1,0:T(8,128)(2,1)S(1)}, u32[]{:S(2)}, u32[]{:S(2)}) collective-permute-start(f16[384,128]{1,0:T(8,128)(2,1)S(1)} %get-tuple-element.58), channel_id=1, source_target_pairs={{0,2},{2,4},{4,6},{6,8},{8,10},{10,12},{12,14},{14,0},{1,3},{3,5},... | collective-permute-start | bytes 294920 | tf_op jit(solution)/shard_map/ppermute | solution.py:429
  4.5 7.5 %collective-permute-start.2 = (f16[384,128]{1,0:T(8,128)(2,1)S(1)}, f16[384,128]{1,0:T(8,128)(2,1)S(1)}, u32[]{:S(2)}, u32[]{:S(2)}) collective-permute-start(f16[384,128]{1,0:T(8,128)(2,1)S(1)} %get-tuple-element.63), channel_id=1, source_target_pairs={{0,14},{2,0},{4,2},{6,4},{8,6},{10,8},{12,10},{14,12},{1,15},{3,1}... | collective-permute-start | bytes 294920 | tf_op jit(solution)/shard_map/ppermute | solution.py:429
  8.2 3.9 %collective-permute-start.3 = (f32[32,128]{1,0:T(8,128)S(1)}, f32[32,128]{1,0:T(8,128)S(1)}, u32[]{:S(2)}, u32[]{:S(2)}) collective-permute-start(f32[32,128]{1,0:T(8,128)S(1)} %get-tuple-element.64), channel_id=1, source_target_pairs={{0,1},{1,0},{2,3},{3,2},{4,5},{5,4},{6,7},{7,6},{8,9},{9,8},{10,11... | collective-permute-start | bytes 49160 | tf_op jit(solution)/shard_map/ppermute | solution.py:426
  12.5 1.7 %collective-permute-start.4 = (f32[40,128]{1,0:T(8,128)S(1)}, f32[40,128]{1,0:T(8,128)S(1)}, u32[]{:S(2)}, u32[]{:S(2)}) collective-permute-start(f32[40,128]{1,0:T(8,128)S(1)} %get-tuple-element.68.own), channel_id=1, source_target_pairs={{0,16},{16,0},{1,17},{17,1},{2,18},{18,2},{3,19},{19,3},{4,20},{20... | collective-permute-start | bytes 61448 | tf_op jit(solution)/shard_map/ppermute | solution.py:433
  12.5 3.8 %collective-permute-start.5 = (f32[32,128]{1,0:T(8,128)S(1)}, f32[32,128]{1,0:T(8,128)S(1)}, u32[]{:S(2)}, u32[]{:S(2)}) collective-permute-start(f32[32,128]{1,0:T(8,128)S(1)} %get-tuple-element.74), channel_id=1, source_target_pairs={{0,1},{1,0},{2,3},{3,2},{4,5},{5,4},{6,7},{7,6},{8,9},{9,8},{10,11... | collective-permute-start | bytes 49160 | tf_op jit(solution)/shard_map/ppermute | solution.py:426

commit v8 on v7

--- a/solution.py
+++ b/solution.py
@@ -120,15 +120,16 @@
         guide[3 + t:4 + t, :] = jnp.broadcast_to(rate[:, t:t + 1], (1, 128))
 
 
-def horizontal(q, east, west, c, d, nu, lane):
-    north = jnp.where(lane == 127, 0.0, pltpu.roll(q, 127, 1))
-    south = jnp.where(lane == 0, 0.0, pltpu.roll(q, 1, 1))
+def horizontal(q, east, west, north, south, c, d, nu):
     return q - c * (east - west) - d * (north - south) + nu * ((east + west) + (north + south) - 4.0 * q)
 
 
+def swapped(packed, lane):
+    return jnp.where(lane % 2 == 0, pltpu.roll(packed, 127, 1), pltpu.roll(packed, 1, 1))
+
+
 def interior(column, strip, nu, weights, store, dims):
     tracers, levels, width = dims
-    lane = lanes_of(levels)
     zero = jnp.zeros((levels, 128), f32)
     for x in range(width):
         c, d = strip(0, x), strip(1, x)
@@ -136,7 +137,8 @@
         for t in range(tracers):
             west = zero if x == 0 else column(t, x - 1)
             east = zero if x == width - 1 else column(t, x + 1)
-            terms.append(horizontal(column(t, x), east, west, c, d, part(nu, t, levels), lane))
+            q = column(t, x)
+            terms.append(horizontal(q, east, west, pltpu.roll(q, 127, 1), pltpu.roll(q, 1, 1), c, d, part(nu, t, levels)))
         solved = product(weights[...], jnp.concatenate(terms, axis=1))
         for t in range(tracers):
             store(t, x, solved[:, t * 128:(t + 1) * 128])
@@ -195,36 +197,33 @@
 
 def inner_kernel(dims, columns, frame, nu, weights, partial, strips, mer_gain, edge_lanes, rows):
     tracers, levels, width = dims
-    size = levels * width
-    lane = lanes_of(levels)
+    lane = lanes_of(levels)
+
+    def store(t, x, value):
+        j = t * width + x
+        partial[j * levels:(j + 1) * levels, :] = value
+
+    def strip(k, x):
+        value = frame[pl.ds(k * levels * width + x, levels, stride=width), :]
+        strips[(k * width + x) * levels:(k * width + x + 1) * levels, :] = value
+        return value
+
+    column = lambda t, x: part(columns, t * width + x, levels)
+    interior(column, strip, nu, weights, store, dims)
     packed = jnp.zeros((levels, 128), f32)
-    for k in range(2):
-        for x in range(width):
-            value = frame[pl.ds(k * size + x, levels, stride=width), :]
-            strips[(k * width + x) * levels:(k * width + x + 1) * levels, :] = value
-            if k == 1:
-                packed = jnp.where(lane // 2 == x, both_edges(value, x), packed)
+    for j in range(tracers * width):
+        packed = jnp.where(lane // 2 == j, both_edges(part(partial, j, levels), j), packed)
+    edge_lanes[...] = packed
+    packed = jnp.zeros((levels, 128), f32)
+    for x in range(width):
+        packed = jnp.where(lane // 2 == x, both_edges(part(strips, width + x, levels), x), packed)
     gain = jnp.zeros((levels, 128), f32)
     for t in range(tracers):
         merid = packed if t == 0 else pltpu.roll(packed, 2 * t * width, 1)
         mine = part(nu, t, levels) + jnp.where(lane % 2 == 0, -merid, merid)
         gain = jnp.where(lane // (2 * width) == t, mine, gain)
     mer_gain[...] = gain
-
-    def store(t, x, value):
-        j = t * width + x
-        partial[j * levels:(j + 1) * levels, :] = value
-
-    column = lambda t, x: part(columns, t * width + x, levels)
-    strip = lambda k, x: part(strips, k * width + x, levels)
-    interior(column, strip, nu, weights, store, dims)
-    level = surface_level(levels)
-    packed = jnp.zeros((levels, 128), f32)
-    for j in range(tracers * width):
-        packed = jnp.where(lane // 2 == j, both_edges(part(partial, j, levels), j), packed)
-    edge_lanes[...] = packed
-    for j in range(tracers * width):
-        rows[j:j + 1, :] = partial[pl.ds(j * levels + level, 1), :]
+    rows[...] = partial[pl.ds(surface_level(levels), tracers * width, stride=levels), :]
 
 
 def side_terms(ref, east, strips, nu, dims):
@@ -252,40 +251,43 @@
     return fresh
 
 
-def west_kernel(dims, strips, nu, weights, spread, edge_lanes, rows, guide, own, other, from_west, solved, incr, half_lanes, surface):
+def west_kernel(dims, mer_count, strips, nu, weights, spread, mer_gain, edge_lanes, rows, guide, own, other, own_mer, from_west, *rest):
     tracers, levels, width = dims
     total = tracers * width
+    rounds = len(rest) - 5
+    recv_mer, (solved, lanes, incr, half_lanes, surface) = rest[:rounds], rest[rounds:]
     lane = lanes_of(levels)
     terms = side_terms(from_west, False, strips, nu, dims)
+    terms.append(mer_gain[...] * (mer_halo(recv_mer, levels, mer_count) - swapped(unfold(own_mer[...]), lane)))
     result = product(weights[...], jnp.concatenate(terms, axis=1))
     flux = increments(own[...], other[...], guide, tracers, width)
     incr[...] = flux
     for t in range(tracers):
         solved[t * levels:(t + 1) * levels, :] = result[:, t * 128:(t + 1) * 128]
+    lanes[...] = result[:, tracers * 128:]
     row = lax.broadcasted_iota(jnp.int32, (total, 128), 0)
     rows_lane = lax.broadcasted_iota(jnp.int32, (total, 128), 1)
     turned = pltpu.roll(flux, 1, 1, stride=2, stride_axis=0)
     turned = jnp.sum(jnp.where(rows_lane // 2 == row, turned, 0.0), axis=0, keepdims=True)
-    half_lanes[...] = side_lanes(edge_lanes[...] + spread[...] * turned, False, solved, lane, dims)
+    half_lanes[...] = side_lanes(edge_lanes[...] + lanes[...] + spread[...] * turned, False, solved, lane, dims)
     level = surface_level(levels)
+    fresh = rows[...] + spread[pl.ds(level, 1), :] * flux
+    line = jnp.broadcast_to(lanes[pl.ds(level, 1), :], (total, 128))
+    line = jnp.take_along_axis(line, 2 * row + (rows_lane == 0).astype(jnp.int32), axis=1)
+    fresh = fresh + jnp.where(jnp.logical_or(rows_lane == 127, rows_lane == 0), line, 0.0)
     surface[total:, :] = jnp.zeros((surface.shape[0] - total, 128), f32)
-    fresh = rows[...] + spread[pl.ds(level, 1), :] * flux
     surface[:total, :] = side_rows(fresh, surface, False, from_west, solved, row, level, dims)
 
 
-def east_kernel(dims, mer_count, strips, nu, weights, mer_gain, half_lanes, half_surface, from_west, from_east, *rest):
+def east_kernel(dims, strips, nu, weights, half_lanes, half_surface, from_west, from_east, solved, surface, own_lanes, *send_mer):
     tracers, levels, width = dims
     total = tracers * width
-    rounds = (len(rest) - 3) // 2
-    recv_mer, (solved, lanes, surface), send_mer = rest[:rounds], rest[rounds:rounds + 3], rest[rounds + 3:]
-    lane = lanes_of(levels)
-    terms = side_terms(from_east, True, strips, nu, dims)
-    terms.append(mer_gain[...] * mer_halo(recv_mer, levels, mer_count))
-    result = product(weights[...], jnp.concatenate(terms, axis=1))
+    lane = lanes_of(levels)
+    result = product(weights[...], jnp.concatenate(side_terms(from_east, True, strips, nu, dims), axis=1))
     for t in range(tracers):
         solved[t * levels:(t + 1) * levels, :] = result[:, t * 128:(t + 1) * 128]
-    lanes[...] = result[:, tracers * 128:]
-    packed = side_lanes(half_lanes[...] + lanes[...], True, solved, lane, dims)
+    packed = side_lanes(half_lanes[...], True, solved, lane, dims)
+    own_lanes[...] = packed
     place = lax.axis_index("mer")
     for r, ref in enumerate(send_mer):
         up = lax.rem(place + 1 + r, 2)
@@ -297,20 +299,15 @@
                 message = jnp.where(lane == 2 * at + up, moved, message)
         ref[...] = fold(message)
     row = lax.broadcasted_iota(jnp.int32, (total, 128), 0)
-    rows_lane = lax.broadcasted_iota(jnp.int32, (total, 128), 1)
-    level = surface_level(levels)
-    line = jnp.broadcast_to(lanes[pl.ds(level, 1), :], (total, 128))
-    line = jnp.take_along_axis(line, 2 * row + (rows_lane == 0).astype(jnp.int32), axis=1)
-    fresh = half_surface[:total, :] + jnp.where(jnp.logical_or(rows_lane == 127, rows_lane == 0), line, 0.0)
     surface[total:, :] = half_surface[total:, :]
-    surface[:total, :] = side_rows(fresh, surface, True, from_east, solved, row, level, dims)
-
-
-def middle_kernel(dims, partial, strips, nu, weights, spread, west_solved, east_solved, lanes, incr, columns, guide, own, other, from_west, from_east, again, edges, flux, inner_gain, outer_gain, fresh):
+    surface[:total, :] = side_rows(half_surface[:total, :], surface, True, from_east, solved, row, surface_level(levels), dims)
+
+
+def middle_kernel(dims, partial, strips, nu, weights, spread, west_solved, east_solved, lanes, incr, columns, guide, own, other, from_west, from_east, again, inner_gain, outer_gain, fresh):
     tracers, levels, width = dims
     total = tracers * width
     lane = lanes_of(levels)
-    flux[...] = increments(own[:total, :], other[:total, :], guide, tracers, width)
+    flux = increments(own[:total, :], other[:total, :], guide, tracers, width)
     extra = increments(own[total:, :], other[total:, :], guide, tracers, 1)
     at_level = lax.broadcasted_iota(jnp.int32, (levels, 128), 0) == surface_level(levels)
     terms, gains = [], []
@@ -323,7 +320,10 @@
         for t in range(tracers):
             mine, beyond = part(columns, t * width + x, levels), part(ref, tracers + t, levels)
             west, east = (mine, beyond) if s == 1 else (beyond, mine)
-            value = horizontal(part(ref, t, levels), east, west, c, d, part(nu, t, levels), lane)
+            q = part(ref, t, levels)
+            north = jnp.where(lane == 127, 0.0, pltpu.roll(q, 127, 1))
+            south = jnp.where(lane == 0, 0.0, pltpu.roll(q, 1, 1))
+            value = horizontal(q, east, west, north, south, c, d, part(nu, t, levels))
             value = value + jnp.where(at_level, jnp.broadcast_to(extra[s * tracers + t:s * tracers + t + 1, :], value.shape), 0.0)
             terms.append(value)
             gain = part(nu, t, levels) + (-own_c if s == 1 else own_c)
@@ -337,8 +337,6 @@
     outer_gain[...] = later
     result = product(weights[...], jnp.concatenate(terms, axis=1))
     result = product(weights[...], result * jnp.concatenate(gains, axis=1))
-    for i in range(2 * tracers):
-        edges[i * levels:(i + 1) * levels, :] = result[:, i * 128:(i + 1) * 128]
     rim = jnp.logical_or(lane == 127, lane == 0)
     for t in range(tracers):
         for x in range(width):
@@ -350,20 +348,25 @@
             fresh[j * levels:(j + 1) * levels, :] = value
 
     def store(t, x, value):
-        again[pl.ds((t * width + x) * levels, levels), :] = value
+        j = t * width + x
+        value = value + spread[...] * flux[j:j + 1, :]
+        if x in (0, width - 1):
+            at = (0 if x == 0 else tracers) + t
+            value = value + result[:, at * 128:(at + 1) * 128]
+        again[j * levels:(j + 1) * levels, :] = value
 
     column = lambda t, x: part(fresh, t * width + x, levels)
     strip = lambda k, x: part(strips, k * width + x, levels)
     interior(column, strip, nu, weights, store, dims)
 
 
-def last_kernel(dims, mer_count, partial, edges, incr, weights, spread, mer_gain, inner_gain, outer_gain, *rest):
+def last_kernel(dims, mer_count, partial, weights, mer_gain, own_lanes, inner_gain, outer_gain, *rest):
     tracers, levels, width = dims
     rounds = len(rest) - 3
     recv_mer, (out, done, sems) = rest[:rounds], rest[rounds:]
     lane = lanes_of(levels)
     halo = mer_halo(recv_mer, levels, mer_count)
-    lanes = product(weights[...], mer_gain[...] * halo)
+    lanes = product(weights[...], mer_gain[...] * (halo - swapped(own_lanes[...], lane)))
     corner = jnp.zeros((levels, 128), f32)
     for value, north, inside in mer_sides(recv_mer, mer_count):
         for s in range(2):
@@ -378,11 +381,8 @@
     for x in list(range(1, width - 1)) + [0, width - 1]:
         for t in range(tracers):
             j = t * width + x
-            value = part(partial, j, levels) + spread[...] * incr[j:j + 1, :]
-            value = value + jnp.where(rim, at_edges(corner if x in (0, width - 1) else lanes, j), 0.0)
-            if x in (0, width - 1):
-                value = value + part(edges, (0 if x == 0 else tracers) + t, levels)
-            done[j] = value
+            edge = at_edges(corner if x in (0, width - 1) else lanes, j)
+            done[j] = part(partial, j, levels) + jnp.where(rim, edge, 0.0)
             copy = pltpu.make_async_copy(done.at[j], out.at[t, :, x, :], sems.at[j])
             copy.start()
             copies.append(copy)
@@ -420,14 +420,15 @@
     folded = shape(levels // 2)
     kept = shape(tracers * size)
     halved = shape(tracers * levels)
-    sided = shape(2 * tracers * levels)
 
     def swap_mer(pieces):
         return [lax.ppermute(piece, "mer", pairs(mer_count, r == 1)) for r, piece in enumerate(pieces)]
 
     def shift_zonal(piece, ahead):
-        moved = lax.ppermute(piece, "zon", ring(zon_count, ahead))
-        return moved.astype(f32) * (1.0 / SCALE)
+        return lax.ppermute(piece, "zon", ring(zon_count, ahead))
+
+    def widen(piece):
+        return piece.astype(f32) * (1.0 / SCALE)
 
     def swap_fluid(piece):
         return lax.ppermute(piece, "fluid", [(0, 1), (1, 0)])
@@ -441,37 +442,40 @@
                  pltpu.SemaphoreType.DMA((5 * tracers + 2 + len(params),))],
     )(*in_hbm)
     east_bound, west_bound = lax.optimization_barrier(((east_bound * SCALE).astype(jnp.float16), (west_bound * SCALE).astype(jnp.float16)))
-    from_west = shift_zonal(east_bound, 1)
+    from_west = widen(shift_zonal(east_bound, 1))
     columns, send_mer, nu, weights, spread, guide = call(
         functools.partial(lanes_kernel, dims), "lanes", [VM] * 6,
         [kept, folded, shape(tracers * levels), jax.ShapeDtypeStruct((levels, 3 * levels), bf16), packed, shape(8)], 1 << 20,
     )(state.reshape(tracers * size, wide), *params)
+    west_bound, send_mer = lax.optimization_barrier((west_bound, send_mer))
     recv_mer = swap_mer([send_mer] * rounds)
     other = swap_fluid(surface)
     from_east = shift_zonal(west_bound, -1)
     partial, strips, mer_gain, edge_lanes, rows = call(
         functools.partial(inner_kernel, dims), "inner", [VM] * 4, [kept, shape(2 * size), packed, packed, shape(total)], 1 << 30,
     )(columns, frame, nu, weights)
-    west_solved, incr, half_lanes, half_surface = call(
-        functools.partial(west_kernel, dims), "west", [VM] * 10,
-        [halved, shape(total), packed, shape(total + 8)], 1 << 33,
-    )(strips, nu, weights, spread, edge_lanes, rows, guide, surface, other, from_west)
-    east_solved, lanes, fresh_surface, *send_mer = call(
-        functools.partial(east_kernel, dims, mer_count), "east", [VM] * (8 + rounds),
-        [halved, packed, shape(total + 8)] + [folded] * rounds, 1 << 26,
-    )(strips, nu, weights, mer_gain, half_lanes, half_surface, from_west, from_east, *recv_mer)
+    west_solved, lanes, incr, half_lanes, half_surface = call(
+        functools.partial(west_kernel, dims, mer_count), "west", [VM] * (12 + rounds),
+        [halved, packed, shape(total), packed, shape(total + 8)], 1 << 33,
+    )(strips, nu, weights, spread, mer_gain, edge_lanes, rows, guide, surface, other, send_mer, from_west, *recv_mer)
+    from_east, half_lanes = lax.optimization_barrier((from_east, half_lanes))
+    from_east = widen(from_east)
+    east_solved, fresh_surface, own_lanes, *send_mer = call(
+        functools.partial(east_kernel, dims), "east", [VM] * 7,
+        [halved, shape(total + 8), packed] + [folded] * rounds, 1 << 26,
+    )(strips, nu, weights, half_lanes, half_surface, from_west, from_east)
     recv_mer = swap_mer(send_mer)
     fresh_other = swap_fluid(fresh_surface)
-    again, edges, flux, inner_gain, outer_gain = call(
+    again, inner_gain, outer_gain = call(
         functools.partial(middle_kernel, dims), "middle", [VM] * 15,
-        [kept, sided, shape(total), packed, packed], 1 << 30, scratch=[pltpu.VMEM((tracers * size, wide), f32)],
+        [kept, packed, packed], 1 << 30, scratch=[pltpu.VMEM((tracers * size, wide), f32)],
     )(partial, strips, nu, weights, spread, west_solved, east_solved, lanes, incr, columns, guide, fresh_surface, fresh_other, from_west, from_east)
     done = call(
-        functools.partial(last_kernel, dims, mer_count), "last", [VM] * (8 + rounds),
+        functools.partial(last_kernel, dims, mer_count), "last", [VM] * (6 + rounds),
         jax.ShapeDtypeStruct(state.shape[1:], f32), 1 << 26,
         out_specs=pl.BlockSpec(memory_space=pl.ANY),
         scratch=[pltpu.VMEM((total, levels, wide), f32), pltpu.SemaphoreType.DMA((total,))],
-    )(again, edges, flux, weights, spread, mer_gain, inner_gain, outer_gain, *recv_mer)
+    )(again, weights, mer_gain, own_lanes, inner_gain, outer_gain, *recv_mer)
     return done[None]
 
 

time: 18.3 us -> 19.2 us (1.049)
  waiting for transfers between devices: 0.68 us -> 2.21 us
  starting transfers between devices: 9.6 us -> 8.83 us
  Pallas kernels: 7.68 us -> 7.88 us
    ppermute x2, starting transfers between devices: 3.36 us -> 2.47 us  [swap_mer(): lax.ppermute(piece, 'mer', pairs(mer_count, r == 1))]
    ppermute x2, waiting for transfers between devices: 0.01 us -> 0.82 us  [shift_zonal(): return lax.ppermute(piece, 'zon', ring(zon_count, ahead))]
    ppermute x2, waiting for transfers between devices: 0.67 us -> 1.1 us  [swap_mer(): lax.ppermute(piece, 'mer', pairs(mer_count, r == 1))]
    ppermute x2, waiting for transfers between devices: 0.01 us -> 0.29 us  [swap_fluid(): return lax.ppermute(piece, 'fluid', [(0, 1), (1, 0)])]
  transfers between devices with their start and end apart: 6 -> 6, of which waited for: 1 -> 3; matrix products, arithmetic and copies ran while one was open for 0% -> 0% of each run, Pallas kernels for 23% -> 23%
where the time goes in v8:
time: 19.2 us; the launch traced here: 19.1 us
  starting transfers between devices  8.83 us (46%)
  Pallas kernels  7.88 us (41%)
  waiting for transfers between devices  2.21 us (12%)
    ppermute x2, starting transfers between devices, shift_zonal(): return lax.ppermute(piece, 'zon', ring(zon_count, ahead))  5.79 us
    ppermute x2, starting transfers between devices, swap_mer(): lax.ppermute(piece, 'mer', pairs(mer_count, r == 1))  2.47 us
    pallas_call x1, Pallas kernels, on_device(): call(functools.partial(inner_kernel, dims), 'inner', [VM] * 4, [kept, sha...  1.92 us
    pallas_call x1, Pallas kernels, on_device(): call(functools.partial(last_kernel, dims, mer_count), 'last', [VM] * (6 +...  1.8 us
    pallas_call x1, Pallas kernels, on_device(): call(functools.partial(middle_kernel, dims), 'middle', [VM] * 15, [kept,...  1.53 us
    pallas_call x1, Pallas kernels, on_device(): call(functools.partial(pack_kernel, dims), 'pack', [HB] * len(in_hbm), [m...  1.38 us
    ppermute x2, waiting for transfers between devices, swap_mer(): lax.ppermute(piece, 'mer', pairs(mer_count, r == 1))  1.1 us
    ppermute x2, waiting for transfers between devices, shift_zonal(): return lax.ppermute(piece, 'zon', ring(zon_count, ahead))  0.82 us
  transfers between devices with their start and end apart: 6, of which 3 were waited for; matrix products, arithmetic and copies ran while one was open for 0% of the time, Pallas kernels for 23%

profile of v8, /device:TPU:0, one launch (start us, length us, event | category | flops | bytes accessed | tf_op | source)
XLA Modules:
  0.0 19.1 jit_solution(12031694340111473426)
XLA Ops:
  0.0 0.0 copy-start
  0.0 1.4 %pack.1 = (f32[384,128]{1,0:T(8,128)S(1)}, f32[384,128]{1,0:T(8,128)S(1)}, f32[32,128]{1,0:T(8,128)S(1)}, f32[2048,128]{1,0:T(8,128)S(1)}, f32[2,64]{1,0:T(2,128...) custom-call(f32[2,64,16,128]{3,2,1,0:T(8,128)} %bitcast.8, ...), custom_call_target="tpu_custom_call" | custom-call | flops 1048576 | bytes 2097152 | tf_op jit(solution)/shard_map/pack/pallas_call | solution.py:438
  1.4 0.5 %collective-permute-start = (f32[32,128]{1,0:T(8,128)S(1)}, f32[32,128]{1,0:T(8,128)S(1)}, u32[]{:S(2)}, u32[]{:S(2)}) collective-permute-start(f32[32,128]{1,0:T(8,128)S(1)} %get-tuple-element.59.own), channel_id=1, source_target_pairs={{0,16},{16,0},{1,17},{17,1},{2,18},{18,2},{3,19},{19,3},{4,20},{20... | collective-permute-start | bytes 49160 | tf_op jit(solution)/shard_map/ppermute | solution.py:434
  2.0 2.6 %collective-permute-start.1 = (f16[384,128]{1,0:T(8,128)(2,1)S(1)}, f16[384,128]{1,0:T(8,128)(2,1)S(1)}, u32[]{:S(2)}, u32[]{:S(2)}) collective-permute-start(f16[384,128]{1,0:T(8,128)(2,1)S(1)} %get-tuple-element.65), channel_id=1, source_target_pairs={{0,2},{2,4},{4,6},{6,8},{8,10},{10,12},{12,14},{14,0},{1,3},{3,5},... | collective-permute-start | bytes 294920 | tf_op jit(solution)/shard_map/ppermute | solution.py:428
  4.5 0.0 copy-done
  4.5 0.6 %lanes.1 = (f32[2048,128]{1,0:T(8,128)S(1)}, f32[32,128]{1,0:T(8,128)S(1)}, f32[128,128]{1,0:T(8,128)S(1)}, bf16[64,192]{1,0:T(8,128)(2,1)S(1)}, f32[64,128]{1,0:T(8,128)S(1)}, /*index=5*/f32[8,128]{1,0:T(8,128)S(1)}) custom-call(f32[2048,128]{1,0:T(8,128)S(1)} %bitcast.9, f32[2,64]{1,0:T(2,128)S(1)} %get-tuple-element.43.diffusion, ...), custom_call_target="tpu_custom_call" | custom-call | flops 1048576 | bytes 2097152 | tf_op jit(solution)/shard_map/lanes/pallas_call | solution.py:446
  5.1 1.6 %collective-permute-start.2 = (f32[32,128]{1,0:T(8,128)S(1)}, f32[32,128]{1,0:T(8,128)S(1)}, u32[]{:S(2)}, u32[]{:S(2)}) collective-permute-start(f32[32,128]{1,0:T(8,128)S(1)} %get-tuple-element.64.own_mer), channel_id=1, source_target_pairs={{0,1},{1,0},{2,3},{3,2},{4,5},{5,4},{6,7},{7,6},{8,9},{9,8},{10,11... | collective-permute-start | bytes 49160 | tf_op jit(solution)/shard_map/ppermute | solution.py:425
  6.7 3.2 %collective-permute-start.3 = (f16[384,128]{1,0:T(8,128)(2,1)S(1)}, f16[384,128]{1,0:T(8,128)(2,1)S(1)}, u32[]{:S(2)}, u32[]{:S(2)}) collective-permute-start(f16[384,128]{1,0:T(8,128)(2,1)S(1)} %get-tuple-element.67), channel_id=1, source_target_pairs={{0,14},{2,0},{4,2},{6,4},{8,6},{10,8},{12,10},{14,12},{1,15},{3,1}... | collective-permute-start | bytes 294920 | tf_op jit(solution)/shard_map/ppermute | solution.py:428
  9.9 1.9 %inner.1 = (f32[2048,128]{1,0:T(8,128)S(1)}, f32[2048,128]{1,0:T(8,128)S(1)}, f32[64,128]{1,0:T(8,128)S(1)}, f32[64,128]{1,0:T(8,128)S(1)}, f32[32,128]{1,0:T(8,128)S(1)}) custom-call(f32[2048,128]{1,0:T(8,128)S(1)} %get-tuple-element.48.columns, f32[2048,128]{1,0:T(8,128)S(1)} %get-tuple-element.49.frame, f32[128,128]{1,0:T(8,128)S(1)} %get-tuple-element.50.nu, ...), custom_call_target="tpu_custom_call" | custom-call | flops 1073741824 | bytes 2097152 | tf_op jit(solution)/shard_map/inner/pallas_call | solution.py:454
  11.8 0.0 collective-permute-done.1
  11.9 0.0 collective-permute-done.other
  11.9 0.0 collective-permute-done.2.rest_0_
  11.9 0.4 %west.1 = (f32[128,128]{1,0:T(8,128)S(1)}, f32[64,128]{1,0:T(8,128)S(1)}, f32[32,128]{1,0:T(8,128)S(1)}, f32[64,128]{1,0:T(8,128)S(1)}, f32[40,128]{1,0:T(8,128)S(1)}) custom-call(f32[2048,128]{1,0:T(8,128)S(1)} %get-tuple-element.53.strips, f32[128,128]{1,0:T(8,128)S(1)} %get-tuple-element.50.nu, bf16[64,192]{1,0:T(8,128)(2,1)S(1)} %get-tuple-element.51.weights, ...), custom_call_target="tpu_custom_call" | custom-call | flops 8589934592 | bytes 2097152 | tf_op jit(solution)/shard_map/west/pallas_call | solution.py:457
  12.3 0.8 %collective-permute-done.3 = f16[384,128]{1,0:T(8,128)(2,1)S(1)} collective-permute-done((f16[384,128]{1,0:T(8,128)(2,1)S(1)}, f16[384,128]{1,0:T(8,128)(2,1)S(1)}, u32[]{:S(2)}, u32[]{:S(2)}) %collective-permute-start.3) | collective-permute-done | bytes 98336 | tf_op jit(solution)/shard_map/ppermute | solution.py:428
  13.1 0.3 %east.1 = (f32[128,128]{1,0:T(8,128)S(1)}, f32[40,128]{1,0:T(8,128)S(1)}, f32[64,128]{1,0:T(8,128)S(1)}, f32[32,128]{1,0:T(8,128)S(1)}) custom-call(f32[2048,128]{1,0:T(8,128)S(1)} %get-tuple-element.53.strips, f32[128,128]{1,0:T(8,128)S(1)} %get-tuple-element.50.nu, bf16[64,192]{1,0:T(8,128)(2,1)S(1)} %get-tuple-element.51.weights, ...), custom_call_target="tpu_custom_call" | custom-call | flops 67108864 | bytes 2097152 | tf_op jit(solution)/shard_map/east/pallas_call | solution.py:463
  13.4 0.1 collective-permute-start.4
  13.5 0.9 %collective-permute-start.5 = (f32[32,128]{1,0:T(8,128)S(1)}, f32[32,128]{1,0:T(8,128)S(1)}, u32[]{:S(2)}, u32[]{:S(2)}) collective-permute-start(f32[32,128]{1,0:T(8,128)S(1)} %get-tuple-element.80), channel_id=1, source_target_pairs={{0,1},{1,0},{2,3},{3,2},{4,5},{5,4},{6,7},{7,6},{8,9},{9,8},{10,11... | collective-permute-start | bytes 49160 | tf_op jit(solution)/shard_map/ppermute | solution.py:425
  14.4 0.3 %collective-permute-done.4.other = f32[40,128]{1,0:T(8,128)S(1)} collective-permute-done((f32[40,128]{1,0:T(8,128)S(1)}, f32[40,128]{1,0:T(8,128)S(1)}, u32[]{:S(2)}, u32[]{:S(2)}) %collective-permute-start.4) | collective-permute-done | bytes 20512 | tf_op jit(solution)/shard_map/ppermute | solution.py:434
  14.7 1.5 %middle.1 = (f32[2048,128]{1,0:T(8,128)S(1)}, f32[64,128]{1,0:T(8,128)S(1)}, f32[64,128]{1,0:T(8,128)S(1)}) custom-call(f32[2048,128]{1,0:T(8,128)S(1)} %get-tuple-element.52.partial, f32[2048,128]{1,0:T(8,128)S(1)} %get-tuple-element.53.strips, f32[128,128]{1,0:T(8,128)S(1)} %get-tuple-element.50.nu, bf16[64,192]{1,0:T(8,128)(2,1)S(1)} %get-tuple-element.51.weights, ...), custom_call_target="tpu_custom_call" | custom-call | flops 1073741824 | bytes 2097152 | tf_op jit(solution)/shard_map/middle/pallas_call | solution.py:469
  16.2 1.1 %collective-permute-done.5.rest_0_ = f32[32,128]{1,0:T(8,128)S(1)} collective-permute-done((f32[32,128]{1,0:T(8,128)S(1)}, f32[32,128]{1,0:T(8,128)S(1)}, u32[]{:S(2)}, u32[]{:S(2)}) %collective-permute-start.5) | collective-permute-done | bytes 16416 | tf_op jit(solution)/shard_map/ppermute | solution.py:425
  17.3 1.8 %last.1 = f32[2,64,16,128]{3,2,1,0:T(8,128)} custom-call(f32[2048,128]{1,0:T(8,128)S(1)} %get-tuple-element.76.partial, bf16[64,192]{1,0:T(8,128)(2,1)S(1)} %get-tuple-element.51.weights, f32[64,128]{1,0:T(8,128)S(1)} %get-tuple-element.55.mer_gain, f32[64,128]{1,0:T(8,128)S(1)} %get-tuple-element.77.own_lanes, f32[64,128]{1,0:T(8,128)S(1)} %get-tuple-element.78.inner_gain, ...), custom_call_target="tpu_custom_call" | custom-call | flops 67108864 | bytes 2097152 | tf_op jit(solution)/shard_map/last/pallas_call | solution.py:473
  (3 shorter events, 0.1 us)
Async XLA Ops:
  0.0 4.5 %copy-start = (f32[1,2,64,16,128]{4,3,2,1,0:T(8,128)S(1)}, f32[1,2,64,16,128]{4,3,2,1,0:T(8,128)}, u32[]{:S(2)}) copy-start(f32[1,2,64,16,128]{4,3,2,1,0:T(8,128)} %param.7) | copy-start | bytes 3145732
  1.4 10.5 %collective-permute-start = (f32[32,128]{1,0:T(8,128)S(1)}, f32[32,128]{1,0:T(8,128)S(1)}, u32[]{:S(2)}, u32[]{:S(2)}) collective-permute-start(f32[32,128]{1,0:T(8,128)S(1)} %get-tuple-element.59.own), channel_id=1, source_target_pairs={{0,16},{16,0},{1,17},{17,1},{2,18},{18,2},{3,19},{19,3},{4,20},{20... | collective-permute-start | bytes 49160 | tf_op jit(solution)/shard_map/ppermute | solution.py:434
  2.0 9.9 %collective-permute-start.1 = (f16[384,128]{1,0:T(8,128)(2,1)S(1)}, f16[384,128]{1,0:T(8,128)(2,1)S(1)}, u32[]{:S(2)}, u32[]{:S(2)}) collective-permute-start(f16[384,128]{1,0:T(8,128)(2,1)S(1)} %get-tuple-element.65), channel_id=1, source_target_pairs={{0,2},{2,4},{4,6},{6,8},{8,10},{10,12},{12,14},{14,0},{1,3},{3,5},... | collective-permute-start | bytes 294920 | tf_op jit(solution)/shard_map/ppermute | solution.py:428
  5.1 6.8 %collective-permute-start.2 = (f32[32,128]{1,0:T(8,128)S(1)}, f32[32,128]{1,0:T(8,128)S(1)}, u32[]{:S(2)}, u32[]{:S(2)}) collective-permute-start(f32[32,128]{1,0:T(8,128)S(1)} %get-tuple-element.64.own_mer), channel_id=1, source_target_pairs={{0,1},{1,0},{2,3},{3,2},{4,5},{5,4},{6,7},{7,6},{8,9},{9,8},{10,11... | collective-permute-start | bytes 49160 | tf_op jit(solution)/shard_map/ppermute | solution.py:425
  6.7 6.4 %collective-permute-start.3 = (f16[384,128]{1,0:T(8,128)(2,1)S(1)}, f16[384,128]{1,0:T(8,128)(2,1)S(1)}, u32[]{:S(2)}, u32[]{:S(2)}) collective-permute-start(f16[384,128]{1,0:T(8,128)(2,1)S(1)} %get-tuple-element.67), channel_id=1, source_target_pairs={{0,14},{2,0},{4,2},{6,4},{8,6},{10,8},{12,10},{14,12},{1,15},{3,1}... | collective-permute-start | bytes 294920 | tf_op jit(solution)/shard_map/ppermute | solution.py:428
  13.4 1.2 %collective-permute-start.4 = (f32[40,128]{1,0:T(8,128)S(1)}, f32[40,128]{1,0:T(8,128)S(1)}, u32[]{:S(2)}, u32[]{:S(2)}) collective-permute-start(f32[40,128]{1,0:T(8,128)S(1)} %get-tuple-element.75.own), channel_id=1, source_target_pairs={{0,16},{16,0},{1,17},{17,1},{2,18},{18,2},{3,19},{19,3},{4,20},{20... | collective-permute-start | bytes 61448 | tf_op jit(solution)/shard_map/ppermute | solution.py:434
  13.5 3.8 %collective-permute-start.5 = (f32[32,128]{1,0:T(8,128)S(1)}, f32[32,128]{1,0:T(8,128)S(1)}, u32[]{:S(2)}, u32[]{:S(2)}) collective-permute-start(f32[32,128]{1,0:T(8,128)S(1)} %get-tuple-element.80), channel_id=1, source_target_pairs={{0,1},{1,0},{2,3},{3,2},{4,5},{5,4},{6,7},{7,6},{8,9},{9,8},{10,11... | collective-permute-start | bytes 49160 | tf_op jit(solution)/shard_map/ppermute | solution.py:425

commit v9 on v7

--- a/solution.py
+++ b/solution.py
@@ -62,9 +62,9 @@
 def mer_sides(recv_mer, mer_count):
     place = lax.axis_index("mer")
     even = 1 - lax.rem(place, 2)
-    for r, ref in enumerate(recv_mer):
+    for r, value in enumerate(recv_mer):
         north = even if r == 0 else 1 - even
-        yield unfold(ref[...]), north, jnp.where(north == 1, place + 1 < mer_count, place > 0)
+        yield value, north, jnp.where(north == 1, place + 1 < mer_count, place > 0)
 
 
 def mer_halo(recv_mer, levels, mer_count):
@@ -174,18 +174,28 @@
         copy.wait()
 
 
-def lanes_kernel(dims, cells, diffusion, solve, rate, block_map, ice_mask, columns, send_mer, nu, weights, spread, guide):
-    tracers, levels, width = dims
+def lanes_kernel(dims, cells, frame, diffusion, solve, rate, block_map, ice_mask, columns, send_mer, nu, weights, spread, guide):
+    tracers, levels, width = dims
+    size = levels * width
     lane = lanes_of(levels)
     packed = jnp.zeros((levels, 128), f32)
+    merid = jnp.zeros((levels, 128), f32)
+    gain = jnp.zeros((levels, 128), f32)
+    for x in range(width):
+        strip = frame[pl.ds(size + x, levels, stride=width), :]
+        merid = jnp.where(lane // 2 == x, both_edges(strip, x), merid)
     for t in range(tracers):
         for x in range(width):
             j = t * width + x
-            value = cells[pl.ds(t * levels * width + x, levels, stride=width), :]
+            value = cells[pl.ds(t * size + x, levels, stride=width), :]
             columns[j * levels:(j + 1) * levels, :] = value
             packed = jnp.where(lane // 2 == j, both_edges(value, j), packed)
-        nu[t * levels:(t + 1) * levels, :] = jnp.transpose(jnp.broadcast_to(diffusion[t:t + 1, :], (128, levels)))
-    send_mer[...] = fold(packed)
+        mine = jnp.transpose(jnp.broadcast_to(diffusion[t:t + 1, :], (128, levels)))
+        nu[t * levels:(t + 1) * levels, :] = mine
+        turned = merid if t == 0 else pltpu.roll(merid, 2 * t * width, 1)
+        mine = mine + jnp.where(lane % 2 == 0, -turned, turned)
+        gain = jnp.where(lane // (2 * width) == t, mine, gain)
+    send_mer[...] = jnp.where(lane < 64, packed, pltpu.roll(gain, 64, 1))
     high, low = split(solve[...])
     weights[...] = jnp.concatenate([high, high, low], axis=1)
     at_level = lax.broadcasted_iota(jnp.int32, (levels, levels), 1) == surface_level(levels)
@@ -193,23 +203,13 @@
     spread[...] = jnp.broadcast_to(jnp.sum(jnp.where(at_level, solve[...], 0.0), axis=1, keepdims=True), (levels, 128))
 
 
-def inner_kernel(dims, columns, frame, nu, weights, partial, strips, mer_gain, edge_lanes, rows):
-    tracers, levels, width = dims
-    size = levels * width
-    lane = lanes_of(levels)
-    packed = jnp.zeros((levels, 128), f32)
+def inner_kernel(dims, columns, frame, nu, weights, partial, strips, edge_lanes, rows):
+    tracers, levels, width = dims
+    lane = lanes_of(levels)
     for k in range(2):
         for x in range(width):
-            value = frame[pl.ds(k * size + x, levels, stride=width), :]
+            value = frame[pl.ds((k * levels * width) + x, levels, stride=width), :]
             strips[(k * width + x) * levels:(k * width + x + 1) * levels, :] = value
-            if k == 1:
-                packed = jnp.where(lane // 2 == x, both_edges(value, x), packed)
-    gain = jnp.zeros((levels, 128), f32)
-    for t in range(tracers):
-        merid = packed if t == 0 else pltpu.roll(packed, 2 * t * width, 1)
-        mine = part(nu, t, levels) + jnp.where(lane % 2 == 0, -merid, merid)
-        gain = jnp.where(lane // (2 * width) == t, mine, gain)
-    mer_gain[...] = gain
 
     def store(t, x, value):
         j = t * width + x
@@ -218,13 +218,11 @@
     column = lambda t, x: part(columns, t * width + x, levels)
     strip = lambda k, x: part(strips, k * width + x, levels)
     interior(column, strip, nu, weights, store, dims)
-    level = surface_level(levels)
     packed = jnp.zeros((levels, 128), f32)
     for j in range(tracers * width):
         packed = jnp.where(lane // 2 == j, both_edges(part(partial, j, levels), j), packed)
     edge_lanes[...] = packed
-    for j in range(tracers * width):
-        rows[j:j + 1, :] = partial[pl.ds(j * levels + level, 1), :]
+    rows[...] = partial[pl.ds(surface_level(levels), tracers * width, stride=levels), :]
 
 
 def side_terms(ref, east, strips, nu, dims):
@@ -241,14 +239,11 @@
     return packed
 
 
-def side_rows(fresh, surface, east, sides, solved, row, level, dims):
-    tracers, levels, width = dims
-    total = tracers * width
+def side_rows(fresh, east, solved, row, level, dims):
+    tracers, levels, width = dims
     for t in range(tracers):
         line = solved[pl.ds(t * levels + level, 1), :]
         fresh = fresh + jnp.where(row == t * width + side_of(east, width), line, 0.0)
-        at = total + int(east) * tracers + t
-        surface[at:at + 1, :] = sides[pl.ds(t * levels + level, 1), :]
     return fresh
 
 
@@ -268,24 +263,18 @@
     turned = jnp.sum(jnp.where(rows_lane // 2 == row, turned, 0.0), axis=0, keepdims=True)
     half_lanes[...] = side_lanes(edge_lanes[...] + spread[...] * turned, False, solved, lane, dims)
     level = surface_level(levels)
-    surface[total:, :] = jnp.zeros((surface.shape[0] - total, 128), f32)
     fresh = rows[...] + spread[pl.ds(level, 1), :] * flux
-    surface[:total, :] = side_rows(fresh, surface, False, from_west, solved, row, level, dims)
-
-
-def east_kernel(dims, mer_count, strips, nu, weights, mer_gain, half_lanes, half_surface, from_west, from_east, *rest):
+    surface[...] = side_rows(fresh, False, solved, row, level, dims)
+
+
+def east_kernel(dims, strips, nu, weights, half_lanes, half_surface, from_west, from_east, solved, surface, outside, *send_mer):
     tracers, levels, width = dims
     total = tracers * width
-    rounds = (len(rest) - 3) // 2
-    recv_mer, (solved, lanes, surface), send_mer = rest[:rounds], rest[rounds:rounds + 3], rest[rounds + 3:]
-    lane = lanes_of(levels)
-    terms = side_terms(from_east, True, strips, nu, dims)
-    terms.append(mer_gain[...] * mer_halo(recv_mer, levels, mer_count))
-    result = product(weights[...], jnp.concatenate(terms, axis=1))
+    lane = lanes_of(levels)
+    result = product(weights[...], jnp.concatenate(side_terms(from_east, True, strips, nu, dims), axis=1))
     for t in range(tracers):
         solved[t * levels:(t + 1) * levels, :] = result[:, t * 128:(t + 1) * 128]
-    lanes[...] = result[:, tracers * 128:]
-    packed = side_lanes(half_lanes[...] + lanes[...], True, solved, lane, dims)
+    packed = side_lanes(half_lanes[...], True, solved, lane, dims)
     place = lax.axis_index("mer")
     for r, ref in enumerate(send_mer):
         up = lax.rem(place + 1 + r, 2)
@@ -295,23 +284,65 @@
                 at = s * tracers + t
                 moved = pltpu.roll(part(cells, t, levels), 2 * at + 2 * up, 1)
                 message = jnp.where(lane == 2 * at + up, moved, message)
-        ref[...] = fold(message)
+        ref[:levels // 2, :] = fold(message)
+        ref[levels // 2:, :] = jnp.zeros((ref.shape[0] - levels // 2, 128), f32)
+    row = lax.broadcasted_iota(jnp.int32, (total, 128), 0)
+    level = surface_level(levels)
+    surface[...] = side_rows(half_surface[...], True, solved, row, level, dims)
+    outside[...] = jnp.zeros(outside.shape, f32)
+    for s, cells in enumerate((from_west, from_east)):
+        for t in range(tracers):
+            outside[s * tracers + t:s * tracers + t + 1, :] = cells[pl.ds(t * levels + level, 1), :]
+
+
+def meet_kernel(dims, mer_count, weights, own_mer, half_surface, *rest):
+    tracers, levels, width = dims
+    total = tracers * width
+    rounds = len(rest) - 3
+    recv_mer, (lanes, beyond, surface) = [ref[...] for ref in rest[:rounds]], rest[rounds:]
+    lane = lanes_of(levels)
+    edge = jnp.where(lane < 64, own_mer[...], 0.0)
+    gain = jnp.where(lane < 64, pltpu.roll(own_mer[...], 64, 1), 0.0)
+    here = gain * mer_halo(recv_mer, levels, mer_count)
+    there = edge * mer_halo([pltpu.roll(value, 64, 1) for value in recv_mer], levels, mer_count)
+    result = product(weights[...], jnp.concatenate([here, there], axis=1))
+    lanes[...] = result[:, :128]
+    beyond[...] = result[:, 128:]
     row = lax.broadcasted_iota(jnp.int32, (total, 128), 0)
     rows_lane = lax.broadcasted_iota(jnp.int32, (total, 128), 1)
-    level = surface_level(levels)
-    line = jnp.broadcast_to(lanes[pl.ds(level, 1), :], (total, 128))
+    line = jnp.broadcast_to(lanes[pl.ds(surface_level(levels), 1), :], (total, 128))
     line = jnp.take_along_axis(line, 2 * row + (rows_lane == 0).astype(jnp.int32), axis=1)
-    fresh = half_surface[:total, :] + jnp.where(jnp.logical_or(rows_lane == 127, rows_lane == 0), line, 0.0)
-    surface[total:, :] = half_surface[total:, :]
-    surface[:total, :] = side_rows(fresh, surface, True, from_east, solved, row, level, dims)
-
-
-def middle_kernel(dims, partial, strips, nu, weights, spread, west_solved, east_solved, lanes, incr, columns, guide, own, other, from_west, from_east, again, edges, flux, inner_gain, outer_gain, fresh):
+    rim = jnp.logical_or(rows_lane == 127, rows_lane == 0)
+    surface[...] = half_surface[...] + jnp.where(rim, line, 0.0)
+
+
+def again_kernel(dims, partial, strips, nu, weights, spread, west_solved, east_solved, lanes, incr, again, fresh):
+    tracers, levels, width = dims
+    lane = lanes_of(levels)
+    rim = jnp.logical_or(lane == 127, lane == 0)
+    for t in range(tracers):
+        for x in range(width):
+            j = t * width + x
+            value = part(partial, j, levels) + spread[...] * incr[j:j + 1, :]
+            value = value + jnp.where(rim, at_edges(lanes[...], j), 0.0)
+            if x in (0, width - 1):
+                value = value + part(west_solved if x == 0 else east_solved, t, levels)
+            fresh[j * levels:(j + 1) * levels, :] = value
+
+    def store(t, x, value):
+        again[pl.ds((t * width + x) * levels, levels), :] = value
+
+    column = lambda t, x: part(fresh, t * width + x, levels)
+    strip = lambda k, x: part(strips, k * width + x, levels)
+    interior(column, strip, nu, weights, store, dims)
+
+
+def sides_kernel(dims, columns, strips, nu, weights, guide, own, other, outside, other_outside, from_west, from_east, edges, flux, inner_gain, outer_gain):
     tracers, levels, width = dims
     total = tracers * width
     lane = lanes_of(levels)
-    flux[...] = increments(own[:total, :], other[:total, :], guide, tracers, width)
-    extra = increments(own[total:, :], other[total:, :], guide, tracers, 1)
+    flux[...] = increments(own[...], other[...], guide, tracers, width)
+    extra = increments(outside[...], other_outside[...], guide, tracers, 1)
     at_level = lax.broadcasted_iota(jnp.int32, (levels, 128), 0) == surface_level(levels)
     terms, gains = [], []
     first = jnp.zeros((levels, 128), f32)
@@ -339,31 +370,16 @@
     result = product(weights[...], result * jnp.concatenate(gains, axis=1))
     for i in range(2 * tracers):
         edges[i * levels:(i + 1) * levels, :] = result[:, i * 128:(i + 1) * 128]
-    rim = jnp.logical_or(lane == 127, lane == 0)
-    for t in range(tracers):
-        for x in range(width):
-            j = t * width + x
-            value = part(partial, j, levels) + spread[...] * incr[j:j + 1, :]
-            value = value + jnp.where(rim, at_edges(lanes[...], j), 0.0)
-            if x in (0, width - 1):
-                value = value + part(west_solved if x == 0 else east_solved, t, levels)
-            fresh[j * levels:(j + 1) * levels, :] = value
-
-    def store(t, x, value):
-        again[pl.ds((t * width + x) * levels, levels), :] = value
-
-    column = lambda t, x: part(fresh, t * width + x, levels)
-    strip = lambda k, x: part(strips, k * width + x, levels)
-    interior(column, strip, nu, weights, store, dims)
-
-
-def last_kernel(dims, mer_count, partial, edges, incr, weights, spread, mer_gain, inner_gain, outer_gain, *rest):
+
+
+def last_kernel(dims, mer_count, partial, edges, incr, weights, spread, own_mer, beyond, inner_gain, outer_gain, *rest):
     tracers, levels, width = dims
     rounds = len(rest) - 3
-    recv_mer, (out, done, sems) = rest[:rounds], rest[rounds:]
-    lane = lanes_of(levels)
-    halo = mer_halo(recv_mer, levels, mer_count)
-    lanes = product(weights[...], mer_gain[...] * halo)
+    recv_mer, (out, done, sems) = [unfold(ref[:levels // 2, :]) for ref in rest[:rounds]], rest[rounds:]
+    lane = lanes_of(levels)
+    halo = mer_halo(recv_mer, levels, mer_count) + beyond[...]
+    gain = jnp.where(lane < 64, pltpu.roll(own_mer[...], 64, 1), 0.0)
+    lanes = product(weights[...], gain * halo)
     corner = jnp.zeros((levels, 128), f32)
     for value, north, inside in mer_sides(recv_mer, mer_count):
         for s in range(2):
@@ -394,7 +410,7 @@
 HB = pl.BlockSpec(memory_space=pltpu.HBM)
 
 
-def call(body, name, in_specs, out_shape, flops, out_specs=None, scratch=()):
+def call(body, name, in_specs, out_shape, flops, out_specs=None, scratch=(), touched=2 << 20):
     many = isinstance(out_shape, list)
     return pl.pallas_call(
         body,
@@ -403,7 +419,7 @@
         out_specs=out_specs or ([VM] * len(out_shape) if many else VM),
         scratch_shapes=scratch,
         name=name,
-        cost_estimate=pl.CostEstimate(flops=flops, bytes_accessed=2 << 20, transcendentals=0),
+        cost_estimate=pl.CostEstimate(flops=flops, bytes_accessed=touched, transcendentals=0),
         compiler_params=pltpu.CompilerParams(vmem_limit_bytes=32 * 1024 * 1024),
     )
 
@@ -417,7 +433,7 @@
     shape = lambda rows, dtype=f32: jax.ShapeDtypeStruct((rows, wide), dtype)
     message = shape((2 * tracers + 2) * levels)
     packed = shape(levels)
-    folded = shape(levels // 2)
+    folded = shape(levels // 2 + 8)
     kept = shape(tracers * size)
     halved = shape(tracers * levels)
     sided = shape(2 * tracers * levels)
@@ -426,8 +442,10 @@
         return [lax.ppermute(piece, "mer", pairs(mer_count, r == 1)) for r, piece in enumerate(pieces)]
 
     def shift_zonal(piece, ahead):
-        moved = lax.ppermute(piece, "zon", ring(zon_count, ahead))
-        return moved.astype(f32) * (1.0 / SCALE)
+        return lax.ppermute(piece, "zon", ring(zon_count, ahead))
+
+    def widen(piece):
+        return piece.astype(f32) * (1.0 / SCALE)
 
     def swap_fluid(piece):
         return lax.ppermute(piece, "fluid", [(0, 1), (1, 0)])
@@ -441,37 +459,44 @@
                  pltpu.SemaphoreType.DMA((5 * tracers + 2 + len(params),))],
     )(*in_hbm)
     east_bound, west_bound = lax.optimization_barrier(((east_bound * SCALE).astype(jnp.float16), (west_bound * SCALE).astype(jnp.float16)))
-    from_west = shift_zonal(east_bound, 1)
-    columns, send_mer, nu, weights, spread, guide = call(
-        functools.partial(lanes_kernel, dims), "lanes", [VM] * 6,
-        [kept, folded, shape(tracers * levels), jax.ShapeDtypeStruct((levels, 3 * levels), bf16), packed, shape(8)], 1 << 20,
-    )(state.reshape(tracers * size, wide), *params)
-    recv_mer = swap_mer([send_mer] * rounds)
+    from_west = widen(shift_zonal(east_bound, 1))
+    columns, own_mer, nu, weights, spread, guide = call(
+        functools.partial(lanes_kernel, dims), "lanes", [VM] * 7,
+        [kept, packed, shape(tracers * levels), jax.ShapeDtypeStruct((levels, 3 * levels), bf16), packed, shape(8)], 1 << 20,
+    )(state.reshape(tracers * size, wide), frame, *params)
+    recv_mer = swap_mer([own_mer] * rounds)
     other = swap_fluid(surface)
     from_east = shift_zonal(west_bound, -1)
-    partial, strips, mer_gain, edge_lanes, rows = call(
-        functools.partial(inner_kernel, dims), "inner", [VM] * 4, [kept, shape(2 * size), packed, packed, shape(total)], 1 << 30,
+    partial, strips, edge_lanes, rows = call(
+        functools.partial(inner_kernel, dims), "inner", [VM] * 4, [kept, shape(2 * size), packed, shape(total)], 1 << 30,
     )(columns, frame, nu, weights)
     west_solved, incr, half_lanes, half_surface = call(
         functools.partial(west_kernel, dims), "west", [VM] * 10,
-        [halved, shape(total), packed, shape(total + 8)], 1 << 33,
+        [halved, shape(total), packed, shape(total)], 1 << 33,
     )(strips, nu, weights, spread, edge_lanes, rows, guide, surface, other, from_west)
-    east_solved, lanes, fresh_surface, *send_mer = call(
-        functools.partial(east_kernel, dims, mer_count), "east", [VM] * (8 + rounds),
-        [halved, packed, shape(total + 8)] + [folded] * rounds, 1 << 26,
-    )(strips, nu, weights, mer_gain, half_lanes, half_surface, from_west, from_east, *recv_mer)
-    recv_mer = swap_mer(send_mer)
+    from_east, half_lanes = lax.optimization_barrier((from_east, half_lanes))
+    from_east = widen(from_east)
+    east_solved, half_surface, outside, *send_mer = call(
+        functools.partial(east_kernel, dims), "east", [VM] * 7, [halved, shape(total), shape(8)] + [folded] * rounds, 1 << 26,
+    )(strips, nu, weights, half_lanes, half_surface, from_west, from_east)
+    recv_again = swap_mer(send_mer)
+    other_outside = swap_fluid(outside)
+    lanes, beyond, fresh_surface = call(
+        functools.partial(meet_kernel, dims, mer_count), "meet", [VM] * (3 + rounds), [packed, packed, shape(total)], 1 << 33,
+    )(weights, own_mer, half_surface, *recv_mer)
     fresh_other = swap_fluid(fresh_surface)
-    again, edges, flux, inner_gain, outer_gain = call(
-        functools.partial(middle_kernel, dims), "middle", [VM] * 15,
-        [kept, sided, shape(total), packed, packed], 1 << 30, scratch=[pltpu.VMEM((tracers * size, wide), f32)],
-    )(partial, strips, nu, weights, spread, west_solved, east_solved, lanes, incr, columns, guide, fresh_surface, fresh_other, from_west, from_east)
+    again = call(
+        functools.partial(again_kernel, dims), "again", [VM] * 9, kept, 1 << 10, touched=1 << 10, scratch=[pltpu.VMEM((tracers * size, wide), f32)],
+    )(partial, strips, nu, weights, spread, west_solved, east_solved, lanes, incr)
+    edges, flux, inner_gain, outer_gain = call(
+        functools.partial(sides_kernel, dims), "sides", [VM] * 11, [sided, shape(total), packed, packed], 1 << 10, touched=1 << 10,
+    )(columns, strips, nu, weights, guide, fresh_surface, fresh_other, outside, other_outside, from_west, from_east)
     done = call(
-        functools.partial(last_kernel, dims, mer_count), "last", [VM] * (8 + rounds),
+        functools.partial(last_kernel, dims, mer_count), "last", [VM] * (9 + rounds),
         jax.ShapeDtypeStruct(state.shape[1:], f32), 1 << 26,
         out_specs=pl.BlockSpec(memory_space=pl.ANY),
         scratch=[pltpu.VMEM((total, levels, wide), f32), pltpu.SemaphoreType.DMA((total,))],
-    )(again, edges, flux, weights, spread, mer_gain, inner_gain, outer_gain, *recv_mer)
+    )(again, edges, flux, weights, spread, own_mer, beyond, inner_gain, outer_gain, *recv_again)
     return done[None]
 
 

time: 18.3 us -> 18.2 us (level)
  waiting for transfers between devices: 0.68 us -> 0.02 us
  Pallas kernels: 7.68 us -> 8.07 us
  starting transfers between devices: 9.6 us -> 9.8 us
    pallas_call x4 -> x6, Pallas kernels: 4.25 us -> 4.96 us  [the longest x1 1.82 us: on_device(): call(functools.partial(last_kernel, dims, mer_count), 'last', [VM] * (9 +...]
    ppermute x2, waiting for transfers between devices: 0.67 us -> 0.01 us  [swap_mer(): lax.ppermute(piece, 'mer', pairs(mer_count, r == 1))]
    ppermute x2, starting transfers between devices: 5.66 us -> 6.17 us  [shift_zonal(): return lax.ppermute(piece, 'zon', ring(zon_count, ahead))]
    pallas_call x1, Pallas kernels: 1.8 us -> 1.49 us  [on_device(): call(functools.partial(inner_kernel, dims), 'inner', [VM] * 4, [kept, sha...]
    ppermute x2, starting transfers between devices: 3.36 us -> 3.11 us  [swap_mer(): lax.ppermute(piece, 'mer', pairs(mer_count, r == 1))]
    ppermute x2 -> x3, starting transfers between devices: 0.57 us -> 0.52 us  [swap_fluid(): return lax.ppermute(piece, 'fluid', [(0, 1), (1, 0)])]
  transfers between devices with their start and end apart: 6 -> 7, of which waited for: 1 -> 0; matrix products, arithmetic and copies ran while one was open for 0% -> 0% of each run, Pallas kernels for 23% -> 27%
where the time goes in v9:
time: 18.2 us; the launch traced here: 18.1 us
  starting transfers between devices  9.8 us (54%)
  Pallas kernels  8.07 us (44%)
    ppermute x2, starting transfers between devices, shift_zonal(): return lax.ppermute(piece, 'zon', ring(zon_count, ahead))  6.17 us
    ppermute x2, starting transfers between devices, swap_mer(): lax.ppermute(piece, 'mer', pairs(mer_count, r == 1))  3.11 us
    pallas_call x1, Pallas kernels, on_device(): call(functools.partial(last_kernel, dims, mer_count), 'last', [VM] * (9 +...  1.82 us
    pallas_call x1, Pallas kernels, on_device(): call(functools.partial(inner_kernel, dims), 'inner', [VM] * 4, [kept, sha...  1.49 us
    pallas_call x1, Pallas kernels, on_device(): call(functools.partial(pack_kernel, dims), 'pack', [HB] * len(in_hbm), [m...  1.38 us
    pallas_call x1, Pallas kernels, on_device(): call(functools.partial(again_kernel, dims), 'again', [VM] * 9, kept, 1 <<...  1.23 us
    pallas_call x1, Pallas kernels, on_device(): call(functools.partial(lanes_kernel, dims), 'lanes', [VM] * 7, [kept, pac...  0.75 us
    ppermute x3, starting transfers between devices, swap_fluid(): return lax.ppermute(piece, 'fluid', [(0, 1), (1, 0)])  0.52 us
  transfers between devices with their start and end apart: 7, of which 0 were waited for; matrix products, arithmetic and copies ran while one was open for 0% of the time, Pallas kernels for 27%

profile of v9, /device:TPU:0, one launch (start us, length us, event | category | flops | bytes accessed | tf_op | source)
XLA Modules:
  0.0 18.1 jit_solution(1151323608184124599)
XLA Ops:
  0.0 0.0 copy-start
  0.0 1.4 %pack.1 = (f32[384,128]{1,0:T(8,128)S(1)}, f32[384,128]{1,0:T(8,128)S(1)}, f32[32,128]{1,0:T(8,128)S(1)}, f32[2048,128]{1,0:T(8,128)S(1)}, f32[2,64]{1,0:T(2,128...) custom-call(f32[2,64,16,128]{3,2,1,0:T(8,128)} %bitcast.8, ...), custom_call_target="tpu_custom_call" | custom-call | flops 1048576 | bytes 2097152 | tf_op jit(solution)/shard_map/pack/pallas_call | solution.py:455
  1.4 3.0 %collective-permute-start.1 = (f16[384,128]{1,0:T(8,128)(2,1)S(1)}, f16[384,128]{1,0:T(8,128)(2,1)S(1)}, u32[]{:S(2)}, u32[]{:S(2)}) collective-permute-start(f16[384,128]{1,0:T(8,128)(2,1)S(1)} %get-tuple-element.61), channel_id=1, source_target_pairs={{0,2},{2,4},{4,6},{6,8},{8,10},{10,12},{12,14},{14,0},{1,3},{3,5},... | collective-permute-start | bytes 294920 | tf_op jit(solution)/shard_map/ppermute | solution.py:445
  4.4 0.0 collective-permute-start
  4.4 3.2 %collective-permute-start.2 = (f16[384,128]{1,0:T(8,128)(2,1)S(1)}, f16[384,128]{1,0:T(8,128)(2,1)S(1)}, u32[]{:S(2)}, u32[]{:S(2)}) collective-permute-start(f16[384,128]{1,0:T(8,128)(2,1)S(1)} %get-tuple-element.63), channel_id=1, source_target_pairs={{0,14},{2,0},{4,2},{6,4},{8,6},{10,8},{12,10},{14,12},{1,15},{3,1}... | collective-permute-start | bytes 294920 | tf_op jit(solution)/shard_map/ppermute | solution.py:445
  7.6 0.0 copy-done
  7.6 0.8 %lanes.1 = (f32[2048,128]{1,0:T(8,128)S(1)}, f32[64,128]{1,0:T(8,128)S(1)}, f32[128,128]{1,0:T(8,128)S(1)}, bf16[64,192]{1,0:T(8,128)(2,1)S(1)}, f32[64,128]{1,0:T(8,128)S(1)}, /*index=5*/f32[8,128]{1,0:T(8,128)S(1)}) custom-call(f32[2048,128]{1,0:T(8,128)S(1)} %bitcast.9, f32[2048,128]{1,0:T(8,128)S(1)} %get-tuple-element.43.frame, ...), custom_call_target="tpu_custom_call" | custom-call | flops 1048576 | bytes 2097152 | tf_op jit(solution)/shard_map/lanes/pallas_call | solution.py:463
  8.4 1.6 %collective-permute-start.3 = (f32[64,128]{1,0:T(8,128)S(1)}, f32[64,128]{1,0:T(8,128)S(1)}, u32[]{:S(2)}, u32[]{:S(2)}) collective-permute-start(f32[64,128]{1,0:T(8,128)S(1)} %get-tuple-element.69.own_mer), channel_id=1, source_target_pairs={{0,1},{1,0},{2,3},{3,2},{4,5},{5,4},{6,7},{7,6},{8,9},{9,8},{10,11... | collective-permute-start | bytes 98312 | tf_op jit(solution)/shard_map/ppermute | solution.py:442
  10.0 1.5 %inner.1 = (f32[2048,128]{1,0:T(8,128)S(1)}, f32[2048,128]{1,0:T(8,128)S(1)}, f32[64,128]{1,0:T(8,128)S(1)}, f32[32,128]{1,0:T(8,128)S(1)}) custom-call(f32[2048,128]{1,0:T(8,128)S(1)} %get-tuple-element.49.columns, f32[2048,128]{1,0:T(8,128)S(1)} %get-tuple-element.43.frame, f32[128,128]{1,0:T(8,128)S(1)} %get-tuple-element.50.nu, ...), custom_call_target="tpu_custom_call" | custom-call | flops 1073741824 | bytes 2097152 | tf_op jit(solution)/shard_map/inner/pallas_call | solution.py:470
  11.5 0.0 collective-permute-done.1
  11.6 0.0 collective-permute-done.other
  11.6 0.2 %west.1 = (f32[128,128]{1,0:T(8,128)S(1)}, f32[32,128]{1,0:T(8,128)S(1)}, f32[64,128]{1,0:T(8,128)S(1)}, f32[32,128]{1,0:T(8,128)S(1)}) custom-call(f32[2048,128]{1,0:T(8,128)S(1)} %get-tuple-element.53.strips, f32[128,128]{1,0:T(8,128)S(1)} %get-tuple-element.50.nu, bf16[64,192]{1,0:T(8,128)(2,1)S(1)} %get-tuple-element.51.weights, ...), custom_call_target="tpu_custom_call" | custom-call | flops 8589934592 | bytes 2097152 | tf_op jit(solution)/shard_map/west/pallas_call | solution.py:473
  11.8 0.0 collective-permute-done.2
  11.9 0.3 %east.1 = (f32[128,128]{1,0:T(8,128)S(1)}, f32[32,128]{1,0:T(8,128)S(1)}, f32[8,128]{1,0:T(8,128)S(1)}, f32[40,128]{1,0:T(8,128)S(1)}) custom-call(f32[2048,128]{1,0:T(8,128)S(1)} %get-tuple-element.53.strips, f32[128,128]{1,0:T(8,128)S(1)} %get-tuple-element.50.nu, bf16[64,192]{1,0:T(8,128)(2,1)S(1)} %get-tuple-element.51.weights, ...), custom_call_target="tpu_custom_call" | custom-call | flops 67108864 | bytes 2097152 | tf_op jit(solution)/shard_map/east/pallas_call | solution.py:479
  12.1 1.5 %collective-permute-start.6 = (f32[40,128]{1,0:T(8,128)S(1)}, f32[40,128]{1,0:T(8,128)S(1)}, u32[]{:S(2)}, u32[]{:S(2)}) collective-permute-start(f32[40,128]{1,0:T(8,128)S(1)} %get-tuple-element.80), channel_id=1, source_target_pairs={{0,1},{1,0},{2,3},{3,2},{4,5},{5,4},{6,7},{7,6},{8,9},{9,8},{10,11... | collective-permute-start | bytes 61448 | tf_op jit(solution)/shard_map/ppermute | solution.py:442
  13.6 0.0 collective-permute-done.3.rest_0_
  13.6 0.4 %meet.1 = (f32[64,128]{1,0:T(8,128)S(1)}, f32[64,128]{1,0:T(8,128)S(1)}, f32[32,128]{1,0:T(8,128)S(1)}) custom-call(bf16[64,192]{1,0:T(8,128)(2,1)S(1)} %get-tuple-element.51.weights, f32[64,128]{1,0:T(8,128)S(1)} %get-tuple-element.69.own_mer, f32[32,128]{1,0:T(8,128)S(1)} %get-tuple-element.70.half_surface, f32[64,128]{1,0:T(8,128)S(1)} %collective-permute-done.3.rest_0_), custom_call_target="tpu_custom_call" | custom-call | flops 8589934592 | bytes 2097152 | tf_op jit(solution)/shard_map/meet/pallas_call | solution.py:484
  14.0 0.0 collective-permute-start.4
  14.0 0.5 %collective-permute-start.5 = (f32[8,128]{1,0:T(8,128)S(1)}, f32[8,128]{1,0:T(8,128)S(1)}, u32[]{:S(2)}, u32[]{:S(2)}) collective-permute-start(f32[8,128]{1,0:T(8,128)S(1)} %get-tuple-element.74.outside), channel_id=1, source_target_pairs={{0,16},{16,0},{1,17},{17,1},{2,18},{18,2},{3,19},{19,3},{4,20},{20... | collective-permute-start | bytes 12296 | tf_op jit(solution)/shard_map/ppermute | solution.py:451
  14.5 1.2 %again.1.partial = f32[2048,128]{1,0:T(8,128)S(1)} custom-call(f32[2048,128]{1,0:T(8,128)S(1)} %get-tuple-element.52.partial, f32[2048,128]{1,0:T(8,128)S(1)} %get-tuple-element.53.strips, f32[128,128]{1,0:T(8,128)S(1)} %get-tuple-element.50.nu, bf16[64,192]{1,0:T(8,128)(2,1)S(1)} %get-tuple-element.51.weights, f32[64,128]{1,0:T(8,128)S(1)} %get-tuple-element.54.spread, ...), custom_call_target="tpu_custom_call" | custom-call | flops 1024 | bytes 1024 | tf_op jit(solution)/shard_map/again/pallas_call | solution.py:488
  15.7 0.0 collective-permute-done.5.other_outside
  15.7 0.0 collective-permute-done.4.other
  15.7 0.5 %sides.1 = (f32[256,128]{1,0:T(8,128)S(1)}, f32[32,128]{1,0:T(8,128)S(1)}, f32[64,128]{1,0:T(8,128)S(1)}, f32[64,128]{1,0:T(8,128)S(1)}) custom-call(f32[2048,128]{1,0:T(8,128)S(1)} %get-tuple-element.49.columns, f32[2048,128]{1,0:T(8,128)S(1)} %get-tuple-element.53.strips, f32[128,128]{1,0:T(8,128)S(1)} %get-tuple-element.50.nu, ...), custom_call_target="tpu_custom_call" | custom-call | flops 1024 | bytes 1024 | tf_op jit(solution)/shard_map/sides/pallas_call | solution.py:491
  16.3 0.0 collective-permute-done.6.rest_0_
  16.3 1.8 %last.1 = f32[2,64,16,128]{3,2,1,0:T(8,128)} custom-call(f32[2048,128]{1,0:T(8,128)S(1)} %again.1.partial, f32[256,128]{1,0:T(8,128)S(1)} %get-tuple-element.75.edges, f32[32,128]{1,0:T(8,128)S(1)} %get-tuple-element.76.incr, bf16[64,192]{1,0:T(8,128)(2,1)S(1)} %get-tuple-element.51.weights, f32[64,128]{1,0:T(8,128)S(1)} %get-tuple-element.54.spread, ...), custom_call_target="tpu_custom_call" | custom-call | flops 67108864 | bytes 2097152 | tf_op jit(solution)/shard_map/last/pallas_call | solution.py:494
  (3 shorter events, 0.1 us)
Async XLA Ops:
  0.0 7.6 %copy-start = (f32[1,2,64,16,128]{4,3,2,1,0:T(8,128)S(1)}, f32[1,2,64,16,128]{4,3,2,1,0:T(8,128)}, u32[]{:S(2)}) copy-start(f32[1,2,64,16,128]{4,3,2,1,0:T(8,128)} %param.7) | copy-start | bytes 3145732
  1.4 10.1 %collective-permute-start.1 = (f16[384,128]{1,0:T(8,128)(2,1)S(1)}, f16[384,128]{1,0:T(8,128)(2,1)S(1)}, u32[]{:S(2)}, u32[]{:S(2)}) collective-permute-start(f16[384,128]{1,0:T(8,128)(2,1)S(1)} %get-tuple-element.61), channel_id=1, source_target_pairs={{0,2},{2,4},{4,6},{6,8},{8,10},{10,12},{12,14},{14,0},{1,3},{3,5},... | collective-permute-start | bytes 294920 | tf_op jit(solution)/shard_map/ppermute | solution.py:445
  4.4 7.1 %collective-permute-start = (f32[32,128]{1,0:T(8,128)S(1)}, f32[32,128]{1,0:T(8,128)S(1)}, u32[]{:S(2)}, u32[]{:S(2)}) collective-permute-start(f32[32,128]{1,0:T(8,128)S(1)} %get-tuple-element.58.own), channel_id=1, source_target_pairs={{0,16},{16,0},{1,17},{17,1},{2,18},{18,2},{3,19},{19,3},{4,20},{20... | collective-permute-start | bytes 49160 | tf_op jit(solution)/shard_map/ppermute | solution.py:451
  4.4 7.4 %collective-permute-start.2 = (f16[384,128]{1,0:T(8,128)(2,1)S(1)}, f16[384,128]{1,0:T(8,128)(2,1)S(1)}, u32[]{:S(2)}, u32[]{:S(2)}) collective-permute-start(f16[384,128]{1,0:T(8,128)(2,1)S(1)} %get-tuple-element.63), channel_id=1, source_target_pairs={{0,14},{2,0},{4,2},{6,4},{8,6},{10,8},{12,10},{14,12},{1,15},{3,1}... | collective-permute-start | bytes 294920 | tf_op jit(solution)/shard_map/ppermute | solution.py:445
  8.4 5.2 %collective-permute-start.3 = (f32[64,128]{1,0:T(8,128)S(1)}, f32[64,128]{1,0:T(8,128)S(1)}, u32[]{:S(2)}, u32[]{:S(2)}) collective-permute-start(f32[64,128]{1,0:T(8,128)S(1)} %get-tuple-element.69.own_mer), channel_id=1, source_target_pairs={{0,1},{1,0},{2,3},{3,2},{4,5},{5,4},{6,7},{7,6},{8,9},{9,8},{10,11... | collective-permute-start | bytes 98312 | tf_op jit(solution)/shard_map/ppermute | solution.py:442
  12.1 4.1 %collective-permute-start.6 = (f32[40,128]{1,0:T(8,128)S(1)}, f32[40,128]{1,0:T(8,128)S(1)}, u32[]{:S(2)}, u32[]{:S(2)}) collective-permute-start(f32[40,128]{1,0:T(8,128)S(1)} %get-tuple-element.80), channel_id=1, source_target_pairs={{0,1},{1,0},{2,3},{3,2},{4,5},{5,4},{6,7},{7,6},{8,9},{9,8},{10,11... | collective-permute-start | bytes 61448 | tf_op jit(solution)/shard_map/ppermute | solution.py:442
  14.0 1.8 %collective-permute-start.4 = (f32[32,128]{1,0:T(8,128)S(1)}, f32[32,128]{1,0:T(8,128)S(1)}, u32[]{:S(2)}, u32[]{:S(2)}) collective-permute-start(f32[32,128]{1,0:T(8,128)S(1)} %get-tuple-element.73.own), channel_id=1, source_target_pairs={{0,16},{16,0},{1,17},{17,1},{2,18},{18,2},{3,19},{19,3},{4,20},{20... | collective-permute-start | bytes 49160 | tf_op jit(solution)/shard_map/ppermute | solution.py:451
  14.0 1.7 %collective-permute-start.5 = (f32[8,128]{1,0:T(8,128)S(1)}, f32[8,128]{1,0:T(8,128)S(1)}, u32[]{:S(2)}, u32[]{:S(2)}) collective-permute-start(f32[8,128]{1,0:T(8,128)S(1)} %get-tuple-element.74.outside), channel_id=1, source_target_pairs={{0,16},{16,0},{1,17},{17,1},{2,18},{18,2},{3,19},{19,3},{4,20},{20... | collective-permute-start | bytes 12296 | tf_op jit(solution)/shard_map/ppermute | solution.py:451

commit v10 on v9

--- a/solution.py
+++ b/solution.py
@@ -267,7 +267,7 @@
     surface[...] = side_rows(fresh, False, solved, row, level, dims)
 
 
-def east_kernel(dims, strips, nu, weights, half_lanes, half_surface, from_west, from_east, solved, surface, outside, *send_mer):
+def east_kernel(dims, strips, nu, weights, half_lanes, half_surface, from_west, from_east, solved, surface, *send_mer):
     tracers, levels, width = dims
     total = tracers * width
     lane = lanes_of(levels)
@@ -287,15 +287,10 @@
         ref[:levels // 2, :] = fold(message)
         ref[levels // 2:, :] = jnp.zeros((ref.shape[0] - levels // 2, 128), f32)
     row = lax.broadcasted_iota(jnp.int32, (total, 128), 0)
-    level = surface_level(levels)
-    surface[...] = side_rows(half_surface[...], True, solved, row, level, dims)
-    outside[...] = jnp.zeros(outside.shape, f32)
-    for s, cells in enumerate((from_west, from_east)):
-        for t in range(tracers):
-            outside[s * tracers + t:s * tracers + t + 1, :] = cells[pl.ds(t * levels + level, 1), :]
-
-
-def meet_kernel(dims, mer_count, weights, own_mer, half_surface, *rest):
+    surface[...] = side_rows(half_surface[...], True, solved, row, surface_level(levels), dims)
+
+
+def meet_kernel(dims, mer_count, weights, own_mer, half_surface, from_west, from_east, *rest):
     tracers, levels, width = dims
     total = tracers * width
     rounds = len(rest) - 3
@@ -313,7 +308,13 @@
     line = jnp.broadcast_to(lanes[pl.ds(surface_level(levels), 1), :], (total, 128))
     line = jnp.take_along_axis(line, 2 * row + (rows_lane == 0).astype(jnp.int32), axis=1)
     rim = jnp.logical_or(rows_lane == 127, rows_lane == 0)
-    surface[...] = half_surface[...] + jnp.where(rim, line, 0.0)
+    surface[:total, :] = half_surface[...] + jnp.where(rim, line, 0.0)
+    surface[total:, :] = jnp.zeros((surface.shape[0] - total, 128), f32)
+    level = surface_level(levels)
+    for s, cells in enumerate((from_west, from_east)):
+        for t in range(tracers):
+            at = total + s * tracers + t
+            surface[at:at + 1, :] = cells[pl.ds(t * levels + level, 1), :]
 
 
 def again_kernel(dims, partial, strips, nu, weights, spread, west_solved, east_solved, lanes, incr, again, fresh):
@@ -337,12 +338,12 @@
     interior(column, strip, nu, weights, store, dims)
 
 
-def sides_kernel(dims, columns, strips, nu, weights, guide, own, other, outside, other_outside, from_west, from_east, edges, flux, inner_gain, outer_gain):
+def sides_kernel(dims, columns, strips, nu, weights, guide, own, other, from_west, from_east, edges, flux, inner_gain, outer_gain):
     tracers, levels, width = dims
     total = tracers * width
     lane = lanes_of(levels)
-    flux[...] = increments(own[...], other[...], guide, tracers, width)
-    extra = increments(outside[...], other_outside[...], guide, tracers, 1)
+    flux[...] = increments(own[:total, :], other[:total, :], guide, tracers, width)
+    extra = increments(own[total:, :], other[total:, :], guide, tracers, 1)
     at_level = lax.broadcasted_iota(jnp.int32, (levels, 128), 0) == surface_level(levels)
     terms, gains = [], []
     first = jnp.zeros((levels, 128), f32)
@@ -433,7 +434,7 @@
     shape = lambda rows, dtype=f32: jax.ShapeDtypeStruct((rows, wide), dtype)
     message = shape((2 * tracers + 2) * levels)
     packed = shape(levels)
-    folded = shape(levels // 2 + 8)
+    folded = shape(levels // 2 + 16)
     kept = shape(tracers * size)
     halved = shape(tracers * levels)
     sided = shape(2 * tracers * levels)
@@ -476,21 +477,20 @@
     )(strips, nu, weights, spread, edge_lanes, rows, guide, surface, other, from_west)
     from_east, half_lanes = lax.optimization_barrier((from_east, half_lanes))
     from_east = widen(from_east)
-    east_solved, half_surface, outside, *send_mer = call(
-        functools.partial(east_kernel, dims), "east", [VM] * 7, [halved, shape(total), shape(8)] + [folded] * rounds, 1 << 26,
+    east_solved, half_surface, *send_mer = call(
+        functools.partial(east_kernel, dims), "east", [VM] * 7, [halved, shape(total)] + [folded] * rounds, 1 << 26,
     )(strips, nu, weights, half_lanes, half_surface, from_west, from_east)
     recv_again = swap_mer(send_mer)
-    other_outside = swap_fluid(outside)
     lanes, beyond, fresh_surface = call(
-        functools.partial(meet_kernel, dims, mer_count), "meet", [VM] * (3 + rounds), [packed, packed, shape(total)], 1 << 33,
-    )(weights, own_mer, half_surface, *recv_mer)
+        functools.partial(meet_kernel, dims, mer_count), "meet", [VM] * (5 + rounds), [packed, packed, shape(total + 8)], 1 << 33,
+    )(weights, own_mer, half_surface, from_west, from_east, *recv_mer)
     fresh_other = swap_fluid(fresh_surface)
     again = call(
         functools.partial(again_kernel, dims), "again", [VM] * 9, kept, 1 << 10, touched=1 << 10, scratch=[pltpu.VMEM((tracers * size, wide), f32)],
     )(partial, strips, nu, weights, spread, west_solved, east_solved, lanes, incr)
     edges, flux, inner_gain, outer_gain = call(
-        functools.partial(sides_kernel, dims), "sides", [VM] * 11, [sided, shape(total), packed, packed], 1 << 10, touched=1 << 10,
-    )(columns, strips, nu, weights, guide, fresh_surface, fresh_other, outside, other_outside, from_west, from_east)
+        functools.partial(sides_kernel, dims), "sides", [VM] * 9, [sided, shape(total), packed, packed], 1 << 10, touched=1 << 10,
+    )(columns, strips, nu, weights, guide, fresh_surface, fresh_other, from_west, from_east)
     done = call(
         functools.partial(last_kernel, dims, mer_count), "last", [VM] * (9 + rounds),
         jax.ShapeDtypeStruct(state.shape[1:], f32), 1 << 26,

time: 18.2 us -> 18 us (0.989)
  starting transfers between devices: 9.8 us -> 9.3 us
  waiting for transfers between devices: 0.02 us -> 0.27 us
    ppermute x3 -> x2, starting transfers between devices: 0.52 us -> 0.02 us  [swap_fluid(): return lax.ppermute(piece, 'fluid', [(0, 1), (1, 0)])]
    ppermute x2, waiting for transfers between devices: 0.01 us -> 0.26 us  [swap_mer(): lax.ppermute(piece, 'mer', pairs(mer_count, r == 1))]
  transfers between devices with their start and end apart: 7 -> 6, of which waited for: 0 -> 1; matrix products, arithmetic and copies ran while one was open for 0% -> 0% of each run, Pallas kernels for 27% -> 27%
where the time goes in v10:
time: 18 us; the launch traced here: 17.8 us
  starting transfers between devices  9.3 us (52%)
  Pallas kernels  8.07 us (45%)
  waiting for transfers between devices  0.27 us (2%)
    ppermute x2, starting transfers between devices, shift_zonal(): return lax.ppermute(piece, 'zon', ring(zon_count, ahead))  6.17 us
    ppermute x2, starting transfers between devices, swap_mer(): lax.ppermute(piece, 'mer', pairs(mer_count, r == 1))  3.11 us
    pallas_call x1, Pallas kernels, on_device(): call(functools.partial(last_kernel, dims, mer_count), 'last', [VM] * (9 +...  1.81 us
    pallas_call x1, Pallas kernels, on_device(): call(functools.partial(inner_kernel, dims), 'inner', [VM] * 4, [kept, sha...  1.49 us
    pallas_call x1, Pallas kernels, on_device(): call(functools.partial(pack_kernel, dims), 'pack', [HB] * len(in_hbm), [m...  1.38 us
    pallas_call x1, Pallas kernels, on_device(): call(functools.partial(again_kernel, dims), 'again', [VM] * 9, kept, 1 <<...  1.22 us
    pallas_call x1, Pallas kernels, on_device(): call(functools.partial(lanes_kernel, dims), 'lanes', [VM] * 7, [kept, pac...  0.75 us
    pallas_call x1, Pallas kernels, on_device(): call(functools.partial(sides_kernel, dims), 'sides', [VM] * 9, [sided, sh...  0.52 us
  transfers between devices with their start and end apart: 6, of which 1 were waited for; matrix products, arithmetic and copies ran while one was open for 0% of the time, Pallas kernels for 27%

profile of v10, /device:TPU:0, one launch (start us, length us, event | category | flops | bytes accessed | tf_op | source)
XLA Modules:
  0.0 17.8 jit_solution(8310135134162208226)
XLA Ops:
  0.0 0.0 copy-start
  0.0 1.4 %pack.1 = (f32[384,128]{1,0:T(8,128)S(1)}, f32[384,128]{1,0:T(8,128)S(1)}, f32[32,128]{1,0:T(8,128)S(1)}, f32[2048,128]{1,0:T(8,128)S(1)}, f32[2,64]{1,0:T(2,128...) custom-call(f32[2,64,16,128]{3,2,1,0:T(8,128)} %bitcast.8, ...), custom_call_target="tpu_custom_call" | custom-call | flops 1048576 | bytes 2097152 | tf_op jit(solution)/shard_map/pack/pallas_call | solution.py:456
  1.4 3.0 %collective-permute-start.1 = (f16[384,128]{1,0:T(8,128)(2,1)S(1)}, f16[384,128]{1,0:T(8,128)(2,1)S(1)}, u32[]{:S(2)}, u32[]{:S(2)}) collective-permute-start(f16[384,128]{1,0:T(8,128)(2,1)S(1)} %get-tuple-element.60), channel_id=1, source_target_pairs={{0,2},{2,4},{4,6},{6,8},{8,10},{10,12},{12,14},{14,0},{1,3},{3,5},... | collective-permute-start | bytes 294920 | tf_op jit(solution)/shard_map/ppermute | solution.py:446
  4.4 0.0 collective-permute-start
  4.4 3.2 %collective-permute-start.2 = (f16[384,128]{1,0:T(8,128)(2,1)S(1)}, f16[384,128]{1,0:T(8,128)(2,1)S(1)}, u32[]{:S(2)}, u32[]{:S(2)}) collective-permute-start(f16[384,128]{1,0:T(8,128)(2,1)S(1)} %get-tuple-element.62), channel_id=1, source_target_pairs={{0,14},{2,0},{4,2},{6,4},{8,6},{10,8},{12,10},{14,12},{1,15},{3,1}... | collective-permute-start | bytes 294920 | tf_op jit(solution)/shard_map/ppermute | solution.py:446
  7.6 0.0 copy-done
  7.6 0.8 %lanes.1 = (f32[2048,128]{1,0:T(8,128)S(1)}, f32[64,128]{1,0:T(8,128)S(1)}, f32[128,128]{1,0:T(8,128)S(1)}, bf16[64,192]{1,0:T(8,128)(2,1)S(1)}, f32[64,128]{1,0:T(8,128)S(1)}, /*index=5*/f32[8,128]{1,0:T(8,128)S(1)}) custom-call(f32[2048,128]{1,0:T(8,128)S(1)} %bitcast.9, f32[2048,128]{1,0:T(8,128)S(1)} %get-tuple-element.42.frame, ...), custom_call_target="tpu_custom_call" | custom-call | flops 1048576 | bytes 2097152 | tf_op jit(solution)/shard_map/lanes/pallas_call | solution.py:464
  8.4 1.6 %collective-permute-start.3 = (f32[64,128]{1,0:T(8,128)S(1)}, f32[64,128]{1,0:T(8,128)S(1)}, u32[]{:S(2)}, u32[]{:S(2)}) collective-permute-start(f32[64,128]{1,0:T(8,128)S(1)} %get-tuple-element.68.own_mer), channel_id=1, source_target_pairs={{0,1},{1,0},{2,3},{3,2},{4,5},{5,4},{6,7},{7,6},{8,9},{9,8},{10,11... | collective-permute-start | bytes 98312 | tf_op jit(solution)/shard_map/ppermute | solution.py:443
  10.0 1.5 %inner.1 = (f32[2048,128]{1,0:T(8,128)S(1)}, f32[2048,128]{1,0:T(8,128)S(1)}, f32[64,128]{1,0:T(8,128)S(1)}, f32[32,128]{1,0:T(8,128)S(1)}) custom-call(f32[2048,128]{1,0:T(8,128)S(1)} %get-tuple-element.48.columns, f32[2048,128]{1,0:T(8,128)S(1)} %get-tuple-element.42.frame, f32[128,128]{1,0:T(8,128)S(1)} %get-tuple-element.49.nu, ...), custom_call_target="tpu_custom_call" | custom-call | flops 1073741824 | bytes 2097152 | tf_op jit(solution)/shard_map/inner/pallas_call | solution.py:471
  11.5 0.0 collective-permute-done.1
  11.6 0.0 collective-permute-done.other
  11.6 0.2 %west.1 = (f32[128,128]{1,0:T(8,128)S(1)}, f32[32,128]{1,0:T(8,128)S(1)}, f32[64,128]{1,0:T(8,128)S(1)}, f32[32,128]{1,0:T(8,128)S(1)}) custom-call(f32[2048,128]{1,0:T(8,128)S(1)} %get-tuple-element.52.strips, f32[128,128]{1,0:T(8,128)S(1)} %get-tuple-element.49.nu, bf16[64,192]{1,0:T(8,128)(2,1)S(1)} %get-tuple-element.50.weights, ...), custom_call_target="tpu_custom_call" | custom-call | flops 8589934592 | bytes 2097152 | tf_op jit(solution)/shard_map/west/pallas_call | solution.py:474
  11.8 0.0 collective-permute-done.2
  11.9 0.3 %east.1 = (f32[128,128]{1,0:T(8,128)S(1)}, f32[32,128]{1,0:T(8,128)S(1)}, f32[48,128]{1,0:T(8,128)S(1)}) custom-call(f32[2048,128]{1,0:T(8,128)S(1)} %get-tuple-element.52.strips, f32[128,128]{1,0:T(8,128)S(1)} %get-tuple-element.49.nu, bf16[64,192]{1,0:T(8,128)(2,1)S(1)} %get-tuple-element.50.weights, f32[64,128]{1,0:T(8,128)S(1)} %get-tuple-element.64.half_lanes, ...), custom_call_target="tpu_custom_call" | custom-call | flops 67108864 | bytes 2097152 | tf_op jit(solution)/shard_map/east/pallas_call | solution.py:480
  12.1 1.5 %collective-permute-start.5 = (f32[48,128]{1,0:T(8,128)S(1)}, f32[48,128]{1,0:T(8,128)S(1)}, u32[]{:S(2)}, u32[]{:S(2)}) collective-permute-start(f32[48,128]{1,0:T(8,128)S(1)} %get-tuple-element.78), channel_id=1, source_target_pairs={{0,1},{1,0},{2,3},{3,2},{4,5},{5,4},{6,7},{7,6},{8,9},{9,8},{10,11... | collective-permute-start | bytes 73736 | tf_op jit(solution)/shard_map/ppermute | solution.py:443
  13.6 0.0 collective-permute-done.3.rest_0_
  13.6 0.4 %meet.1 = (f32[64,128]{1,0:T(8,128)S(1)}, f32[64,128]{1,0:T(8,128)S(1)}, f32[40,128]{1,0:T(8,128)S(1)}) custom-call(bf16[64,192]{1,0:T(8,128)(2,1)S(1)} %get-tuple-element.50.weights, f32[64,128]{1,0:T(8,128)S(1)} %get-tuple-element.68.own_mer, f32[32,128]{1,0:T(8,128)S(1)} %get-tuple-element.69.half_surface, ...), custom_call_target="tpu_custom_call" | custom-call | flops 8589934592 | bytes 2097152 | tf_op jit(solution)/shard_map/meet/pallas_call | solution.py:484
  14.0 0.0 collective-permute-start.4
  14.0 1.2 %again.1.partial = f32[2048,128]{1,0:T(8,128)S(1)} custom-call(f32[2048,128]{1,0:T(8,128)S(1)} %get-tuple-element.51.partial, f32[2048,128]{1,0:T(8,128)S(1)} %get-tuple-element.52.strips, f32[128,128]{1,0:T(8,128)S(1)} %get-tuple-element.49.nu, bf16[64,192]{1,0:T(8,128)(2,1)S(1)} %get-tuple-element.50.weights, f32[64,128]{1,0:T(8,128)S(1)} %get-tuple-element.53.spread, ...), custom_call_target="tpu_custom_call" | custom-call | flops 1024 | bytes 1024 | tf_op jit(solution)/shard_map/again/pallas_call | solution.py:488
  15.2 0.0 collective-permute-done.4.other
  15.2 0.5 %sides.1 = (f32[256,128]{1,0:T(8,128)S(1)}, f32[32,128]{1,0:T(8,128)S(1)}, f32[64,128]{1,0:T(8,128)S(1)}, f32[64,128]{1,0:T(8,128)S(1)}) custom-call(f32[2048,128]{1,0:T(8,128)S(1)} %get-tuple-element.48.columns, f32[2048,128]{1,0:T(8,128)S(1)} %get-tuple-element.52.strips, f32[128,128]{1,0:T(8,128)S(1)} %get-tuple-element.49.nu, ...), custom_call_target="tpu_custom_call" | custom-call | flops 1024 | bytes 1024 | tf_op jit(solution)/shard_map/sides/pallas_call | solution.py:491
  15.8 0.3 %collective-permute-done.5.rest_0_ = f32[48,128]{1,0:T(8,128)S(1)} collective-permute-done((f32[48,128]{1,0:T(8,128)S(1)}, f32[48,128]{1,0:T(8,128)S(1)}, u32[]{:S(2)}, u32[]{:S(2)}) %collective-permute-start.5) | collective-permute-done | bytes 24608 | tf_op jit(solution)/shard_map/ppermute | solution.py:443
  16.0 1.8 %last.1 = f32[2,64,16,128]{3,2,1,0:T(8,128)} custom-call(f32[2048,128]{1,0:T(8,128)S(1)} %again.1.partial, f32[256,128]{1,0:T(8,128)S(1)} %get-tuple-element.73.edges, f32[32,128]{1,0:T(8,128)S(1)} %get-tuple-element.74.incr, bf16[64,192]{1,0:T(8,128)(2,1)S(1)} %get-tuple-element.50.weights, f32[64,128]{1,0:T(8,128)S(1)} %get-tuple-element.53.spread, ...), custom_call_target="tpu_custom_call" | custom-call | flops 67108864 | bytes 2097152 | tf_op jit(solution)/shard_map/last/pallas_call | solution.py:494
  (3 shorter events, 0.1 us)
Async XLA Ops:
  0.0 7.6 %copy-start = (f32[1,2,64,16,128]{4,3,2,1,0:T(8,128)S(1)}, f32[1,2,64,16,128]{4,3,2,1,0:T(8,128)}, u32[]{:S(2)}) copy-start(f32[1,2,64,16,128]{4,3,2,1,0:T(8,128)} %param.7) | copy-start | bytes 3145732
  1.4 10.1 %collective-permute-start.1 = (f16[384,128]{1,0:T(8,128)(2,1)S(1)}, f16[384,128]{1,0:T(8,128)(2,1)S(1)}, u32[]{:S(2)}, u32[]{:S(2)}) collective-permute-start(f16[384,128]{1,0:T(8,128)(2,1)S(1)} %get-tuple-element.60), channel_id=1, source_target_pairs={{0,2},{2,4},{4,6},{6,8},{8,10},{10,12},{12,14},{14,0},{1,3},{3,5},... | collective-permute-start | bytes 294920 | tf_op jit(solution)/shard_map/ppermute | solution.py:446
  4.4 7.1 %collective-permute-start = (f32[32,128]{1,0:T(8,128)S(1)}, f32[32,128]{1,0:T(8,128)S(1)}, u32[]{:S(2)}, u32[]{:S(2)}) collective-permute-start(f32[32,128]{1,0:T(8,128)S(1)} %get-tuple-element.57.own), channel_id=1, source_target_pairs={{0,16},{16,0},{1,17},{17,1},{2,18},{18,2},{3,19},{19,3},{4,20},{20... | collective-permute-start | bytes 49160 | tf_op jit(solution)/shard_map/ppermute | solution.py:452
  4.4 7.4 %collective-permute-start.2 = (f16[384,128]{1,0:T(8,128)(2,1)S(1)}, f16[384,128]{1,0:T(8,128)(2,1)S(1)}, u32[]{:S(2)}, u32[]{:S(2)}) collective-permute-start(f16[384,128]{1,0:T(8,128)(2,1)S(1)} %get-tuple-element.62), channel_id=1, source_target_pairs={{0,14},{2,0},{4,2},{6,4},{8,6},{10,8},{12,10},{14,12},{1,15},{3,1}... | collective-permute-start | bytes 294920 | tf_op jit(solution)/shard_map/ppermute | solution.py:446
  8.4 5.2 %collective-permute-start.3 = (f32[64,128]{1,0:T(8,128)S(1)}, f32[64,128]{1,0:T(8,128)S(1)}, u32[]{:S(2)}, u32[]{:S(2)}) collective-permute-start(f32[64,128]{1,0:T(8,128)S(1)} %get-tuple-element.68.own_mer), channel_id=1, source_target_pairs={{0,1},{1,0},{2,3},{3,2},{4,5},{5,4},{6,7},{7,6},{8,9},{9,8},{10,11... | collective-permute-start | bytes 98312 | tf_op jit(solution)/shard_map/ppermute | solution.py:443
  12.1 3.9 %collective-permute-start.5 = (f32[48,128]{1,0:T(8,128)S(1)}, f32[48,128]{1,0:T(8,128)S(1)}, u32[]{:S(2)}, u32[]{:S(2)}) collective-permute-start(f32[48,128]{1,0:T(8,128)S(1)} %get-tuple-element.78), channel_id=1, source_target_pairs={{0,1},{1,0},{2,3},{3,2},{4,5},{5,4},{6,7},{7,6},{8,9},{9,8},{10,11... | collective-permute-start | bytes 73736 | tf_op jit(solution)/shard_map/ppermute | solution.py:443
  14.0 1.2 %collective-permute-start.4 = (f32[40,128]{1,0:T(8,128)S(1)}, f32[40,128]{1,0:T(8,128)S(1)}, u32[]{:S(2)}, u32[]{:S(2)}) collective-permute-start(f32[40,128]{1,0:T(8,128)S(1)} %get-tuple-element.72.own), channel_id=1, source_target_pairs={{0,16},{16,0},{1,17},{17,1},{2,18},{18,2},{3,19},{19,3},{4,20},{20... | collective-permute-start | bytes 61448 | tf_op jit(solution)/shard_map/ppermute | solution.py:452

commit v11 on v10

--- a/solution.py
+++ b/solution.py
@@ -10,7 +10,7 @@
 f32, bf16 = jnp.float32, jnp.bfloat16
 
 
-SCALE = 8192.0
+SCALE = 4096.0
 
 
 def ring(count, ahead):
@@ -145,33 +145,47 @@
 def pack_kernel(dims, state, flow, *rest):
     tracers, levels, width = dims
     size = levels * width
-    fixed = len(rest) - 6 >> 1
+    fixed = len(rest) - 7 >> 1
     east_bound, west_bound, surface, frame = rest[fixed:fixed + 4]
-    raw, sems = rest[2 * fixed + 4:]
+    raw, inner, sems = rest[2 * fixed + 4:]
     level = surface_level(levels)
     wait_flow, copies = [], []
     for k in range(2):
         wait_flow.append(pltpu.make_async_copy(flow.at[k], raw.at[k], sems.at[k]))
-    for ref, places in ((east_bound, (width - 1, width - 2)), (west_bound, (0, 1))):
-        for i, x in enumerate(places):
-            for t in range(tracers):
-                target = ref.at[pl.ds((i * tracers + t) * levels, levels), :]
-                copies.append(pltpu.make_async_copy(state.at[t, :, x, :], target, sems.at[2 + len(copies)]))
+    for i in range(fixed):
+        copies.append(pltpu.make_async_copy(rest[i], rest[fixed + 4 + i], sems.at[2 + len(copies)]))
+    sides = ((east_bound, width - 1, width - 2), (west_bound, 0, 1))
+    for s, (ref, edge, second) in enumerate(sides):
+        for t in range(tracers):
+            target = ref.at[pl.ds(t * levels, levels), :]
+            copies.append(pltpu.make_async_copy(state.at[t, :, edge, :], target, sems.at[2 + len(copies)]))
+            copies.append(pltpu.make_async_copy(state.at[t, :, second, :], inner.at[s * tracers + t], sems.at[2 + len(copies)]))
     for t in range(tracers):
         target = surface.at[pl.ds(t * width, width), :]
         copies.append(pltpu.make_async_copy(state.at[t, level], target, sems.at[2 + len(copies)]))
-    for i in range(fixed):
-        copies.append(pltpu.make_async_copy(rest[i], rest[fixed + 4 + i], sems.at[2 + len(copies)]))
     for copy in wait_flow + copies:
         copy.start()
-    for k, copy in enumerate(wait_flow):
-        copy.wait()
-        frame[k * size:(k + 1) * size, :] = raw[k].reshape(size, 128).astype(f32) * 0.5
-        for ref, x in ((east_bound, width - 1), (west_bound, 0)):
-            strip = frame[pl.ds(k * size + x, levels, stride=width), :]
-            ref[(2 * tracers + k) * levels:(2 * tracers + k + 1) * levels, :] = strip
     for copy in copies:
         copy.wait()
+    diffusion = rest[fixed + 4]
+    lane = lanes_of(levels)
+    row = lax.broadcasted_iota(jnp.int32, (levels, 128), 0)
+    nu = [jnp.transpose(jnp.broadcast_to(diffusion[t:t + 1, :], (128, levels))) for t in range(tracers)]
+    for k in range(2):
+        wait_flow[k].wait()
+        frame[k * size:(k + 1) * size, :] = raw[k].reshape(size, 128).astype(f32) * 0.5
+    for s, (ref, edge, _) in enumerate(sides):
+        c, d = (frame[pl.ds(k * size + edge, levels, stride=width), :] for k in range(2))
+        toward = c if s == 0 else -c
+        for t in range(tracers):
+            q = ref[t * levels:(t + 1) * levels, :]
+            north = jnp.where(lane == 127, 0.0, pltpu.roll(q, 127, 1))
+            south = jnp.where(lane == 0, 0.0, pltpu.roll(q, 1, 1))
+            value = (1.0 - 4.0 * nu[t]) * q + (nu[t] + toward) * inner[s * tracers + t] + (nu[t] - d) * north + (nu[t] + d) * south
+            ref[(tracers + t) * levels:(tracers + t + 1) * levels, :] = value
+        ref[2 * tracers * levels:(2 * tracers + 1) * levels, :] = c
+        rims = jnp.where(lane == row, d[:, 127:128], 0.0) + jnp.where(lane == row + 64, d[:, 0:1], 0.0)
+        ref[(2 * tracers + 1) * levels:, :] = jnp.broadcast_to(jnp.sum(rims, axis=0, keepdims=True), (16, 128))
 
 
 def lanes_kernel(dims, cells, frame, diffusion, solve, rate, block_map, ice_mask, columns, send_mer, nu, weights, spread, guide):
@@ -344,27 +358,28 @@
     lane = lanes_of(levels)
     flux[...] = increments(own[:total, :], other[:total, :], guide, tracers, width)
     extra = increments(own[total:, :], other[total:, :], guide, tracers, 1)
-    at_level = lax.broadcasted_iota(jnp.int32, (levels, 128), 0) == surface_level(levels)
+    level_row = lax.broadcasted_iota(jnp.int32, (levels, 128), 0)
+    at_level = level_row == surface_level(levels)
     terms, gains = [], []
     first = jnp.zeros((levels, 128), f32)
     later = jnp.zeros((levels, 128), f32)
     for s, ref in enumerate((from_west, from_east)):
         x = side_of(s == 1, width)
-        c, d = (part(ref, 2 * tracers + k, levels) for k in range(2))
+        c = part(ref, 2 * tracers, levels)
+        rims = ref[(2 * tracers + 1) * levels:(2 * tracers + 1) * levels + 1, :]
+        d_north = jnp.sum(jnp.where(lane == level_row, rims, 0.0), axis=1, keepdims=True)
+        d_south = jnp.sum(jnp.where(lane == level_row + 64, rims, 0.0), axis=1, keepdims=True)
         own_c = part(strips, x, levels)
         for t in range(tracers):
-            mine, beyond = part(columns, t * width + x, levels), part(ref, tracers + t, levels)
-            west, east = (mine, beyond) if s == 1 else (beyond, mine)
-            value = horizontal(part(ref, t, levels), east, west, c, d, part(nu, t, levels), lane)
+            mine = part(columns, t * width + x, levels)
+            value = part(ref, tracers + t, levels) + (part(nu, t, levels) + (c if s == 1 else -c)) * mine
             value = value + jnp.where(at_level, jnp.broadcast_to(extra[s * tracers + t:s * tracers + t + 1, :], value.shape), 0.0)
             terms.append(value)
             gain = part(nu, t, levels) + (-own_c if s == 1 else own_c)
             gains.append(gain)
-            j = t * width + x
-            here = lane // 2 == j
-            packed = both_edges(d, j)
-            first = jnp.where(here, part(nu, t, levels) + jnp.where(lane % 2 == 0, -packed, packed), first)
-            later = jnp.where(here, both_edges(gain, j), later)
+            here = lane // 2 == t * width + x
+            first = jnp.where(here, part(nu, t, levels) + jnp.where(lane % 2 == 0, -d_north, d_south), first)
+            later = jnp.where(here, both_edges(gain, t * width + x), later)
     inner_gain[...] = first
     outer_gain[...] = later
     result = product(weights[...], jnp.concatenate(terms, axis=1))
@@ -432,7 +447,7 @@
     dims = (tracers, levels, width)
     size, total = levels * width, tracers * width
     shape = lambda rows, dtype=f32: jax.ShapeDtypeStruct((rows, wide), dtype)
-    message = shape((2 * tracers + 2) * levels)
+    message = shape((2 * tracers + 1) * levels + 16)
     packed = shape(levels)
     folded = shape(levels // 2 + 16)
     kept = shape(tracers * size)
@@ -456,7 +471,7 @@
     east_bound, west_bound, surface, frame, *params = call(
         functools.partial(pack_kernel, dims), "pack", [HB] * len(in_hbm),
         [message, message, shape(total), shape(2 * size)] + [jax.ShapeDtypeStruct(p.shape, p.dtype) for p in params], 1 << 20,
-        scratch=[pltpu.VMEM((2, levels, width, wide), bf16),
+        scratch=[pltpu.VMEM((2, levels, width, wide), bf16), pltpu.VMEM((2 * tracers, levels, wide), f32),
                  pltpu.SemaphoreType.DMA((5 * tracers + 2 + len(params),))],
     )(*in_hbm)
     east_bound, west_bound = lax.optimization_barrier(((east_bound * SCALE).astype(jnp.float16), (west_bound * SCALE).astype(jnp.float16)))

time: 18 us -> 18.2 us (1.011)
  waiting for transfers between devices: 0.27 us -> 0.78 us
  starting transfers between devices: 9.3 us -> 8.84 us
    ppermute x2, waiting for transfers between devices: 0.26 us -> 0.77 us  [swap_mer(): lax.ppermute(piece, 'mer', pairs(mer_count, r == 1))]
    ppermute x2, starting transfers between devices: 3.11 us -> 2.65 us  [swap_mer(): lax.ppermute(piece, 'mer', pairs(mer_count, r == 1))]
    pallas_call x1, Pallas kernels: 1.38 us -> 1.67 us  [on_device(): call(functools.partial(pack_kernel, dims), 'pack', [HB] * len(in_hbm), [m...]
  transfers between devices with their start and end apart: 6 -> 6, of which waited for: 1 -> 1; matrix products, arithmetic and copies ran while one was open for 0% -> 0% of each run, Pallas kernels for 27% -> 26%
where the time goes in v11:
time: 18.2 us; the launch traced here: 18 us
  starting transfers between devices  8.84 us (49%)
  Pallas kernels  8.24 us (45%)
  waiting for transfers between devices  0.78 us (4%)
    ppermute x2, starting transfers between devices, shift_zonal(): return lax.ppermute(piece, 'zon', ring(zon_count, ahead))  6.17 us
    ppermute x2, starting transfers between devices, swap_mer(): lax.ppermute(piece, 'mer', pairs(mer_count, r == 1))  2.65 us
    pallas_call x1, Pallas kernels, on_device(): call(functools.partial(last_kernel, dims, mer_count), 'last', [VM] * (9 +...  1.81 us
    pallas_call x1, Pallas kernels, on_device(): call(functools.partial(pack_kernel, dims), 'pack', [HB] * len(in_hbm), [m...  1.67 us
    pallas_call x1, Pallas kernels, on_device(): call(functools.partial(inner_kernel, dims), 'inner', [VM] * 4, [kept, sha...  1.42 us
    pallas_call x1, Pallas kernels, on_device(): call(functools.partial(again_kernel, dims), 'again', [VM] * 9, kept, 1 <<...  1.2 us
    ppermute x2, waiting for transfers between devices, swap_mer(): lax.ppermute(piece, 'mer', pairs(mer_count, r == 1))  0.77 us
    pallas_call x1, Pallas kernels, on_device(): call(functools.partial(lanes_kernel, dims), 'lanes', [VM] * 7, [kept, pac...  0.75 us
  transfers between devices with their start and end apart: 6, of which 1 were waited for; matrix products, arithmetic and copies ran while one was open for 0% of the time, Pallas kernels for 26%

profile of v11, /device:TPU:0, one launch (start us, length us, event | category | flops | bytes accessed | tf_op | source)
XLA Modules:
  0.0 18.0 jit_solution(16224161664443420753)
XLA Ops:
  0.0 0.0 copy-start
  0.0 1.7 %pack.1 = (f32[336,128]{1,0:T(8,128)S(1)}, f32[336,128]{1,0:T(8,128)S(1)}, f32[32,128]{1,0:T(8,128)S(1)}, f32[2048,128]{1,0:T(8,128)S(1)}, f32[2,64]{1,0:T(2,128...) custom-call(f32[2,64,16,128]{3,2,1,0:T(8,128)} %bitcast.8, ...), custom_call_target="tpu_custom_call" | custom-call | flops 1048576 | bytes 2097152 | tf_op jit(solution)/shard_map/pack/pallas_call | solution.py:471
  1.7 3.0 %collective-permute-start.1 = (f16[336,128]{1,0:T(8,128)(2,1)S(1)}, f16[336,128]{1,0:T(8,128)(2,1)S(1)}, u32[]{:S(2)}, u32[]{:S(2)}) collective-permute-start(f16[336,128]{1,0:T(8,128)(2,1)S(1)} %get-tuple-element.60), channel_id=1, source_target_pairs={{0,2},{2,4},{4,6},{6,8},{8,10},{10,12},{12,14},{14,0},{1,3},{3,5},... | collective-permute-start | bytes 258056 | tf_op jit(solution)/shard_map/ppermute | solution.py:461
  4.7 0.0 collective-permute-start
  4.7 3.2 %collective-permute-start.2 = (f16[336,128]{1,0:T(8,128)(2,1)S(1)}, f16[336,128]{1,0:T(8,128)(2,1)S(1)}, u32[]{:S(2)}, u32[]{:S(2)}) collective-permute-start(f16[336,128]{1,0:T(8,128)(2,1)S(1)} %get-tuple-element.62), channel_id=1, source_target_pairs={{0,14},{2,0},{4,2},{6,4},{8,6},{10,8},{12,10},{14,12},{1,15},{3,1}... | collective-permute-start | bytes 258056 | tf_op jit(solution)/shard_map/ppermute | solution.py:461
  7.9 0.0 copy-done
  7.9 0.8 %lanes.1 = (f32[2048,128]{1,0:T(8,128)S(1)}, f32[64,128]{1,0:T(8,128)S(1)}, f32[128,128]{1,0:T(8,128)S(1)}, bf16[64,192]{1,0:T(8,128)(2,1)S(1)}, f32[64,128]{1,0:T(8,128)S(1)}, /*index=5*/f32[8,128]{1,0:T(8,128)S(1)}) custom-call(f32[2048,128]{1,0:T(8,128)S(1)} %bitcast.9, f32[2048,128]{1,0:T(8,128)S(1)} %get-tuple-element.42.frame, ...), custom_call_target="tpu_custom_call" | custom-call | flops 1048576 | bytes 2097152 | tf_op jit(solution)/shard_map/lanes/pallas_call | solution.py:479
  8.7 1.6 %collective-permute-start.3 = (f32[64,128]{1,0:T(8,128)S(1)}, f32[64,128]{1,0:T(8,128)S(1)}, u32[]{:S(2)}, u32[]{:S(2)}) collective-permute-start(f32[64,128]{1,0:T(8,128)S(1)} %get-tuple-element.68.own_mer), channel_id=1, source_target_pairs={{0,1},{1,0},{2,3},{3,2},{4,5},{5,4},{6,7},{7,6},{8,9},{9,8},{10,11... | collective-permute-start | bytes 98312 | tf_op jit(solution)/shard_map/ppermute | solution.py:458
  10.3 1.4 %inner.1 = (f32[2048,128]{1,0:T(8,128)S(1)}, f32[2048,128]{1,0:T(8,128)S(1)}, f32[64,128]{1,0:T(8,128)S(1)}, f32[32,128]{1,0:T(8,128)S(1)}) custom-call(f32[2048,128]{1,0:T(8,128)S(1)} %get-tuple-element.48.columns, f32[2048,128]{1,0:T(8,128)S(1)} %get-tuple-element.42.frame, f32[128,128]{1,0:T(8,128)S(1)} %get-tuple-element.49.nu, ...), custom_call_target="tpu_custom_call" | custom-call | flops 1073741824 | bytes 2097152 | tf_op jit(solution)/shard_map/inner/pallas_call | solution.py:486
  11.7 0.0 collective-permute-done.1
  11.8 0.0 collective-permute-done.other
  11.8 0.2 %west.1 = (f32[128,128]{1,0:T(8,128)S(1)}, f32[32,128]{1,0:T(8,128)S(1)}, f32[64,128]{1,0:T(8,128)S(1)}, f32[32,128]{1,0:T(8,128)S(1)}) custom-call(f32[2048,128]{1,0:T(8,128)S(1)} %get-tuple-element.52.strips, f32[128,128]{1,0:T(8,128)S(1)} %get-tuple-element.49.nu, bf16[64,192]{1,0:T(8,128)(2,1)S(1)} %get-tuple-element.50.weights, ...), custom_call_target="tpu_custom_call" | custom-call | flops 8589934592 | bytes 2097152 | tf_op jit(solution)/shard_map/west/pallas_call | solution.py:489
  12.0 0.0 collective-permute-done.2
  12.1 0.3 %east.1 = (f32[128,128]{1,0:T(8,128)S(1)}, f32[32,128]{1,0:T(8,128)S(1)}, f32[48,128]{1,0:T(8,128)S(1)}) custom-call(f32[2048,128]{1,0:T(8,128)S(1)} %get-tuple-element.52.strips, f32[128,128]{1,0:T(8,128)S(1)} %get-tuple-element.49.nu, bf16[64,192]{1,0:T(8,128)(2,1)S(1)} %get-tuple-element.50.weights, f32[64,128]{1,0:T(8,128)S(1)} %get-tuple-element.64.half_lanes, ...), custom_call_target="tpu_custom_call" | custom-call | flops 67108864 | bytes 2097152 | tf_op jit(solution)/shard_map/east/pallas_call | solution.py:495
  12.4 1.0 %collective-permute-start.5 = (f32[48,128]{1,0:T(8,128)S(1)}, f32[48,128]{1,0:T(8,128)S(1)}, u32[]{:S(2)}, u32[]{:S(2)}) collective-permute-start(f32[48,128]{1,0:T(8,128)S(1)} %get-tuple-element.78), channel_id=1, source_target_pairs={{0,1},{1,0},{2,3},{3,2},{4,5},{5,4},{6,7},{7,6},{8,9},{9,8},{10,11... | collective-permute-start | bytes 73736 | tf_op jit(solution)/shard_map/ppermute | solution.py:458
  13.4 0.0 collective-permute-done.3.rest_0_
  13.4 0.4 %meet.1 = (f32[64,128]{1,0:T(8,128)S(1)}, f32[64,128]{1,0:T(8,128)S(1)}, f32[40,128]{1,0:T(8,128)S(1)}) custom-call(bf16[64,192]{1,0:T(8,128)(2,1)S(1)} %get-tuple-element.50.weights, f32[64,128]{1,0:T(8,128)S(1)} %get-tuple-element.68.own_mer, f32[32,128]{1,0:T(8,128)S(1)} %get-tuple-element.69.half_surface, ...), custom_call_target="tpu_custom_call" | custom-call | flops 8589934592 | bytes 2097152 | tf_op jit(solution)/shard_map/meet/pallas_call | solution.py:499
  13.7 0.0 collective-permute-start.4
  13.8 1.2 %again.1.partial = f32[2048,128]{1,0:T(8,128)S(1)} custom-call(f32[2048,128]{1,0:T(8,128)S(1)} %get-tuple-element.51.partial, f32[2048,128]{1,0:T(8,128)S(1)} %get-tuple-element.52.strips, f32[128,128]{1,0:T(8,128)S(1)} %get-tuple-element.49.nu, bf16[64,192]{1,0:T(8,128)(2,1)S(1)} %get-tuple-element.50.weights, f32[64,128]{1,0:T(8,128)S(1)} %get-tuple-element.53.spread, ...), custom_call_target="tpu_custom_call" | custom-call | flops 1024 | bytes 1024 | tf_op jit(solution)/shard_map/again/pallas_call | solution.py:503
  15.0 0.0 collective-permute-done.4.other
  15.0 0.5 %sides.1 = (f32[256,128]{1,0:T(8,128)S(1)}, f32[32,128]{1,0:T(8,128)S(1)}, f32[64,128]{1,0:T(8,128)S(1)}, f32[64,128]{1,0:T(8,128)S(1)}) custom-call(f32[2048,128]{1,0:T(8,128)S(1)} %get-tuple-element.48.columns, f32[2048,128]{1,0:T(8,128)S(1)} %get-tuple-element.52.strips, f32[128,128]{1,0:T(8,128)S(1)} %get-tuple-element.49.nu, ...), custom_call_target="tpu_custom_call" | custom-call | flops 1024 | bytes 1024 | tf_op jit(solution)/shard_map/sides/pallas_call | solution.py:506
  15.5 0.8 %collective-permute-done.5.rest_0_ = f32[48,128]{1,0:T(8,128)S(1)} collective-permute-done((f32[48,128]{1,0:T(8,128)S(1)}, f32[48,128]{1,0:T(8,128)S(1)}, u32[]{:S(2)}, u32[]{:S(2)}) %collective-permute-start.5) | collective-permute-done | bytes 24608 | tf_op jit(solution)/shard_map/ppermute | solution.py:458
  16.2 1.8 %last.1 = f32[2,64,16,128]{3,2,1,0:T(8,128)} custom-call(f32[2048,128]{1,0:T(8,128)S(1)} %again.1.partial, f32[256,128]{1,0:T(8,128)S(1)} %get-tuple-element.73.edges, f32[32,128]{1,0:T(8,128)S(1)} %get-tuple-element.74.incr, bf16[64,192]{1,0:T(8,128)(2,1)S(1)} %get-tuple-element.50.weights, f32[64,128]{1,0:T(8,128)S(1)} %get-tuple-element.53.spread, ...), custom_call_target="tpu_custom_call" | custom-call | flops 67108864 | bytes 2097152 | tf_op jit(solution)/shard_map/last/pallas_call | solution.py:509
  (3 shorter events, 0.1 us)
Async XLA Ops:
  0.0 7.9 %copy-start = (f32[1,2,64,16,128]{4,3,2,1,0:T(8,128)S(1)}, f32[1,2,64,16,128]{4,3,2,1,0:T(8,128)}, u32[]{:S(2)}) copy-start(f32[1,2,64,16,128]{4,3,2,1,0:T(8,128)} %param.7) | copy-start | bytes 3145732
  1.7 10.0 %collective-permute-start.1 = (f16[336,128]{1,0:T(8,128)(2,1)S(1)}, f16[336,128]{1,0:T(8,128)(2,1)S(1)}, u32[]{:S(2)}, u32[]{:S(2)}) collective-permute-start(f16[336,128]{1,0:T(8,128)(2,1)S(1)} %get-tuple-element.60), channel_id=1, source_target_pairs={{0,2},{2,4},{4,6},{6,8},{8,10},{10,12},{12,14},{14,0},{1,3},{3,5},... | collective-permute-start | bytes 258056 | tf_op jit(solution)/shard_map/ppermute | solution.py:461
  4.7 7.1 %collective-permute-start = (f32[32,128]{1,0:T(8,128)S(1)}, f32[32,128]{1,0:T(8,128)S(1)}, u32[]{:S(2)}, u32[]{:S(2)}) collective-permute-start(f32[32,128]{1,0:T(8,128)S(1)} %get-tuple-element.57.own), channel_id=1, source_target_pairs={{0,16},{16,0},{1,17},{17,1},{2,18},{18,2},{3,19},{19,3},{4,20},{20... | collective-permute-start | bytes 49160 | tf_op jit(solution)/shard_map/ppermute | solution.py:467
  4.7 7.3 %collective-permute-start.2 = (f16[336,128]{1,0:T(8,128)(2,1)S(1)}, f16[336,128]{1,0:T(8,128)(2,1)S(1)}, u32[]{:S(2)}, u32[]{:S(2)}) collective-permute-start(f16[336,128]{1,0:T(8,128)(2,1)S(1)} %get-tuple-element.62), channel_id=1, source_target_pairs={{0,14},{2,0},{4,2},{6,4},{8,6},{10,8},{12,10},{14,12},{1,15},{3,1}... | collective-permute-start | bytes 258056 | tf_op jit(solution)/shard_map/ppermute | solution.py:461
  8.7 4.7 %collective-permute-start.3 = (f32[64,128]{1,0:T(8,128)S(1)}, f32[64,128]{1,0:T(8,128)S(1)}, u32[]{:S(2)}, u32[]{:S(2)}) collective-permute-start(f32[64,128]{1,0:T(8,128)S(1)} %get-tuple-element.68.own_mer), channel_id=1, source_target_pairs={{0,1},{1,0},{2,3},{3,2},{4,5},{5,4},{6,7},{7,6},{8,9},{9,8},{10,11... | collective-permute-start | bytes 98312 | tf_op jit(solution)/shard_map/ppermute | solution.py:458
  12.4 3.9 %collective-permute-start.5 = (f32[48,128]{1,0:T(8,128)S(1)}, f32[48,128]{1,0:T(8,128)S(1)}, u32[]{:S(2)}, u32[]{:S(2)}) collective-permute-start(f32[48,128]{1,0:T(8,128)S(1)} %get-tuple-element.78), channel_id=1, source_target_pairs={{0,1},{1,0},{2,3},{3,2},{4,5},{5,4},{6,7},{7,6},{8,9},{9,8},{10,11... | collective-permute-start | bytes 73736 | tf_op jit(solution)/shard_map/ppermute | solution.py:458
  13.7 1.2 %collective-permute-start.4 = (f32[40,128]{1,0:T(8,128)S(1)}, f32[40,128]{1,0:T(8,128)S(1)}, u32[]{:S(2)}, u32[]{:S(2)}) collective-permute-start(f32[40,128]{1,0:T(8,128)S(1)} %get-tuple-element.72.own), channel_id=1, source_target_pairs={{0,16},{16,0},{1,17},{17,1},{2,18},{18,2},{3,19},{19,3},{4,20},{20... | collective-permute-start | bytes 61448 | tf_op jit(solution)/shard_map/ppermute | solution.py:467

commit v12 on v10

--- a/solution.py
+++ b/solution.py
@@ -149,27 +149,22 @@
     east_bound, west_bound, surface, frame = rest[fixed:fixed + 4]
     raw, sems = rest[2 * fixed + 4:]
     level = surface_level(levels)
-    wait_flow, copies = [], []
-    for k in range(2):
-        wait_flow.append(pltpu.make_async_copy(flow.at[k], raw.at[k], sems.at[k]))
+    transfers = [(flow.at[k], raw.at[k]) for k in range(2)]
     for ref, places in ((east_bound, (width - 1, width - 2)), (west_bound, (0, 1))):
         for i, x in enumerate(places):
-            for t in range(tracers):
-                target = ref.at[pl.ds((i * tracers + t) * levels, levels), :]
-                copies.append(pltpu.make_async_copy(state.at[t, :, x, :], target, sems.at[2 + len(copies)]))
-    for t in range(tracers):
-        target = surface.at[pl.ds(t * width, width), :]
-        copies.append(pltpu.make_async_copy(state.at[t, level], target, sems.at[2 + len(copies)]))
-    for i in range(fixed):
-        copies.append(pltpu.make_async_copy(rest[i], rest[fixed + 4 + i], sems.at[2 + len(copies)]))
-    for copy in wait_flow + copies:
+            transfers.append((state.at[:, :, x, :], ref.at[pl.ds(i * tracers, tracers)]))
+    transfers.append((state.at[:, level], surface))
+    transfers += [(rest[i], rest[fixed + 4 + i]) for i in range(fixed)]
+    copies = [pltpu.make_async_copy(source, target, sems.at[i]) for i, (source, target) in enumerate(transfers)]
+    for copy in copies:
         copy.start()
+    wait_flow, copies = copies[:2], copies[2:]
     for k, copy in enumerate(wait_flow):
         copy.wait()
         frame[k * size:(k + 1) * size, :] = raw[k].reshape(size, 128).astype(f32) * 0.5
         for ref, x in ((east_bound, width - 1), (west_bound, 0)):
             strip = frame[pl.ds(k * size + x, levels, stride=width), :]
-            ref[(2 * tracers + k) * levels:(2 * tracers + k + 1) * levels, :] = strip
+            ref[2 * tracers + k] = strip
     for copy in copies:
         copy.wait()
 
@@ -203,7 +198,7 @@
     spread[...] = jnp.broadcast_to(jnp.sum(jnp.where(at_level, solve[...], 0.0), axis=1, keepdims=True), (levels, 128))
 
 
-def inner_kernel(dims, columns, frame, nu, weights, partial, strips, edge_lanes, rows):
+def inner_kernel(dims, columns, frame, nu, weights, guide, own, other, partial, strips, edge_lanes, rows, incr):
     tracers, levels, width = dims
     lane = lanes_of(levels)
     for k in range(2):
@@ -223,6 +218,7 @@
         packed = jnp.where(lane // 2 == j, both_edges(part(partial, j, levels), j), packed)
     edge_lanes[...] = packed
     rows[...] = partial[pl.ds(surface_level(levels), tracers * width, stride=levels), :]
+    incr[...] = increments(own[...], other[...], guide, tracers, width)
 
 
 def side_terms(ref, east, strips, nu, dims):
@@ -247,14 +243,13 @@
     return fresh
 
 
-def west_kernel(dims, strips, nu, weights, spread, edge_lanes, rows, guide, own, other, from_west, solved, incr, half_lanes, surface):
+def west_kernel(dims, strips, nu, weights, spread, edge_lanes, rows, incr, from_west, solved, half_lanes, surface):
     tracers, levels, width = dims
     total = tracers * width
     lane = lanes_of(levels)
     terms = side_terms(from_west, False, strips, nu, dims)
     result = product(weights[...], jnp.concatenate(terms, axis=1))
-    flux = increments(own[...], other[...], guide, tracers, width)
-    incr[...] = flux
+    flux = incr[...]
     for t in range(tracers):
         solved[t * levels:(t + 1) * levels, :] = result[:, t * 128:(t + 1) * 128]
     row = lax.broadcasted_iota(jnp.int32, (total, 128), 0)
@@ -433,6 +428,7 @@
     size, total = levels * width, tracers * width
     shape = lambda rows, dtype=f32: jax.ShapeDtypeStruct((rows, wide), dtype)
     message = shape((2 * tracers + 2) * levels)
+    blocks = jax.ShapeDtypeStruct((2 * tracers + 2, levels, wide), f32)
     packed = shape(levels)
     folded = shape(levels // 2 + 16)
     kept = shape(tracers * size)
@@ -455,10 +451,11 @@
     in_hbm = [pltpu.with_memory_space_constraint(value, pltpu.HBM) for value in (state[0], flow[0]) + params]
     east_bound, west_bound, surface, frame, *params = call(
         functools.partial(pack_kernel, dims), "pack", [HB] * len(in_hbm),
-        [message, message, shape(total), shape(2 * size)] + [jax.ShapeDtypeStruct(p.shape, p.dtype) for p in params], 1 << 20,
+        [blocks, blocks, jax.ShapeDtypeStruct((tracers, width, wide), f32), shape(2 * size)] + [jax.ShapeDtypeStruct(p.shape, p.dtype) for p in params], 1 << 20,
         scratch=[pltpu.VMEM((2, levels, width, wide), bf16),
-                 pltpu.SemaphoreType.DMA((5 * tracers + 2 + len(params),))],
+                 pltpu.SemaphoreType.DMA((7 + len(params),))],
     )(*in_hbm)
+    east_bound, west_bound, surface = (value.reshape(-1, wide) for value in (east_bound, west_bound, surface))
     east_bound, west_bound = lax.optimization_barrier(((east_bound * SCALE).astype(jnp.float16), (west_bound * SCALE).astype(jnp.float16)))
     from_west = widen(shift_zonal(east_bound, 1))
     columns, own_mer, nu, weights, spread, guide = call(
@@ -468,13 +465,12 @@
     recv_mer = swap_mer([own_mer] * rounds)
     other = swap_fluid(surface)
     from_east = shift_zonal(west_bound, -1)
-    partial, strips, edge_lanes, rows = call(
-        functools.partial(inner_kernel, dims), "inner", [VM] * 4, [kept, shape(2 * size), packed, shape(total)], 1 << 30,
-    )(columns, frame, nu, weights)
-    west_solved, incr, half_lanes, half_surface = call(
-        functools.partial(west_kernel, dims), "west", [VM] * 10,
-        [halved, shape(total), packed, shape(total)], 1 << 33,
-    )(strips, nu, weights, spread, edge_lanes, rows, guide, surface, other, from_west)
+    partial, strips, edge_lanes, rows, incr = call(
+        functools.partial(inner_kernel, dims), "inner", [VM] * 7, [kept, shape(2 * size), packed, shape(total), shape(total)], 1 << 30,
+    )(columns, frame, nu, weights, guide, surface, other)
+    west_solved, half_lanes, half_surface = call(
+        functools.partial(west_kernel, dims), "west", [VM] * 8, [halved, packed, shape(total)], 1 << 33,
+    )(strips, nu, weights, spread, edge_lanes, rows, incr, from_west)
     from_east, half_lanes = lax.optimization_barrier((from_east, half_lanes))
     from_east = widen(from_east)
     east_solved, half_surface, *send_mer = call(

time: 18 us -> 18.2 us (1.011)
  waiting for transfers between devices: 0.27 us -> 0.76 us
  starting transfers between devices: 9.3 us -> 8.87 us
  Pallas kernels: 8.07 us -> 8.28 us
    ppermute x2, starting transfers between devices: 0.02 us -> 0.53 us  [swap_fluid(): return lax.ppermute(piece, 'fluid', [(0, 1), (1, 0)])]
    ppermute x2, starting transfers between devices: 6.17 us -> 5.66 us  [shift_zonal(): return lax.ppermute(piece, 'zon', ring(zon_count, ahead))]
    ppermute x2, waiting for transfers between devices: 0.26 us -> 0.74 us  [swap_mer(): lax.ppermute(piece, 'mer', pairs(mer_count, r == 1))]
    ppermute x2, starting transfers between devices: 3.11 us -> 2.68 us  [swap_mer(): lax.ppermute(piece, 'mer', pairs(mer_count, r == 1))]
  transfers between devices with their start and end apart: 6 -> 6, of which waited for: 1 -> 1; matrix products, arithmetic and copies ran while one was open for 0% -> 0% of each run, Pallas kernels for 27% -> 28%
where the time goes in v12:
time: 18.2 us; the launch traced here: 18.1 us
  starting transfers between devices  8.87 us (49%)
  Pallas kernels  8.28 us (45%)
  waiting for transfers between devices  0.76 us (4%)
    ppermute x2, starting transfers between devices, shift_zonal(): return lax.ppermute(piece, 'zon', ring(zon_count, ahead))  5.66 us
    ppermute x2, starting transfers between devices, swap_mer(): lax.ppermute(piece, 'mer', pairs(mer_count, r == 1))  2.68 us
    pallas_call x1, Pallas kernels, on_device(): call(functools.partial(last_kernel, dims, mer_count), 'last', [VM] * (9 +...  1.81 us
    pallas_call x1, Pallas kernels, on_device(): call(functools.partial(inner_kernel, dims), 'inner', [VM] * 7, [kept, sha...  1.72 us
    pallas_call x1, Pallas kernels, on_device(): call(functools.partial(pack_kernel, dims), 'pack', [HB] * len(in_hbm), [b...  1.33 us
    pallas_call x1, Pallas kernels, on_device(): call(functools.partial(again_kernel, dims), 'again', [VM] * 9, kept, 1 <<...  1.27 us
    pallas_call x1, Pallas kernels, on_device(): call(functools.partial(lanes_kernel, dims), 'lanes', [VM] * 7, [kept, pac...  0.75 us
    ppermute x2, waiting for transfers between devices, swap_mer(): lax.ppermute(piece, 'mer', pairs(mer_count, r == 1))  0.74 us
  transfers between devices with their start and end apart: 6, of which 1 were waited for; matrix products, arithmetic and copies ran while one was open for 0% of the time, Pallas kernels for 28%

profile of v12, /device:TPU:0, one launch (start us, length us, event | category | flops | bytes accessed | tf_op | source)
XLA Modules:
  0.0 18.1 jit_solution(1302587980120062492)
XLA Ops:
  0.0 0.0 copy-start
  0.0 1.3 %pack.1 = (f32[6,64,128]{2,1,0:T(8,128)S(1)}, f32[6,64,128]{2,1,0:T(8,128)S(1)}, f32[2,16,128]{2,1,0:T(8,128)S(1)}, f32[2048,128]{1,0:T(8,128)S(1)}, f32[2,64]{1...) custom-call(f32[2,64,16,128]{3,2,1,0:T(8,128)} %bitcast.11, ...), custom_call_target="tpu_custom_call" | custom-call | flops 1048576 | bytes 2097152 | tf_op jit(solution)/shard_map/pack/pallas_call | solution.py:452
  1.3 0.5 %collective-permute-start = (f32[32,128]{1,0:T(8,128)S(1)}, f32[32,128]{1,0:T(8,128)S(1)}, u32[]{:S(2)}, u32[]{:S(2)}) collective-permute-start(f32[32,128]{1,0:T(8,128)S(1)} %bitcast.13), channel_id=1, source_target_pairs={{0,16},{16,0},{1,17},{17,1},{2,18},{18,2},{3,19},{19,3},{4,20},{20... | collective-permute-start | bytes 49160 | tf_op jit(solution)/shard_map/ppermute | solution.py:448
  1.9 2.6 %collective-permute-start.1 = (f16[384,128]{1,0:T(8,128)(2,1)S(1)}, f16[384,128]{1,0:T(8,128)(2,1)S(1)}, u32[]{:S(2)}, u32[]{:S(2)}) collective-permute-start(f16[384,128]{1,0:T(8,128)(2,1)S(1)} %bitcast.17), channel_id=1, source_target_pairs={{0,2},{2,4},{4,6},{6,8},{8,10},{10,12},{12,14},{14,0},{1,3},{3,5},... | collective-permute-start | bytes 294920 | tf_op jit(solution)/shard_map/ppermute | solution.py:442
  4.5 3.1 %collective-permute-start.2 = (f16[384,128]{1,0:T(8,128)(2,1)S(1)}, f16[384,128]{1,0:T(8,128)(2,1)S(1)}, u32[]{:S(2)}, u32[]{:S(2)}) collective-permute-start(f16[384,128]{1,0:T(8,128)(2,1)S(1)} %bitcast.16), channel_id=1, source_target_pairs={{0,14},{2,0},{4,2},{6,4},{8,6},{10,8},{12,10},{14,12},{1,15},{3,1}... | collective-permute-start | bytes 294920 | tf_op jit(solution)/shard_map/ppermute | solution.py:442
  7.6 0.0 copy-done
  7.6 0.8 %lanes.1 = (f32[2048,128]{1,0:T(8,128)S(1)}, f32[64,128]{1,0:T(8,128)S(1)}, f32[128,128]{1,0:T(8,128)S(1)}, bf16[64,192]{1,0:T(8,128)(2,1)S(1)}, f32[64,128]{1,0:T(8,128)S(1)}, /*index=5*/f32[8,128]{1,0:T(8,128)S(1)}) custom-call(f32[2048,128]{1,0:T(8,128)S(1)} %bitcast.12, f32[2048,128]{1,0:T(8,128)S(1)} %get-tuple-element.42.frame, ...), custom_call_target="tpu_custom_call" | custom-call | flops 1048576 | bytes 2097152 | tf_op jit(solution)/shard_map/lanes/pallas_call | solution.py:461
  8.3 1.7 %collective-permute-start.3 = (f32[64,128]{1,0:T(8,128)S(1)}, f32[64,128]{1,0:T(8,128)S(1)}, u32[]{:S(2)}, u32[]{:S(2)}) collective-permute-start(f32[64,128]{1,0:T(8,128)S(1)} %get-tuple-element.69.own_mer), channel_id=1, source_target_pairs={{0,1},{1,0},{2,3},{3,2},{4,5},{5,4},{6,7},{7,6},{8,9},{9,8},{10,11... | collective-permute-start | bytes 98312 | tf_op jit(solution)/shard_map/ppermute | solution.py:439
  10.1 0.0 collective-permute-done.other
  10.1 1.7 %inner.1 = (f32[2048,128]{1,0:T(8,128)S(1)}, f32[2048,128]{1,0:T(8,128)S(1)}, f32[64,128]{1,0:T(8,128)S(1)}, f32[32,128]{1,0:T(8,128)S(1)}, f32[32,128]{1,0:T(8,128)S(1)}) custom-call(f32[2048,128]{1,0:T(8,128)S(1)} %get-tuple-element.48.columns, f32[2048,128]{1,0:T(8,128)S(1)} %get-tuple-element.42.frame, f32[128,128]{1,0:T(8,128)S(1)} %get-tuple-element.49.nu, ...), custom_call_target="tpu_custom_call" | custom-call | flops 1073741824 | bytes 2097152 | tf_op jit(solution)/shard_map/inner/pallas_call | solution.py:468
  11.8 0.0 collective-permute-done.1
  11.8 0.2 %west.1 = (f32[128,128]{1,0:T(8,128)S(1)}, f32[64,128]{1,0:T(8,128)S(1)}, f32[32,128]{1,0:T(8,128)S(1)}) custom-call(f32[2048,128]{1,0:T(8,128)S(1)} %get-tuple-element.54.strips, f32[128,128]{1,0:T(8,128)S(1)} %get-tuple-element.49.nu, bf16[64,192]{1,0:T(8,128)(2,1)S(1)} %get-tuple-element.50.weights, f32[64,128]{1,0:T(8,128)S(1)} %get-tuple-element.55.spread, ...), custom_call_target="tpu_custom_call" | custom-call | flops 8589934592 | bytes 2097152 | tf_op jit(solution)/shard_map/west/pallas_call | solution.py:471
  12.1 0.0 collective-permute-done.2
  12.1 0.3 %east.1 = (f32[128,128]{1,0:T(8,128)S(1)}, f32[32,128]{1,0:T(8,128)S(1)}, f32[48,128]{1,0:T(8,128)S(1)}) custom-call(f32[2048,128]{1,0:T(8,128)S(1)} %get-tuple-element.54.strips, f32[128,128]{1,0:T(8,128)S(1)} %get-tuple-element.49.nu, bf16[64,192]{1,0:T(8,128)(2,1)S(1)} %get-tuple-element.50.weights, f32[64,128]{1,0:T(8,128)S(1)} %get-tuple-element.65.half_lanes, ...), custom_call_target="tpu_custom_call" | custom-call | flops 67108864 | bytes 2097152 | tf_op jit(solution)/shard_map/east/pallas_call | solution.py:476
  12.4 1.0 %collective-permute-start.5 = (f32[48,128]{1,0:T(8,128)S(1)}, f32[48,128]{1,0:T(8,128)S(1)}, u32[]{:S(2)}, u32[]{:S(2)}) collective-permute-start(f32[48,128]{1,0:T(8,128)S(1)} %get-tuple-element.78), channel_id=1, source_target_pairs={{0,1},{1,0},{2,3},{3,2},{4,5},{5,4},{6,7},{7,6},{8,9},{9,8},{10,11... | collective-permute-start | bytes 73736 | tf_op jit(solution)/shard_map/ppermute | solution.py:439
  13.4 0.0 collective-permute-done.3.rest_0_
  13.4 0.4 %meet.1 = (f32[64,128]{1,0:T(8,128)S(1)}, f32[64,128]{1,0:T(8,128)S(1)}, f32[40,128]{1,0:T(8,128)S(1)}) custom-call(bf16[64,192]{1,0:T(8,128)(2,1)S(1)} %get-tuple-element.50.weights, f32[64,128]{1,0:T(8,128)S(1)} %get-tuple-element.69.own_mer, f32[32,128]{1,0:T(8,128)S(1)} %get-tuple-element.70.half_surface, ...), custom_call_target="tpu_custom_call" | custom-call | flops 8589934592 | bytes 2097152 | tf_op jit(solution)/shard_map/meet/pallas_call | solution.py:480
  13.7 0.0 collective-permute-start.4
  13.7 1.3 %again.1.partial = f32[2048,128]{1,0:T(8,128)S(1)} custom-call(f32[2048,128]{1,0:T(8,128)S(1)} %get-tuple-element.53.partial, f32[2048,128]{1,0:T(8,128)S(1)} %get-tuple-element.54.strips, f32[128,128]{1,0:T(8,128)S(1)} %get-tuple-element.49.nu, bf16[64,192]{1,0:T(8,128)(2,1)S(1)} %get-tuple-element.50.weights, f32[64,128]{1,0:T(8,128)S(1)} %get-tuple-element.55.spread, ...), custom_call_target="tpu_custom_call" | custom-call | flops 1024 | bytes 1024 | tf_op jit(solution)/shard_map/again/pallas_call | solution.py:484
  15.0 0.0 collective-permute-done.4.other
  15.0 0.5 %sides.1 = (f32[256,128]{1,0:T(8,128)S(1)}, f32[32,128]{1,0:T(8,128)S(1)}, f32[64,128]{1,0:T(8,128)S(1)}, f32[64,128]{1,0:T(8,128)S(1)}) custom-call(f32[2048,128]{1,0:T(8,128)S(1)} %get-tuple-element.48.columns, f32[2048,128]{1,0:T(8,128)S(1)} %get-tuple-element.54.strips, f32[128,128]{1,0:T(8,128)S(1)} %get-tuple-element.49.nu, ...), custom_call_target="tpu_custom_call" | custom-call | flops 1024 | bytes 1024 | tf_op jit(solution)/shard_map/sides/pallas_call | solution.py:487
  15.5 0.7 %collective-permute-done.5.rest_0_ = f32[48,128]{1,0:T(8,128)S(1)} collective-permute-done((f32[48,128]{1,0:T(8,128)S(1)}, f32[48,128]{1,0:T(8,128)S(1)}, u32[]{:S(2)}, u32[]{:S(2)}) %collective-permute-start.5) | collective-permute-done | bytes 24608 | tf_op jit(solution)/shard_map/ppermute | solution.py:439
  16.3 1.8 %last.1 = f32[2,64,16,128]{3,2,1,0:T(8,128)} custom-call(f32[2048,128]{1,0:T(8,128)S(1)} %again.1.partial, f32[256,128]{1,0:T(8,128)S(1)} %get-tuple-element.73.edges, f32[32,128]{1,0:T(8,128)S(1)} %get-tuple-element.74.incr, bf16[64,192]{1,0:T(8,128)(2,1)S(1)} %get-tuple-element.50.weights, f32[64,128]{1,0:T(8,128)S(1)} %get-tuple-element.55.spread, ...), custom_call_target="tpu_custom_call" | custom-call | flops 67108864 | bytes 2097152 | tf_op jit(solution)/shard_map/last/pallas_call | solution.py:490
  (3 shorter events, 0.1 us)
Async XLA Ops:
  0.0 7.6 %copy-start = (f32[1,2,64,16,128]{4,3,2,1,0:T(8,128)S(1)}, f32[1,2,64,16,128]{4,3,2,1,0:T(8,128)}, u32[]{:S(2)}) copy-start(f32[1,2,64,16,128]{4,3,2,1,0:T(8,128)} %param.7) | copy-start | bytes 3145732
  1.3 8.7 %collective-permute-start = (f32[32,128]{1,0:T(8,128)S(1)}, f32[32,128]{1,0:T(8,128)S(1)}, u32[]{:S(2)}, u32[]{:S(2)}) collective-permute-start(f32[32,128]{1,0:T(8,128)S(1)} %bitcast.13), channel_id=1, source_target_pairs={{0,16},{16,0},{1,17},{17,1},{2,18},{18,2},{3,19},{19,3},{4,20},{20... | collective-permute-start | bytes 49160 | tf_op jit(solution)/shard_map/ppermute | solution.py:448
  1.9 9.9 %collective-permute-start.1 = (f16[384,128]{1,0:T(8,128)(2,1)S(1)}, f16[384,128]{1,0:T(8,128)(2,1)S(1)}, u32[]{:S(2)}, u32[]{:S(2)}) collective-permute-start(f16[384,128]{1,0:T(8,128)(2,1)S(1)} %bitcast.17), channel_id=1, source_target_pairs={{0,2},{2,4},{4,6},{6,8},{8,10},{10,12},{12,14},{14,0},{1,3},{3,5},... | collective-permute-start | bytes 294920 | tf_op jit(solution)/shard_map/ppermute | solution.py:442
  4.5 7.6 %collective-permute-start.2 = (f16[384,128]{1,0:T(8,128)(2,1)S(1)}, f16[384,128]{1,0:T(8,128)(2,1)S(1)}, u32[]{:S(2)}, u32[]{:S(2)}) collective-permute-start(f16[384,128]{1,0:T(8,128)(2,1)S(1)} %bitcast.16), channel_id=1, source_target_pairs={{0,14},{2,0},{4,2},{6,4},{8,6},{10,8},{12,10},{14,12},{1,15},{3,1}... | collective-permute-start | bytes 294920 | tf_op jit(solution)/shard_map/ppermute | solution.py:442
  8.3 5.0 %collective-permute-start.3 = (f32[64,128]{1,0:T(8,128)S(1)}, f32[64,128]{1,0:T(8,128)S(1)}, u32[]{:S(2)}, u32[]{:S(2)}) collective-permute-start(f32[64,128]{1,0:T(8,128)S(1)} %get-tuple-element.69.own_mer), channel_id=1, source_target_pairs={{0,1},{1,0},{2,3},{3,2},{4,5},{5,4},{6,7},{7,6},{8,9},{9,8},{10,11... | collective-permute-start | bytes 98312 | tf_op jit(solution)/shard_map/ppermute | solution.py:439
  12.4 3.9 %collective-permute-start.5 = (f32[48,128]{1,0:T(8,128)S(1)}, f32[48,128]{1,0:T(8,128)S(1)}, u32[]{:S(2)}, u32[]{:S(2)}) collective-permute-start(f32[48,128]{1,0:T(8,128)S(1)} %get-tuple-element.78), channel_id=1, source_target_pairs={{0,1},{1,0},{2,3},{3,2},{4,5},{5,4},{6,7},{7,6},{8,9},{9,8},{10,11... | collective-permute-start | bytes 73736 | tf_op jit(solution)/shard_map/ppermute | solution.py:439
  13.7 1.3 %collective-permute-start.4 = (f32[40,128]{1,0:T(8,128)S(1)}, f32[40,128]{1,0:T(8,128)S(1)}, u32[]{:S(2)}, u32[]{:S(2)}) collective-permute-start(f32[40,128]{1,0:T(8,128)S(1)} %get-tuple-element.72.own), channel_id=1, source_target_pairs={{0,16},{16,0},{1,17},{17,1},{2,18},{18,2},{3,19},{19,3},{4,20},{20... | collective-permute-start | bytes 61448 | tf_op jit(solution)/shard_map/ppermute | solution.py:448

commit v13 on v12

--- a/solution.py
+++ b/solution.py
@@ -198,7 +198,7 @@
     spread[...] = jnp.broadcast_to(jnp.sum(jnp.where(at_level, solve[...], 0.0), axis=1, keepdims=True), (levels, 128))
 
 
-def inner_kernel(dims, columns, frame, nu, weights, guide, own, other, partial, strips, edge_lanes, rows, incr):
+def inner_kernel(dims, columns, frame, nu, weights, other, partial, strips, edge_lanes, rows):
     tracers, levels, width = dims
     lane = lanes_of(levels)
     for k in range(2):
@@ -218,7 +218,6 @@
         packed = jnp.where(lane // 2 == j, both_edges(part(partial, j, levels), j), packed)
     edge_lanes[...] = packed
     rows[...] = partial[pl.ds(surface_level(levels), tracers * width, stride=levels), :]
-    incr[...] = increments(own[...], other[...], guide, tracers, width)
 
 
 def side_terms(ref, east, strips, nu, dims):
@@ -243,13 +242,14 @@
     return fresh
 
 
-def west_kernel(dims, strips, nu, weights, spread, edge_lanes, rows, incr, from_west, solved, half_lanes, surface):
+def west_kernel(dims, strips, nu, weights, spread, edge_lanes, rows, guide, own, other, from_west, solved, incr, half_lanes, surface):
     tracers, levels, width = dims
     total = tracers * width
     lane = lanes_of(levels)
     terms = side_terms(from_west, False, strips, nu, dims)
     result = product(weights[...], jnp.concatenate(terms, axis=1))
-    flux = incr[...]
+    flux = increments(own[...], other[...], guide, tracers, width)
+    incr[...] = flux
     for t in range(tracers):
         solved[t * levels:(t + 1) * levels, :] = result[:, t * 128:(t + 1) * 128]
     row = lax.broadcasted_iota(jnp.int32, (total, 128), 0)
@@ -465,12 +465,12 @@
     recv_mer = swap_mer([own_mer] * rounds)
     other = swap_fluid(surface)
     from_east = shift_zonal(west_bound, -1)
-    partial, strips, edge_lanes, rows, incr = call(
-        functools.partial(inner_kernel, dims), "inner", [VM] * 7, [kept, shape(2 * size), packed, shape(total), shape(total)], 1 << 30,
-    )(columns, frame, nu, weights, guide, surface, other)
-    west_solved, half_lanes, half_surface = call(
-        functools.partial(west_kernel, dims), "west", [VM] * 8, [halved, packed, shape(total)], 1 << 33,
-    )(strips, nu, weights, spread, edge_lanes, rows, incr, from_west)
+    partial, strips, edge_lanes, rows = call(
+        functools.partial(inner_kernel, dims), "inner", [VM] * 5, [kept, shape(2 * size), packed, shape(total)], 1 << 30,
+    )(columns, frame, nu, weights, other)
+    west_solved, incr, half_lanes, half_surface = call(
+        functools.partial(west_kernel, dims), "west", [VM] * 10, [halved, shape(total), packed, shape(total)], 1 << 33,
+    )(strips, nu, weights, spread, edge_lanes, rows, guide, surface, other, from_west)
     from_east, half_lanes = lax.optimization_barrier((from_east, half_lanes))
     from_east = widen(from_east)
     east_solved, half_surface, *send_mer = call(

time: 18.2 us -> 18 us (0.989)
  Pallas kernels: 8.28 us -> 8.02 us
  starting transfers between devices: 8.87 us -> 9.09 us
  waiting for transfers between devices: 0.76 us -> 0.57 us
    pallas_call x2, Pallas kernels: 1.96 us -> 1.74 us  [the longest x1 1.49 us: on_device(): call(functools.partial(inner_kernel, dims), 'inner', [VM] * 5, [kept, sha...]
    ppermute x2, starting transfers between devices: 2.68 us -> 2.9 us  [swap_mer(): lax.ppermute(piece, 'mer', pairs(mer_count, r == 1))]
    ppermute x2, waiting for transfers between devices: 0.74 us -> 0.56 us  [swap_mer(): lax.ppermute(piece, 'mer', pairs(mer_count, r == 1))]
  transfers between devices with their start and end apart: 6 -> 6, of which waited for: 1 -> 1; matrix products, arithmetic and copies ran while one was open for 0% -> 0% of each run, Pallas kernels for 28% -> 27%
where the time goes in v13:
time: 18 us; the launch traced here: 17.9 us
  starting transfers between devices  9.09 us (50%)
  Pallas kernels  8.02 us (45%)
  waiting for transfers between devices  0.57 us (3%)
    ppermute x2, starting transfers between devices, shift_zonal(): return lax.ppermute(piece, 'zon', ring(zon_count, ahead))  5.66 us
    ppermute x2, starting transfers between devices, swap_mer(): lax.ppermute(piece, 'mer', pairs(mer_count, r == 1))  2.9 us
    pallas_call x1, Pallas kernels, on_device(): call(functools.partial(last_kernel, dims, mer_count), 'last', [VM] * (9 +...  1.81 us
    pallas_call x1, Pallas kernels, on_device(): call(functools.partial(inner_kernel, dims), 'inner', [VM] * 5, [kept, sha...  1.49 us
    pallas_call x1, Pallas kernels, on_device(): call(functools.partial(pack_kernel, dims), 'pack', [HB] * len(in_hbm), [b...  1.33 us
    pallas_call x1, Pallas kernels, on_device(): call(functools.partial(again_kernel, dims), 'again', [VM] * 9, kept, 1 <<...  1.23 us
    pallas_call x1, Pallas kernels, on_device(): call(functools.partial(lanes_kernel, dims), 'lanes', [VM] * 7, [kept, pac...  0.75 us
    ppermute x2, waiting for transfers between devices, swap_mer(): lax.ppermute(piece, 'mer', pairs(mer_count, r == 1))  0.56 us
  transfers between devices with their start and end apart: 6, of which 1 were waited for; matrix products, arithmetic and copies ran while one was open for 0% of the time, Pallas kernels for 27%

profile of v13, /device:TPU:0, one launch (start us, length us, event | category | flops | bytes accessed | tf_op | source)
XLA Modules:
  0.0 17.9 jit_solution(3828752991179645475)
XLA Ops:
  0.0 0.0 copy-start
  0.0 1.3 %pack.1 = (f32[6,64,128]{2,1,0:T(8,128)S(1)}, f32[6,64,128]{2,1,0:T(8,128)S(1)}, f32[2,16,128]{2,1,0:T(8,128)S(1)}, f32[2048,128]{1,0:T(8,128)S(1)}, f32[2,64]{1...) custom-call(f32[2,64,16,128]{3,2,1,0:T(8,128)} %bitcast.11, ...), custom_call_target="tpu_custom_call" | custom-call | flops 1048576 | bytes 2097152 | tf_op jit(solution)/shard_map/pack/pallas_call | solution.py:452
  1.3 0.5 %collective-permute-start = (f32[32,128]{1,0:T(8,128)S(1)}, f32[32,128]{1,0:T(8,128)S(1)}, u32[]{:S(2)}, u32[]{:S(2)}) collective-permute-start(f32[32,128]{1,0:T(8,128)S(1)} %bitcast.13), channel_id=1, source_target_pairs={{0,16},{16,0},{1,17},{17,1},{2,18},{18,2},{3,19},{19,3},{4,20},{20... | collective-permute-start | bytes 49160 | tf_op jit(solution)/shard_map/ppermute | solution.py:448
  1.9 2.6 %collective-permute-start.1 = (f16[384,128]{1,0:T(8,128)(2,1)S(1)}, f16[384,128]{1,0:T(8,128)(2,1)S(1)}, u32[]{:S(2)}, u32[]{:S(2)}) collective-permute-start(f16[384,128]{1,0:T(8,128)(2,1)S(1)} %bitcast.17), channel_id=1, source_target_pairs={{0,2},{2,4},{4,6},{6,8},{8,10},{10,12},{12,14},{14,0},{1,3},{3,5},... | collective-permute-start | bytes 294920 | tf_op jit(solution)/shard_map/ppermute | solution.py:442
  4.5 3.1 %collective-permute-start.2 = (f16[384,128]{1,0:T(8,128)(2,1)S(1)}, f16[384,128]{1,0:T(8,128)(2,1)S(1)}, u32[]{:S(2)}, u32[]{:S(2)}) collective-permute-start(f16[384,128]{1,0:T(8,128)(2,1)S(1)} %bitcast.16), channel_id=1, source_target_pairs={{0,14},{2,0},{4,2},{6,4},{8,6},{10,8},{12,10},{14,12},{1,15},{3,1}... | collective-permute-start | bytes 294920 | tf_op jit(solution)/shard_map/ppermute | solution.py:442
  7.6 0.0 copy-done
  7.6 0.8 %lanes.1 = (f32[2048,128]{1,0:T(8,128)S(1)}, f32[64,128]{1,0:T(8,128)S(1)}, f32[128,128]{1,0:T(8,128)S(1)}, bf16[64,192]{1,0:T(8,128)(2,1)S(1)}, f32[64,128]{1,0:T(8,128)S(1)}, /*index=5*/f32[8,128]{1,0:T(8,128)S(1)}) custom-call(f32[2048,128]{1,0:T(8,128)S(1)} %bitcast.12, f32[2048,128]{1,0:T(8,128)S(1)} %get-tuple-element.42.frame, ...), custom_call_target="tpu_custom_call" | custom-call | flops 1048576 | bytes 2097152 | tf_op jit(solution)/shard_map/lanes/pallas_call | solution.py:461
  8.3 1.7 %collective-permute-start.3 = (f32[64,128]{1,0:T(8,128)S(1)}, f32[64,128]{1,0:T(8,128)S(1)}, u32[]{:S(2)}, u32[]{:S(2)}) collective-permute-start(f32[64,128]{1,0:T(8,128)S(1)} %get-tuple-element.68.own_mer), channel_id=1, source_target_pairs={{0,1},{1,0},{2,3},{3,2},{4,5},{5,4},{6,7},{7,6},{8,9},{9,8},{10,11... | collective-permute-start | bytes 98312 | tf_op jit(solution)/shard_map/ppermute | solution.py:439
  10.1 0.0 collective-permute-done.other
  10.1 1.5 %inner.1 = (f32[2048,128]{1,0:T(8,128)S(1)}, f32[2048,128]{1,0:T(8,128)S(1)}, f32[64,128]{1,0:T(8,128)S(1)}, f32[32,128]{1,0:T(8,128)S(1)}) custom-call(f32[2048,128]{1,0:T(8,128)S(1)} %get-tuple-element.48.columns, f32[2048,128]{1,0:T(8,128)S(1)} %get-tuple-element.42.frame, f32[128,128]{1,0:T(8,128)S(1)} %get-tuple-element.49.nu, ...), custom_call_target="tpu_custom_call" | custom-call | flops 1073741824 | bytes 2097152 | tf_op jit(solution)/shard_map/inner/pallas_call | solution.py:468
  11.6 0.0 collective-permute-done.1
  11.6 0.2 %west.1 = (f32[128,128]{1,0:T(8,128)S(1)}, f32[32,128]{1,0:T(8,128)S(1)}, f32[64,128]{1,0:T(8,128)S(1)}, f32[32,128]{1,0:T(8,128)S(1)}) custom-call(f32[2048,128]{1,0:T(8,128)S(1)} %get-tuple-element.53.strips, f32[128,128]{1,0:T(8,128)S(1)} %get-tuple-element.49.nu, bf16[64,192]{1,0:T(8,128)(2,1)S(1)} %get-tuple-element.50.weights, ...), custom_call_target="tpu_custom_call" | custom-call | flops 8589934592 | bytes 2097152 | tf_op jit(solution)/shard_map/west/pallas_call | solution.py:471
  11.8 0.0 collective-permute-done.2
  11.9 0.3 %east.1 = (f32[128,128]{1,0:T(8,128)S(1)}, f32[32,128]{1,0:T(8,128)S(1)}, f32[48,128]{1,0:T(8,128)S(1)}) custom-call(f32[2048,128]{1,0:T(8,128)S(1)} %get-tuple-element.53.strips, f32[128,128]{1,0:T(8,128)S(1)} %get-tuple-element.49.nu, bf16[64,192]{1,0:T(8,128)(2,1)S(1)} %get-tuple-element.50.weights, f32[64,128]{1,0:T(8,128)S(1)} %get-tuple-element.64.half_lanes, ...), custom_call_target="tpu_custom_call" | custom-call | flops 67108864 | bytes 2097152 | tf_op jit(solution)/shard_map/east/pallas_call | solution.py:476
  12.2 1.2 %collective-permute-start.5 = (f32[48,128]{1,0:T(8,128)S(1)}, f32[48,128]{1,0:T(8,128)S(1)}, u32[]{:S(2)}, u32[]{:S(2)}) collective-permute-start(f32[48,128]{1,0:T(8,128)S(1)} %get-tuple-element.78), channel_id=1, source_target_pairs={{0,1},{1,0},{2,3},{3,2},{4,5},{5,4},{6,7},{7,6},{8,9},{9,8},{10,11... | collective-permute-start | bytes 73736 | tf_op jit(solution)/shard_map/ppermute | solution.py:439
  13.4 0.0 collective-permute-done.3.rest_0_
  13.4 0.4 %meet.1 = (f32[64,128]{1,0:T(8,128)S(1)}, f32[64,128]{1,0:T(8,128)S(1)}, f32[40,128]{1,0:T(8,128)S(1)}) custom-call(bf16[64,192]{1,0:T(8,128)(2,1)S(1)} %get-tuple-element.50.weights, f32[64,128]{1,0:T(8,128)S(1)} %get-tuple-element.68.own_mer, f32[32,128]{1,0:T(8,128)S(1)} %get-tuple-element.69.half_surface, ...), custom_call_target="tpu_custom_call" | custom-call | flops 8589934592 | bytes 2097152 | tf_op jit(solution)/shard_map/meet/pallas_call | solution.py:480
  13.7 0.0 collective-permute-start.4
  13.7 1.2 %again.1.partial = f32[2048,128]{1,0:T(8,128)S(1)} custom-call(f32[2048,128]{1,0:T(8,128)S(1)} %get-tuple-element.52.partial, f32[2048,128]{1,0:T(8,128)S(1)} %get-tuple-element.53.strips, f32[128,128]{1,0:T(8,128)S(1)} %get-tuple-element.49.nu, bf16[64,192]{1,0:T(8,128)(2,1)S(1)} %get-tuple-element.50.weights, f32[64,128]{1,0:T(8,128)S(1)} %get-tuple-element.54.spread, ...), custom_call_target="tpu_custom_call" | custom-call | flops 1024 | bytes 1024 | tf_op jit(solution)/shard_map/again/pallas_call | solution.py:484
  15.0 0.0 collective-permute-done.4.other
  15.0 0.5 %sides.1 = (f32[256,128]{1,0:T(8,128)S(1)}, f32[32,128]{1,0:T(8,128)S(1)}, f32[64,128]{1,0:T(8,128)S(1)}, f32[64,128]{1,0:T(8,128)S(1)}) custom-call(f32[2048,128]{1,0:T(8,128)S(1)} %get-tuple-element.48.columns, f32[2048,128]{1,0:T(8,128)S(1)} %get-tuple-element.53.strips, f32[128,128]{1,0:T(8,128)S(1)} %get-tuple-element.49.nu, ...), custom_call_target="tpu_custom_call" | custom-call | flops 1024 | bytes 1024 | tf_op jit(solution)/shard_map/sides/pallas_call | solution.py:487
  15.5 0.6 %collective-permute-done.5.rest_0_ = f32[48,128]{1,0:T(8,128)S(1)} collective-permute-done((f32[48,128]{1,0:T(8,128)S(1)}, f32[48,128]{1,0:T(8,128)S(1)}, u32[]{:S(2)}, u32[]{:S(2)}) %collective-permute-start.5) | collective-permute-done | bytes 24608 | tf_op jit(solution)/shard_map/ppermute | solution.py:439
  16.0 1.8 %last.1 = f32[2,64,16,128]{3,2,1,0:T(8,128)} custom-call(f32[2048,128]{1,0:T(8,128)S(1)} %again.1.partial, f32[256,128]{1,0:T(8,128)S(1)} %get-tuple-element.73.edges, f32[32,128]{1,0:T(8,128)S(1)} %get-tuple-element.74.incr, bf16[64,192]{1,0:T(8,128)(2,1)S(1)} %get-tuple-element.50.weights, f32[64,128]{1,0:T(8,128)S(1)} %get-tuple-element.54.spread, ...), custom_call_target="tpu_custom_call" | custom-call | flops 67108864 | bytes 2097152 | tf_op jit(solution)/shard_map/last/pallas_call | solution.py:490
  (3 shorter events, 0.1 us)
Async XLA Ops:
  0.0 7.6 %copy-start = (f32[1,2,64,16,128]{4,3,2,1,0:T(8,128)S(1)}, f32[1,2,64,16,128]{4,3,2,1,0:T(8,128)}, u32[]{:S(2)}) copy-start(f32[1,2,64,16,128]{4,3,2,1,0:T(8,128)} %param.7) | copy-start | bytes 3145732
  1.3 8.7 %collective-permute-start = (f32[32,128]{1,0:T(8,128)S(1)}, f32[32,128]{1,0:T(8,128)S(1)}, u32[]{:S(2)}, u32[]{:S(2)}) collective-permute-start(f32[32,128]{1,0:T(8,128)S(1)} %bitcast.13), channel_id=1, source_target_pairs={{0,16},{16,0},{1,17},{17,1},{2,18},{18,2},{3,19},{19,3},{4,20},{20... | collective-permute-start | bytes 49160 | tf_op jit(solution)/shard_map/ppermute | solution.py:448
  1.9 9.7 %collective-permute-start.1 = (f16[384,128]{1,0:T(8,128)(2,1)S(1)}, f16[384,128]{1,0:T(8,128)(2,1)S(1)}, u32[]{:S(2)}, u32[]{:S(2)}) collective-permute-start(f16[384,128]{1,0:T(8,128)(2,1)S(1)} %bitcast.17), channel_id=1, source_target_pairs={{0,2},{2,4},{4,6},{6,8},{8,10},{10,12},{12,14},{14,0},{1,3},{3,5},... | collective-permute-start | bytes 294920 | tf_op jit(solution)/shard_map/ppermute | solution.py:442
  4.5 7.4 %collective-permute-start.2 = (f16[384,128]{1,0:T(8,128)(2,1)S(1)}, f16[384,128]{1,0:T(8,128)(2,1)S(1)}, u32[]{:S(2)}, u32[]{:S(2)}) collective-permute-start(f16[384,128]{1,0:T(8,128)(2,1)S(1)} %bitcast.16), channel_id=1, source_target_pairs={{0,14},{2,0},{4,2},{6,4},{8,6},{10,8},{12,10},{14,12},{1,15},{3,1}... | collective-permute-start | bytes 294920 | tf_op jit(solution)/shard_map/ppermute | solution.py:442
  8.3 5.0 %collective-permute-start.3 = (f32[64,128]{1,0:T(8,128)S(1)}, f32[64,128]{1,0:T(8,128)S(1)}, u32[]{:S(2)}, u32[]{:S(2)}) collective-permute-start(f32[64,128]{1,0:T(8,128)S(1)} %get-tuple-element.68.own_mer), channel_id=1, source_target_pairs={{0,1},{1,0},{2,3},{3,2},{4,5},{5,4},{6,7},{7,6},{8,9},{9,8},{10,11... | collective-permute-start | bytes 98312 | tf_op jit(solution)/shard_map/ppermute | solution.py:439
  12.2 3.9 %collective-permute-start.5 = (f32[48,128]{1,0:T(8,128)S(1)}, f32[48,128]{1,0:T(8,128)S(1)}, u32[]{:S(2)}, u32[]{:S(2)}) collective-permute-start(f32[48,128]{1,0:T(8,128)S(1)} %get-tuple-element.78), channel_id=1, source_target_pairs={{0,1},{1,0},{2,3},{3,2},{4,5},{5,4},{6,7},{7,6},{8,9},{9,8},{10,11... | collective-permute-start | bytes 73736 | tf_op jit(solution)/shard_map/ppermute | solution.py:439
  13.7 1.3 %collective-permute-start.4 = (f32[40,128]{1,0:T(8,128)S(1)}, f32[40,128]{1,0:T(8,128)S(1)}, u32[]{:S(2)}, u32[]{:S(2)}) collective-permute-start(f32[40,128]{1,0:T(8,128)S(1)} %get-tuple-element.72.own), channel_id=1, source_target_pairs={{0,16},{16,0},{1,17},{17,1},{2,18},{18,2},{3,19},{19,3},{4,20},{20... | collective-permute-start | bytes 61448 | tf_op jit(solution)/shard_map/ppermute | solution.py:448

commit v14 on v13

--- a/solution.py
+++ b/solution.py
@@ -242,34 +242,23 @@
     return fresh
 
 
-def west_kernel(dims, strips, nu, weights, spread, edge_lanes, rows, guide, own, other, from_west, solved, incr, half_lanes, surface):
+def join_kernel(dims, strips, nu, weights, spread, edge_lanes, rows, guide, own, other, from_west, from_east, west_solved, east_solved, incr, surface, *send_mer):
     tracers, levels, width = dims
     total = tracers * width
     lane = lanes_of(levels)
-    terms = side_terms(from_west, False, strips, nu, dims)
+    terms = side_terms(from_west, False, strips, nu, dims) + side_terms(from_east, True, strips, nu, dims)
     result = product(weights[...], jnp.concatenate(terms, axis=1))
     flux = increments(own[...], other[...], guide, tracers, width)
     incr[...] = flux
-    for t in range(tracers):
-        solved[t * levels:(t + 1) * levels, :] = result[:, t * 128:(t + 1) * 128]
     row = lax.broadcasted_iota(jnp.int32, (total, 128), 0)
     rows_lane = lax.broadcasted_iota(jnp.int32, (total, 128), 1)
     turned = pltpu.roll(flux, 1, 1, stride=2, stride_axis=0)
     turned = jnp.sum(jnp.where(rows_lane // 2 == row, turned, 0.0), axis=0, keepdims=True)
-    half_lanes[...] = side_lanes(edge_lanes[...] + spread[...] * turned, False, solved, lane, dims)
-    level = surface_level(levels)
-    fresh = rows[...] + spread[pl.ds(level, 1), :] * flux
-    surface[...] = side_rows(fresh, False, solved, row, level, dims)
-
-
-def east_kernel(dims, strips, nu, weights, half_lanes, half_surface, from_west, from_east, solved, surface, *send_mer):
-    tracers, levels, width = dims
-    total = tracers * width
-    lane = lanes_of(levels)
-    result = product(weights[...], jnp.concatenate(side_terms(from_east, True, strips, nu, dims), axis=1))
+    packed = edge_lanes[...] + spread[...] * turned
     for t in range(tracers):
-        solved[t * levels:(t + 1) * levels, :] = result[:, t * 128:(t + 1) * 128]
-    packed = side_lanes(half_lanes[...], True, solved, lane, dims)
+        west_solved[t * levels:(t + 1) * levels, :] = result[:, t * 128:(t + 1) * 128]
+        east_solved[t * levels:(t + 1) * levels, :] = result[:, (tracers + t) * 128:(tracers + t + 1) * 128]
+    packed = side_lanes(side_lanes(packed, False, west_solved, lane, dims), True, east_solved, lane, dims)
     place = lax.axis_index("mer")
     for r, ref in enumerate(send_mer):
         up = lax.rem(place + 1 + r, 2)
@@ -281,8 +270,10 @@
                 message = jnp.where(lane == 2 * at + up, moved, message)
         ref[:levels // 2, :] = fold(message)
         ref[levels // 2:, :] = jnp.zeros((ref.shape[0] - levels // 2, 128), f32)
-    row = lax.broadcasted_iota(jnp.int32, (total, 128), 0)
-    surface[...] = side_rows(half_surface[...], True, solved, row, surface_level(levels), dims)
+    level = surface_level(levels)
+    fresh = rows[...] + spread[pl.ds(level, 1), :] * flux
+    fresh = side_rows(fresh, False, west_solved, row, level, dims)
+    surface[...] = side_rows(fresh, True, east_solved, row, level, dims)
 
 
 def meet_kernel(dims, mer_count, weights, own_mer, half_surface, from_west, from_east, *rest):
@@ -304,7 +295,6 @@
     line = jnp.take_along_axis(line, 2 * row + (rows_lane == 0).astype(jnp.int32), axis=1)
     rim = jnp.logical_or(rows_lane == 127, rows_lane == 0)
     surface[:total, :] = half_surface[...] + jnp.where(rim, line, 0.0)
-    surface[total:, :] = jnp.zeros((surface.shape[0] - total, 128), f32)
     level = surface_level(levels)
     for s, cells in enumerate((from_west, from_east)):
         for t in range(tracers):
@@ -430,7 +420,7 @@
     message = shape((2 * tracers + 2) * levels)
     blocks = jax.ShapeDtypeStruct((2 * tracers + 2, levels, wide), f32)
     packed = shape(levels)
-    folded = shape(levels // 2 + 16)
+    folded = shape(levels // 2 + 8)
     kept = shape(tracers * size)
     halved = shape(tracers * levels)
     sided = shape(2 * tracers * levels)
@@ -468,17 +458,14 @@
     partial, strips, edge_lanes, rows = call(
         functools.partial(inner_kernel, dims), "inner", [VM] * 5, [kept, shape(2 * size), packed, shape(total)], 1 << 30,
     )(columns, frame, nu, weights, other)
-    west_solved, incr, half_lanes, half_surface = call(
-        functools.partial(west_kernel, dims), "west", [VM] * 10, [halved, shape(total), packed, shape(total)], 1 << 33,
-    )(strips, nu, weights, spread, edge_lanes, rows, guide, surface, other, from_west)
-    from_east, half_lanes = lax.optimization_barrier((from_east, half_lanes))
+    from_east, from_west = lax.optimization_barrier((from_east, from_west))
     from_east = widen(from_east)
-    east_solved, half_surface, *send_mer = call(
-        functools.partial(east_kernel, dims), "east", [VM] * 7, [halved, shape(total)] + [folded] * rounds, 1 << 26,
-    )(strips, nu, weights, half_lanes, half_surface, from_west, from_east)
+    west_solved, east_solved, incr, half_surface, *send_mer = call(
+        functools.partial(join_kernel, dims), "join", [VM] * 11, [halved, halved, shape(total), shape(total)] + [folded] * rounds, 1 << 33,
+    )(strips, nu, weights, spread, edge_lanes, rows, guide, surface, other, from_west, from_east)
     recv_again = swap_mer(send_mer)
     lanes, beyond, fresh_surface = call(
-        functools.partial(meet_kernel, dims, mer_count), "meet", [VM] * (5 + rounds), [packed, packed, shape(total + 8)], 1 << 33,
+        functools.partial(meet_kernel, dims, mer_count), "meet", [VM] * (5 + rounds), [packed, packed, shape(total + 2 * tracers)], 1 << 33,
     )(weights, own_mer, half_surface, from_west, from_east, *recv_mer)
     fresh_other = swap_fluid(fresh_surface)
     again = call(

time: 18 us -> 17.7 us (0.983)
  waiting for transfers between devices: 0.57 us -> 0.26 us
  starting transfers between devices: 9.09 us -> 9.34 us
  Pallas kernels: 8.02 us -> 7.82 us
    ppermute x2, waiting for transfers between devices: 0.56 us -> 0.25 us  [swap_mer(): lax.ppermute(piece, 'mer', pairs(mer_count, r == 1))]
    ppermute x2, starting transfers between devices: 2.9 us -> 3.15 us  [swap_mer(): lax.ppermute(piece, 'mer', pairs(mer_count, r == 1))]
    pallas_call x2 -> x1, Pallas kernels: 0.54 us -> 0.34 us  [on_device(): call(functools.partial(join_kernel, dims), 'join', [VM] * 11, [halved, ha...]
where the time goes in v14:
time: 17.7 us; the launch traced here: 17.6 us
  starting transfers between devices  9.34 us (53%)
  Pallas kernels  7.82 us (44%)
  waiting for transfers between devices  0.26 us (1%)
    ppermute x2, starting transfers between devices, shift_zonal(): return lax.ppermute(piece, 'zon', ring(zon_count, ahead))  5.66 us
    ppermute x2, starting transfers between devices, swap_mer(): lax.ppermute(piece, 'mer', pairs(mer_count, r == 1))  3.15 us
    pallas_call x1, Pallas kernels, on_device(): call(functools.partial(last_kernel, dims, mer_count), 'last', [VM] * (9 +...  1.81 us
    pallas_call x1, Pallas kernels, on_device(): call(functools.partial(inner_kernel, dims), 'inner', [VM] * 5, [kept, sha...  1.49 us
    pallas_call x1, Pallas kernels, on_device(): call(functools.partial(pack_kernel, dims), 'pack', [HB] * len(in_hbm), [b...  1.33 us
    pallas_call x1, Pallas kernels, on_device(): call(functools.partial(again_kernel, dims), 'again', [VM] * 9, kept, 1 <<...  1.23 us
    pallas_call x1, Pallas kernels, on_device(): call(functools.partial(lanes_kernel, dims), 'lanes', [VM] * 7, [kept, pac...  0.75 us
    ppermute x2, starting transfers between devices, swap_fluid(): return lax.ppermute(piece, 'fluid', [(0, 1), (1, 0)])  0.53 us
  transfers between devices with their start and end apart: 6, of which 1 were waited for; matrix products, arithmetic and copies ran while one was open for 0% of the time, Pallas kernels for 27%

profile of v14, /device:TPU:0, one launch (start us, length us, event | category | flops | bytes accessed | tf_op | source)
XLA Modules:
  0.0 17.6 jit_solution(13861356899365461387)
XLA Ops:
  0.0 0.0 copy-start
  0.0 1.3 %pack.1 = (f32[6,64,128]{2,1,0:T(8,128)S(1)}, f32[6,64,128]{2,1,0:T(8,128)S(1)}, f32[2,16,128]{2,1,0:T(8,128)S(1)}, f32[2048,128]{1,0:T(8,128)S(1)}, f32[2,64]{1...) custom-call(f32[2,64,16,128]{3,2,1,0:T(8,128)} %bitcast.11, ...), custom_call_target="tpu_custom_call" | custom-call | flops 1048576 | bytes 2097152 | tf_op jit(solution)/shard_map/pack/pallas_call | solution.py:442
  1.3 0.5 %collective-permute-start = (f32[32,128]{1,0:T(8,128)S(1)}, f32[32,128]{1,0:T(8,128)S(1)}, u32[]{:S(2)}, u32[]{:S(2)}) collective-permute-start(f32[32,128]{1,0:T(8,128)S(1)} %bitcast.13), channel_id=1, source_target_pairs={{0,16},{16,0},{1,17},{17,1},{2,18},{18,2},{3,19},{19,3},{4,20},{20... | collective-permute-start | bytes 49160 | tf_op jit(solution)/shard_map/ppermute | solution.py:438
  1.9 2.6 %collective-permute-start.2 = (f16[384,128]{1,0:T(8,128)(2,1)S(1)}, f16[384,128]{1,0:T(8,128)(2,1)S(1)}, u32[]{:S(2)}, u32[]{:S(2)}) collective-permute-start(f16[384,128]{1,0:T(8,128)(2,1)S(1)} %bitcast.17), channel_id=1, source_target_pairs={{0,2},{2,4},{4,6},{6,8},{8,10},{10,12},{12,14},{14,0},{1,3},{3,5},... | collective-permute-start | bytes 294920 | tf_op jit(solution)/shard_map/ppermute | solution.py:432
  4.5 3.1 %collective-permute-start.1 = (f16[384,128]{1,0:T(8,128)(2,1)S(1)}, f16[384,128]{1,0:T(8,128)(2,1)S(1)}, u32[]{:S(2)}, u32[]{:S(2)}) collective-permute-start(f16[384,128]{1,0:T(8,128)(2,1)S(1)} %bitcast.16), channel_id=1, source_target_pairs={{0,14},{2,0},{4,2},{6,4},{8,6},{10,8},{12,10},{14,12},{1,15},{3,1}... | collective-permute-start | bytes 294920 | tf_op jit(solution)/shard_map/ppermute | solution.py:432
  7.6 0.0 copy-done
  7.6 0.8 %lanes.1 = (f32[2048,128]{1,0:T(8,128)S(1)}, f32[64,128]{1,0:T(8,128)S(1)}, f32[128,128]{1,0:T(8,128)S(1)}, bf16[64,192]{1,0:T(8,128)(2,1)S(1)}, f32[64,128]{1,0:T(8,128)S(1)}, /*index=5*/f32[8,128]{1,0:T(8,128)S(1)}) custom-call(f32[2048,128]{1,0:T(8,128)S(1)} %bitcast.12, f32[2048,128]{1,0:T(8,128)S(1)} %get-tuple-element.40.frame, ...), custom_call_target="tpu_custom_call" | custom-call | flops 1048576 | bytes 2097152 | tf_op jit(solution)/shard_map/lanes/pallas_call | solution.py:451
  8.3 1.7 %collective-permute-start.3 = (f32[64,128]{1,0:T(8,128)S(1)}, f32[64,128]{1,0:T(8,128)S(1)}, u32[]{:S(2)}, u32[]{:S(2)}) collective-permute-start(f32[64,128]{1,0:T(8,128)S(1)} %get-tuple-element.64.own_mer), channel_id=1, source_target_pairs={{0,1},{1,0},{2,3},{3,2},{4,5},{5,4},{6,7},{7,6},{8,9},{9,8},{10,11... | collective-permute-start | bytes 98312 | tf_op jit(solution)/shard_map/ppermute | solution.py:429
  10.1 0.0 collective-permute-done.other
  10.1 1.5 %inner.1 = (f32[2048,128]{1,0:T(8,128)S(1)}, f32[2048,128]{1,0:T(8,128)S(1)}, f32[64,128]{1,0:T(8,128)S(1)}, f32[32,128]{1,0:T(8,128)S(1)}) custom-call(f32[2048,128]{1,0:T(8,128)S(1)} %get-tuple-element.46.columns, f32[2048,128]{1,0:T(8,128)S(1)} %get-tuple-element.40.frame, f32[128,128]{1,0:T(8,128)S(1)} %get-tuple-element.47.nu, ...), custom_call_target="tpu_custom_call" | custom-call | flops 1073741824 | bytes 2097152 | tf_op jit(solution)/shard_map/inner/pallas_call | solution.py:458
  11.6 0.0 collective-permute-done.2
  11.6 0.0 collective-permute-done.1
  11.6 0.3 %join.1 = (f32[128,128]{1,0:T(8,128)S(1)}, f32[128,128]{1,0:T(8,128)S(1)}, f32[32,128]{1,0:T(8,128)S(1)}, f32[32,128]{1,0:T(8,128)S(1)}, f32[40,128]{1,0:T(8,128)S(1)}) custom-call(f32[2048,128]{1,0:T(8,128)S(1)} %get-tuple-element.51.strips, f32[128,128]{1,0:T(8,128)S(1)} %get-tuple-element.47.nu, bf16[64,192]{1,0:T(8,128)(2,1)S(1)} %get-tuple-element.48.weights, ...), custom_call_target="tpu_custom_call" | custom-call | flops 8589934592 | bytes 2097152 | tf_op jit(solution)/shard_map/join/pallas_call | solution.py:463
  12.0 1.4 %collective-permute-start.5 = (f32[40,128]{1,0:T(8,128)S(1)}, f32[40,128]{1,0:T(8,128)S(1)}, u32[]{:S(2)}, u32[]{:S(2)}) collective-permute-start(f32[40,128]{1,0:T(8,128)S(1)} %get-tuple-element.74), channel_id=1, source_target_pairs={{0,1},{1,0},{2,3},{3,2},{4,5},{5,4},{6,7},{7,6},{8,9},{9,8},{10,11... | collective-permute-start | bytes 61448 | tf_op jit(solution)/shard_map/ppermute | solution.py:429
  13.4 0.0 collective-permute-done.3.rest_0_
  13.4 0.4 %meet.1 = (f32[64,128]{1,0:T(8,128)S(1)}, f32[64,128]{1,0:T(8,128)S(1)}, f32[36,128]{1,0:T(8,128)S(1)}) custom-call(bf16[64,192]{1,0:T(8,128)(2,1)S(1)} %get-tuple-element.48.weights, f32[64,128]{1,0:T(8,128)S(1)} %get-tuple-element.64.own_mer, f32[32,128]{1,0:T(8,128)S(1)} %get-tuple-element.65.half_surface, ...), custom_call_target="tpu_custom_call" | custom-call | flops 8589934592 | bytes 2097152 | tf_op jit(solution)/shard_map/meet/pallas_call | solution.py:467
  13.8 0.0 collective-permute-start.4
  13.8 1.2 %again.1.partial = f32[2048,128]{1,0:T(8,128)S(1)} custom-call(f32[2048,128]{1,0:T(8,128)S(1)} %get-tuple-element.50.partial, f32[2048,128]{1,0:T(8,128)S(1)} %get-tuple-element.51.strips, f32[128,128]{1,0:T(8,128)S(1)} %get-tuple-element.47.nu, bf16[64,192]{1,0:T(8,128)(2,1)S(1)} %get-tuple-element.48.weights, f32[64,128]{1,0:T(8,128)S(1)} %get-tuple-element.52.spread, ...), custom_call_target="tpu_custom_call" | custom-call | flops 1024 | bytes 1024 | tf_op jit(solution)/shard_map/again/pallas_call | solution.py:471
  15.0 0.0 collective-permute-done.4.other
  15.0 0.5 %sides.1 = (f32[256,128]{1,0:T(8,128)S(1)}, f32[32,128]{1,0:T(8,128)S(1)}, f32[64,128]{1,0:T(8,128)S(1)}, f32[64,128]{1,0:T(8,128)S(1)}) custom-call(f32[2048,128]{1,0:T(8,128)S(1)} %get-tuple-element.46.columns, f32[2048,128]{1,0:T(8,128)S(1)} %get-tuple-element.51.strips, f32[128,128]{1,0:T(8,128)S(1)} %get-tuple-element.47.nu, ...), custom_call_target="tpu_custom_call" | custom-call | flops 1024 | bytes 1024 | tf_op jit(solution)/shard_map/sides/pallas_call | solution.py:474
  15.5 0.2 %collective-permute-done.5.rest_0_ = f32[40,128]{1,0:T(8,128)S(1)} collective-permute-done((f32[40,128]{1,0:T(8,128)S(1)}, f32[40,128]{1,0:T(8,128)S(1)}, u32[]{:S(2)}, u32[]{:S(2)}) %collective-permute-start.5) | collective-permute-done | bytes 20512 | tf_op jit(solution)/shard_map/ppermute | solution.py:429
  15.8 1.8 %last.1 = f32[2,64,16,128]{3,2,1,0:T(8,128)} custom-call(f32[2048,128]{1,0:T(8,128)S(1)} %again.1.partial, f32[256,128]{1,0:T(8,128)S(1)} %get-tuple-element.69.edges, f32[32,128]{1,0:T(8,128)S(1)} %get-tuple-element.70.incr, bf16[64,192]{1,0:T(8,128)(2,1)S(1)} %get-tuple-element.48.weights, f32[64,128]{1,0:T(8,128)S(1)} %get-tuple-element.52.spread, ...), custom_call_target="tpu_custom_call" | custom-call | flops 67108864 | bytes 2097152 | tf_op jit(solution)/shard_map/last/pallas_call | solution.py:477
  (3 shorter events, 0.1 us)
Async XLA Ops:
  0.0 7.6 %copy-start = (f32[1,2,64,16,128]{4,3,2,1,0:T(8,128)S(1)}, f32[1,2,64,16,128]{4,3,2,1,0:T(8,128)}, u32[]{:S(2)}) copy-start(f32[1,2,64,16,128]{4,3,2,1,0:T(8,128)} %param.7) | copy-start | bytes 3145732
  1.3 8.7 %collective-permute-start = (f32[32,128]{1,0:T(8,128)S(1)}, f32[32,128]{1,0:T(8,128)S(1)}, u32[]{:S(2)}, u32[]{:S(2)}) collective-permute-start(f32[32,128]{1,0:T(8,128)S(1)} %bitcast.13), channel_id=1, source_target_pairs={{0,16},{16,0},{1,17},{17,1},{2,18},{18,2},{3,19},{19,3},{4,20},{20... | collective-permute-start | bytes 49160 | tf_op jit(solution)/shard_map/ppermute | solution.py:438
  1.9 9.7 %collective-permute-start.2 = (f16[384,128]{1,0:T(8,128)(2,1)S(1)}, f16[384,128]{1,0:T(8,128)(2,1)S(1)}, u32[]{:S(2)}, u32[]{:S(2)}) collective-permute-start(f16[384,128]{1,0:T(8,128)(2,1)S(1)} %bitcast.17), channel_id=1, source_target_pairs={{0,2},{2,4},{4,6},{6,8},{8,10},{10,12},{12,14},{14,0},{1,3},{3,5},... | collective-permute-start | bytes 294920 | tf_op jit(solution)/shard_map/ppermute | solution.py:432
  4.5 7.1 %collective-permute-start.1 = (f16[384,128]{1,0:T(8,128)(2,1)S(1)}, f16[384,128]{1,0:T(8,128)(2,1)S(1)}, u32[]{:S(2)}, u32[]{:S(2)}) collective-permute-start(f16[384,128]{1,0:T(8,128)(2,1)S(1)} %bitcast.16), channel_id=1, source_target_pairs={{0,14},{2,0},{4,2},{6,4},{8,6},{10,8},{12,10},{14,12},{1,15},{3,1}... | collective-permute-start | bytes 294920 | tf_op jit(solution)/shard_map/ppermute | solution.py:432
  8.3 5.1 %collective-permute-start.3 = (f32[64,128]{1,0:T(8,128)S(1)}, f32[64,128]{1,0:T(8,128)S(1)}, u32[]{:S(2)}, u32[]{:S(2)}) collective-permute-start(f32[64,128]{1,0:T(8,128)S(1)} %get-tuple-element.64.own_mer), channel_id=1, source_target_pairs={{0,1},{1,0},{2,3},{3,2},{4,5},{5,4},{6,7},{7,6},{8,9},{9,8},{10,11... | collective-permute-start | bytes 98312 | tf_op jit(solution)/shard_map/ppermute | solution.py:429
  12.0 3.8 %collective-permute-start.5 = (f32[40,128]{1,0:T(8,128)S(1)}, f32[40,128]{1,0:T(8,128)S(1)}, u32[]{:S(2)}, u32[]{:S(2)}) collective-permute-start(f32[40,128]{1,0:T(8,128)S(1)} %get-tuple-element.74), channel_id=1, source_target_pairs={{0,1},{1,0},{2,3},{3,2},{4,5},{5,4},{6,7},{7,6},{8,9},{9,8},{10,11... | collective-permute-start | bytes 61448 | tf_op jit(solution)/shard_map/ppermute | solution.py:429
  13.8 1.3 %collective-permute-start.4 = (f32[36,128]{1,0:T(8,128)S(1)}, f32[36,128]{1,0:T(8,128)S(1)}, u32[]{:S(2)}, u32[]{:S(2)}) collective-permute-start(f32[36,128]{1,0:T(8,128)S(1)} %get-tuple-element.68.own), channel_id=1, source_target_pairs={{0,16},{16,0},{1,17},{17,1},{2,18},{18,2},{3,19},{19,3},{4,20},{20... | collective-permute-start | bytes 55304 | tf_op jit(solution)/shard_map/ppermute | solution.py:438

commit v15 on v14

--- a/solution.py
+++ b/solution.py
@@ -169,7 +169,15 @@
         copy.wait()
 
 
-def lanes_kernel(dims, cells, frame, diffusion, solve, rate, block_map, ice_mask, columns, send_mer, nu, weights, spread, guide):
+def lay_out(dims, frame, strips):
+    tracers, levels, width = dims
+    for k in range(2):
+        for x in range(width):
+            value = frame[pl.ds(k * levels * width + x, levels, stride=width), :]
+            strips[(k * width + x) * levels:(k * width + x + 1) * levels, :] = value
+
+
+def lanes_kernel(dims, cells, frame, diffusion, solve, rate, block_map, ice_mask, columns, send_mer, nu, weights, spread, guide, strips):
     tracers, levels, width = dims
     size = levels * width
     lane = lanes_of(levels)
@@ -197,14 +205,18 @@
     fill_guide(guide, rate, block_map, ice_mask, tracers)
     spread[...] = jnp.broadcast_to(jnp.sum(jnp.where(at_level, solve[...], 0.0), axis=1, keepdims=True), (levels, 128))
 
-
-def inner_kernel(dims, columns, frame, nu, weights, other, partial, strips, edge_lanes, rows):
-    tracers, levels, width = dims
-    lane = lanes_of(levels)
-    for k in range(2):
-        for x in range(width):
-            value = frame[pl.ds((k * levels * width) + x, levels, stride=width), :]
-            strips[(k * width + x) * levels:(k * width + x + 1) * levels, :] = value
+    @pl.when(lax.rem(lax.axis_index("mer"), 2) == 0)
+    def _():
+        lay_out(dims, frame, strips)
+
+
+def inner_kernel(dims, columns, frame, nu, weights, other, _, partial, strips, edge_lanes, rows):
+    tracers, levels, width = dims
+    lane = lanes_of(levels)
+
+    @pl.when(lax.rem(lax.axis_index("mer"), 2) == 1)
+    def _():
+        lay_out(dims, frame, strips)
 
     def store(t, x, value):
         j = t * width + x
@@ -396,7 +408,7 @@
 HB = pl.BlockSpec(memory_space=pltpu.HBM)
 
 
-def call(body, name, in_specs, out_shape, flops, out_specs=None, scratch=(), touched=2 << 20):
+def call(body, name, in_specs, out_shape, flops, out_specs=None, scratch=(), touched=2 << 20, aliases=None):
     many = isinstance(out_shape, list)
     return pl.pallas_call(
         body,
@@ -405,6 +417,7 @@
         out_specs=out_specs or ([VM] * len(out_shape) if many else VM),
         scratch_shapes=scratch,
         name=name,
+        input_output_aliases=aliases or {},
         cost_estimate=pl.CostEstimate(flops=flops, bytes_accessed=touched, transcendentals=0),
         compiler_params=pltpu.CompilerParams(vmem_limit_bytes=32 * 1024 * 1024),
     )
@@ -448,16 +461,18 @@
     east_bound, west_bound, surface = (value.reshape(-1, wide) for value in (east_bound, west_bound, surface))
     east_bound, west_bound = lax.optimization_barrier(((east_bound * SCALE).astype(jnp.float16), (west_bound * SCALE).astype(jnp.float16)))
     from_west = widen(shift_zonal(east_bound, 1))
-    columns, own_mer, nu, weights, spread, guide = call(
+    columns, own_mer, nu, weights, spread, guide, strips = call(
         functools.partial(lanes_kernel, dims), "lanes", [VM] * 7,
-        [kept, packed, shape(tracers * levels), jax.ShapeDtypeStruct((levels, 3 * levels), bf16), packed, shape(8)], 1 << 20,
+        [kept, packed, shape(tracers * levels), jax.ShapeDtypeStruct((levels, 3 * levels), bf16), packed, shape(8), shape(2 * size)],
+        1 << 20,
     )(state.reshape(tracers * size, wide), frame, *params)
     recv_mer = swap_mer([own_mer] * rounds)
     other = swap_fluid(surface)
     from_east = shift_zonal(west_bound, -1)
     partial, strips, edge_lanes, rows = call(
-        functools.partial(inner_kernel, dims), "inner", [VM] * 5, [kept, shape(2 * size), packed, shape(total)], 1 << 30,
-    )(columns, frame, nu, weights, other)
+        functools.partial(inner_kernel, dims), "inner", [VM] * 6, [kept, shape(2 * size), packed, shape(total)], 1 << 30,
+        aliases={5: 1},
+    )(columns, frame, nu, weights, other, strips)
     from_east, from_west = lax.optimization_barrier((from_east, from_west))
     from_east = widen(from_east)
     west_solved, east_solved, incr, half_surface, *send_mer = call(

time: 17.7 us -> 17.6 us (level)
    pallas_call x1, Pallas kernels: 1.49 us -> 1.19 us  [on_device(): call(functools.partial(inner_kernel, dims), 'inner', [VM] * 6, [kept, sha...]
    pallas_call x1, Pallas kernels: 0.75 us -> 1.05 us  [on_device(): call(functools.partial(lanes_kernel, dims), 'lanes', [VM] * 7, [kept, pac...]
    ppermute x2, waiting for transfers between devices: 0.01 us -> 0.2 us  [shift_zonal(): return lax.ppermute(piece, 'zon', ring(zon_count, ahead))]
  transfers between devices with their start and end apart: 6 -> 6, of which waited for: 1 -> 2; matrix products, arithmetic and copies ran while one was open for 0% -> 0% of each run, Pallas kernels for 27% -> 27%
where the time goes in v15:
time: 17.6 us; the launch traced here: 17.5 us
  starting transfers between devices  9.17 us (52%)
  Pallas kernels  7.8 us (44%)
  waiting for transfers between devices  0.35 us (2%)
    ppermute x2, starting transfers between devices, shift_zonal(): return lax.ppermute(piece, 'zon', ring(zon_count, ahead))  5.66 us
    ppermute x2, starting transfers between devices, swap_mer(): lax.ppermute(piece, 'mer', pairs(mer_count, r == 1))  2.98 us
    pallas_call x1, Pallas kernels, on_device(): call(functools.partial(last_kernel, dims, mer_count), 'last', [VM] * (9 +...  1.81 us
    pallas_call x1, Pallas kernels, on_device(): call(functools.partial(pack_kernel, dims), 'pack', [HB] * len(in_hbm), [b...  1.33 us
    pallas_call x1, Pallas kernels, on_device(): call(functools.partial(again_kernel, dims), 'again', [VM] * 9, kept, 1 <<...  1.21 us
    pallas_call x1, Pallas kernels, on_device(): call(functools.partial(inner_kernel, dims), 'inner', [VM] * 6, [kept, sha...  1.19 us
    pallas_call x1, Pallas kernels, on_device(): call(functools.partial(lanes_kernel, dims), 'lanes', [VM] * 7, [kept, pac...  1.05 us
    ppermute x2, starting transfers between devices, swap_fluid(): return lax.ppermute(piece, 'fluid', [(0, 1), (1, 0)])  0.53 us
  transfers between devices with their start and end apart: 6, of which 2 were waited for; matrix products, arithmetic and copies ran while one was open for 0% of the time, Pallas kernels for 27%

profile of v15, /device:TPU:0, one launch (start us, length us, event | category | flops | bytes accessed | tf_op | source)
XLA Modules:
  0.0 17.5 jit_solution(2359895783600530473)
XLA Ops:
  0.0 0.0 copy-start
  0.0 1.3 %pack.1 = (f32[6,64,128]{2,1,0:T(8,128)S(1)}, f32[6,64,128]{2,1,0:T(8,128)S(1)}, f32[2,16,128]{2,1,0:T(8,128)S(1)}, f32[2048,128]{1,0:T(8,128)S(1)}, f32[2,64]{1...) custom-call(f32[2,64,16,128]{3,2,1,0:T(8,128)} %bitcast.11, ...), custom_call_target="tpu_custom_call" | custom-call | flops 1048576 | bytes 2097152 | tf_op jit(solution)/shard_map/pack/pallas_call | solution.py:455
  1.3 0.5 %collective-permute-start = (f32[32,128]{1,0:T(8,128)S(1)}, f32[32,128]{1,0:T(8,128)S(1)}, u32[]{:S(2)}, u32[]{:S(2)}) collective-permute-start(f32[32,128]{1,0:T(8,128)S(1)} %bitcast.13), channel_id=1, source_target_pairs={{0,16},{16,0},{1,17},{17,1},{2,18},{18,2},{3,19},{19,3},{4,20},{20... | collective-permute-start | bytes 49160 | tf_op jit(solution)/shard_map/ppermute | solution.py:451
  1.9 2.6 %collective-permute-start.2 = (f16[384,128]{1,0:T(8,128)(2,1)S(1)}, f16[384,128]{1,0:T(8,128)(2,1)S(1)}, u32[]{:S(2)}, u32[]{:S(2)}) collective-permute-start(f16[384,128]{1,0:T(8,128)(2,1)S(1)} %bitcast.17), channel_id=1, source_target_pairs={{0,2},{2,4},{4,6},{6,8},{8,10},{10,12},{12,14},{14,0},{1,3},{3,5},... | collective-permute-start | bytes 294920 | tf_op jit(solution)/shard_map/ppermute | solution.py:445
  4.5 3.1 %collective-permute-start.1 = (f16[384,128]{1,0:T(8,128)(2,1)S(1)}, f16[384,128]{1,0:T(8,128)(2,1)S(1)}, u32[]{:S(2)}, u32[]{:S(2)}) collective-permute-start(f16[384,128]{1,0:T(8,128)(2,1)S(1)} %bitcast.16), channel_id=1, source_target_pairs={{0,14},{2,0},{4,2},{6,4},{8,6},{10,8},{12,10},{14,12},{1,15},{3,1}... | collective-permute-start | bytes 294920 | tf_op jit(solution)/shard_map/ppermute | solution.py:445
  7.6 0.0 copy-done
  7.6 1.0 %lanes.1 = (f32[2048,128]{1,0:T(8,128)S(1)}, f32[64,128]{1,0:T(8,128)S(1)}, f32[128,128]{1,0:T(8,128)S(1)}, bf16[64,192]{1,0:T(8,128)(2,1)S(1)}, f32[64,128]{1,0...) custom-call(f32[2048,128]{1,0:T(8,128)S(1)} %bitcast.12, f32[2048,128]{1,0:T(8,128)S(1)} %get-tuple-element.41.frame, ...), custom_call_target="tpu_custom_call" | custom-call | flops 1048576 | bytes 2097152 | tf_op jit(solution)/shard_map/lanes/pallas_call | solution.py:464
  8.6 1.4 %collective-permute-start.3 = (f32[64,128]{1,0:T(8,128)S(1)}, f32[64,128]{1,0:T(8,128)S(1)}, u32[]{:S(2)}, u32[]{:S(2)}) collective-permute-start(f32[64,128]{1,0:T(8,128)S(1)} %get-tuple-element.66.own_mer), channel_id=1, source_target_pairs={{0,1},{1,0},{2,3},{3,2},{4,5},{5,4},{6,7},{7,6},{8,9},{9,8},{10,11... | collective-permute-start | bytes 98312 | tf_op jit(solution)/shard_map/ppermute | solution.py:442
  10.1 0.0 collective-permute-done.other
  10.1 1.2 %inner.1 = (f32[2048,128]{1,0:T(8,128)S(1)}, f32[2048,128]{1,0:T(8,128)S(1)}, f32[64,128]{1,0:T(8,128)S(1)}, f32[32,128]{1,0:T(8,128)S(1)}) custom-call(f32[2048,128]{1,0:T(8,128)S(1)} %get-tuple-element.47.columns, f32[2048,128]{1,0:T(8,128)S(1)} %get-tuple-element.41.frame, f32[128,128]{1,0:T(8,128)S(1)} %get-tuple-element.48.nu, ...), custom_call_target="tpu_custom_call", output_to_operand_aliasing={{1}: (5, {})} | custom-call | flops 1073741824 | bytes 2097152 | tf_op jit(solution)/shard_map/inner/pallas_call | solution.py:472
  11.3 0.0 collective-permute-done.2
  11.3 0.2 %collective-permute-done.1 = f16[384,128]{1,0:T(8,128)(2,1)S(1)} collective-permute-done((f16[384,128]{1,0:T(8,128)(2,1)S(1)}, f16[384,128]{1,0:T(8,128)(2,1)S(1)}, u32[]{:S(2)}, u32[]{:S(2)}) %collective-permute-start.1) | collective-permute-done | bytes 98336 | tf_op jit(solution)/shard_map/ppermute | solution.py:445
  11.5 0.3 %join.1 = (f32[128,128]{1,0:T(8,128)S(1)}, f32[128,128]{1,0:T(8,128)S(1)}, f32[32,128]{1,0:T(8,128)S(1)}, f32[32,128]{1,0:T(8,128)S(1)}, f32[40,128]{1,0:T(8,128)S(1)}) custom-call(f32[2048,128]{1,0:T(8,128)S(1)} %get-tuple-element.53.strips, f32[128,128]{1,0:T(8,128)S(1)} %get-tuple-element.48.nu, bf16[64,192]{1,0:T(8,128)(2,1)S(1)} %get-tuple-element.49.weights, ...), custom_call_target="tpu_custom_call" | custom-call | flops 8589934592 | bytes 2097152 | tf_op jit(solution)/shard_map/join/pallas_call | solution.py:478
  11.8 1.6 %collective-permute-start.5 = (f32[40,128]{1,0:T(8,128)S(1)}, f32[40,128]{1,0:T(8,128)S(1)}, u32[]{:S(2)}, u32[]{:S(2)}) collective-permute-start(f32[40,128]{1,0:T(8,128)S(1)} %get-tuple-element.76), channel_id=1, source_target_pairs={{0,1},{1,0},{2,3},{3,2},{4,5},{5,4},{6,7},{7,6},{8,9},{9,8},{10,11... | collective-permute-start | bytes 61448 | tf_op jit(solution)/shard_map/ppermute | solution.py:442
  13.4 0.0 collective-permute-done.3.rest_0_
  13.4 0.4 %meet.1 = (f32[64,128]{1,0:T(8,128)S(1)}, f32[64,128]{1,0:T(8,128)S(1)}, f32[36,128]{1,0:T(8,128)S(1)}) custom-call(bf16[64,192]{1,0:T(8,128)(2,1)S(1)} %get-tuple-element.49.weights, f32[64,128]{1,0:T(8,128)S(1)} %get-tuple-element.66.own_mer, f32[32,128]{1,0:T(8,128)S(1)} %get-tuple-element.67.half_surface, ...), custom_call_target="tpu_custom_call" | custom-call | flops 8589934592 | bytes 2097152 | tf_op jit(solution)/shard_map/meet/pallas_call | solution.py:482
  13.8 0.0 collective-permute-start.4
  13.8 1.2 %again.1.partial = f32[2048,128]{1,0:T(8,128)S(1)} custom-call(f32[2048,128]{1,0:T(8,128)S(1)} %get-tuple-element.52.partial, f32[2048,128]{1,0:T(8,128)S(1)} %get-tuple-element.53.strips, f32[128,128]{1,0:T(8,128)S(1)} %get-tuple-element.48.nu, bf16[64,192]{1,0:T(8,128)(2,1)S(1)} %get-tuple-element.49.weights, f32[64,128]{1,0:T(8,128)S(1)} %get-tuple-element.54.spread, ...), custom_call_target="tpu_custom_call" | custom-call | flops 1024 | bytes 1024 | tf_op jit(solution)/shard_map/again/pallas_call | solution.py:486
  15.0 0.0 collective-permute-done.4.other
  15.0 0.5 %sides.1 = (f32[256,128]{1,0:T(8,128)S(1)}, f32[32,128]{1,0:T(8,128)S(1)}, f32[64,128]{1,0:T(8,128)S(1)}, f32[64,128]{1,0:T(8,128)S(1)}) custom-call(f32[2048,128]{1,0:T(8,128)S(1)} %get-tuple-element.47.columns, f32[2048,128]{1,0:T(8,128)S(1)} %get-tuple-element.53.strips, f32[128,128]{1,0:T(8,128)S(1)} %get-tuple-element.48.nu, ...), custom_call_target="tpu_custom_call" | custom-call | flops 1024 | bytes 1024 | tf_op jit(solution)/shard_map/sides/pallas_call | solution.py:489
  15.5 0.1 collective-permute-done.5.rest_0_
  15.7 1.8 %last.1 = f32[2,64,16,128]{3,2,1,0:T(8,128)} custom-call(f32[2048,128]{1,0:T(8,128)S(1)} %again.1.partial, f32[256,128]{1,0:T(8,128)S(1)} %get-tuple-element.71.edges, f32[32,128]{1,0:T(8,128)S(1)} %get-tuple-element.72.incr, bf16[64,192]{1,0:T(8,128)(2,1)S(1)} %get-tuple-element.49.weights, f32[64,128]{1,0:T(8,128)S(1)} %get-tuple-element.54.spread, ...), custom_call_target="tpu_custom_call" | custom-call | flops 67108864 | bytes 2097152 | tf_op jit(solution)/shard_map/last/pallas_call | solution.py:492
  (3 shorter events, 0.1 us)
Async XLA Ops:
  0.0 7.6 %copy-start = (f32[1,2,64,16,128]{4,3,2,1,0:T(8,128)S(1)}, f32[1,2,64,16,128]{4,3,2,1,0:T(8,128)}, u32[]{:S(2)}) copy-start(f32[1,2,64,16,128]{4,3,2,1,0:T(8,128)} %param.7) | copy-start | bytes 3145732
  1.3 8.7 %collective-permute-start = (f32[32,128]{1,0:T(8,128)S(1)}, f32[32,128]{1,0:T(8,128)S(1)}, u32[]{:S(2)}, u32[]{:S(2)}) collective-permute-start(f32[32,128]{1,0:T(8,128)S(1)} %bitcast.13), channel_id=1, source_target_pairs={{0,16},{16,0},{1,17},{17,1},{2,18},{18,2},{3,19},{19,3},{4,20},{20... | collective-permute-start | bytes 49160 | tf_op jit(solution)/shard_map/ppermute | solution.py:451
  1.9 9.3 %collective-permute-start.2 = (f16[384,128]{1,0:T(8,128)(2,1)S(1)}, f16[384,128]{1,0:T(8,128)(2,1)S(1)}, u32[]{:S(2)}, u32[]{:S(2)}) collective-permute-start(f16[384,128]{1,0:T(8,128)(2,1)S(1)} %bitcast.17), channel_id=1, source_target_pairs={{0,2},{2,4},{4,6},{6,8},{8,10},{10,12},{12,14},{14,0},{1,3},{3,5},... | collective-permute-start | bytes 294920 | tf_op jit(solution)/shard_map/ppermute | solution.py:445
  4.5 7.0 %collective-permute-start.1 = (f16[384,128]{1,0:T(8,128)(2,1)S(1)}, f16[384,128]{1,0:T(8,128)(2,1)S(1)}, u32[]{:S(2)}, u32[]{:S(2)}) collective-permute-start(f16[384,128]{1,0:T(8,128)(2,1)S(1)} %bitcast.16), channel_id=1, source_target_pairs={{0,14},{2,0},{4,2},{6,4},{8,6},{10,8},{12,10},{14,12},{1,15},{3,1}... | collective-permute-start | bytes 294920 | tf_op jit(solution)/shard_map/ppermute | solution.py:445
  8.6 4.8 %collective-permute-start.3 = (f32[64,128]{1,0:T(8,128)S(1)}, f32[64,128]{1,0:T(8,128)S(1)}, u32[]{:S(2)}, u32[]{:S(2)}) collective-permute-start(f32[64,128]{1,0:T(8,128)S(1)} %get-tuple-element.66.own_mer), channel_id=1, source_target_pairs={{0,1},{1,0},{2,3},{3,2},{4,5},{5,4},{6,7},{7,6},{8,9},{9,8},{10,11... | collective-permute-start | bytes 98312 | tf_op jit(solution)/shard_map/ppermute | solution.py:442
  11.8 3.8 %collective-permute-start.5 = (f32[40,128]{1,0:T(8,128)S(1)}, f32[40,128]{1,0:T(8,128)S(1)}, u32[]{:S(2)}, u32[]{:S(2)}) collective-permute-start(f32[40,128]{1,0:T(8,128)S(1)} %get-tuple-element.76), channel_id=1, source_target_pairs={{0,1},{1,0},{2,3},{3,2},{4,5},{5,4},{6,7},{7,6},{8,9},{9,8},{10,11... | collective-permute-start | bytes 61448 | tf_op jit(solution)/shard_map/ppermute | solution.py:442
  13.8 1.2 %collective-permute-start.4 = (f32[36,128]{1,0:T(8,128)S(1)}, f32[36,128]{1,0:T(8,128)S(1)}, u32[]{:S(2)}, u32[]{:S(2)}) collective-permute-start(f32[36,128]{1,0:T(8,128)S(1)} %get-tuple-element.70.own), channel_id=1, source_target_pairs={{0,16},{16,0},{1,17},{17,1},{2,18},{18,2},{3,19},{19,3},{4,20},{20... | collective-permute-start | bytes 55304 | tf_op jit(solution)/shard_map/ppermute | solution.py:451
